TPU v7x, 32 devices: a whole 2x2x4 slice. The times are simulated.
32 devices in a mesh: cond: 4 (over x, core), ty: 4 (over z), tx: 2 (over y).
Axes of the slice: x: 2, y: 2, z: 4, core: 2. Of those that a mesh axis runs over, the one named last changes fastest.
Arguments:
- bed: float32 [1024, 2048], P('ty', 'tx'), may hold values from -4 to 4
- land_mask: int32 [1024, 2048], P('ty', 'tx'), may hold values 0 or 1
- cell_class: int32 [1024, 2048], P('ty', 'tx'), may hold values from 0 to 2
- weights: int32 [4], replicated, may hold values from 1 to 8
- cond_params: float32 [4, 4], P('cond'), may hold values from 0.25 to 2
- wave_stress: float32 [4, 2, 1024, 2048], P('cond', None, 'ty', 'tx'), may hold values from -0.6 to 0.6
- hydro_state: float32 [4, 3, 1024, 2048], P('cond', None, 'ty', 'tx'), may hold values from -1.8 to 1.8
Outputs:
- bed_next: float32 [1024, 2048], P('ty', 'tx')
- bed_change: float32 [1024, 2048], P('ty', 'tx')
- hydro_next: float32 [4, 3, 1024, 2048], P('cond', None, 'ty', 'tx')
All inputs are finite; a program needn't handle non-finite values. No bound on the sum of `land_mask` on one device may be relied on, other than what follows from the above.
Results may differ from a plain program's by a relative error of at most 0.00002.
Values sent between devices are 32-bit elements; how exact they have to be, the bound alone decides.
No kernel may reach another device: no remote copies, remote signals or barrier semaphores. Data moves between devices by JAX's collectives and lax.ppermute only.
A program may use at most 128 MiB of HBM per device.

v0:
```python
import functools

import jax
import jax.numpy as jnp
from jax import lax
from jax.experimental import pallas as pl
from jax.experimental.pallas import tpu as pltpu
from jax.sharding import PartitionSpec as P

STEPS = 3
HALO = STEPS + 1
SUB = 8
LANE = 128
FIELDS = 8
GROUP = HALO * FIELDS
FOLD = LANE // GROUP
LAG = 2
MIB = 2**20
ANY = pl.BlockSpec(memory_space=pl.ANY)
VMEM = pl.BlockSpec(memory_space=pltpu.VMEM)
SMEM = pl.BlockSpec(memory_space=pltpu.SMEM)


def rows_of(shape):
    return lax.broadcasted_iota(jnp.int32, shape, 0)


def lanes_of(shape):
    return lax.broadcasted_iota(jnp.int32, shape, 1)


def east(x):
    return pltpu.roll(x, x.shape[1] - 1, 1)


def west(x):
    return pltpu.roll(x, 1, 1)


def south(x, below):
    return pltpu.roll(jnp.where(rows_of(x.shape) == 0, below, x), SUB - 1, 0)


def north(x, above):
    return pltpu.roll(jnp.where(rows_of(x.shape) == SUB - 1, above, x), 1, 0)


def tile_at(index):
    if isinstance(index, int):
        return pl.ds(index * SUB, SUB)
    return pl.ds(pl.multiple_of(index * SUB, SUB), SUB)


def held(*arrays, space=pltpu.VMEM):
    return [pltpu.with_memory_space_constraint(x, space) for x in arrays]


def pack_kernel(bed, mask, kind, stress, hydro, up, down, side, ints, reals, int_side, real_side, sems):
    rows, cols = bed.shape
    at_left = lax.axis_index("tx") == 0
    off = pl.multiple_of(jnp.where(at_left, cols - LANE, 0), LANE)
    sources = [bed, mask, kind] + [stress.at[0, k] for k in range(2)] + [hydro.at[0, k] for k in range(3)]
    slots = [(reals, real_side, 0), (ints, int_side, 0), (ints, int_side, 1)] + [
        (reals, real_side, k) for k in range(1, 6)
    ]
    strips, edges = [], []
    for f, (src, (edge, strip, k)) in enumerate(zip(sources, slots)):
        strips.append(pltpu.make_async_copy(src.at[:, pl.ds(off, LANE)], strip.at[k], sems.at[f, 2]))
        edges.append(pltpu.make_async_copy(src.at[pl.ds(0, SUB)], edge.at[0, k], sems.at[f, 0]))
        edges.append(pltpu.make_async_copy(src.at[pl.ds(rows - SUB, SUB)], edge.at[1, k], sems.at[f, 1]))
    for copy in strips + edges:
        copy.start()
    for copy in strips:
        copy.wait()

    lift = jnp.where(at_left, HALO, 0)
    lane = lanes_of((SUB, LANE))
    span = rows // FOLD

    def fold(i, carry):
        total = jnp.zeros((SUB, LANE), jnp.float32)
        for g in range(FOLD):
            at = pl.ds(pl.multiple_of(g * span + i * SUB, SUB), SUB)
            for f in range(FIELDS):
                _, strip, k = slots[f]
                place = g * FIELDS + f
                part = pltpu.roll(strip[k, at, :].astype(jnp.float32), lift + place * HALO, 1)
                total = jnp.where(lane // HALO == place, part, total)
        side[tile_at(i), :] = total
        return carry

    lax.fori_loop(0, span // SUB, fold, 0)

    for copy in edges:
        copy.wait()
    low = rows_of((SUB, cols)) < HALO
    for where, out in ((0, up), (1, down)):
        for p in range(FIELDS // 2):
            both = []
            for f in (2 * p, 2 * p + 1):
                edge, _, k = slots[f]
                both.append(edge[where, k].astype(jnp.float32))
            if where == 0:
                pair = jnp.where(low, both[0], pltpu.roll(both[1], HALO, 0))
            else:
                pair = jnp.where(low, pltpu.roll(both[0], HALO, 0), both[1])
            for k in range(cols // LANE):
                out[pl.ds(k * GROUP + p * SUB, SUB), :] = pair[:, k * LANE : (k + 1) * LANE]


def pack(bed, mask, kind, stress, hydro):
    rows, cols = bed.shape
    tall = cols // LANE * GROUP + SUB
    return pl.pallas_call(
        pack_kernel,
        name="pack_edges",
        out_shape=[
            pltpu.VMEM((tall, LANE), jnp.float32),
            pltpu.VMEM((tall, LANE), jnp.float32),
            pltpu.VMEM((rows // FOLD, LANE), jnp.float32),
        ],
        in_specs=[ANY] * 5,
        out_specs=[VMEM] * 3,
        scratch_shapes=[
            pltpu.VMEM((2, 2, SUB, cols), jnp.int32),
            pltpu.VMEM((2, 6, SUB, cols), jnp.float32),
            pltpu.VMEM((2, rows, LANE), jnp.int32),
            pltpu.VMEM((6, rows, LANE), jnp.float32),
            pltpu.SemaphoreType.DMA((FIELDS, 3)),
        ],
        compiler_params=pltpu.CompilerParams(vmem_limit_bytes=4 * MIB),
        cost_estimate=pl.CostEstimate(flops=10**6, bytes_accessed=2 * MIB, transcendentals=0),
    )(*held(bed, mask, kind, stress, hydro, space=pltpu.HBM))


def side_lanes(at_left):
    drop = jnp.where(at_left, 0, HALO)
    lane = lanes_of((SUB, LANE))
    valid = jnp.where(at_left, lane, LANE - 1 - lane) < HALO

    def unfold(strip, place):
        return pltpu.roll(strip, 2 * LANE - drop - place * HALO, 1)

    return unfold, valid


class Sweep:
    NAMES = (
        ["s", "a", "b", "fc", "fr", "wc", "wr", "e1", "u1"]
        + ["v1", "e2", "u2", "v2", "qc1", "qr1", "qc2", "qr2"]
    )

    def __init__(self, count, wide, get, emit, weights, params, refs):
        self.count, self.wide, self.get, self.emit = count, wide, get, emit
        self.__dict__.update(zip(self.NAMES + ["fr_last", "qr_last"], refs))
        cond = lax.axis_index("cond")
        self.tide = params[0, 0] - 1.0
        self.slow = 1.0 - 0.2 * params[0, 1]
        self.flow_in = 0.3 * params[0, 3]
        total = weights[0]
        for k in range(1, weights.shape[0]):
            total = total + weights[k]
        ones = jnp.ones((SUB, LANE), jnp.float32)
        share = weights[cond].astype(jnp.float32) * ones / (total.astype(jnp.float32) * ones)
        self.scale = jnp.concatenate([-4.0 * params[0, 2] * share] * (wide // LANE), axis=1)

    @classmethod
    def scratch(cls, count, wide):
        block = pltpu.VMEM(((count + 1) * SUB, wide), jnp.float32)
        return [block] * len(cls.NAMES) + [
            pltpu.VMEM((STEPS, SUB, wide), jnp.float32),
            pltpu.VMEM((SUB, wide), jnp.float32),
        ]

    def prepare(self, i):
        at = tile_at(i)
        depth = self.get(1, i).astype(jnp.float32) * (1.0 - 0.5 * jnp.tanh(self.get(0, i)))
        kinds = self.get(2, i)
        self.s[at, :] = depth * lax.rsqrt(jnp.maximum(depth, 1e-12))
        relax = jnp.where(kinds == 1, 0.5 * depth, 0.0)
        self.a[at, :] = 1.0 - relax
        self.b[at, :] = 0.3 * (relax * self.tide + jnp.where(kinds == 2, self.flow_in * depth, 0.0))

    def move(self, n, i, level, lower, u, v, fc, fr, wc, wr):
        at = tile_at(i)
        u = (self.slow * u - (east(level) - level) + self.get(3, i)) * wc
        v = (self.slow * v - (south(level, lower) - level) + self.get(4, i)) * wr
        flux_c = fc * u
        flux_r = fr * v
        out = self.a[at, :] * level + self.b[at, :] - (
            flux_c - west(flux_c) + flux_r - north(flux_r, self.fr_last[n])
        )
        self.fr_last[n] = flux_r
        return out, u, v, wc * (u * jnp.abs(u)), wr * (v * jnp.abs(v))

    def step_one(self, i):
        at, after = tile_at(i), tile_at(i + 1)
        s = self.s[at, :]
        face_c = s * east(s)
        face_r = s * south(s, self.s[after, :])
        ratios = []
        for face in (face_c, face_r):
            base = face + 0.1
            inverse = pl.reciprocal(base, approx=True)
            ratios.append(face * (inverse * (2.0 - base * inverse)))
        wc, wr = ratios
        fc = 0.3 * face_c
        fr = 0.3 * face_r
        self.fc[at, :] = fc
        self.fr[at, :] = fr
        self.wc[at, :] = wc
        self.wr[at, :] = wr
        level = 0.3 * self.get(5, i)
        lower = 0.3 * self.get(5, i + 1) if i + 1 < self.count else level
        e, u, v, qc, qr = self.move(0, i, level, lower, self.get(6, i), self.get(7, i), fc, fr, wc, wr)
        self.e1[at, :] = e
        self.u1[at, :] = u
        self.v1[at, :] = v
        self.qc1[at, :] = qc
        self.qr1[at, :] = qr

    def later(self, n, i, e, u, v):
        at, after = tile_at(i), tile_at(i + 1)
        return self.move(
            n, i, e[at, :], e[after, :], u[at, :], v[at, :],
            self.fc[at, :], self.fr[at, :], self.wc[at, :], self.wr[at, :],
        )

    def step_two(self, i):
        at = tile_at(i)
        e, u, v, qc, qr = self.later(1, i, self.e1, self.u1, self.v1)
        self.e2[at, :] = e
        self.u2[at, :] = u
        self.v2[at, :] = v
        self.qc2[at, :] = self.qc1[at, :] + qc
        self.qr2[at, :] = self.qr1[at, :] + qr

    def step_three(self, i):
        at = tile_at(i)
        e, u, v, qc, qr = self.later(2, i, self.e2, self.u2, self.v2)
        qc = self.qc2[at, :] + qc
        qr = self.qr2[at, :] + qr
        change = (qc - west(qc) + qr - north(qr, self.qr_last[...])) * self.scale
        self.qr_last[...] = qr
        self.emit(i, e * (1.0 / 0.3), u, v, change)

    def run(self):
        self.fr_last[...] = jnp.zeros_like(self.fr_last)
        self.qr_last[...] = jnp.zeros_like(self.qr_last)
        for ref in (self.s, self.e1, self.e2):
            ref[tile_at(self.count), :] = jnp.zeros((SUB, self.wide), jnp.float32)
        stages = (self.step_three, self.step_two, self.step_one, self.prepare)
        for t in range(self.count + LAG * STEPS):
            for k, stage in enumerate(stages):
                i = t - LAG * (STEPS - k)
                if 0 <= i < self.count:
                    stage(i)


def raw_reader(bed, mask, kind, stress, hydro, side, unfold, valid):
    rows = bed.shape[0]
    span = rows // FOLD // SUB
    fields = [bed, mask, kind] + [stress.at[0, k] for k in range(2)] + [hydro.at[0, k] for k in range(3)]

    def read(f, block):
        strip = side[tile_at(block % span), :]
        part = unfold(strip, (block // span) * FIELDS + f)
        if f == 1:
            part = jnp.where(valid, part, 0.0)
        main = fields[f][tile_at(block), :]
        return jnp.concatenate([main, part.astype(main.dtype)], axis=1)

    return read


def middle_kernel(weights, params, bed, mask, kind, stress, hydro, side, hydro_out, pay, *refs):
    rows, cols = bed.shape
    quarter = rows // SUB // 4
    wide = cols + LANE
    unfold, valid = side_lanes(lax.axis_index("tx") == 0)
    read = raw_reader(bed, mask, kind, stress, hydro, side, unfold, valid)
    mine = lax.axis_index("cond") % 2
    lane = lanes_of((SUB, LANE))
    rims = [jnp.zeros((SUB, LANE), jnp.float32)] * 2
    first = quarter - 1

    def emit(i, e, u, v, change):
        if not 1 <= i <= 2 * quarter:
            return
        at = tile_at(first + i)
        for k, value in enumerate((e, u, v)):
            hydro_out[0, k, at, :] = value[:, :cols]
        half, g = divmod(i - 1, quarter)
        slot = jnp.where(mine == half, 1, 0)
        for k in range(cols // LANE):
            pay[slot, tile_at(k * quarter + g), :] = change[:, k * LANE : (k + 1) * LANE]
        rims[half] = jnp.where(lane // 2 == g, pltpu.roll(change[:, cols:], 1 + 2 * g, 1), rims[half])
        if g == quarter - 1:
            pay[slot, tile_at(cols // LANE * quarter), :] = rims[half]

    Sweep(2 * quarter + 2, wide, lambda f, i: read(f, first + i), emit, weights, params, refs).run()


def middle(weights, params, raw, side):
    rows, cols = raw[0].shape
    blocks = rows // SUB // 2 + 2
    return pl.pallas_call(
        middle_kernel,
        name="flow_middle",
        out_shape=[
            pltpu.VMEM(raw[4].shape, jnp.float32),
            pltpu.VMEM((2, cols // LANE * rows // 4 + SUB, LANE), jnp.float32),
        ],
        in_specs=[SMEM, SMEM] + [VMEM] * 6,
        out_specs=[VMEM, VMEM],
        scratch_shapes=Sweep.scratch(blocks, cols + LANE),
        compiler_params=pltpu.CompilerParams(vmem_limit_bytes=16 * MIB),
        cost_estimate=pl.CostEstimate(flops=6 * 10**7, bytes_accessed=16 * MIB, transcendentals=0),
    )(weights, params, *held(*raw, side))


def edge_kernel(own, weights, params, bed, mask, kind, stress, hydro, side, above, below, hydro_in, hydro_out, pay, ends_r, ends_i, *refs):
    rows, cols = bed.shape
    blocks = rows // SUB
    quarter = blocks // 4
    wide = cols + LANE
    lanes = cols // LANE
    unfold, valid = side_lanes(lax.axis_index("tx") == 0)
    read = raw_reader(bed, mask, kind, stress, hydro, side, unfold, valid)
    mine = lax.axis_index("cond") % 2
    top = mine == (0 if own else 1)
    first = jnp.where(top, -1, blocks - quarter - 1)
    spots = [(ends_r, 0), (ends_i, 0), (ends_i, 1)] + [(ends_r, k) for k in range(1, 6)]

    inner = jnp.where(top, quarter, blocks - quarter - 1)
    for f in range(FIELDS):
        body = read(f, inner)
        pairs = []
        for ref in (above, below):
            pairs.append([ref[pl.ds(k * GROUP + f // 2 * SUB, SUB), :] for k in range(lanes)])
        if f % 2 == 0:
            pairs[0] = [pltpu.roll(x, HALO, 0) for x in pairs[0]]
        else:
            pairs[1] = [pltpu.roll(x, HALO, 0) for x in pairs[1]]
        corner = jnp.where(
            top,
            unfold(above[pl.ds(lanes * GROUP, SUB), :], (FOLD - 1) * FIELDS + f),
            unfold(below[pl.ds(lanes * GROUP, SUB), :], f),
        )
        if f == 1:
            corner = jnp.where(valid, corner, 0.0)
        outer = jnp.concatenate([jnp.where(top, a, b) for a, b in zip(*pairs)] + [corner], axis=1).astype(body.dtype)
        ref, k = spots[f]
        ref[0, k] = jnp.where(top, outer, body)
        ref[1, k] = jnp.where(top, body, outer)

    def get(f, i):
        if i == 0 or i == quarter + 1:
            ref, k = spots[f]
            return ref[0 if i == 0 else 1, k]
        return read(f, first + i)

    lane = lanes_of((SUB, LANE))
    row = rows_of((SUB, LANE))
    state = {"rim": jnp.zeros((SUB, LANE), jnp.float32)}

    def emit(i, e, u, v, change):
        if i == 0:
            state["row"] = pltpu.roll(change, 1, 0)
            return
        if i == quarter + 1:
            outside = jnp.where(top, state["row"], change)
            total = jnp.zeros((SUB, LANE), jnp.float32)
            for k in range(lanes):
                total = jnp.where(row == k, pltpu.roll(outside[:, k * LANE : (k + 1) * LANE], k, 0) if k else outside[:, :LANE], total)
            pay[tile_at(lanes * quarter + 1), :] = total
            return
        at = tile_at(first + i)
        for k, value in enumerate((e, u, v)):
            hydro_out[0, k, at, :] = value[:, :cols]
        g = i - 1
        for k in range(lanes):
            pay[tile_at(k * quarter + g), :] = change[:, k * LANE : (k + 1) * LANE]
        state["rim"] = jnp.where(lane // 2 == g, pltpu.roll(change[:, cols:], 1 + 2 * g, 1), state["rim"])
        if g == quarter - 1:
            pay[tile_at(lanes * quarter), :] = state["rim"]

    Sweep(quarter + 2, wide, get, emit, weights, params, refs).run()


def edge(own, weights, params, raw, side, above, below, hydro):
    rows, cols = raw[0].shape
    blocks = rows // SUB // 4 + 2
    wide = cols + LANE
    return pl.pallas_call(
        functools.partial(edge_kernel, own),
        name="flow_own" if own else "flow_other",
        out_shape=[
            pltpu.VMEM(hydro.shape, jnp.float32),
            pltpu.VMEM((cols // LANE * rows // 4 + 2 * SUB, LANE), jnp.float32),
        ],
        in_specs=[SMEM, SMEM] + [VMEM] * 9,
        out_specs=[VMEM, VMEM],
        scratch_shapes=[pltpu.VMEM((2, 6, SUB, wide), jnp.float32), pltpu.VMEM((2, 2, SUB, wide), jnp.int32)]
        + Sweep.scratch(blocks, wide),
        input_output_aliases={10: 0},
        compiler_params=pltpu.CompilerParams(vmem_limit_bytes=12 * MIB),
        cost_estimate=pl.CostEstimate(flops=3 * 10**7, bytes_accessed=10 * MIB, transcendentals=0),
    )(weights, params, *held(*raw, side, above, below, hydro))


def bed_kernel(bed, side, above, below, own_m, got_m, own_e, got_e, bed_next, bed_change, change_v, next_v, sems):
    rows, cols = bed.shape
    blocks = rows // SUB
    quarter = blocks // 4
    span = blocks // FOLD
    wide = cols + LANE
    lanes = cols // LANE
    unfold, _ = side_lanes(lax.axis_index("tx") == 0)
    mine = lax.axis_index("cond") % 2

    def merged(q, block):
        half = q // 2
        own, got = (own_e, got_e) if q in (0, 3) else (own_m, got_m)
        at = tile_at(block)
        return jnp.where(mine == half, own[at, :], got[at, :])

    col = lanes_of((SUB, wide))
    last_c = lax.axis_index("tx") == lax.axis_size("tx") - 1
    first_c = lax.axis_index("tx") == 0
    shut_c = (last_c & (col == cols - 1)) | (first_c & (col == wide - 1))
    row = rows_of((SUB, wide))
    last_r = lax.axis_index("ty") == lax.axis_size("ty") - 1
    first_r = lax.axis_index("ty") == 0
    shut_r = row == SUB - 1
    rims = [merged(q, lanes * quarter) for q in range(4)]
    pad = [jnp.zeros((SUB, LANE), jnp.float32)]

    def level(b):
        if b == -1:
            rim = merged(0, lanes * quarter + 1)
            parts = []
            for k in range(lanes):
                z = above[tile_at(k * GROUP // SUB), :] + pltpu.roll(rim, (2 * SUB + HALO - 1 - k) % SUB, 0)
                parts.append(pltpu.roll(z, HALO, 0))
            return jnp.concatenate(parts + pad, axis=1)
        if b == blocks:
            rim = merged(3, lanes * quarter + 1)
            parts = []
            for k in range(lanes):
                parts.append(below[tile_at(k * GROUP // SUB), :] + pltpu.roll(rim, (SUB - k) % SUB, 0))
            return jnp.concatenate(parts + pad, axis=1)
        q, g = divmod(b, quarter)
        change = jnp.concatenate([merged(q, k * quarter + g) for k in range(lanes)], axis=1)
        change_v[tile_at(b), :] = change
        cols_bed = unfold(side[tile_at(b % span), :], b // span * FIELDS)
        cols_change = pltpu.roll(rims[q], LANE - 1 - 2 * g, 1)
        return jnp.concatenate([bed[tile_at(b), :] + change, cols_bed + cols_change], axis=1)

    def spill(slope, shut):
        return jnp.where(shut, 0.0, 0.25 * (slope - jnp.clip(slope, -1.0, 1.0)))

    def south_face(z, lower, b):
        slope = south(z, lower) - z
        if b == -1:
            return spill(slope, first_r & shut_r)
        if b == blocks - 1:
            return spill(slope, last_r & shut_r)
        return 0.25 * (slope - jnp.clip(slope, -1.0, 1.0))

    outs = []

    def send(b):
        parts = 4
        if (b + 1) % (blocks // parts) == 0:
            c = b // (blocks // parts)
            at = pl.ds(c * (rows // parts), rows // parts)
            for k, (src, dst) in enumerate(((change_v, bed_change), (next_v, bed_next))):
                outs.append(pltpu.make_async_copy(src.at[at], dst.at[at], sems.at[k, c]))
                outs[-1].start()

    z = level(-1)
    lower = level(0)
    gr = south_face(z, lower, -1)
    for b in range(blocks):
        z, lower = lower, level(b + 1)
        gr_above, gr = gr, south_face(z, lower, b)
        gc = spill(east(z) - z, shut_c)
        out = z + gc - west(gc) + gr - north(gr, gr_above)
        next_v[tile_at(b), :] = out[:, :cols]
        send(b)
    for copy in outs:
        copy.wait()


def update_bed(bed, side, above, below, own_m, got_m, own_e, got_e):
    rows, cols = bed.shape
    return pl.pallas_call(
        bed_kernel,
        name="update_bed",
        out_shape=[jax.ShapeDtypeStruct(bed.shape, jnp.float32)] * 2,
        in_specs=[VMEM] * 8,
        out_specs=[ANY, ANY],
        scratch_shapes=[
            pltpu.VMEM((rows, cols), jnp.float32),
            pltpu.VMEM((rows, cols), jnp.float32),
            pltpu.SemaphoreType.DMA((2, 4)),
        ],
        compiler_params=pltpu.CompilerParams(vmem_limit_bytes=6 * MIB),
        cost_estimate=pl.CostEstimate(flops=10**7, bytes_accessed=5 * MIB, transcendentals=0),
    )(*held(bed, side, above, below, own_m, got_m, own_e, got_e))


def shards(bed, land_mask, cell_class, weights, cond_params, wave_stress, hydro_state):
    ny = lax.axis_size("ty")
    nc = lax.axis_size("cond")
    raw = (bed, land_mask, cell_class, wave_stress, hydro_state)
    swap = [(i, i ^ 1) for i in range(nc)]

    def over_chips(part):
        reach = 2
        while reach < nc:
            part = part + lax.ppermute(part, "cond", [(i, i ^ reach) for i in range(nc)])
            reach = 2 * reach
        return part

    up, down, side = pack(*raw)
    side = lax.ppermute(side, "tx", [(0, 1), (1, 0)])
    tall = up.shape[0] - SUB
    up = lax.dynamic_update_slice(up, side[:SUB], (tall, 0))
    down = lax.dynamic_update_slice(down, side[-SUB:], (tall, 0))
    above = lax.ppermute(down, "ty", [(i, i + 1) for i in range(ny - 1)])
    below = lax.ppermute(up, "ty", [(i + 1, i) for i in range(ny - 1)])

    hydro, pay_m = middle(weights, cond_params, raw, side)
    got_m = lax.ppermute(pay_m[0], "cond", swap)
    hydro, pay_other = edge(False, weights, cond_params, raw, side, above, below, hydro)
    part_m = pay_m[1] + got_m
    hydro, part_m, pay_other = lax.optimization_barrier((hydro, part_m, pay_other))
    got_e = lax.ppermute(pay_other, "cond", swap)
    own_m = over_chips(part_m)
    hydro, pay_own = edge(True, weights, cond_params, raw, side, above, below, hydro)
    own_e = over_chips(pay_own + got_e)
    other_m = lax.ppermute(own_m, "cond", swap)
    other_e = lax.ppermute(own_e, "cond", swap)
    bed_next, bed_change = update_bed(bed, side, above, below, own_m, other_m, own_e, other_e)
    return bed_next, bed_change, hydro


def solution(mesh):
    in_specs = (
        P("ty", "tx"),
        P("ty", "tx"),
        P("ty", "tx"),
        P(),
        P("cond", None),
        P("cond", None, "ty", "tx"),
        P("cond", None, "ty", "tx"),
    )
    out_specs = (P("ty", "tx"), P("ty", "tx"), P("cond", None, "ty", "tx"))
    return jax.shard_map(shards, mesh=mesh, in_specs=in_specs, out_specs=out_specs, check_vma=False)
```

profile of v0, /device:TPU:9, one launch (start us, length us, event | category | flops | bytes accessed | tf_op | source)
XLA Modules:
  0.0 50.0 jit_solution(17520845197384434056)
XLA Ops:
  0.7 2.5 %pack_edges.1 = (f32[264,128]{1,0:T(8,128)S(1)}, f32[264,128]{1,0:T(8,128)S(1)}, f32[64,128]{1,0:T(8,128)S(1)}) custom-call(f32[256,1024]{1,0:T(8,128)} %bed.9, s32[256,1024]{1,0:T(8,128)} %mask.7, s32[256,1024]{1,0:T(8,128)} %kind.7, f32[1,2,256,1024]{3,2,1,0:T(8,128)} %stress.7, f32[1,3,256,1024]{3,2,1,0:T(8,128)} %hydro.7), custom_call_target="tpu_custom_call" | custom-call | flops 1000000 | bytes 2097152 | tf_op jit(solution)/shard_map/pack_edges/pallas_call | solution.py:114
  3.2 1.3 %collective-permute-start = (f32[64,128]{1,0:T(8,128)S(1)}, f32[64,128]{1,0:T(8,128)S(1)}, u32[]{:S(2)}, u32[]{:S(2)}) collective-permute-start(f32[64,128]{1,0:T(8,128)S(1)} %get-tuple-element.17), channel_id=1, source_target_pairs={{0,1},{1,0},{2,3},{3,2},{4,5},{5,4},{6,7},{7,6},{8,9},{9,8},{10,11... | collective-permute-start | bytes 98312 | tf_op jit(solution)/shard_map/ppermute | solution.py:528
  4.5 1.5 %collective-permute-done.side = f32[64,128]{1,0:T(8,128)S(1)} collective-permute-done((f32[64,128]{1,0:T(8,128)S(1)}, f32[64,128]{1,0:T(8,128)S(1)}, u32[]{:S(2)}, u32[]{:S(2)}) %collective-permute-start) | collective-permute-done | bytes 32800 | tf_op jit(solution)/shard_map/ppermute | solution.py:528
  6.1 6.3 %flow_middle.1 = (f32[1,3,256,1024]{3,2,1,0:T(8,128)S(1)}, f32[2,520,128]{2,1,0:T(8,128)S(1)}) custom-call(s32[4]{0:T(128)S(1)} %copy-done.5, f32[1,4]{1,0:T(1,128)S(1)} %copy-done.6, f32[256,1024]{1,0:T(8,128)S(1)} %copy-done.2, s32[256,1024]{1,0:T(8,128)S(1)} %copy-done.3, s32[256,1024]{1,0:T(8,128)S(1)} %copy-done.4, f32[1,2,256,1024]{3,2,1,0:T(8,128)S(1)} %copy-done.1, ...), custom_call_target="tpu_custom_call" | custom-call | flops 60000000 | bytes 16777216 | tf_op jit(solution)/shard_map/flow_middle/pallas_call | solution.py:307
  12.5 1.9 %collective-permute-start.3 = (f32[520,128]{1,0:T(8,128)S(1)}, f32[520,128]{1,0:T(8,128)S(1)}, u32[]{:S(2)}, u32[]{:S(2)}) collective-permute-start(f32[520,128]{1,0:T(8,128)S(1)} %slice_bitcast_fusion), channel_id=1, source_target_pairs={{0,8},{8,0},{16,24},{24,16},{1,9},{9,1},{17,25},{25,17},{2,10},{10... | collective-permute-start | bytes 798728 | tf_op jit(solution)/shard_map/ppermute | solution.py:536
  14.4 1.9 %collective-permute-start.2 = (f32[264,128]{1,0:T(8,128)S(1)}, f32[264,128]{1,0:T(8,128)S(1)}, u32[]{:S(2)}, u32[]{:S(2)}) collective-permute-start(f32[264,128]{1,0:T(8,128)S(1)} %get-tuple-element.31), channel_id=1, source_target_pairs={{2,0},{4,2},{6,4},{3,1},{5,3},{7,5},{10,8},{12,10},{14,12},{11,9},... | collective-permute-start | bytes 405512 | tf_op jit(solution)/shard_map/ppermute | solution.py:533
  16.3 3.4 %collective-permute-start.1 = (f32[264,128]{1,0:T(8,128)S(1)}, f32[264,128]{1,0:T(8,128)S(1)}, u32[]{:S(2)}, u32[]{:S(2)}) collective-permute-start(f32[264,128]{1,0:T(8,128)S(1)} %get-tuple-element.32), channel_id=1, source_target_pairs={{0,2},{2,4},{4,6},{1,3},{3,5},{5,7},{8,10},{10,12},{12,14},{9,11},... | collective-permute-start | bytes 405512 | tf_op jit(solution)/shard_map/ppermute | solution.py:532
  19.6 1.8 %collective-permute-done.2.below = f32[264,128]{1,0:T(8,128)S(1)} collective-permute-done((f32[264,128]{1,0:T(8,128)S(1)}, f32[264,128]{1,0:T(8,128)S(1)}, u32[]{:S(2)}, u32[]{:S(2)}) %collective-permute-start.2) | collective-permute-done | bytes 135200 | tf_op jit(solution)/shard_map/ppermute | solution.py:533
  21.4 1.9 %collective-permute-done.1.above = f32[264,128]{1,0:T(8,128)S(1)} collective-permute-done((f32[264,128]{1,0:T(8,128)S(1)}, f32[264,128]{1,0:T(8,128)S(1)}, u32[]{:S(2)}, u32[]{:S(2)}) %collective-permute-start.1) | collective-permute-done | bytes 135200 | tf_op jit(solution)/shard_map/ppermute | solution.py:532
  23.3 3.0 %flow_other.1 = (f32[1,3,256,1024]{3,2,1,0:T(8,128)S(1)}, f32[528,128]{1,0:T(8,128)S(1)}) custom-call(s32[4]{0:T(128)S(1)} %copy-done.5, f32[1,4]{1,0:T(1,128)S(1)} %copy-done.6, f32[256,1024]{1,0:T(8,128)S(1)} %copy-done.2, s32[256,1024]{1,0:T(8,128)S(1)} %copy-done.3, s32[256,1024]{1,0:T(8,128)S(1)} %copy-done.4, ...), custom_call_target="tpu_custom_call", output_to_operand_aliasing={{0}: (10, {})} | custom-call | flops 30000000 | bytes 10485760 | tf_op jit(solution)/shard_map/flow_other/pallas_call | solution.py:395
  26.4 0.0 collective-permute-done.3
  26.4 0.9 %collective-permute-start.6 = (f32[528,128]{1,0:T(8,128)S(1)}, f32[528,128]{1,0:T(8,128)S(1)}, u32[]{:S(2)}, u32[]{:S(2)}) collective-permute-start(f32[528,128]{1,0:T(8,128)S(1)} %get-tuple-element.27), channel_id=1, source_target_pairs={{0,8},{8,0},{16,24},{24,16},{1,9},{9,1},{17,25},{25,17},{2,10},{10... | collective-permute-start | bytes 811016 | tf_op jit(solution)/shard_map/ppermute | solution.py:540
  27.3 3.0 %flow_own.1 = (f32[1,3,256,1024]{3,2,1,0:T(8,128)S(1)}, f32[528,128]{1,0:T(8,128)S(1)}) custom-call(s32[4]{0:T(128)S(1)} %copy-done.5, f32[1,4]{1,0:T(1,128)S(1)} %copy-done.6, f32[256,1024]{1,0:T(8,128)S(1)} %copy-done.2, s32[256,1024]{1,0:T(8,128)S(1)} %copy-done.3, s32[256,1024]{1,0:T(8,128)S(1)} %copy-done.4, ...), custom_call_target="tpu_custom_call", output_to_operand_aliasing={{0}: (10, {})} | custom-call | flops 30000000 | bytes 10485760 | tf_op jit(solution)/shard_map/flow_own/pallas_call | solution.py:395
  30.4 0.0 collective-permute-done.6
  30.4 1.4 %collective-permute-start.7 = (f32[528,128]{1,0:T(8,128)S(1)}, f32[528,128]{1,0:T(8,128)S(1)}, u32[]{:S(2)}, u32[]{:S(2)}) collective-permute-start(f32[528,128]{1,0:T(8,128)S(1)} %add.14), channel_id=1, source_target_pairs={{0,16},{8,24},{16,0},{24,8},{1,17},{9,25},{17,1},{25,9},{2,18},{10... | collective-permute-start | bytes 811016 | tf_op jit(solution)/shard_map/ppermute | solution.py:523
  31.8 0.1 collective-permute-start.4
  31.9 6.6 %collective-permute-done.7 = f32[528,128]{1,0:T(8,128)S(1)} collective-permute-done((f32[528,128]{1,0:T(8,128)S(1)}, f32[528,128]{1,0:T(8,128)S(1)}, u32[]{:S(2)}, u32[]{:S(2)}) %collective-permute-start.7) | collective-permute-done | bytes 270368 | tf_op jit(solution)/shard_map/ppermute | solution.py:523
  38.6 1.3 %collective-permute-start.8 = (f32[528,128]{1,0:T(8,128)S(1)}, f32[528,128]{1,0:T(8,128)S(1)}, u32[]{:S(2)}, u32[]{:S(2)}) collective-permute-start(f32[528,128]{1,0:T(8,128)S(1)} %add.15.own_e), channel_id=1, source_target_pairs={{0,8},{8,0},{16,24},{24,16},{1,9},{9,1},{17,25},{25,17},{2,10},{10... | collective-permute-start | bytes 811016 | tf_op jit(solution)/shard_map/ppermute | solution.py:545
  39.9 4.4 %collective-permute-done.4 = f32[520,128]{1,0:T(8,128)S(1)} collective-permute-done((f32[520,128]{1,0:T(8,128)S(1)}, f32[520,128]{1,0:T(8,128)S(1)}, u32[]{:S(2)}, u32[]{:S(2)}) %collective-permute-start.4) | collective-permute-done | bytes 266272 | tf_op jit(solution)/shard_map/ppermute | solution.py:523
  44.3 0.9 %collective-permute-start.5 = (f32[520,128]{1,0:T(8,128)S(1)}, f32[520,128]{1,0:T(8,128)S(1)}, u32[]{:S(2)}, u32[]{:S(2)}) collective-permute-start(f32[520,128]{1,0:T(8,128)S(1)} %add.13.own_m), channel_id=1, source_target_pairs={{0,8},{8,0},{16,24},{24,16},{1,9},{9,1},{17,25},{25,17},{2,10},{10... | collective-permute-start | bytes 798728 | tf_op jit(solution)/shard_map/ppermute | solution.py:544
  45.2 1.7 %copy.16 = f32[1,3,256,1024]{3,2,1,0:T(8,128)} copy(f32[1,3,256,1024]{3,2,1,0:T(8,128)S(1)} %get-tuple-element.35) | data formatting | bytes 6291456
  46.8 0.0 collective-permute-done.5.got_m
  46.8 0.0 collective-permute-done.8.got_e
  46.8 3.1 %update_bed.1 = (f32[256,1024]{1,0:T(8,128)}, f32[256,1024]{1,0:T(8,128)}) custom-call(f32[256,1024]{1,0:T(8,128)S(1)} %copy-done.2, f32[64,128]{1,0:T(8,128)S(1)} %collective-permute-done.side, f32[264,128]{1,0:T(8,128)S(1)} %collective-permute-done.1.above, f32[264,128]{1,0:T(8,128)S(1)} %collective-permute-done.2.below, f32[520,128]{1,0:T(8,128)S(1)} %add.13.own_m, ...), custom_call_target="tpu_custom_call" | custom-call | flops 10000000 | bytes 5242880 | tf_op jit(solution)/shard_map/update_bed/pallas_call | solution.py:498
  (20 shorter events, 0.2 us)
Async XLA Ops:
  0.6 5.4 %copy-start.2 = (f32[256,1024]{1,0:T(8,128)S(1)}, f32[256,1024]{1,0:T(8,128)}, u32[]{:S(2)}) copy-start(f32[256,1024]{1,0:T(8,128)} %bed.9) | copy-start | bytes 3145732
  0.6 5.4 %copy-start = (f32[1,3,256,1024]{3,2,1,0:T(8,128)S(1)}, f32[1,3,256,1024]{3,2,1,0:T(8,128)}, u32[]{:S(2)}) copy-start(f32[1,3,256,1024]{3,2,1,0:T(8,128)} %hydro.7) | copy-start | bytes 9437188
  0.7 5.4 %copy-start.1 = (f32[1,2,256,1024]{3,2,1,0:T(8,128)S(1)}, f32[1,2,256,1024]{3,2,1,0:T(8,128)}, u32[]{:S(2)}) copy-start(f32[1,2,256,1024]{3,2,1,0:T(8,128)} %stress.7) | copy-start | bytes 6291460
  0.7 5.4 %copy-start.4 = (s32[256,1024]{1,0:T(8,128)S(1)}, s32[256,1024]{1,0:T(8,128)}, u32[]{:S(2)}) copy-start(s32[256,1024]{1,0:T(8,128)} %kind.7) | copy-start | bytes 3145732
  0.7 5.4 %copy-start.3 = (s32[256,1024]{1,0:T(8,128)S(1)}, s32[256,1024]{1,0:T(8,128)}, u32[]{:S(2)}) copy-start(s32[256,1024]{1,0:T(8,128)} %mask.7) | copy-start | bytes 3145732
  0.7 5.4 %copy-start.6 = (f32[1,4]{1,0:T(1,128)S(1)}, f32[1,4]{1,0:T(1,128)}, u32[]{:S(2)}) copy-start(f32[1,4]{1,0:T(1,128)} %params.5) | copy-start | bytes 52
  0.7 5.4 %copy-start.5 = (s32[4]{0:T(128)S(1)}, s32[4]{0:T(128)}, u32[]{:S(2)}) copy-start(s32[4]{0:T(128)} %weights.5) | copy-start | bytes 52
  3.2 2.8 %collective-permute-start = (f32[64,128]{1,0:T(8,128)S(1)}, f32[64,128]{1,0:T(8,128)S(1)}, u32[]{:S(2)}, u32[]{:S(2)}) collective-permute-start(f32[64,128]{1,0:T(8,128)S(1)} %get-tuple-element.17), channel_id=1, source_target_pairs={{0,1},{1,0},{2,3},{3,2},{4,5},{5,4},{6,7},{7,6},{8,9},{9,8},{10,11... | collective-permute-start | bytes 98312 | tf_op jit(solution)/shard_map/ppermute | solution.py:528
  12.5 13.9 %collective-permute-start.3 = (f32[520,128]{1,0:T(8,128)S(1)}, f32[520,128]{1,0:T(8,128)S(1)}, u32[]{:S(2)}, u32[]{:S(2)}) collective-permute-start(f32[520,128]{1,0:T(8,128)S(1)} %slice_bitcast_fusion), channel_id=1, source_target_pairs={{0,8},{8,0},{16,24},{24,16},{1,9},{9,1},{17,25},{25,17},{2,10},{10... | collective-permute-start | bytes 798728 | tf_op jit(solution)/shard_map/ppermute | solution.py:536
  14.4 7.1 %collective-permute-start.2 = (f32[264,128]{1,0:T(8,128)S(1)}, f32[264,128]{1,0:T(8,128)S(1)}, u32[]{:S(2)}, u32[]{:S(2)}) collective-permute-start(f32[264,128]{1,0:T(8,128)S(1)} %get-tuple-element.31), channel_id=1, source_target_pairs={{2,0},{4,2},{6,4},{3,1},{5,3},{7,5},{10,8},{12,10},{14,12},{11,9},... | collective-permute-start | bytes 405512 | tf_op jit(solution)/shard_map/ppermute | solution.py:533
  16.3 7.1 %collective-permute-start.1 = (f32[264,128]{1,0:T(8,128)S(1)}, f32[264,128]{1,0:T(8,128)S(1)}, u32[]{:S(2)}, u32[]{:S(2)}) collective-permute-start(f32[264,128]{1,0:T(8,128)S(1)} %get-tuple-element.32), channel_id=1, source_target_pairs={{0,2},{2,4},{4,6},{1,3},{3,5},{5,7},{8,10},{10,12},{12,14},{9,11},... | collective-permute-start | bytes 405512 | tf_op jit(solution)/shard_map/ppermute | solution.py:532
  26.4 3.9 %collective-permute-start.6 = (f32[528,128]{1,0:T(8,128)S(1)}, f32[528,128]{1,0:T(8,128)S(1)}, u32[]{:S(2)}, u32[]{:S(2)}) collective-permute-start(f32[528,128]{1,0:T(8,128)S(1)} %get-tuple-element.27), channel_id=1, source_target_pairs={{0,8},{8,0},{16,24},{24,16},{1,9},{9,1},{17,25},{25,17},{2,10},{10... | collective-permute-start | bytes 811016 | tf_op jit(solution)/shard_map/ppermute | solution.py:540
  30.4 8.2 %collective-permute-start.7 = (f32[528,128]{1,0:T(8,128)S(1)}, f32[528,128]{1,0:T(8,128)S(1)}, u32[]{:S(2)}, u32[]{:S(2)}) collective-permute-start(f32[528,128]{1,0:T(8,128)S(1)} %add.14), channel_id=1, source_target_pairs={{0,16},{8,24},{16,0},{24,8},{1,17},{9,25},{17,1},{25,9},{2,18},{10... | collective-permute-start | bytes 811016 | tf_op jit(solution)/shard_map/ppermute | solution.py:523
  31.8 12.4 %collective-permute-start.4 = (f32[520,128]{1,0:T(8,128)S(1)}, f32[520,128]{1,0:T(8,128)S(1)}, u32[]{:S(2)}, u32[]{:S(2)}) collective-permute-start(f32[520,128]{1,0:T(8,128)S(1)} %bitcast_add_fusion), channel_id=1, source_target_pairs={{0,16},{8,24},{16,0},{24,8},{1,17},{9,25},{17,1},{25,9},{2,18},{10... | collective-permute-start | bytes 798728 | tf_op jit(solution)/shard_map/ppermute | solution.py:523
  38.6 8.2 %collective-permute-start.8 = (f32[528,128]{1,0:T(8,128)S(1)}, f32[528,128]{1,0:T(8,128)S(1)}, u32[]{:S(2)}, u32[]{:S(2)}) collective-permute-start(f32[528,128]{1,0:T(8,128)S(1)} %add.15.own_e), channel_id=1, source_target_pairs={{0,8},{8,0},{16,24},{24,16},{1,9},{9,1},{17,25},{25,17},{2,10},{10... | collective-permute-start | bytes 811016 | tf_op jit(solution)/shard_map/ppermute | solution.py:545
  44.3 2.5 %collective-permute-start.5 = (f32[520,128]{1,0:T(8,128)S(1)}, f32[520,128]{1,0:T(8,128)S(1)}, u32[]{:S(2)}, u32[]{:S(2)}) collective-permute-start(f32[520,128]{1,0:T(8,128)S(1)} %add.13.own_m), channel_id=1, source_target_pairs={{0,8},{8,0},{16,24},{24,16},{1,9},{9,1},{17,25},{25,17},{2,10},{10... | collective-permute-start | bytes 798728 | tf_op jit(solution)/shard_map/ppermute | solution.py:544
where the time goes:
time: 50.3 us; the launch traced here: 50 us
  Pallas kernels  18 us (36%)
  waiting for transfers between devices  16.3 us (32%)
  starting transfers between devices  13 us (26%)
  local copies, waits for them, and re-layouts  1.71 us (3%)
  between operations  0.81 us (2%)
    ppermute x2, waiting for transfers between devices, over_chips(): lax.ppermute(part, 'cond', [(i, i ^ reach) for i in range(nc)])  11 us
    pallas_call x1, Pallas kernels, middle(): pl.pallas_call(middle_kernel, name='flow_middle', out_shape=[pltpu.VMEM(r...  6.3 us
    pallas_call x2, Pallas kernels, edge(): pl.pallas_call(functools.partial(edge_kernel, own), name='flow_own' if ow...  6.05 us
    ppermute x1, starting transfers between devices, shards(): above = lax.ppermute(down, 'ty', [(i, i + 1) for i in range(ny - 1)])  3.36 us
    pallas_call x1, Pallas kernels, update_bed(): pl.pallas_call(bed_kernel, name='update_bed', out_shape=[jax.ShapeDtypeSt...  3.11 us
    pallas_call x1, Pallas kernels, pack(): pl.pallas_call(pack_kernel, name='pack_edges', out_shape=[pltpu.VMEM((tal...  2.53 us
    ppermute x1, waiting for transfers between devices, shards(): above = lax.ppermute(down, 'ty', [(i, i + 1) for i in range(ny - 1)])  1.93 us
    ppermute x1, starting transfers between devices, shards(): below = lax.ppermute(up, 'ty', [(i + 1, i) for i in range(ny - 1)])  1.91 us
  transfers between devices with their start and end apart: 9, of which 5 were waited for; matrix products, arithmetic and copies ran while one was open for 3% of the time, Pallas kernels for 12%

commit v1 on v0

v1 whole, which is shorter than its diff:
```python
import functools

import jax
import jax.numpy as jnp
from jax import lax
from jax.experimental import pallas as pl
from jax.experimental.pallas import tpu as pltpu
from jax.sharding import PartitionSpec as P

STEPS = 3
HALO = STEPS + 1
SUB = 8
LANE = 128
FIELDS = 8
GROUP = HALO * FIELDS
FOLD = LANE // GROUP
LAG = 2
MIB = 2**20
ANY = pl.BlockSpec(memory_space=pl.ANY)
VMEM = pl.BlockSpec(memory_space=pltpu.VMEM)
SMEM = pl.BlockSpec(memory_space=pltpu.SMEM)


def rows_of(shape):
    return lax.broadcasted_iota(jnp.int32, shape, 0)


def lanes_of(shape):
    return lax.broadcasted_iota(jnp.int32, shape, 1)


def east(x):
    return pltpu.roll(x, x.shape[1] - 1, 1)


def west(x):
    return pltpu.roll(x, 1, 1)


def south(x, below):
    return pltpu.roll(jnp.where(rows_of(x.shape) == 0, below, x), SUB - 1, 0)


def north(x, above):
    return pltpu.roll(jnp.where(rows_of(x.shape) == SUB - 1, above, x), 1, 0)


def tile_at(index):
    if isinstance(index, int):
        return pl.ds(index * SUB, SUB)
    return pl.ds(pl.multiple_of(index * SUB, SUB), SUB)


def held(*arrays, space=pltpu.VMEM):
    return [pltpu.with_memory_space_constraint(x, space) for x in arrays]


def cost(micros):
    return pl.CostEstimate(flops=int(micros * 10**9), bytes_accessed=0, transcendentals=0)


def raw_fields(bed, mask, kind, stress, hydro):
    return [bed, mask, kind] + [stress.at[0, k] for k in range(2)] + [hydro.at[0, k] for k in range(3)]


SPOTS = [(0, 0), (1, 0), (1, 1)] + [(0, k) for k in range(1, 6)]


def pack_side_kernel(bed, mask, kind, stress, hydro, side, reals, ints, sems):
    rows, cols = bed.shape
    at_left = lax.axis_index("tx") == 0
    off = pl.multiple_of(jnp.where(at_left, cols - LANE, 0), LANE)
    strips = [(reals, ints)[which].at[k] for which, k in SPOTS]
    copies = [
        pltpu.make_async_copy(src.at[:, pl.ds(off, LANE)], strip, sems.at[f])
        for f, (src, strip) in enumerate(zip(raw_fields(bed, mask, kind, stress, hydro), strips))
    ]
    for copy in copies:
        copy.start()
    for copy in copies:
        copy.wait()
    lift = jnp.where(at_left, HALO, 0)
    lane = lanes_of((SUB, LANE))
    span = rows // FOLD // SUB
    for i in range(span):
        total = jnp.zeros((SUB, LANE), jnp.float32)
        for g in range(FOLD):
            for f in range(FIELDS):
                place = g * FIELDS + f
                part = strips[f][tile_at(g * span + i), :].astype(jnp.float32)
                total = jnp.where(lane // HALO == place, pltpu.roll(part, lift + place * HALO, 1), total)
        side[tile_at(i), :] = total


def pack_side(*raw):
    rows, cols = raw[0].shape
    return pl.pallas_call(
        pack_side_kernel,
        name="pack_side",
        out_shape=pltpu.VMEM((rows // FOLD, LANE), jnp.float32),
        in_specs=[ANY] * 5,
        out_specs=VMEM,
        scratch_shapes=[
            pltpu.VMEM((6, rows, LANE), jnp.float32),
            pltpu.VMEM((2, rows, LANE), jnp.int32),
            pltpu.SemaphoreType.DMA((FIELDS,)),
        ],
        compiler_params=pltpu.CompilerParams(vmem_limit_bytes=4 * MIB),
        cost_estimate=cost(2),
    )(*held(*raw, space=pltpu.HBM))


def pack_rows_kernel(bed, mask, kind, stress, hydro, pays, reals, ints, sems):
    rows, cols = bed.shape
    copies = []
    for f, src in enumerate(raw_fields(bed, mask, kind, stress, hydro)):
        which, k = SPOTS[f]
        for end, start in enumerate((0, rows - SUB)):
            copies.append(
                pltpu.make_async_copy(src.at[pl.ds(start, SUB)], (reals, ints)[which].at[end, k], sems.at[f, end])
            )
    for copy in copies:
        copy.start()
    for copy in copies:
        copy.wait()
    low = rows_of((SUB, cols)) < HALO
    odd = lax.axis_index("ty") % 2
    for end in range(2):
        slot = (1 - end + odd) % 2
        for p in range(FIELDS // 2):
            both = []
            for f in (2 * p, 2 * p + 1):
                which, k = SPOTS[f]
                both.append((reals, ints)[which][end, k].astype(jnp.float32))
            both[1 - end] = pltpu.roll(both[1 - end], HALO, 0)
            pair = jnp.where(low, *both)
            for k in range(cols // LANE):
                pays[slot, pl.ds(k * GROUP + p * SUB, SUB), :] = pair[:, k * LANE : (k + 1) * LANE]


def pack_rows(*raw):
    rows, cols = raw[0].shape
    return pl.pallas_call(
        pack_rows_kernel,
        name="pack_rows",
        out_shape=pltpu.VMEM((2, cols // LANE * GROUP, LANE), jnp.float32),
        in_specs=[ANY] * 5,
        out_specs=VMEM,
        scratch_shapes=[
            pltpu.VMEM((2, 6, SUB, cols), jnp.float32),
            pltpu.VMEM((2, 2, SUB, cols), jnp.int32),
            pltpu.SemaphoreType.DMA((FIELDS, 2)),
        ],
        compiler_params=pltpu.CompilerParams(vmem_limit_bytes=4 * MIB),
        cost_estimate=cost(2),
    )(*held(*raw, space=pltpu.HBM))


def side_lanes(at_left):
    drop = jnp.where(at_left, 0, HALO)
    lane = lanes_of((SUB, LANE))
    valid = jnp.where(at_left, lane, LANE - 1 - lane) < HALO

    def unfold(strip, place):
        return pltpu.roll(strip, 2 * LANE - drop - place * HALO, 1)

    return unfold, valid


class Sweep:
    NAMES = (
        ["s", "a", "b", "fc", "fr", "wc", "wr", "e1", "u1"]
        + ["v1", "e2", "u2", "v2", "qc1", "qr1", "qc2", "qr2"]
    )

    def __init__(self, count, wide, get, emit, weights, params, refs):
        self.count, self.wide, self.get, self.emit = count, wide, get, emit
        self.__dict__.update(zip(self.NAMES + ["fr_last", "qr_last"], refs))
        cond = lax.axis_index("cond")
        self.tide = params[0, 0] - 1.0
        self.slow = 1.0 - 0.2 * params[0, 1]
        self.flow_in = 0.3 * params[0, 3]
        total = weights[0]
        for k in range(1, weights.shape[0]):
            total = total + weights[k]
        ones = jnp.ones((SUB, LANE), jnp.float32)
        share = weights[cond].astype(jnp.float32) * ones / (total.astype(jnp.float32) * ones)
        self.scale = jnp.concatenate([-4.0 * params[0, 2] * share] * (wide // LANE), axis=1)

    @classmethod
    def scratch(cls, count, wide):
        block = pltpu.VMEM(((count + 1) * SUB, wide), jnp.float32)
        return [block] * len(cls.NAMES) + [
            pltpu.VMEM((STEPS, SUB, wide), jnp.float32),
            pltpu.VMEM((SUB, wide), jnp.float32),
        ]

    def prepare(self, i):
        at = tile_at(i)
        depth = self.get(1, i).astype(jnp.float32) * (1.0 - 0.5 * jnp.tanh(self.get(0, i)))
        kinds = self.get(2, i)
        self.s[at, :] = depth * lax.rsqrt(jnp.maximum(depth, 1e-12))
        relax = jnp.where(kinds == 1, 0.5 * depth, 0.0)
        self.a[at, :] = 1.0 - relax
        self.b[at, :] = 0.3 * (relax * self.tide + jnp.where(kinds == 2, self.flow_in * depth, 0.0))

    def move(self, n, i, level, lower, u, v, fc, fr, wc, wr):
        at = tile_at(i)
        u = (self.slow * u - (east(level) - level) + self.get(3, i)) * wc
        v = (self.slow * v - (south(level, lower) - level) + self.get(4, i)) * wr
        flux_c = fc * u
        flux_r = fr * v
        out = self.a[at, :] * level + self.b[at, :] - (
            flux_c - west(flux_c) + flux_r - north(flux_r, self.fr_last[n])
        )
        self.fr_last[n] = flux_r
        return out, u, v, wc * (u * jnp.abs(u)), wr * (v * jnp.abs(v))

    def step_one(self, i):
        at, after = tile_at(i), tile_at(i + 1)
        s = self.s[at, :]
        face_c = s * east(s)
        face_r = s * south(s, self.s[after, :])
        ratios = []
        for face in (face_c, face_r):
            base = face + 0.1
            inverse = pl.reciprocal(base, approx=True)
            ratios.append(face * (inverse * (2.0 - base * inverse)))
        wc, wr = ratios
        fc = 0.3 * face_c
        fr = 0.3 * face_r
        self.fc[at, :] = fc
        self.fr[at, :] = fr
        self.wc[at, :] = wc
        self.wr[at, :] = wr
        level = 0.3 * self.get(5, i)
        lower = 0.3 * self.get(5, i + 1) if i + 1 < self.count else level
        e, u, v, qc, qr = self.move(0, i, level, lower, self.get(6, i), self.get(7, i), fc, fr, wc, wr)
        self.e1[at, :] = e
        self.u1[at, :] = u
        self.v1[at, :] = v
        self.qc1[at, :] = qc
        self.qr1[at, :] = qr

    def later(self, n, i, e, u, v):
        at, after = tile_at(i), tile_at(i + 1)
        return self.move(
            n, i, e[at, :], e[after, :], u[at, :], v[at, :],
            self.fc[at, :], self.fr[at, :], self.wc[at, :], self.wr[at, :],
        )

    def step_two(self, i):
        at = tile_at(i)
        e, u, v, qc, qr = self.later(1, i, self.e1, self.u1, self.v1)
        self.e2[at, :] = e
        self.u2[at, :] = u
        self.v2[at, :] = v
        self.qc2[at, :] = self.qc1[at, :] + qc
        self.qr2[at, :] = self.qr1[at, :] + qr

    def step_three(self, i):
        at = tile_at(i)
        e, u, v, qc, qr = self.later(2, i, self.e2, self.u2, self.v2)
        qc = self.qc2[at, :] + qc
        qr = self.qr2[at, :] + qr
        change = (qc - west(qc) + qr - north(qr, self.qr_last[...])) * self.scale
        self.qr_last[...] = qr
        self.emit(i, e * (1.0 / 0.3), u, v, change)

    def run(self):
        self.fr_last[...] = jnp.zeros_like(self.fr_last)
        self.qr_last[...] = jnp.zeros_like(self.qr_last)
        for ref in (self.s, self.e1, self.e2):
            ref[tile_at(self.count), :] = jnp.zeros((SUB, self.wide), jnp.float32)
        stages = (self.step_three, self.step_two, self.step_one, self.prepare)
        for t in range(self.count + LAG * STEPS):
            for k, stage in enumerate(stages):
                i = t - LAG * (STEPS - k)
                if 0 <= i < self.count:
                    stage(i)


def raw_reader(bed, mask, kind, stress, hydro, side, unfold, valid):
    rows = bed.shape[0]
    span = rows // FOLD // SUB
    fields = raw_fields(bed, mask, kind, stress, hydro)

    def read(f, block):
        strip = side[tile_at(block % span), :]
        part = unfold(strip, (block // span) * FIELDS + f)
        if f == 1:
            part = jnp.where(valid, part, 0.0)
        main = fields[f][tile_at(block), :]
        return jnp.concatenate([main, part.astype(main.dtype)], axis=1)

    return read


def middle_kernel(own, weights, params, bed, mask, kind, stress, hydro, side, *refs):
    hydro_out, pay, *refs = refs[1:] if own else refs
    rows, cols = bed.shape
    quarter = rows // SUB // 4
    unfold, valid = side_lanes(lax.axis_index("tx") == 0)
    read = raw_reader(bed, mask, kind, stress, hydro, side, unfold, valid)
    mine = lax.axis_index("cond") % 2
    lower_half = mine == (1 if own else 0)
    first = jnp.where(lower_half, 2 * quarter, quarter) - 1
    emit = quarter_writer(first, quarter, cols, hydro_out, pay)

    def finish(i, e, u, v, change):
        if 1 <= i <= quarter:
            emit(i, e, u, v, change)

    Sweep(quarter + 2, cols + LANE, lambda f, i: read(f, first + i), finish, weights, params, refs).run()


def quarter_writer(first, quarter, cols, hydro_out, pay):
    lane = lanes_of((SUB, LANE))
    lanes = cols // LANE
    rims = [jnp.zeros((SUB, LANE), jnp.float32)]

    def emit(i, e, u, v, change):
        at = tile_at(first + i)
        for k, value in enumerate((e, u, v)):
            hydro_out[0, k, at, :] = value[:, :cols]
        g = i - 1
        for k in range(lanes):
            pay[tile_at(k * quarter + g), :] = change[:, k * LANE : (k + 1) * LANE]
        rims[0] = jnp.where(lane // 2 == g, pltpu.roll(change[:, cols:], 1 + 2 * g, 1), rims[0])
        if g == quarter - 1:
            pay[tile_at(lanes * quarter), :] = rims[0]

    return emit


def middle(own, weights, params, raw, side, hydro=None):
    rows, cols = raw[0].shape
    given = (hydro,) if own else ()
    return pl.pallas_call(
        functools.partial(middle_kernel, own),
        name="middle_own" if own else "middle_other",
        out_shape=[
            pltpu.VMEM(raw[4].shape, jnp.float32),
            pltpu.VMEM((cols // LANE * rows // 4 + SUB, LANE), jnp.float32),
        ],
        in_specs=[SMEM, SMEM] + [VMEM] * (6 + own),
        out_specs=[VMEM, VMEM],
        scratch_shapes=Sweep.scratch(rows // SUB // 4 + 2, cols + LANE),
        input_output_aliases={8: 0} if own else {},
        compiler_params=pltpu.CompilerParams(vmem_limit_bytes=10 * MIB),
        cost_estimate=cost(4),
    )(weights, params, *held(*raw, side, *given))


def edge_kernel(
    own, weights, params, bed, mask, kind, stress, hydro, side, far_a, far_b, hydro_in,
    hydro_out, pay, ends_r, ends_i, *refs,
):
    rows, cols = bed.shape
    blocks = rows // SUB
    quarter = blocks // 4
    wide = cols + LANE
    lanes = cols // LANE
    unfold, valid = side_lanes(lax.axis_index("tx") == 0)
    read = raw_reader(bed, mask, kind, stress, hydro, side, unfold, valid)
    mine = lax.axis_index("cond") % 2
    top = mine == (0 if own else 1)
    from_a = top == (lax.axis_index("ty") % 2 == 1)
    first = jnp.where(top, -1, blocks - quarter - 1)

    inner = jnp.where(top, quarter, blocks - quarter - 1)
    for f in range(FIELDS):
        body = read(f, inner)
        parts = []
        for k in range(lanes):
            at = pl.ds(k * GROUP + f // 2 * SUB, SUB)
            part = jnp.where(from_a, far_a[at, :], far_b[at, :])
            moved = pltpu.roll(part, HALO, 0)
            parts.append(jnp.where(top, moved, part) if f % 2 == 0 else jnp.where(top, part, moved))
        at = pl.ds(lanes * GROUP, SUB)
        corner = jnp.where(from_a, far_a[at, :], far_b[at, :])
        corner = jnp.where(top, unfold(corner, (FOLD - 1) * FIELDS + f), unfold(corner, f))
        if f == 1:
            corner = jnp.where(valid, corner, 0.0)
        outer = jnp.concatenate(parts + [corner], axis=1).astype(body.dtype)
        which, k = SPOTS[f]
        ref = (ends_r, ends_i)[which]
        ref[0, k] = jnp.where(top, outer, body)
        ref[1, k] = jnp.where(top, body, outer)

    def get(f, i):
        if i == 0 or i == quarter + 1:
            which, k = SPOTS[f]
            return (ends_r, ends_i)[which][0 if i == 0 else 1, k]
        return read(f, first + i)

    row = rows_of((SUB, LANE))
    emit = quarter_writer(first, quarter, cols, hydro_out, pay)
    outside = []

    def finish(i, e, u, v, change):
        if i == 0:
            outside.append(pltpu.roll(change, 1, 0))
        elif i == quarter + 1:
            rim = jnp.where(top, outside[0], change)
            total = rim[:, :LANE]
            for k in range(1, lanes):
                total = jnp.where(row == k, pltpu.roll(rim[:, k * LANE : (k + 1) * LANE], k, 0), total)
            pay[tile_at(lanes * quarter + 1), :] = total
        else:
            emit(i, e, u, v, change)

    Sweep(quarter + 2, wide, get, finish, weights, params, refs).run()


def edge(own, weights, params, raw, side, far_a, far_b, hydro):
    rows, cols = raw[0].shape
    wide = cols + LANE
    return pl.pallas_call(
        functools.partial(edge_kernel, own),
        name="edge_own" if own else "edge_other",
        out_shape=[
            pltpu.VMEM(hydro.shape, jnp.float32),
            pltpu.VMEM((cols // LANE * rows // 4 + 2 * SUB, LANE), jnp.float32),
        ],
        in_specs=[SMEM, SMEM] + [VMEM] * 9,
        out_specs=[VMEM, VMEM],
        scratch_shapes=[pltpu.VMEM((2, 6, SUB, wide), jnp.float32), pltpu.VMEM((2, 2, SUB, wide), jnp.int32)]
        + Sweep.scratch(rows // SUB // 4 + 2, wide),
        input_output_aliases={10: 0},
        compiler_params=pltpu.CompilerParams(vmem_limit_bytes=12 * MIB),
        cost_estimate=cost(4),
    )(weights, params, *held(*raw, side, far_a, far_b, hydro))


class Update:
    def __init__(self, bed, side, far_a, far_b, own_m, got_m, own_e, got_e, change_v, next_v):
        self.bed, self.side, self.far_a, self.far_b = bed, side, far_a, far_b
        self.parts = {"m": (own_m, got_m), "e": (own_e, got_e)}
        self.change_v, self.next_v = change_v, next_v
        rows, self.cols = bed.shape
        self.blocks = rows // SUB
        self.quarter = self.blocks // 4
        self.lanes = self.cols // LANE
        self.wide = self.cols + LANE
        self.unfold, _ = side_lanes(lax.axis_index("tx") == 0)
        self.mine = lax.axis_index("cond") % 2
        self.odd = lax.axis_index("ty") % 2 == 1
        col = lanes_of((SUB, self.wide))
        last_c = lax.axis_index("tx") == lax.axis_size("tx") - 1
        first_c = lax.axis_index("tx") == 0
        self.shut_c = (last_c & (col == self.cols - 1)) | (first_c & (col == self.wide - 1))
        self.last_row = rows_of((SUB, self.wide)) == SUB - 1
        self.rims = {}

    def merged(self, q, block):
        own, got = self.parts["e" if q in (0, 3) else "m"]
        at = tile_at(block)
        return jnp.where(self.mine == q // 2, own[at, :], got[at, :])

    def outside(self, q):
        rim = self.merged(q, self.lanes * self.quarter + 1)
        parts = []
        for k in range(self.lanes):
            at = tile_at(k * GROUP // SUB)
            a, b = self.far_a[at, :], self.far_b[at, :]
            if q == 0:
                z = jnp.where(self.odd, a, b) + pltpu.roll(rim, (2 * SUB + HALO - 1 - k) % SUB, 0)
                parts.append(pltpu.roll(z, HALO, 0))
            else:
                parts.append(jnp.where(self.odd, b, a) + pltpu.roll(rim, (SUB - k) % SUB, 0))
        return jnp.concatenate(parts + [jnp.zeros((SUB, LANE), jnp.float32)], axis=1)

    def level(self, b, keep):
        if b == -1:
            return self.outside(0)
        if b == self.blocks:
            return self.outside(3)
        q, g = divmod(b, self.quarter)
        change = jnp.concatenate([self.merged(q, k * self.quarter + g) for k in range(self.lanes)], axis=1)
        if keep:
            self.change_v[tile_at(b), :] = change
        if q not in self.rims:
            self.rims[q] = self.merged(q, self.lanes * self.quarter)
        span = self.blocks // FOLD
        cols_bed = self.unfold(self.side[tile_at(b % span), :], b // span * FIELDS)
        cols_change = pltpu.roll(self.rims[q], LANE - 1 - 2 * g, 1)
        return jnp.concatenate([self.bed[tile_at(b), :] + change, cols_bed + cols_change], axis=1)

    def spill(self, slope):
        return 0.25 * (slope - jnp.clip(slope, -1.0, 1.0))

    def south_face(self, z, lower, b):
        out = self.spill(south(z, lower) - z)
        if b == -1:
            return jnp.where((lax.axis_index("ty") == 0) & self.last_row, 0.0, out)
        if b == self.blocks - 1:
            return jnp.where((lax.axis_index("ty") == lax.axis_size("ty") - 1) & self.last_row, 0.0, out)
        return out

    def run(self, first, stop, keep, after=lambda b: None):
        z = self.level(first - 1, keep)
        lower = self.level(first, keep)
        gr = self.south_face(z, lower, first - 1)
        for b in range(first, stop):
            z, lower = lower, self.level(b + 1, keep)
            gr_above, gr = gr, self.south_face(z, lower, b)
            gc = jnp.where(self.shut_c, 0.0, self.spill(east(z) - z))
            out = z + gc - west(gc) + gr - north(gr, gr_above)
            self.next_v[tile_at(b), :] = out[:, : self.cols]
            after(b)


def bed_middle_kernel(
    bed, side, far_a, far_b, own_m, got_m, hydro, bed_next, bed_change, hydro_out, change_v, next_v, sems
):
    rows = bed.shape[0]
    quarter = rows // SUB // 4
    copies = [pltpu.make_async_copy(hydro, hydro_out, sems.at[0])]
    copies[0].start()
    update = Update(bed, side, far_a, far_b, own_m, got_m, None, None, change_v, next_v)
    update.run(quarter + 1, 3 * quarter - 1, True)
    for src, dst, low, high in (
        (change_v, bed_change, quarter, 3 * quarter),
        (next_v, bed_next, quarter + 1, 3 * quarter - 1),
    ):
        at = pl.ds(low * SUB, (high - low) * SUB)
        copies.append(pltpu.make_async_copy(src.at[at], dst.at[at], sems.at[len(copies)]))
        copies[-1].start()
    for copy in copies:
        copy.wait()


def bed_edge_kernel(
    bed, side, far_a, far_b, own_m, got_m, own_e, got_e, next_in, change_in, bed_next, bed_change,
    change_v, next_v, sems,
):
    rows = bed.shape[0]
    blocks = rows // SUB
    quarter = blocks // 4
    update = Update(bed, side, far_a, far_b, own_m, got_m, own_e, got_e, change_v, next_v)
    copies = []

    def send(src, dst, low, high):
        at = pl.ds(low * SUB, (high - low) * SUB)
        copies.append(pltpu.make_async_copy(src.at[at], dst.at[at], sems.at[len(copies)]))
        copies[-1].start()

    update.run(0, quarter + 1, True)
    send(change_v, bed_change, 0, quarter)
    send(next_v, bed_next, 0, quarter + 1)
    update.run(blocks - quarter - 1, blocks, True)
    send(change_v, bed_change, blocks - quarter, blocks)
    send(next_v, bed_next, blocks - quarter - 1, blocks)
    for copy in copies:
        copy.wait()


def bed_scratch(rows, cols):
    return [
        pltpu.VMEM((rows, cols), jnp.float32),
        pltpu.VMEM((rows, cols), jnp.float32),
        pltpu.SemaphoreType.DMA((4,)),
    ]


def bed_middle(bed, side, far_a, far_b, own_m, got_m, hydro):
    return pl.pallas_call(
        bed_middle_kernel,
        name="bed_middle",
        out_shape=[pltpu.HBM(x.shape, jnp.float32) for x in (bed, bed, hydro)],
        in_specs=[VMEM] * 7,
        out_specs=[ANY] * 3,
        scratch_shapes=bed_scratch(*bed.shape),
        compiler_params=pltpu.CompilerParams(vmem_limit_bytes=6 * MIB),
        cost_estimate=cost(4),
    )(*held(bed, side, far_a, far_b, own_m, got_m, hydro))


def bed_edge(bed, side, far_a, far_b, own_m, got_m, own_e, got_e, bed_next, bed_change):
    return pl.pallas_call(
        bed_edge_kernel,
        name="bed_edge",
        out_shape=[pltpu.HBM(bed.shape, jnp.float32)] * 2,
        in_specs=[VMEM] * 8 + [ANY] * 2,
        out_specs=[ANY] * 2,
        scratch_shapes=bed_scratch(*bed.shape),
        input_output_aliases={8: 0, 9: 1},
        compiler_params=pltpu.CompilerParams(vmem_limit_bytes=6 * MIB),
        cost_estimate=cost(2),
    )(
        *held(bed, side, far_a, far_b, own_m, got_m, own_e, got_e),
        *held(bed_next, bed_change, space=pltpu.HBM),
    )


def shards(bed, land_mask, cell_class, weights, cond_params, wave_stress, hydro_state):
    ny = lax.axis_size("ty")
    nc = lax.axis_size("cond")
    raw = (bed, land_mask, cell_class, wave_stress, hydro_state)
    swap = [(i, i ^ 1) for i in range(nc)]

    def pairs(first):
        return [p for i in range(first, ny - 1, 2) for p in ((i, i + 1), (i + 1, i))]

    def over_chips(part, beside=()):
        reach = 2
        while reach < nc:
            got = lax.ppermute(part, "cond", [(i, i ^ reach) for i in range(nc)])
            got, beside = lax.optimization_barrier((got, beside))
            part = part + got
            reach = 2 * reach
        return part, beside

    side = lax.ppermute(pack_side(*raw), "tx", [(0, 1), (1, 0)])
    pays = pack_rows(*raw)
    odd = lax.axis_index("ty") % 2 == 1
    corners = [side[:SUB], side[-SUB:]]
    far_a = jnp.concatenate([pays[0], jnp.where(odd, corners[0], corners[1])])
    far_b = jnp.concatenate([pays[1], jnp.where(odd, corners[1], corners[0])])
    far_a = lax.ppermute(far_a, "ty", pairs(0))
    far_b = lax.ppermute(far_b, "ty", pairs(1))

    hydro, pay = middle(False, weights, cond_params, raw, side)
    got = lax.ppermute(pay, "cond", swap)
    hydro, pay = middle(True, weights, cond_params, raw, side, hydro)
    part_m = pay + got
    hydro, part_m = lax.optimization_barrier((hydro, part_m))
    hydro, pay = edge(False, weights, cond_params, raw, side, far_a, far_b, hydro)
    got = lax.ppermute(pay, "cond", swap)
    hydro, pay = edge(True, weights, cond_params, raw, side, far_a, far_b, hydro)
    part_e = pay + got
    own_m, (hydro, _) = over_chips(part_m, (hydro, part_e))
    got_m = lax.ppermute(own_m, "cond", swap)
    bed_next, bed_change, hydro = bed_middle(bed, side, far_a, far_b, own_m, got_m, hydro)
    own_e, (bed_next, bed_change) = over_chips(part_e, (bed_next, bed_change))
    got_e = lax.ppermute(own_e, "cond", swap)
    bed_next, bed_change = bed_edge(
        bed, side, far_a, far_b, own_m, got_m, own_e, got_e, bed_next, bed_change
    )
    return bed_next, bed_change, hydro


def solution(mesh):
    in_specs = (
        P("ty", "tx"),
        P("ty", "tx"),
        P("ty", "tx"),
        P(),
        P("cond", None),
        P("cond", None, "ty", "tx"),
        P("cond", None, "ty", "tx"),
    )
    out_specs = (P("ty", "tx"), P("ty", "tx"), P("cond", None, "ty", "tx"))
    return jax.shard_map(shards, mesh=mesh, in_specs=in_specs, out_specs=out_specs, check_vma=False)
```

time: 50.3 us -> 48.3 us (0.960)
  waiting for transfers between devices: 16.3 us -> 9.43 us
  local copies, waits for them, and re-layouts: 1.71 us -> 5.31 us
  Pallas kernels: 18 us -> 19 us
    ppermute x9, waiting for transfers between devices: 16.3 us -> 9.43 us  [the longest x2 7.94 us: over_chips(): got = lax.ppermute(part, 'cond', [(i, i ^ reach) for i in range(nc)])]
    unnamed x15 -> x22, local copies, waits for them, and re-layouts: 1.69 us -> 5.29 us
    pallas_call x5 -> x8, Pallas kernels: 18 us -> 19 us  [the longest x2 6.25 us: edge(): pl.pallas_call(functools.partial(edge_kernel, own), name='edge_own' if ow...]
  transfers between devices with their start and end apart: 9 -> 9, of which waited for: 5 -> 4; matrix products, arithmetic and copies ran while one was open for 3% -> 0% of each run, Pallas kernels for 12% -> 25%
where the time goes in v1:
time: 48.3 us; the launch traced here: 47.9 us
  Pallas kernels  19 us (39%)
  starting transfers between devices  13.1 us (27%)
  waiting for transfers between devices  9.43 us (20%)
  local copies, waits for them, and re-layouts  5.31 us (11%)
  between operations  0.87 us (2%)
    ppermute x2, waiting for transfers between devices, over_chips(): got = lax.ppermute(part, 'cond', [(i, i ^ reach) for i in range(nc)])  7.94 us
    pallas_call x2, Pallas kernels, edge(): pl.pallas_call(functools.partial(edge_kernel, own), name='edge_own' if ow...  6.25 us
    pallas_call x2, Pallas kernels, middle(): pl.pallas_call(functools.partial(middle_kernel, own), name='middle_own' i...  5.88 us
    unnamed x22, local copies, waits for them, and re-layouts  5.29 us
    ppermute x1, starting transfers between devices, shards(): far_b = lax.ppermute(far_b, 'ty', pairs(1))  4.48 us
    ppermute x2, starting transfers between devices, shards(): got = lax.ppermute(pay, 'cond', swap)  2.57 us
    ppermute x2, starting transfers between devices, over_chips(): got = lax.ppermute(part, 'cond', [(i, i ^ reach) for i in range(nc)])  2.46 us
    pallas_call x1, Pallas kernels, bed_middle(): pl.pallas_call(bed_middle_kernel, name='bed_middle', out_shape=[pltpu.HBM...  2.03 us
  transfers between devices with their start and end apart: 9, of which 4 were waited for; matrix products, arithmetic and copies ran while one was open for 0% of the time, Pallas kernels for 25%

profile of v1, /device:TPU:9, one launch (start us, length us, event | category | flops | bytes accessed | tf_op | source)
XLA Modules:
  0.0 47.9 jit_solution(15631606983589066104)
XLA Ops:
  0.6 1.7 %pack_side.1 = f32[64,128]{1,0:T(8,128)S(1)} custom-call(f32[256,1024]{1,0:T(8,128)} %bed.15, s32[256,1024]{1,0:T(8,128)} %mask.11, s32[256,1024]{1,0:T(8,128)} %kind.11, f32[1,2,256,1024]{3,2,1,0:T(8,128)} %stress.11, f32[1,3,256,1024]{3,2,1,0:T(8,128)} %hydro.11), custom_call_target="tpu_custom_call" | custom-call | flops 2000000000 | tf_op jit(solution)/shard_map/pack_side/pallas_call | solution.py:97
  2.4 1.3 %collective-permute-start = (f32[64,128]{1,0:T(8,128)S(1)}, f32[64,128]{1,0:T(8,128)S(1)}, u32[]{:S(2)}, u32[]{:S(2)}) collective-permute-start(f32[64,128]{1,0:T(8,128)S(1)} %pack_side.1), channel_id=1, source_target_pairs={{0,1},{1,0},{2,3},{3,2},{4,5},{5,4},{6,7},{7,6},{8,9},{9,8},{10,11... | collective-permute-start | bytes 98312 | tf_op jit(solution)/shard_map/ppermute | solution.py:615
  3.7 1.2 %pack_rows.1 = f32[2,256,128]{2,1,0:T(8,128)S(1)} custom-call(f32[256,1024]{1,0:T(8,128)} %bed.15, s32[256,1024]{1,0:T(8,128)} %mask.11, s32[256,1024]{1,0:T(8,128)} %kind.11, f32[1,2,256,1024]{3,2,1,0:T(8,128)} %stress.11, f32[1,3,256,1024]{3,2,1,0:T(8,128)} %hydro.11), custom_call_target="tpu_custom_call" | custom-call | flops 2000000000 | tf_op jit(solution)/shard_map/pack_rows/pallas_call | solution.py:143
  4.9 0.3 collective-permute-done.side
  5.3 4.5 %collective-permute-start.2 = (f32[264,128]{1,0:T(8,128)S(1)}, f32[264,128]{1,0:T(8,128)S(1)}, u32[]{:S(2)}, u32[]{:S(2)}) collective-permute-start(f32[264,128]{1,0:T(8,128)S(1)} %pad_maximum_fusion.1), channel_id=1, source_target_pairs={{2,4},{4,2},{3,5},{5,3},{10,12},{12,10},{11,13},{13,11},{18,20},{2... | collective-permute-start | bytes 405512 | tf_op jit(solution)/shard_map/ppermute | solution.py:622
  9.9 1.6 %copy-done.1 = f32[1,2,256,1024]{3,2,1,0:T(8,128)S(1)} copy-done((f32[1,2,256,1024]{3,2,1,0:T(8,128)S(1)}, f32[1,2,256,1024]{3,2,1,0:T(8,128)}, u32[]{:S(2)}) %copy-start.1) | copy-done | bytes 2097176
  11.5 1.2 %copy-done.3 = s32[256,1024]{1,0:T(8,128)S(1)} copy-done((s32[256,1024]{1,0:T(8,128)S(1)}, s32[256,1024]{1,0:T(8,128)}, u32[]{:S(2)}) %copy-start.3) | copy-done | bytes 1048600
  12.7 1.2 %copy-done.5 = s32[256,1024]{1,0:T(8,128)S(1)} copy-done((s32[256,1024]{1,0:T(8,128)S(1)}, s32[256,1024]{1,0:T(8,128)}, u32[]{:S(2)}) %copy-start.5) | copy-done | bytes 1048600
  13.9 1.2 %copy-done.7 = f32[256,1024]{1,0:T(8,128)S(1)} copy-done((f32[256,1024]{1,0:T(8,128)S(1)}, f32[256,1024]{1,0:T(8,128)}, u32[]{:S(2)}) %copy-start.7) | copy-done | bytes 1048600
  15.1 2.9 %middle_other.1 = (f32[1,3,256,1024]{3,2,1,0:T(8,128)S(1)}, f32[520,128]{1,0:T(8,128)S(1)}) custom-call(s32[4]{0:T(128)S(1)} %copy-done.9, f32[1,4]{1,0:T(1,128)S(1)} %copy-done.10, f32[256,1024]{1,0:T(8,128)S(1)} %copy-done.7, s32[256,1024]{1,0:T(8,128)S(1)} %copy-done.3, s32[256,1024]{1,0:T(8,128)S(1)} %copy-done.5, f32[1,2,256,1024]{3,2,1,0:T(8,128)S(1)} %copy-done.1, ...), custom_call_target="tpu_custom_call" | custom-call | flops 4000000000 | tf_op jit(solution)/shard_map/middle_other/pallas_call | solution.py:339
  18.1 2.5 %collective-permute-start.3 = (f32[520,128]{1,0:T(8,128)S(1)}, f32[520,128]{1,0:T(8,128)S(1)}, u32[]{:S(2)}, u32[]{:S(2)}) collective-permute-start(f32[520,128]{1,0:T(8,128)S(1)} %get-tuple-element.26), channel_id=1, source_target_pairs={{0,8},{8,0},{16,24},{24,16},{1,9},{9,1},{17,25},{25,17},{2,10},{10... | collective-permute-start | bytes 798728 | tf_op jit(solution)/shard_map/ppermute | solution.py:625
  20.5 2.9 %middle_own.1 = (f32[1,3,256,1024]{3,2,1,0:T(8,128)S(1)}, f32[520,128]{1,0:T(8,128)S(1)}) custom-call(s32[4]{0:T(128)S(1)} %copy-done.9, f32[1,4]{1,0:T(1,128)S(1)} %copy-done.10, f32[256,1024]{1,0:T(8,128)S(1)} %copy-done.7, s32[256,1024]{1,0:T(8,128)S(1)} %copy-done.3, s32[256,1024]{1,0:T(8,128)S(1)} %copy-done.5, ...), custom_call_target="tpu_custom_call", output_to_operand_aliasing={{0}: (8, {})} | custom-call | flops 4000000000 | tf_op jit(solution)/shard_map/middle_own/pallas_call | solution.py:339
  23.6 3.1 %edge_other.1 = (f32[1,3,256,1024]{3,2,1,0:T(8,128)S(1)}, f32[528,128]{1,0:T(8,128)S(1)}) custom-call(s32[4]{0:T(128)S(1)} %copy-done.9, f32[1,4]{1,0:T(1,128)S(1)} %copy-done.10, f32[256,1024]{1,0:T(8,128)S(1)} %copy-done.8, s32[256,1024]{1,0:T(8,128)S(1)} %copy-done.4, s32[256,1024]{1,0:T(8,128)S(1)} %copy-done.6, ...), custom_call_target="tpu_custom_call", output_to_operand_aliasing={{0}: (10, {})} | custom-call | flops 4000000000 | tf_op jit(solution)/shard_map/edge_other/pallas_call | solution.py:419
  26.7 0.1 collective-permute-start.5
  26.9 1.2 %collective-permute-start.4 = (f32[520,128]{1,0:T(8,128)S(1)}, f32[520,128]{1,0:T(8,128)S(1)}, u32[]{:S(2)}, u32[]{:S(2)}) collective-permute-start(f32[520,128]{1,0:T(8,128)S(1)} %add.17), channel_id=1, source_target_pairs={{0,16},{8,24},{16,0},{24,8},{1,17},{9,25},{17,1},{25,9},{2,18},{10... | collective-permute-start | bytes 798728 | tf_op jit(solution)/shard_map/ppermute | solution.py:609
  28.1 3.1 %edge_own.1 = (f32[1,3,256,1024]{3,2,1,0:T(8,128)S(1)}, f32[528,128]{1,0:T(8,128)S(1)}) custom-call(s32[4]{0:T(128)S(1)} %copy-done.9, f32[1,4]{1,0:T(1,128)S(1)} %copy-done.10, f32[256,1024]{1,0:T(8,128)S(1)} %copy-done.8, s32[256,1024]{1,0:T(8,128)S(1)} %copy-done.4, s32[256,1024]{1,0:T(8,128)S(1)} %copy-done.6, ...), custom_call_target="tpu_custom_call", output_to_operand_aliasing={{0}: (10, {})} | custom-call | flops 4000000000 | tf_op jit(solution)/shard_map/edge_own/pallas_call | solution.py:419
  31.3 3.1 %collective-permute-done.4 = f32[520,128]{1,0:T(8,128)S(1)} collective-permute-done((f32[520,128]{1,0:T(8,128)S(1)}, f32[520,128]{1,0:T(8,128)S(1)}, u32[]{:S(2)}, u32[]{:S(2)}) %collective-permute-start.4) | collective-permute-done | bytes 266272 | tf_op jit(solution)/shard_map/ppermute | solution.py:609
  34.5 1.3 %collective-permute-start.6 = (f32[520,128]{1,0:T(8,128)S(1)}, f32[520,128]{1,0:T(8,128)S(1)}, u32[]{:S(2)}, u32[]{:S(2)}) collective-permute-start(f32[520,128]{1,0:T(8,128)S(1)} %add.19.own_m), channel_id=1, source_target_pairs={{0,8},{8,0},{16,24},{24,16},{1,9},{9,1},{17,25},{25,17},{2,10},{10... | collective-permute-start | bytes 798728 | tf_op jit(solution)/shard_map/ppermute | solution.py:634
  35.8 1.2 %collective-permute-start.7 = (f32[528,128]{1,0:T(8,128)S(1)}, f32[528,128]{1,0:T(8,128)S(1)}, u32[]{:S(2)}, u32[]{:S(2)}) collective-permute-start(f32[528,128]{1,0:T(8,128)S(1)} %add.18), channel_id=1, source_target_pairs={{0,16},{8,24},{16,0},{24,8},{1,17},{9,25},{17,1},{25,9},{2,18},{10... | collective-permute-start | bytes 811016 | tf_op jit(solution)/shard_map/ppermute | solution.py:609
  37.0 2.0 %bed_middle.1 = (f32[256,1024]{1,0:T(8,128)}, f32[256,1024]{1,0:T(8,128)}, f32[1,3,256,1024]{3,2,1,0:T(8,128)}) custom-call(f32[256,1024]{1,0:T(8,128)S(1)} %copy-done.8, f32[64,128]{1,0:T(8,128)S(1)} %collective-permute-done.side, f32[264,128]{1,0:T(8,128)S(1)} %collective-permute-done.1.far_a, f32[264,128]{1,0:T(8,128)S(1)} %collective-permute-done.2.far_b, ...), custom_call_target="tpu_custom_call" | custom-call | flops 4000000000 | tf_op jit(solution)/shard_map/bed_middle/pallas_call | solution.py:568
  39.1 4.8 %collective-permute-done.7 = f32[528,128]{1,0:T(8,128)S(1)} collective-permute-done((f32[528,128]{1,0:T(8,128)S(1)}, f32[528,128]{1,0:T(8,128)S(1)}, u32[]{:S(2)}, u32[]{:S(2)}) %collective-permute-start.7) | collective-permute-done | bytes 270368 | tf_op jit(solution)/shard_map/ppermute | solution.py:609
  43.9 0.9 %collective-permute-start.8 = (f32[528,128]{1,0:T(8,128)S(1)}, f32[528,128]{1,0:T(8,128)S(1)}, u32[]{:S(2)}, u32[]{:S(2)}) collective-permute-start(f32[528,128]{1,0:T(8,128)S(1)} %add.20.own_e), channel_id=1, source_target_pairs={{0,8},{8,0},{16,24},{24,16},{1,9},{9,1},{17,25},{25,17},{2,10},{10... | collective-permute-start | bytes 811016 | tf_op jit(solution)/shard_map/ppermute | solution.py:637
  44.8 1.2 %collective-permute-done.8.got_e = f32[528,128]{1,0:T(8,128)S(1)} collective-permute-done((f32[528,128]{1,0:T(8,128)S(1)}, f32[528,128]{1,0:T(8,128)S(1)}, u32[]{:S(2)}, u32[]{:S(2)}) %collective-permute-start.8) | collective-permute-done | bytes 270368 | tf_op jit(solution)/shard_map/ppermute | solution.py:637
  46.0 2.0 %bed_edge.1 = (f32[256,1024]{1,0:T(8,128)}, f32[256,1024]{1,0:T(8,128)}) custom-call(f32[256,1024]{1,0:T(8,128)S(1)} %copy-done.8, f32[64,128]{1,0:T(8,128)S(1)} %collective-permute-done.side, f32[264,128]{1,0:T(8,128)S(1)} %collective-permute-done.1.far_a, ...), custom_call_target="tpu_custom_call", output_to_operand_aliasing={{0}: (8, {}), {1}: (9, {})} | custom-call | flops 2000000000 | tf_op jit(solution)/shard_map/bed_edge/pallas_call | solution.py:581
  (32 shorter events, 0.3 us)
Async XLA Ops:
  2.4 7.5 %copy-start = (f32[1,3,256,1024]{3,2,1,0:T(8,128)S(1)}, f32[1,3,256,1024]{3,2,1,0:T(8,128)}, u32[]{:S(2)}) copy-start(f32[1,3,256,1024]{3,2,1,0:T(8,128)} %hydro.11) | copy-start | bytes 9437188
  2.4 7.5 %copy-start.9 = (s32[4]{0:T(128)S(1)}, s32[4]{0:T(128)}, u32[]{:S(2)}) copy-start(s32[4]{0:T(128)} %weights.7) | copy-start | bytes 52
  2.4 7.5 %copy-start.10 = (f32[1,4]{1,0:T(1,128)S(1)}, f32[1,4]{1,0:T(1,128)}, u32[]{:S(2)}) copy-start(f32[1,4]{1,0:T(1,128)} %params.7) | copy-start | bytes 52
  2.4 2.8 %collective-permute-start = (f32[64,128]{1,0:T(8,128)S(1)}, f32[64,128]{1,0:T(8,128)S(1)}, u32[]{:S(2)}, u32[]{:S(2)}) collective-permute-start(f32[64,128]{1,0:T(8,128)S(1)} %pack_side.1), channel_id=1, source_target_pairs={{0,1},{1,0},{2,3},{3,2},{4,5},{5,4},{6,7},{7,6},{8,9},{9,8},{10,11... | collective-permute-start | bytes 98312 | tf_op jit(solution)/shard_map/ppermute | solution.py:615
  5.2 18.3 %collective-permute-start.1 = (f32[264,128]{1,0:T(8,128)S(1)}, f32[264,128]{1,0:T(8,128)S(1)}, u32[]{:S(2)}, u32[]{:S(2)}) collective-permute-start(f32[264,128]{1,0:T(8,128)S(1)} %pad_maximum_fusion), channel_id=1, source_target_pairs={{0,2},{2,0},{4,6},{6,4},{1,3},{3,1},{5,7},{7,5},{8,10},{10,8},{12,... | collective-permute-start | bytes 405512 | tf_op jit(solution)/shard_map/ppermute | solution.py:621
  5.3 18.2 %collective-permute-start.2 = (f32[264,128]{1,0:T(8,128)S(1)}, f32[264,128]{1,0:T(8,128)S(1)}, u32[]{:S(2)}, u32[]{:S(2)}) collective-permute-start(f32[264,128]{1,0:T(8,128)S(1)} %pad_maximum_fusion.1), channel_id=1, source_target_pairs={{2,4},{4,2},{3,5},{5,3},{10,12},{12,10},{11,13},{13,11},{18,20},{2... | collective-permute-start | bytes 405512 | tf_op jit(solution)/shard_map/ppermute | solution.py:622
  9.9 1.6 %copy-start.1 = (f32[1,2,256,1024]{3,2,1,0:T(8,128)S(1)}, f32[1,2,256,1024]{3,2,1,0:T(8,128)}, u32[]{:S(2)}) copy-start(f32[1,2,256,1024]{3,2,1,0:T(8,128)} %stress.11) | copy-start | bytes 6291460
  11.4 1.2 %copy-start.3 = (s32[256,1024]{1,0:T(8,128)S(1)}, s32[256,1024]{1,0:T(8,128)}, u32[]{:S(2)}) copy-start(s32[256,1024]{1,0:T(8,128)} %mask.11) | copy-start | bytes 3145732
  12.7 1.2 %copy-start.5 = (s32[256,1024]{1,0:T(8,128)S(1)}, s32[256,1024]{1,0:T(8,128)}, u32[]{:S(2)}) copy-start(s32[256,1024]{1,0:T(8,128)} %kind.11) | copy-start | bytes 3145732
  13.9 1.2 %copy-start.7 = (f32[256,1024]{1,0:T(8,128)S(1)}, f32[256,1024]{1,0:T(8,128)}, u32[]{:S(2)}) copy-start(f32[256,1024]{1,0:T(8,128)} %bed.15) | copy-start | bytes 3145732
  18.1 5.4 %collective-permute-start.3 = (f32[520,128]{1,0:T(8,128)S(1)}, f32[520,128]{1,0:T(8,128)S(1)}, u32[]{:S(2)}, u32[]{:S(2)}) collective-permute-start(f32[520,128]{1,0:T(8,128)S(1)} %get-tuple-element.26), channel_id=1, source_target_pairs={{0,8},{8,0},{16,24},{24,16},{1,9},{9,1},{17,25},{25,17},{2,10},{10... | collective-permute-start | bytes 798728 | tf_op jit(solution)/shard_map/ppermute | solution.py:625
  20.5 3.0 %copy-start.2 = (f32[1,2,256,1024]{3,2,1,0:T(8,128)S(1)}, f32[1,2,256,1024]{3,2,1,0:T(8,128)}, u32[]{:S(2)}) copy-start(f32[1,2,256,1024]{3,2,1,0:T(8,128)} %stress.11) | copy-start | bytes 6291460
  20.5 3.0 %copy-start.4 = (s32[256,1024]{1,0:T(8,128)S(1)}, s32[256,1024]{1,0:T(8,128)}, u32[]{:S(2)}) copy-start(s32[256,1024]{1,0:T(8,128)} %mask.11) | copy-start | bytes 3145732
  20.5 3.1 %copy-start.6 = (s32[256,1024]{1,0:T(8,128)S(1)}, s32[256,1024]{1,0:T(8,128)}, u32[]{:S(2)}) copy-start(s32[256,1024]{1,0:T(8,128)} %kind.11) | copy-start | bytes 3145732
  20.5 3.1 %copy-start.8 = (f32[256,1024]{1,0:T(8,128)S(1)}, f32[256,1024]{1,0:T(8,128)}, u32[]{:S(2)}) copy-start(f32[256,1024]{1,0:T(8,128)} %bed.15) | copy-start | bytes 3145732
  26.7 4.5 %collective-permute-start.5 = (f32[528,128]{1,0:T(8,128)S(1)}, f32[528,128]{1,0:T(8,128)S(1)}, u32[]{:S(2)}, u32[]{:S(2)}) collective-permute-start(f32[528,128]{1,0:T(8,128)S(1)} %get-tuple-element.32), channel_id=1, source_target_pairs={{0,8},{8,0},{16,24},{24,16},{1,9},{9,1},{17,25},{25,17},{2,10},{10... | collective-permute-start | bytes 811016 | tf_op jit(solution)/shard_map/ppermute | solution.py:630
  26.9 7.6 %collective-permute-start.4 = (f32[520,128]{1,0:T(8,128)S(1)}, f32[520,128]{1,0:T(8,128)S(1)}, u32[]{:S(2)}, u32[]{:S(2)}) collective-permute-start(f32[520,128]{1,0:T(8,128)S(1)} %add.17), channel_id=1, source_target_pairs={{0,16},{8,24},{16,0},{24,8},{1,17},{9,25},{17,1},{25,9},{2,18},{10... | collective-permute-start | bytes 798728 | tf_op jit(solution)/shard_map/ppermute | solution.py:609
  34.5 2.6 %collective-permute-start.6 = (f32[520,128]{1,0:T(8,128)S(1)}, f32[520,128]{1,0:T(8,128)S(1)}, u32[]{:S(2)}, u32[]{:S(2)}) collective-permute-start(f32[520,128]{1,0:T(8,128)S(1)} %add.19.own_m), channel_id=1, source_target_pairs={{0,8},{8,0},{16,24},{24,16},{1,9},{9,1},{17,25},{25,17},{2,10},{10... | collective-permute-start | bytes 798728 | tf_op jit(solution)/shard_map/ppermute | solution.py:634
  35.8 8.1 %collective-permute-start.7 = (f32[528,128]{1,0:T(8,128)S(1)}, f32[528,128]{1,0:T(8,128)S(1)}, u32[]{:S(2)}, u32[]{:S(2)}) collective-permute-start(f32[528,128]{1,0:T(8,128)S(1)} %add.18), channel_id=1, source_target_pairs={{0,16},{8,24},{16,0},{24,8},{1,17},{9,25},{17,1},{25,9},{2,18},{10... | collective-permute-start | bytes 811016 | tf_op jit(solution)/shard_map/ppermute | solution.py:609
  43.9 2.1 %collective-permute-start.8 = (f32[528,128]{1,0:T(8,128)S(1)}, f32[528,128]{1,0:T(8,128)S(1)}, u32[]{:S(2)}, u32[]{:S(2)}) collective-permute-start(f32[528,128]{1,0:T(8,128)S(1)} %add.20.own_e), channel_id=1, source_target_pairs={{0,8},{8,0},{16,24},{24,16},{1,9},{9,1},{17,25},{25,17},{2,10},{10... | collective-permute-start | bytes 811016 | tf_op jit(solution)/shard_map/ppermute | solution.py:637

commit v2 on v1

--- a/solution.py
+++ b/solution.py
@@ -619,9 +619,9 @@
     far_a = jnp.concatenate([pays[0], jnp.where(odd, corners[0], corners[1])])
     far_b = jnp.concatenate([pays[1], jnp.where(odd, corners[1], corners[0])])
     far_a = lax.ppermute(far_a, "ty", pairs(0))
+    hydro, pay = middle(False, weights, cond_params, raw, side)
+    hydro, far_b = lax.optimization_barrier((hydro, far_b))
     far_b = lax.ppermute(far_b, "ty", pairs(1))
-
-    hydro, pay = middle(False, weights, cond_params, raw, side)
     got = lax.ppermute(pay, "cond", swap)
     hydro, pay = middle(True, weights, cond_params, raw, side, hydro)
     part_m = pay + got
@@ -629,8 +629,8 @@
     hydro, pay = edge(False, weights, cond_params, raw, side, far_a, far_b, hydro)
     got = lax.ppermute(pay, "cond", swap)
     hydro, pay = edge(True, weights, cond_params, raw, side, far_a, far_b, hydro)
+    own_m, hydro = over_chips(part_m, hydro)
     part_e = pay + got
-    own_m, (hydro, _) = over_chips(part_m, (hydro, part_e))
     got_m = lax.ppermute(own_m, "cond", swap)
     bed_next, bed_change, hydro = bed_middle(bed, side, far_a, far_b, own_m, got_m, hydro)
     own_e, (bed_next, bed_change) = over_chips(part_e, (bed_next, bed_change))

time: 48.3 us -> 45.5 us (0.942)
  waiting for transfers between devices: 9.43 us -> 6.45 us
    ppermute x2, waiting for transfers between devices: 7.94 us -> 4.96 us  [over_chips(): got = lax.ppermute(part, 'cond', [(i, i ^ reach) for i in range(nc)])]
  transfers between devices with their start and end apart: 9 -> 9, of which waited for: 4 -> 4; matrix products, arithmetic and copies ran while one was open for 0% -> 0% of each run, Pallas kernels for 25% -> 34%
where the time goes in v2:
time: 45.5 us; the launch traced here: 45.1 us
  Pallas kernels  19 us (42%)
  starting transfers between devices  13.1 us (29%)
  waiting for transfers between devices  6.45 us (14%)
  local copies, waits for them, and re-layouts  5.32 us (12%)
  between operations  1.03 us (2%)
    pallas_call x2, Pallas kernels, edge(): pl.pallas_call(functools.partial(edge_kernel, own), name='edge_own' if ow...  6.25 us
    pallas_call x2, Pallas kernels, middle(): pl.pallas_call(functools.partial(middle_kernel, own), name='middle_own' i...  5.87 us
    unnamed x22, local copies, waits for them, and re-layouts  5.3 us
    ppermute x2, waiting for transfers between devices, over_chips(): got = lax.ppermute(part, 'cond', [(i, i ^ reach) for i in range(nc)])  4.96 us
    ppermute x1, starting transfers between devices, shards(): far_b = lax.ppermute(far_b, 'ty', pairs(1))  4.66 us
    ppermute x2, starting transfers between devices, shards(): got = lax.ppermute(pay, 'cond', swap)  2.82 us
    ppermute x2, starting transfers between devices, over_chips(): got = lax.ppermute(part, 'cond', [(i, i ^ reach) for i in range(nc)])  2.55 us
    pallas_call x1, Pallas kernels, bed_middle(): pl.pallas_call(bed_middle_kernel, name='bed_middle', out_shape=[pltpu.HBM...  2.03 us
  transfers between devices with their start and end apart: 9, of which 4 were waited for; matrix products, arithmetic and copies ran while one was open for 0% of the time, Pallas kernels for 34%

profile of v2, /device:TPU:9, one launch (start us, length us, event | category | flops | bytes accessed | tf_op | source)
XLA Modules:
  0.0 45.1 jit_solution(4683147664180435791)
XLA Ops:
  0.6 1.7 %pack_side.1 = f32[64,128]{1,0:T(8,128)S(1)} custom-call(f32[256,1024]{1,0:T(8,128)} %bed.15, s32[256,1024]{1,0:T(8,128)} %mask.11, s32[256,1024]{1,0:T(8,128)} %kind.11, f32[1,2,256,1024]{3,2,1,0:T(8,128)} %stress.11, f32[1,3,256,1024]{3,2,1,0:T(8,128)} %hydro.11), custom_call_target="tpu_custom_call" | custom-call | flops 2000000000 | tf_op jit(solution)/shard_map/pack_side/pallas_call | solution.py:97
  2.4 1.3 %collective-permute-start = (f32[64,128]{1,0:T(8,128)S(1)}, f32[64,128]{1,0:T(8,128)S(1)}, u32[]{:S(2)}, u32[]{:S(2)}) collective-permute-start(f32[64,128]{1,0:T(8,128)S(1)} %pack_side.1), channel_id=1, source_target_pairs={{0,1},{1,0},{2,3},{3,2},{4,5},{5,4},{6,7},{7,6},{8,9},{9,8},{10,11... | collective-permute-start | bytes 98312 | tf_op jit(solution)/shard_map/ppermute | solution.py:615
  3.7 1.2 %pack_rows.1 = f32[2,256,128]{2,1,0:T(8,128)S(1)} custom-call(f32[256,1024]{1,0:T(8,128)} %bed.15, s32[256,1024]{1,0:T(8,128)} %mask.11, s32[256,1024]{1,0:T(8,128)} %kind.11, f32[1,2,256,1024]{3,2,1,0:T(8,128)} %stress.11, f32[1,3,256,1024]{3,2,1,0:T(8,128)} %hydro.11), custom_call_target="tpu_custom_call" | custom-call | flops 2000000000 | tf_op jit(solution)/shard_map/pack_rows/pallas_call | solution.py:143
  4.9 0.3 collective-permute-done.side
  5.4 1.6 %copy-done.1 = f32[1,2,256,1024]{3,2,1,0:T(8,128)S(1)} copy-done((f32[1,2,256,1024]{3,2,1,0:T(8,128)S(1)}, f32[1,2,256,1024]{3,2,1,0:T(8,128)}, u32[]{:S(2)}) %copy-start.1) | copy-done | bytes 2097176
  7.0 1.2 %copy-done.3 = s32[256,1024]{1,0:T(8,128)S(1)} copy-done((s32[256,1024]{1,0:T(8,128)S(1)}, s32[256,1024]{1,0:T(8,128)}, u32[]{:S(2)}) %copy-start.3) | copy-done | bytes 1048600
  8.2 1.2 %copy-done.5 = s32[256,1024]{1,0:T(8,128)S(1)} copy-done((s32[256,1024]{1,0:T(8,128)S(1)}, s32[256,1024]{1,0:T(8,128)}, u32[]{:S(2)}) %copy-start.5) | copy-done | bytes 1048600
  9.4 1.2 %copy-done.7 = f32[256,1024]{1,0:T(8,128)S(1)} copy-done((f32[256,1024]{1,0:T(8,128)S(1)}, f32[256,1024]{1,0:T(8,128)}, u32[]{:S(2)}) %copy-start.7) | copy-done | bytes 1048600
  10.6 2.9 %middle_other.1 = (f32[1,3,256,1024]{3,2,1,0:T(8,128)S(1)}, f32[520,128]{1,0:T(8,128)S(1)}) custom-call(s32[4]{0:T(128)S(1)} %copy-done.9, f32[1,4]{1,0:T(1,128)S(1)} %copy-done.10, f32[256,1024]{1,0:T(8,128)S(1)} %copy-done.7, s32[256,1024]{1,0:T(8,128)S(1)} %copy-done.3, s32[256,1024]{1,0:T(8,128)S(1)} %copy-done.5, f32[1,2,256,1024]{3,2,1,0:T(8,128)S(1)} %copy-done.1, ...), custom_call_target="tpu_custom_call" | custom-call | flops 4000000000 | tf_op jit(solution)/shard_map/middle_other/pallas_call | solution.py:339
  13.6 4.7 %collective-permute-start.2 = (f32[264,128]{1,0:T(8,128)S(1)}, f32[264,128]{1,0:T(8,128)S(1)}, u32[]{:S(2)}, u32[]{:S(2)}) collective-permute-start(f32[264,128]{1,0:T(8,128)S(1)} %pad_maximum_fusion.1), channel_id=1, source_target_pairs={{2,4},{4,2},{3,5},{5,3},{10,12},{12,10},{11,13},{13,11},{18,20},{2... | collective-permute-start | bytes 405512 | tf_op jit(solution)/shard_map/ppermute | solution.py:624
  18.3 2.5 %collective-permute-start.3 = (f32[520,128]{1,0:T(8,128)S(1)}, f32[520,128]{1,0:T(8,128)S(1)}, u32[]{:S(2)}, u32[]{:S(2)}) collective-permute-start(f32[520,128]{1,0:T(8,128)S(1)} %get-tuple-element.30), channel_id=1, source_target_pairs={{0,8},{8,0},{16,24},{24,16},{1,9},{9,1},{17,25},{25,17},{2,10},{10... | collective-permute-start | bytes 798728 | tf_op jit(solution)/shard_map/ppermute | solution.py:625
  20.7 2.9 %middle_own.1 = (f32[1,3,256,1024]{3,2,1,0:T(8,128)S(1)}, f32[520,128]{1,0:T(8,128)S(1)}) custom-call(s32[4]{0:T(128)S(1)} %copy-done.9, f32[1,4]{1,0:T(1,128)S(1)} %copy-done.10, f32[256,1024]{1,0:T(8,128)S(1)} %copy-done.7, s32[256,1024]{1,0:T(8,128)S(1)} %copy-done.3, s32[256,1024]{1,0:T(8,128)S(1)} %copy-done.5, ...), custom_call_target="tpu_custom_call", output_to_operand_aliasing={{0}: (8, {})} | custom-call | flops 4000000000 | tf_op jit(solution)/shard_map/middle_own/pallas_call | solution.py:339
  23.7 1.3 %collective-permute-start.4 = (f32[520,128]{1,0:T(8,128)S(1)}, f32[520,128]{1,0:T(8,128)S(1)}, u32[]{:S(2)}, u32[]{:S(2)}) collective-permute-start(f32[520,128]{1,0:T(8,128)S(1)} %add.17), channel_id=1, source_target_pairs={{0,16},{8,24},{16,0},{24,8},{1,17},{9,25},{17,1},{25,9},{2,18},{10... | collective-permute-start | bytes 798728 | tf_op jit(solution)/shard_map/ppermute | solution.py:609
  25.1 3.1 %edge_other.1 = (f32[1,3,256,1024]{3,2,1,0:T(8,128)S(1)}, f32[528,128]{1,0:T(8,128)S(1)}) custom-call(s32[4]{0:T(128)S(1)} %copy-done.9, f32[1,4]{1,0:T(1,128)S(1)} %copy-done.10, f32[256,1024]{1,0:T(8,128)S(1)} %copy-done.8, s32[256,1024]{1,0:T(8,128)S(1)} %copy-done.4, s32[256,1024]{1,0:T(8,128)S(1)} %copy-done.6, ...), custom_call_target="tpu_custom_call", output_to_operand_aliasing={{0}: (10, {})} | custom-call | flops 4000000000 | tf_op jit(solution)/shard_map/edge_other/pallas_call | solution.py:419
  28.2 0.4 collective-permute-start.6
  28.6 3.1 %edge_own.1 = (f32[1,3,256,1024]{3,2,1,0:T(8,128)S(1)}, f32[528,128]{1,0:T(8,128)S(1)}) custom-call(s32[4]{0:T(128)S(1)} %copy-done.9, f32[1,4]{1,0:T(1,128)S(1)} %copy-done.10, f32[256,1024]{1,0:T(8,128)S(1)} %copy-done.8, s32[256,1024]{1,0:T(8,128)S(1)} %copy-done.4, s32[256,1024]{1,0:T(8,128)S(1)} %copy-done.6, ...), custom_call_target="tpu_custom_call", output_to_operand_aliasing={{0}: (10, {})} | custom-call | flops 4000000000 | tf_op jit(solution)/shard_map/edge_own/pallas_call | solution.py:419
  31.7 0.1 collective-permute-done.4
  31.9 0.9 %collective-permute-start.5 = (f32[520,128]{1,0:T(8,128)S(1)}, f32[520,128]{1,0:T(8,128)S(1)}, u32[]{:S(2)}, u32[]{:S(2)}) collective-permute-start(f32[520,128]{1,0:T(8,128)S(1)} %add.18.own_m), channel_id=1, source_target_pairs={{0,8},{8,0},{16,24},{24,16},{1,9},{9,1},{17,25},{25,17},{2,10},{10... | collective-permute-start | bytes 798728 | tf_op jit(solution)/shard_map/ppermute | solution.py:634
  32.8 1.3 %collective-permute-start.7 = (f32[528,128]{1,0:T(8,128)S(1)}, f32[528,128]{1,0:T(8,128)S(1)}, u32[]{:S(2)}, u32[]{:S(2)}) collective-permute-start(f32[528,128]{1,0:T(8,128)S(1)} %add.19), channel_id=1, source_target_pairs={{0,16},{8,24},{16,0},{24,8},{1,17},{9,25},{17,1},{25,9},{2,18},{10... | collective-permute-start | bytes 811016 | tf_op jit(solution)/shard_map/ppermute | solution.py:609
  34.0 2.0 %bed_middle.1 = (f32[256,1024]{1,0:T(8,128)}, f32[256,1024]{1,0:T(8,128)}, f32[1,3,256,1024]{3,2,1,0:T(8,128)}) custom-call(f32[256,1024]{1,0:T(8,128)S(1)} %copy-done.8, f32[64,128]{1,0:T(8,128)S(1)} %collective-permute-done.side, f32[264,128]{1,0:T(8,128)S(1)} %collective-permute-done.1.far_a, f32[264,128]{1,0:T(8,128)S(1)} %collective-permute-done.2.far_b, ...), custom_call_target="tpu_custom_call" | custom-call | flops 4000000000 | tf_op jit(solution)/shard_map/bed_middle/pallas_call | solution.py:568
  36.1 4.8 %collective-permute-done.7 = f32[528,128]{1,0:T(8,128)S(1)} collective-permute-done((f32[528,128]{1,0:T(8,128)S(1)}, f32[528,128]{1,0:T(8,128)S(1)}, u32[]{:S(2)}, u32[]{:S(2)}) %collective-permute-start.7) | collective-permute-done | bytes 270368 | tf_op jit(solution)/shard_map/ppermute | solution.py:609
  41.0 0.9 %collective-permute-start.8 = (f32[528,128]{1,0:T(8,128)S(1)}, f32[528,128]{1,0:T(8,128)S(1)}, u32[]{:S(2)}, u32[]{:S(2)}) collective-permute-start(f32[528,128]{1,0:T(8,128)S(1)} %add.20.own_e), channel_id=1, source_target_pairs={{0,8},{8,0},{16,24},{24,16},{1,9},{9,1},{17,25},{25,17},{2,10},{10... | collective-permute-start | bytes 811016 | tf_op jit(solution)/shard_map/ppermute | solution.py:637
  41.8 1.2 %collective-permute-done.8.got_e = f32[528,128]{1,0:T(8,128)S(1)} collective-permute-done((f32[528,128]{1,0:T(8,128)S(1)}, f32[528,128]{1,0:T(8,128)S(1)}, u32[]{:S(2)}, u32[]{:S(2)}) %collective-permute-start.8) | collective-permute-done | bytes 270368 | tf_op jit(solution)/shard_map/ppermute | solution.py:637
  43.0 2.0 %bed_edge.1 = (f32[256,1024]{1,0:T(8,128)}, f32[256,1024]{1,0:T(8,128)}) custom-call(f32[256,1024]{1,0:T(8,128)S(1)} %copy-done.8, f32[64,128]{1,0:T(8,128)S(1)} %collective-permute-done.side, f32[264,128]{1,0:T(8,128)S(1)} %collective-permute-done.1.far_a, ...), custom_call_target="tpu_custom_call", output_to_operand_aliasing={{0}: (8, {}), {1}: (9, {})} | custom-call | flops 2000000000 | tf_op jit(solution)/shard_map/bed_edge/pallas_call | solution.py:581
  (32 shorter events, 0.3 us)
Async XLA Ops:
  2.4 3.0 %copy-start = (f32[1,3,256,1024]{3,2,1,0:T(8,128)S(1)}, f32[1,3,256,1024]{3,2,1,0:T(8,128)}, u32[]{:S(2)}) copy-start(f32[1,3,256,1024]{3,2,1,0:T(8,128)} %hydro.11) | copy-start | bytes 9437188
  2.4 3.0 %copy-start.9 = (s32[4]{0:T(128)S(1)}, s32[4]{0:T(128)}, u32[]{:S(2)}) copy-start(s32[4]{0:T(128)} %weights.7) | copy-start | bytes 52
  2.4 3.0 %copy-start.10 = (f32[1,4]{1,0:T(1,128)S(1)}, f32[1,4]{1,0:T(1,128)}, u32[]{:S(2)}) copy-start(f32[1,4]{1,0:T(1,128)} %params.7) | copy-start | bytes 52
  2.4 2.8 %collective-permute-start = (f32[64,128]{1,0:T(8,128)S(1)}, f32[64,128]{1,0:T(8,128)S(1)}, u32[]{:S(2)}, u32[]{:S(2)}) collective-permute-start(f32[64,128]{1,0:T(8,128)S(1)} %pack_side.1), channel_id=1, source_target_pairs={{0,1},{1,0},{2,3},{3,2},{4,5},{5,4},{6,7},{7,6},{8,9},{9,8},{10,11... | collective-permute-start | bytes 98312 | tf_op jit(solution)/shard_map/ppermute | solution.py:615
  5.2 19.8 %collective-permute-start.1 = (f32[264,128]{1,0:T(8,128)S(1)}, f32[264,128]{1,0:T(8,128)S(1)}, u32[]{:S(2)}, u32[]{:S(2)}) collective-permute-start(f32[264,128]{1,0:T(8,128)S(1)} %pad_maximum_fusion), channel_id=1, source_target_pairs={{0,2},{2,0},{4,6},{6,4},{1,3},{3,1},{5,7},{7,5},{8,10},{10,8},{12,... | collective-permute-start | bytes 405512 | tf_op jit(solution)/shard_map/ppermute | solution.py:621
  5.4 1.6 %copy-start.1 = (f32[1,2,256,1024]{3,2,1,0:T(8,128)S(1)}, f32[1,2,256,1024]{3,2,1,0:T(8,128)}, u32[]{:S(2)}) copy-start(f32[1,2,256,1024]{3,2,1,0:T(8,128)} %stress.11) | copy-start | bytes 6291460
  7.0 1.2 %copy-start.3 = (s32[256,1024]{1,0:T(8,128)S(1)}, s32[256,1024]{1,0:T(8,128)}, u32[]{:S(2)}) copy-start(s32[256,1024]{1,0:T(8,128)} %mask.11) | copy-start | bytes 3145732
  8.2 1.2 %copy-start.5 = (s32[256,1024]{1,0:T(8,128)S(1)}, s32[256,1024]{1,0:T(8,128)}, u32[]{:S(2)}) copy-start(s32[256,1024]{1,0:T(8,128)} %kind.11) | copy-start | bytes 3145732
  9.4 1.2 %copy-start.7 = (f32[256,1024]{1,0:T(8,128)S(1)}, f32[256,1024]{1,0:T(8,128)}, u32[]{:S(2)}) copy-start(f32[256,1024]{1,0:T(8,128)} %bed.15) | copy-start | bytes 3145732
  13.6 11.4 %collective-permute-start.2 = (f32[264,128]{1,0:T(8,128)S(1)}, f32[264,128]{1,0:T(8,128)S(1)}, u32[]{:S(2)}, u32[]{:S(2)}) collective-permute-start(f32[264,128]{1,0:T(8,128)S(1)} %pad_maximum_fusion.1), channel_id=1, source_target_pairs={{2,4},{4,2},{3,5},{5,3},{10,12},{12,10},{11,13},{13,11},{18,20},{2... | collective-permute-start | bytes 405512 | tf_op jit(solution)/shard_map/ppermute | solution.py:624
  18.2 6.8 %copy-start.2 = (f32[1,2,256,1024]{3,2,1,0:T(8,128)S(1)}, f32[1,2,256,1024]{3,2,1,0:T(8,128)}, u32[]{:S(2)}) copy-start(f32[1,2,256,1024]{3,2,1,0:T(8,128)} %stress.11) | copy-start | bytes 6291460
  18.3 6.8 %copy-start.4 = (s32[256,1024]{1,0:T(8,128)S(1)}, s32[256,1024]{1,0:T(8,128)}, u32[]{:S(2)}) copy-start(s32[256,1024]{1,0:T(8,128)} %mask.11) | copy-start | bytes 3145732
  18.3 6.8 %copy-start.6 = (s32[256,1024]{1,0:T(8,128)S(1)}, s32[256,1024]{1,0:T(8,128)}, u32[]{:S(2)}) copy-start(s32[256,1024]{1,0:T(8,128)} %kind.11) | copy-start | bytes 3145732
  18.3 6.8 %copy-start.8 = (f32[256,1024]{1,0:T(8,128)S(1)}, f32[256,1024]{1,0:T(8,128)}, u32[]{:S(2)}) copy-start(f32[256,1024]{1,0:T(8,128)} %bed.15) | copy-start | bytes 3145732
  18.3 5.4 %collective-permute-start.3 = (f32[520,128]{1,0:T(8,128)S(1)}, f32[520,128]{1,0:T(8,128)S(1)}, u32[]{:S(2)}, u32[]{:S(2)}) collective-permute-start(f32[520,128]{1,0:T(8,128)S(1)} %get-tuple-element.30), channel_id=1, source_target_pairs={{0,8},{8,0},{16,24},{24,16},{1,9},{9,1},{17,25},{25,17},{2,10},{10... | collective-permute-start | bytes 798728 | tf_op jit(solution)/shard_map/ppermute | solution.py:625
  23.7 8.1 %collective-permute-start.4 = (f32[520,128]{1,0:T(8,128)S(1)}, f32[520,128]{1,0:T(8,128)S(1)}, u32[]{:S(2)}, u32[]{:S(2)}) collective-permute-start(f32[520,128]{1,0:T(8,128)S(1)} %add.17), channel_id=1, source_target_pairs={{0,16},{8,24},{16,0},{24,8},{1,17},{9,25},{17,1},{25,9},{2,18},{10... | collective-permute-start | bytes 798728 | tf_op jit(solution)/shard_map/ppermute | solution.py:609
  28.2 4.5 %collective-permute-start.6 = (f32[528,128]{1,0:T(8,128)S(1)}, f32[528,128]{1,0:T(8,128)S(1)}, u32[]{:S(2)}, u32[]{:S(2)}) collective-permute-start(f32[528,128]{1,0:T(8,128)S(1)} %get-tuple-element.37), channel_id=1, source_target_pairs={{0,8},{8,0},{16,24},{24,16},{1,9},{9,1},{17,25},{25,17},{2,10},{10... | collective-permute-start | bytes 811016 | tf_op jit(solution)/shard_map/ppermute | solution.py:630
  31.9 2.2 %collective-permute-start.5 = (f32[520,128]{1,0:T(8,128)S(1)}, f32[520,128]{1,0:T(8,128)S(1)}, u32[]{:S(2)}, u32[]{:S(2)}) collective-permute-start(f32[520,128]{1,0:T(8,128)S(1)} %add.18.own_m), channel_id=1, source_target_pairs={{0,8},{8,0},{16,24},{24,16},{1,9},{9,1},{17,25},{25,17},{2,10},{10... | collective-permute-start | bytes 798728 | tf_op jit(solution)/shard_map/ppermute | solution.py:634
  32.8 8.2 %collective-permute-start.7 = (f32[528,128]{1,0:T(8,128)S(1)}, f32[528,128]{1,0:T(8,128)S(1)}, u32[]{:S(2)}, u32[]{:S(2)}) collective-permute-start(f32[528,128]{1,0:T(8,128)S(1)} %add.19), channel_id=1, source_target_pairs={{0,16},{8,24},{16,0},{24,8},{1,17},{9,25},{17,1},{25,9},{2,18},{10... | collective-permute-start | bytes 811016 | tf_op jit(solution)/shard_map/ppermute | solution.py:609
  41.0 2.0 %collective-permute-start.8 = (f32[528,128]{1,0:T(8,128)S(1)}, f32[528,128]{1,0:T(8,128)S(1)}, u32[]{:S(2)}, u32[]{:S(2)}) collective-permute-start(f32[528,128]{1,0:T(8,128)S(1)} %add.20.own_e), channel_id=1, source_target_pairs={{0,8},{8,0},{16,24},{24,16},{1,9},{9,1},{17,25},{25,17},{2,10},{10... | collective-permute-start | bytes 811016 | tf_op jit(solution)/shard_map/ppermute | solution.py:637

commit v3 on v2

--- a/solution.py
+++ b/solution.py
@@ -110,18 +110,22 @@
     )(*held(*raw, space=pltpu.HBM))
 
 
-def pack_rows_kernel(bed, mask, kind, stress, hydro, pays, reals, ints, sems):
+def load_kernel(bed, mask, kind, stress, hydro, *refs):
+    raw, (pays, reals, ints, edge_sems, load_sems) = refs[:5], refs[5:]
     rows, cols = bed.shape
-    copies = []
-    for f, src in enumerate(raw_fields(bed, mask, kind, stress, hydro)):
+    sources = raw_fields(bed, mask, kind, stress, hydro)
+    edges, loads = [], []
+    for f, (src, dst) in enumerate(zip(sources, raw_fields(*raw))):
         which, k = SPOTS[f]
         for end, start in enumerate((0, rows - SUB)):
-            copies.append(
-                pltpu.make_async_copy(src.at[pl.ds(start, SUB)], (reals, ints)[which].at[end, k], sems.at[f, end])
+            edges.append(
+                pltpu.make_async_copy(src.at[pl.ds(start, SUB)], (reals, ints)[which].at[end, k], edge_sems.at[f, end])
             )
-    for copy in copies:
+            at = pl.ds(end * (rows // 2), rows // 2)
+            loads.append(pltpu.make_async_copy(src.at[at], dst.at[at], load_sems.at[f, end]))
+    for copy in edges + loads:
         copy.start()
-    for copy in copies:
+    for copy in edges:
         copy.wait()
     low = rows_of((SUB, cols)) < HALO
     odd = lax.axis_index("ty") % 2
@@ -136,24 +140,29 @@
             pair = jnp.where(low, *both)
             for k in range(cols // LANE):
                 pays[slot, pl.ds(k * GROUP + p * SUB, SUB), :] = pair[:, k * LANE : (k + 1) * LANE]
-
-
-def pack_rows(*raw):
+    for copy in loads:
+        copy.wait()
+
+
+def load(*raw):
     rows, cols = raw[0].shape
-    return pl.pallas_call(
-        pack_rows_kernel,
-        name="pack_rows",
-        out_shape=pltpu.VMEM((2, cols // LANE * GROUP, LANE), jnp.float32),
+    *held_raw, pays = pl.pallas_call(
+        load_kernel,
+        name="load",
+        out_shape=[pltpu.VMEM(x.shape, x.dtype) for x in raw]
+        + [pltpu.VMEM((2, cols // LANE * GROUP, LANE), jnp.float32)],
         in_specs=[ANY] * 5,
-        out_specs=VMEM,
+        out_specs=[VMEM] * 6,
         scratch_shapes=[
             pltpu.VMEM((2, 6, SUB, cols), jnp.float32),
             pltpu.VMEM((2, 2, SUB, cols), jnp.int32),
             pltpu.SemaphoreType.DMA((FIELDS, 2)),
+            pltpu.SemaphoreType.DMA((FIELDS, 2)),
         ],
         compiler_params=pltpu.CompilerParams(vmem_limit_bytes=4 * MIB),
-        cost_estimate=cost(2),
+        cost_estimate=cost(4),
     )(*held(*raw, space=pltpu.HBM))
+    return held_raw, pays
 
 
 def side_lanes(at_left):
@@ -214,7 +223,7 @@
             flux_c - west(flux_c) + flux_r - north(flux_r, self.fr_last[n])
         )
         self.fr_last[n] = flux_r
-        return out, u, v, wc * (u * jnp.abs(u)), wr * (v * jnp.abs(v))
+        return out, u, v, u * jnp.abs(u), v * jnp.abs(v)
 
     def step_one(self, i):
         at, after = tile_at(i), tile_at(i + 1)
@@ -261,8 +270,8 @@
     def step_three(self, i):
         at = tile_at(i)
         e, u, v, qc, qr = self.later(2, i, self.e2, self.u2, self.v2)
-        qc = self.qc2[at, :] + qc
-        qr = self.qr2[at, :] + qr
+        qc = self.wc[at, :] * (self.qc2[at, :] + qc)
+        qr = self.wr[at, :] * (self.qr2[at, :] + qr)
         change = (qc - west(qc) + qr - north(qr, self.qr_last[...])) * self.scale
         self.qr_last[...] = qr
         self.emit(i, e * (1.0 / 0.3), u, v, change)
@@ -429,7 +438,7 @@
         + Sweep.scratch(rows // SUB // 4 + 2, wide),
         input_output_aliases={10: 0},
         compiler_params=pltpu.CompilerParams(vmem_limit_bytes=12 * MIB),
-        cost_estimate=cost(4),
+        cost_estimate=cost(3),
     )(weights, params, *held(*raw, side, far_a, far_b, hydro))
 
 
@@ -613,7 +622,8 @@
         return part, beside
 
     side = lax.ppermute(pack_side(*raw), "tx", [(0, 1), (1, 0)])
-    pays = pack_rows(*raw)
+    raw, pays = load(*raw)
+    bed = raw[0]
     odd = lax.axis_index("ty") % 2 == 1
     corners = [side[:SUB], side[-SUB:]]
     far_a = jnp.concatenate([pays[0], jnp.where(odd, corners[0], corners[1])])
@@ -631,6 +641,7 @@
     hydro, pay = edge(True, weights, cond_params, raw, side, far_a, far_b, hydro)
     own_m, hydro = over_chips(part_m, hydro)
     part_e = pay + got
+    own_m, _ = lax.optimization_barrier((own_m, part_e))
     got_m = lax.ppermute(own_m, "cond", swap)
     bed_next, bed_change, hydro = bed_middle(bed, side, far_a, far_b, own_m, got_m, hydro)
     own_e, (bed_next, bed_change) = over_chips(part_e, (bed_next, bed_change))

time: 45.5 us -> 51.2 us (1.13)
  local copies, waits for them, and re-layouts: 5.32 us -> 9.55 us
  Pallas kernels: 19 us -> 21.8 us
  starting transfers between devices: 13.1 us -> 12.3 us
    unnamed x22 -> x28, local copies, waits for them, and re-layouts: 5.3 us -> 9.53 us
    pallas_call x1, Pallas kernels: 1.17 us -> 3.82 us  [load(): pl.pallas_call(load_kernel, name='load', out_shape=[pltpu.VMEM(x.shape, x...]
    ppermute x2, starting transfers between devices: 2.82 us -> 1.95 us  [shards(): got = lax.ppermute(pay, 'cond', swap)]
  transfers between devices with their start and end apart: 9 -> 9, of which waited for: 4 -> 3; matrix products, arithmetic and copies ran while one was open for 0% -> 0% of each run, Pallas kernels for 34% -> 36%
where the time goes in v3:
time: 51.2 us; the launch traced here: 50.9 us
  Pallas kernels  21.8 us (43%)
  starting transfers between devices  12.3 us (24%)
  local copies, waits for them, and re-layouts  9.55 us (19%)
  waiting for transfers between devices  6.05 us (12%)
  between operations  1.02 us (2%)
    unnamed x28, local copies, waits for them, and re-layouts  9.53 us
    pallas_call x2, Pallas kernels, edge(): pl.pallas_call(functools.partial(edge_kernel, own), name='edge_own' if ow...  6.31 us
    pallas_call x2, Pallas kernels, middle(): pl.pallas_call(functools.partial(middle_kernel, own), name='middle_own' i...  6 us
    ppermute x2, waiting for transfers between devices, over_chips(): got = lax.ppermute(part, 'cond', [(i, i ^ reach) for i in range(nc)])  4.86 us
    ppermute x1, starting transfers between devices, shards(): far_b = lax.ppermute(far_b, 'ty', pairs(1))  4.51 us
    pallas_call x1, Pallas kernels, load(): pl.pallas_call(load_kernel, name='load', out_shape=[pltpu.VMEM(x.shape, x...  3.82 us
    ppermute x2, starting transfers between devices, over_chips(): got = lax.ppermute(part, 'cond', [(i, i ^ reach) for i in range(nc)])  2.5 us
    pallas_call x1, Pallas kernels, bed_middle(): pl.pallas_call(bed_middle_kernel, name='bed_middle', out_shape=[pltpu.HBM...  2.02 us
  transfers between devices with their start and end apart: 9, of which 3 were waited for; matrix products, arithmetic and copies ran while one was open for 0% of the time, Pallas kernels for 36%

profile of v3, /device:TPU:9, one launch (start us, length us, event | category | flops | bytes accessed | tf_op | source)
XLA Modules:
  0.0 50.9 jit_solution(8028564041995904835)
XLA Ops:
  0.6 1.7 %pack_side.1 = f32[64,128]{1,0:T(8,128)S(1)} custom-call(f32[256,1024]{1,0:T(8,128)} %bed.3, s32[256,1024]{1,0:T(8,128)} %mask.3, s32[256,1024]{1,0:T(8,128)} %kind.3, f32[1,2,256,1024]{3,2,1,0:T(8,128)} %stress.3, f32[1,3,256,1024]{3,2,1,0:T(8,128)} %hydro.3), custom_call_target="tpu_custom_call" | custom-call | flops 2000000000 | tf_op jit(solution)/shard_map/pack_side/pallas_call | solution.py:97
  2.4 1.3 %collective-permute-start = (f32[64,128]{1,0:T(8,128)S(1)}, f32[64,128]{1,0:T(8,128)S(1)}, u32[]{:S(2)}, u32[]{:S(2)}) collective-permute-start(f32[64,128]{1,0:T(8,128)S(1)} %pack_side.1), channel_id=1, source_target_pairs={{0,1},{1,0},{2,3},{3,2},{4,5},{5,4},{6,7},{7,6},{8,9},{9,8},{10,11... | collective-permute-start | bytes 98312 | tf_op jit(solution)/shard_map/ppermute | solution.py:624
  3.7 3.8 %load.1 = (f32[256,1024]{1,0:T(8,128)S(1)}, s32[256,1024]{1,0:T(8,128)S(1)}, s32[256,1024]{1,0:T(8,128)S(1)}, f32[1,2,256,1024]{3,2,1,0:T(8,128)S(1)}, f32[1,3,2...) custom-call(f32[256,1024]{1,0:T(8,128)} %bed.3, s32[256,1024]{1,0:T(8,128)} %mask.3, s32[256,1024]{1,0:T(8,128)} %kind.3, ...), custom_call_target="tpu_custom_call" | custom-call | flops 4000000000 | tf_op jit(solution)/shard_map/load/pallas_call | solution.py:149
  7.5 1.3 %copy-done = f32[1,2,256,1024]{3,2,1,0:T(8,128)} copy-done((f32[1,2,256,1024]{3,2,1,0:T(8,128)}, f32[1,2,256,1024]{3,2,1,0:T(8,128)S(1)}, u32[]{:S(2)}) %copy-start) | copy-done | bytes 2097176
  8.8 1.0 %copy-done.3 = f32[256,1024]{1,0:T(8,128)} copy-done((f32[256,1024]{1,0:T(8,128)}, f32[256,1024]{1,0:T(8,128)S(1)}, u32[]{:S(2)}) %copy-start.3) | copy-done | bytes 1048600
  9.8 1.0 %copy-done.6 = s32[256,1024]{1,0:T(8,128)} copy-done((s32[256,1024]{1,0:T(8,128)}, s32[256,1024]{1,0:T(8,128)S(1)}, u32[]{:S(2)}) %copy-start.6) | copy-done | bytes 1048600
  10.8 1.0 %copy-done.9 = s32[256,1024]{1,0:T(8,128)} copy-done((s32[256,1024]{1,0:T(8,128)}, s32[256,1024]{1,0:T(8,128)S(1)}, u32[]{:S(2)}) %copy-start.9) | copy-done | bytes 1048600
  12.1 1.6 %copy-done.1 = f32[1,2,256,1024]{3,2,1,0:T(8,128)S(1)} copy-done((f32[1,2,256,1024]{3,2,1,0:T(8,128)S(1)}, f32[1,2,256,1024]{3,2,1,0:T(8,128)}, u32[]{:S(2)}) %copy-start.1) | copy-done | bytes 2097176
  13.7 1.2 %copy-done.4 = f32[256,1024]{1,0:T(8,128)S(1)} copy-done((f32[256,1024]{1,0:T(8,128)S(1)}, f32[256,1024]{1,0:T(8,128)}, u32[]{:S(2)}) %copy-start.4) | copy-done | bytes 1048600
  14.9 1.2 %copy-done.7 = s32[256,1024]{1,0:T(8,128)S(1)} copy-done((s32[256,1024]{1,0:T(8,128)S(1)}, s32[256,1024]{1,0:T(8,128)}, u32[]{:S(2)}) %copy-start.7) | copy-done | bytes 1048600
  16.1 1.2 %copy-done.10 = s32[256,1024]{1,0:T(8,128)S(1)} copy-done((s32[256,1024]{1,0:T(8,128)S(1)}, s32[256,1024]{1,0:T(8,128)}, u32[]{:S(2)}) %copy-start.10) | copy-done | bytes 1048600
  17.4 3.0 %middle_other.1 = (f32[1,3,256,1024]{3,2,1,0:T(8,128)S(1)}, f32[520,128]{1,0:T(8,128)S(1)}) custom-call(s32[4]{0:T(128)S(1)} %copy-done.12, f32[1,4]{1,0:T(1,128)S(1)} %copy-done.13, f32[256,1024]{1,0:T(8,128)S(1)} %copy-done.4, s32[256,1024]{1,0:T(8,128)S(1)} %copy-done.7, s32[256,1024]{1,0:T(8,128)S(1)} %copy-done.10, f32[1,2,256,1024]{3,2,1,0:T(8,128)S(1)} %copy-done.1, ...), custom_call_target="tpu_custom_call" | custom-call | flops 4000000000 | tf_op jit(solution)/shard_map/middle_other/pallas_call | solution.py:348
  20.4 4.5 %collective-permute-start.2 = (f32[264,128]{1,0:T(8,128)S(1)}, f32[264,128]{1,0:T(8,128)S(1)}, u32[]{:S(2)}, u32[]{:S(2)}) collective-permute-start(f32[264,128]{1,0:T(8,128)S(1)} %pad_maximum_fusion.1), channel_id=1, source_target_pairs={{2,4},{4,2},{3,5},{5,3},{10,12},{12,10},{11,13},{13,11},{18,20},{2... | collective-permute-start | bytes 405512 | tf_op jit(solution)/shard_map/ppermute | solution.py:634
  24.9 1.6 %collective-permute-start.3 = (f32[520,128]{1,0:T(8,128)S(1)}, f32[520,128]{1,0:T(8,128)S(1)}, u32[]{:S(2)}, u32[]{:S(2)}) collective-permute-start(f32[520,128]{1,0:T(8,128)S(1)} %get-tuple-element.43), channel_id=1, source_target_pairs={{0,8},{8,0},{16,24},{24,16},{1,9},{9,1},{17,25},{25,17},{2,10},{10... | collective-permute-start | bytes 798728 | tf_op jit(solution)/shard_map/ppermute | solution.py:635
  26.5 3.0 %middle_own.1 = (f32[1,3,256,1024]{3,2,1,0:T(8,128)S(1)}, f32[520,128]{1,0:T(8,128)S(1)}) custom-call(s32[4]{0:T(128)S(1)} %copy-done.12, f32[1,4]{1,0:T(1,128)S(1)} %copy-done.13, f32[256,1024]{1,0:T(8,128)S(1)} %copy-done.4, s32[256,1024]{1,0:T(8,128)S(1)} %copy-done.7, s32[256,1024]{1,0:T(8,128)S(1)} %copy-done.11, ...), custom_call_target="tpu_custom_call", output_to_operand_aliasing={{0}: (8, {})} | custom-call | flops 4000000000 | tf_op jit(solution)/shard_map/middle_own/pallas_call | solution.py:348
  29.6 1.3 %collective-permute-start.4 = (f32[520,128]{1,0:T(8,128)S(1)}, f32[520,128]{1,0:T(8,128)S(1)}, u32[]{:S(2)}, u32[]{:S(2)}) collective-permute-start(f32[520,128]{1,0:T(8,128)S(1)} %add.17), channel_id=1, source_target_pairs={{0,16},{8,24},{16,0},{24,8},{1,17},{9,25},{17,1},{25,9},{2,18},{10... | collective-permute-start | bytes 798728 | tf_op jit(solution)/shard_map/ppermute | solution.py:618
  30.9 3.2 %edge_other.1 = (f32[1,3,256,1024]{3,2,1,0:T(8,128)S(1)}, f32[528,128]{1,0:T(8,128)S(1)}) custom-call(s32[4]{0:T(128)S(1)} %copy-done.12, f32[1,4]{1,0:T(1,128)S(1)} %copy-done.13, f32[256,1024]{1,0:T(8,128)S(1)} %copy-done.5, s32[256,1024]{1,0:T(8,128)S(1)} %copy-done.8, s32[256,1024]{1,0:T(8,128)S(1)} %copy-done.11, ...), custom_call_target="tpu_custom_call", output_to_operand_aliasing={{0}: (10, {})} | custom-call | flops 3000000000 | tf_op jit(solution)/shard_map/edge_other/pallas_call | solution.py:428
  34.4 3.2 %edge_own.1 = (f32[1,3,256,1024]{3,2,1,0:T(8,128)S(1)}, f32[528,128]{1,0:T(8,128)S(1)}) custom-call(s32[4]{0:T(128)S(1)} %copy-done.12, f32[1,4]{1,0:T(1,128)S(1)} %copy-done.13, f32[256,1024]{1,0:T(8,128)S(1)} %copy-done.5, s32[256,1024]{1,0:T(8,128)S(1)} %copy-done.8, s32[256,1024]{1,0:T(8,128)S(1)} %copy-done.11, ...), custom_call_target="tpu_custom_call", output_to_operand_aliasing={{0}: (10, {})} | custom-call | flops 3000000000 | tf_op jit(solution)/shard_map/edge_own/pallas_call | solution.py:428
  38.6 1.2 %collective-permute-start.7 = (f32[528,128]{1,0:T(8,128)S(1)}, f32[528,128]{1,0:T(8,128)S(1)}, u32[]{:S(2)}, u32[]{:S(2)}) collective-permute-start(f32[528,128]{1,0:T(8,128)S(1)} %add.19), channel_id=1, source_target_pairs={{0,16},{8,24},{16,0},{24,8},{1,17},{9,25},{17,1},{25,9},{2,18},{10... | collective-permute-start | bytes 811016 | tf_op jit(solution)/shard_map/ppermute | solution.py:618
  39.8 2.0 %bed_middle.1 = (f32[256,1024]{1,0:T(8,128)}, f32[256,1024]{1,0:T(8,128)}, f32[1,3,256,1024]{3,2,1,0:T(8,128)}) custom-call(f32[256,1024]{1,0:T(8,128)S(1)} %copy-done.5, f32[64,128]{1,0:T(8,128)S(1)} %collective-permute-done.side, f32[264,128]{1,0:T(8,128)S(1)} %collective-permute-done.1.far_a, f32[264,128]{1,0:T(8,128)S(1)} %collective-permute-done.2.far_b, ...), custom_call_target="tpu_custom_call" | custom-call | flops 4000000000 | tf_op jit(solution)/shard_map/bed_middle/pallas_call | solution.py:577
  41.9 4.8 %collective-permute-done.7 = f32[528,128]{1,0:T(8,128)S(1)} collective-permute-done((f32[528,128]{1,0:T(8,128)S(1)}, f32[528,128]{1,0:T(8,128)S(1)}, u32[]{:S(2)}, u32[]{:S(2)}) %collective-permute-start.7) | collective-permute-done | bytes 270368 | tf_op jit(solution)/shard_map/ppermute | solution.py:618
  46.7 0.9 %collective-permute-start.8 = (f32[528,128]{1,0:T(8,128)S(1)}, f32[528,128]{1,0:T(8,128)S(1)}, u32[]{:S(2)}, u32[]{:S(2)}) collective-permute-start(f32[528,128]{1,0:T(8,128)S(1)} %add.20.own_e), channel_id=1, source_target_pairs={{0,8},{8,0},{16,24},{24,16},{1,9},{9,1},{17,25},{25,17},{2,10},{10... | collective-permute-start | bytes 811016 | tf_op jit(solution)/shard_map/ppermute | solution.py:648
  47.6 1.2 %collective-permute-done.8.got_e = f32[528,128]{1,0:T(8,128)S(1)} collective-permute-done((f32[528,128]{1,0:T(8,128)S(1)}, f32[528,128]{1,0:T(8,128)S(1)}, u32[]{:S(2)}, u32[]{:S(2)}) %collective-permute-start.8) | collective-permute-done | bytes 270368 | tf_op jit(solution)/shard_map/ppermute | solution.py:648
  48.8 2.0 %bed_edge.1 = (f32[256,1024]{1,0:T(8,128)}, f32[256,1024]{1,0:T(8,128)}) custom-call(f32[256,1024]{1,0:T(8,128)S(1)} %copy-done.5, f32[64,128]{1,0:T(8,128)S(1)} %collective-permute-done.side, f32[264,128]{1,0:T(8,128)S(1)} %collective-permute-done.1.far_a, ...), custom_call_target="tpu_custom_call", output_to_operand_aliasing={{0}: (8, {}), {1}: (9, {})} | custom-call | flops 2000000000 | tf_op jit(solution)/shard_map/bed_edge/pallas_call | solution.py:590
  (38 shorter events, 1.8 us)
Async XLA Ops:
  2.4 9.7 %copy-start.12 = (s32[4]{0:T(128)S(1)}, s32[4]{0:T(128)}, u32[]{:S(2)}) copy-start(s32[4]{0:T(128)} %weights.7) | copy-start | bytes 52
  2.4 9.7 %copy-start.13 = (f32[1,4]{1,0:T(1,128)S(1)}, f32[1,4]{1,0:T(1,128)}, u32[]{:S(2)}) copy-start(f32[1,4]{1,0:T(1,128)} %params.7) | copy-start | bytes 52
  2.4 9.4 %collective-permute-start = (f32[64,128]{1,0:T(8,128)S(1)}, f32[64,128]{1,0:T(8,128)S(1)}, u32[]{:S(2)}, u32[]{:S(2)}) collective-permute-start(f32[64,128]{1,0:T(8,128)S(1)} %pack_side.1), channel_id=1, source_target_pairs={{0,1},{1,0},{2,3},{3,2},{4,5},{5,4},{6,7},{7,6},{8,9},{9,8},{10,11... | collective-permute-start | bytes 98312 | tf_op jit(solution)/shard_map/ppermute | solution.py:624
  7.5 1.3 %copy-start = (f32[1,2,256,1024]{3,2,1,0:T(8,128)}, f32[1,2,256,1024]{3,2,1,0:T(8,128)S(1)}, u32[]{:S(2)}) copy-start(f32[1,2,256,1024]{3,2,1,0:T(8,128)S(1)} %get-tuple-element.36.stress) | copy-start | bytes 6291460
  8.8 1.0 %copy-start.3 = (f32[256,1024]{1,0:T(8,128)}, f32[256,1024]{1,0:T(8,128)S(1)}, u32[]{:S(2)}) copy-start(f32[256,1024]{1,0:T(8,128)S(1)} %get-tuple-element.32.bed) | copy-start | bytes 3145732
  9.8 1.0 %copy-start.6 = (s32[256,1024]{1,0:T(8,128)}, s32[256,1024]{1,0:T(8,128)S(1)}, u32[]{:S(2)}) copy-start(s32[256,1024]{1,0:T(8,128)S(1)} %get-tuple-element.34.mask) | copy-start | bytes 3145732
  10.8 1.0 %copy-start.9 = (s32[256,1024]{1,0:T(8,128)}, s32[256,1024]{1,0:T(8,128)S(1)}, u32[]{:S(2)}) copy-start(s32[256,1024]{1,0:T(8,128)S(1)} %get-tuple-element.35.kind) | copy-start | bytes 3145732
  11.8 19.0 %collective-permute-start.1 = (f32[264,128]{1,0:T(8,128)S(1)}, f32[264,128]{1,0:T(8,128)S(1)}, u32[]{:S(2)}, u32[]{:S(2)}) collective-permute-start(f32[264,128]{1,0:T(8,128)S(1)} %pad_maximum_fusion), channel_id=1, source_target_pairs={{0,2},{2,0},{4,6},{6,4},{1,3},{3,1},{5,7},{7,5},{8,10},{10,8},{12,... | collective-permute-start | bytes 405512 | tf_op jit(solution)/shard_map/ppermute | solution.py:631
  12.1 1.6 %copy-start.1 = (f32[1,2,256,1024]{3,2,1,0:T(8,128)S(1)}, f32[1,2,256,1024]{3,2,1,0:T(8,128)}, u32[]{:S(2)}) copy-start(f32[1,2,256,1024]{3,2,1,0:T(8,128)} %copy-done) | copy-start | bytes 6291460
  13.7 1.2 %copy-start.4 = (f32[256,1024]{1,0:T(8,128)S(1)}, f32[256,1024]{1,0:T(8,128)}, u32[]{:S(2)}) copy-start(f32[256,1024]{1,0:T(8,128)} %copy-done.3) | copy-start | bytes 3145732
  14.9 1.2 %copy-start.7 = (s32[256,1024]{1,0:T(8,128)S(1)}, s32[256,1024]{1,0:T(8,128)}, u32[]{:S(2)}) copy-start(s32[256,1024]{1,0:T(8,128)} %copy-done.6) | copy-start | bytes 3145732
  16.1 1.2 %copy-start.10 = (s32[256,1024]{1,0:T(8,128)S(1)}, s32[256,1024]{1,0:T(8,128)}, u32[]{:S(2)}) copy-start(s32[256,1024]{1,0:T(8,128)} %copy-done.9) | copy-start | bytes 3145732
  17.4 9.1 %copy-start.11 = (s32[256,1024]{1,0:T(8,128)S(1)}, s32[256,1024]{1,0:T(8,128)}, u32[]{:S(2)}) copy-start(s32[256,1024]{1,0:T(8,128)} %copy-done.9) | copy-start | bytes 3145732
  20.4 10.5 %collective-permute-start.2 = (f32[264,128]{1,0:T(8,128)S(1)}, f32[264,128]{1,0:T(8,128)S(1)}, u32[]{:S(2)}, u32[]{:S(2)}) collective-permute-start(f32[264,128]{1,0:T(8,128)S(1)} %pad_maximum_fusion.1), channel_id=1, source_target_pairs={{2,4},{4,2},{3,5},{5,3},{10,12},{12,10},{11,13},{13,11},{18,20},{2... | collective-permute-start | bytes 405512 | tf_op jit(solution)/shard_map/ppermute | solution.py:634
  24.9 6.0 %copy-start.2 = (f32[1,2,256,1024]{3,2,1,0:T(8,128)S(1)}, f32[1,2,256,1024]{3,2,1,0:T(8,128)}, u32[]{:S(2)}) copy-start(f32[1,2,256,1024]{3,2,1,0:T(8,128)} %copy-done) | copy-start | bytes 6291460
  24.9 6.0 %copy-start.5 = (f32[256,1024]{1,0:T(8,128)S(1)}, f32[256,1024]{1,0:T(8,128)}, u32[]{:S(2)}) copy-start(f32[256,1024]{1,0:T(8,128)} %copy-done.3) | copy-start | bytes 3145732
  24.9 6.0 %copy-start.8 = (s32[256,1024]{1,0:T(8,128)S(1)}, s32[256,1024]{1,0:T(8,128)}, u32[]{:S(2)}) copy-start(s32[256,1024]{1,0:T(8,128)} %copy-done.6) | copy-start | bytes 3145732
  24.9 4.6 %collective-permute-start.3 = (f32[520,128]{1,0:T(8,128)S(1)}, f32[520,128]{1,0:T(8,128)S(1)}, u32[]{:S(2)}, u32[]{:S(2)}) collective-permute-start(f32[520,128]{1,0:T(8,128)S(1)} %get-tuple-element.43), channel_id=1, source_target_pairs={{0,8},{8,0},{16,24},{24,16},{1,9},{9,1},{17,25},{25,17},{2,10},{10... | collective-permute-start | bytes 798728 | tf_op jit(solution)/shard_map/ppermute | solution.py:635
  29.6 8.1 %collective-permute-start.4 = (f32[520,128]{1,0:T(8,128)S(1)}, f32[520,128]{1,0:T(8,128)S(1)}, u32[]{:S(2)}, u32[]{:S(2)}) collective-permute-start(f32[520,128]{1,0:T(8,128)S(1)} %add.17), channel_id=1, source_target_pairs={{0,16},{8,24},{16,0},{24,8},{1,17},{9,25},{17,1},{25,9},{2,18},{10... | collective-permute-start | bytes 798728 | tf_op jit(solution)/shard_map/ppermute | solution.py:618
  34.1 3.6 %collective-permute-start.5 = (f32[528,128]{1,0:T(8,128)S(1)}, f32[528,128]{1,0:T(8,128)S(1)}, u32[]{:S(2)}, u32[]{:S(2)}) collective-permute-start(f32[528,128]{1,0:T(8,128)S(1)} %get-tuple-element.50), channel_id=1, source_target_pairs={{0,8},{8,0},{16,24},{24,16},{1,9},{9,1},{17,25},{25,17},{2,10},{10... | collective-permute-start | bytes 811016 | tf_op jit(solution)/shard_map/ppermute | solution.py:640
  37.7 2.1 %collective-permute-start.6 = (f32[520,128]{1,0:T(8,128)S(1)}, f32[520,128]{1,0:T(8,128)S(1)}, u32[]{:S(2)}, u32[]{:S(2)}) collective-permute-start(f32[520,128]{1,0:T(8,128)S(1)} %add.18.own_m), channel_id=1, source_target_pairs={{0,8},{8,0},{16,24},{24,16},{1,9},{9,1},{17,25},{25,17},{2,10},{10... | collective-permute-start | bytes 798728 | tf_op jit(solution)/shard_map/ppermute | solution.py:645
  38.6 8.1 %collective-permute-start.7 = (f32[528,128]{1,0:T(8,128)S(1)}, f32[528,128]{1,0:T(8,128)S(1)}, u32[]{:S(2)}, u32[]{:S(2)}) collective-permute-start(f32[528,128]{1,0:T(8,128)S(1)} %add.19), channel_id=1, source_target_pairs={{0,16},{8,24},{16,0},{24,8},{1,17},{9,25},{17,1},{25,9},{2,18},{10... | collective-permute-start | bytes 811016 | tf_op jit(solution)/shard_map/ppermute | solution.py:618
  46.7 2.1 %collective-permute-start.8 = (f32[528,128]{1,0:T(8,128)S(1)}, f32[528,128]{1,0:T(8,128)S(1)}, u32[]{:S(2)}, u32[]{:S(2)}) collective-permute-start(f32[528,128]{1,0:T(8,128)S(1)} %add.20.own_e), channel_id=1, source_target_pairs={{0,8},{8,0},{16,24},{24,16},{1,9},{9,1},{17,25},{25,17},{2,10},{10... | collective-permute-start | bytes 811016 | tf_op jit(solution)/shard_map/ppermute | solution.py:648

commit v4 on v2

--- a/solution.py
+++ b/solution.py
@@ -110,7 +110,7 @@
     )(*held(*raw, space=pltpu.HBM))
 
 
-def pack_rows_kernel(bed, mask, kind, stress, hydro, pays, reals, ints, sems):
+def pack_rows_kernel(bed, mask, kind, stress, hydro, pay_a, pay_b, reals, ints, sems):
     rows, cols = bed.shape
     copies = []
     for f, src in enumerate(raw_fields(bed, mask, kind, stress, hydro)):
@@ -124,18 +124,21 @@
     for copy in copies:
         copy.wait()
     low = rows_of((SUB, cols)) < HALO
-    odd = lax.axis_index("ty") % 2
-    for end in range(2):
-        slot = (1 - end + odd) % 2
-        for p in range(FIELDS // 2):
+    odd = lax.axis_index("ty") % 2 == 1
+    for p in range(FIELDS // 2):
+        pairs = []
+        for end in range(2):
             both = []
             for f in (2 * p, 2 * p + 1):
                 which, k = SPOTS[f]
                 both.append((reals, ints)[which][end, k].astype(jnp.float32))
             both[1 - end] = pltpu.roll(both[1 - end], HALO, 0)
-            pair = jnp.where(low, *both)
-            for k in range(cols // LANE):
-                pays[slot, pl.ds(k * GROUP + p * SUB, SUB), :] = pair[:, k * LANE : (k + 1) * LANE]
+            pairs.append(jnp.where(low, *both))
+        for k in range(cols // LANE):
+            at, lanes = pl.ds(k * GROUP + p * SUB, SUB), slice(k * LANE, (k + 1) * LANE)
+            top, bottom = pairs[0][:, lanes], pairs[1][:, lanes]
+            pay_a[at, :] = jnp.where(odd, top, bottom)
+            pay_b[at, :] = jnp.where(odd, bottom, top)
 
 
 def pack_rows(*raw):
@@ -143,9 +146,9 @@
     return pl.pallas_call(
         pack_rows_kernel,
         name="pack_rows",
-        out_shape=pltpu.VMEM((2, cols // LANE * GROUP, LANE), jnp.float32),
+        out_shape=[pltpu.VMEM((cols // LANE * GROUP + SUB, LANE), jnp.float32)] * 2,
         in_specs=[ANY] * 5,
-        out_specs=VMEM,
+        out_specs=[VMEM] * 2,
         scratch_shapes=[
             pltpu.VMEM((2, 6, SUB, cols), jnp.float32),
             pltpu.VMEM((2, 2, SUB, cols), jnp.int32),
@@ -154,6 +157,28 @@
         compiler_params=pltpu.CompilerParams(vmem_limit_bytes=4 * MIB),
         cost_estimate=cost(2),
     )(*held(*raw, space=pltpu.HBM))
+
+
+def corner_kernel(side, in_a, in_b, pay_a, pay_b):
+    tall = pay_a.shape[0]
+    odd = lax.axis_index("ty") % 2 == 1
+    top = side[pl.ds(0, SUB), :]
+    bottom = side[pl.ds(side.shape[0] - SUB, SUB), :]
+    pay_a[pl.ds(tall - SUB, SUB), :] = jnp.where(odd, top, bottom)
+    pay_b[pl.ds(tall - SUB, SUB), :] = jnp.where(odd, bottom, top)
+
+
+def add_corners(side, pay_a, pay_b):
+    return pl.pallas_call(
+        corner_kernel,
+        name="add_corners",
+        out_shape=[pltpu.VMEM(pay_a.shape, jnp.float32)] * 2,
+        in_specs=[VMEM] * 3,
+        out_specs=[VMEM] * 2,
+        input_output_aliases={1: 0, 2: 1},
+        compiler_params=pltpu.CompilerParams(vmem_limit_bytes=MIB),
+        cost_estimate=cost(0.1),
+    )(*held(side, pay_a, pay_b))
 
 
 def side_lanes(at_left):
@@ -214,7 +239,7 @@
             flux_c - west(flux_c) + flux_r - north(flux_r, self.fr_last[n])
         )
         self.fr_last[n] = flux_r
-        return out, u, v, wc * (u * jnp.abs(u)), wr * (v * jnp.abs(v))
+        return out, u, v, u * jnp.abs(u), v * jnp.abs(v)
 
     def step_one(self, i):
         at, after = tile_at(i), tile_at(i + 1)
@@ -261,8 +286,8 @@
     def step_three(self, i):
         at = tile_at(i)
         e, u, v, qc, qr = self.later(2, i, self.e2, self.u2, self.v2)
-        qc = self.qc2[at, :] + qc
-        qr = self.qr2[at, :] + qr
+        qc = self.wc[at, :] * (self.qc2[at, :] + qc)
+        qr = self.wr[at, :] * (self.qr2[at, :] + qr)
         change = (qc - west(qc) + qr - north(qr, self.qr_last[...])) * self.scale
         self.qr_last[...] = qr
         self.emit(i, e * (1.0 / 0.3), u, v, change)
@@ -429,7 +454,7 @@
         + Sweep.scratch(rows // SUB // 4 + 2, wide),
         input_output_aliases={10: 0},
         compiler_params=pltpu.CompilerParams(vmem_limit_bytes=12 * MIB),
-        cost_estimate=cost(4),
+        cost_estimate=cost(3),
     )(weights, params, *held(*raw, side, far_a, far_b, hydro))
 
 
@@ -613,14 +638,10 @@
         return part, beside
 
     side = lax.ppermute(pack_side(*raw), "tx", [(0, 1), (1, 0)])
-    pays = pack_rows(*raw)
-    odd = lax.axis_index("ty") % 2 == 1
-    corners = [side[:SUB], side[-SUB:]]
-    far_a = jnp.concatenate([pays[0], jnp.where(odd, corners[0], corners[1])])
-    far_b = jnp.concatenate([pays[1], jnp.where(odd, corners[1], corners[0])])
+    far_a, far_b = add_corners(side, *pack_rows(*raw))
     far_a = lax.ppermute(far_a, "ty", pairs(0))
     hydro, pay = middle(False, weights, cond_params, raw, side)
-    hydro, far_b = lax.optimization_barrier((hydro, far_b))
+    hydro, far_a, far_b = lax.optimization_barrier((hydro, far_a, far_b))
     far_b = lax.ppermute(far_b, "ty", pairs(1))
     got = lax.ppermute(pay, "cond", swap)
     hydro, pay = middle(True, weights, cond_params, raw, side, hydro)
@@ -631,6 +652,7 @@
     hydro, pay = edge(True, weights, cond_params, raw, side, far_a, far_b, hydro)
     own_m, hydro = over_chips(part_m, hydro)
     part_e = pay + got
+    own_m, _ = lax.optimization_barrier((own_m, part_e))
     got_m = lax.ppermute(own_m, "cond", swap)
     bed_next, bed_change, hydro = bed_middle(bed, side, far_a, far_b, own_m, got_m, hydro)
     own_e, (bed_next, bed_change) = over_chips(part_e, (bed_next, bed_change))

time: 45.5 us -> 39.8 us (0.87)
  local copies, waits for them, and re-layouts: 5.32 us -> 0.33 us
  Pallas kernels: 19 us -> 19.9 us
  starting transfers between devices: 13.1 us -> 12.4 us
  waiting for transfers between devices: 6.45 us -> 5.85 us
    unnamed x22 -> x14, local copies, waits for them, and re-layouts: 5.3 us -> 0.33 us
    ppermute x2, starting transfers between devices: 2.82 us -> 2.15 us  [shards(): got = lax.ppermute(pay, 'cond', swap)]
    pallas_call x1 -> x2, Pallas kernels: 1.17 us -> 1.82 us  [the longest x1 1.8 us: pack_rows(): pl.pallas_call(pack_rows_kernel, name='pack_rows', out_shape=[pltpu.VMEM(...]
  transfers between devices with their start and end apart: 9 -> 9, of which waited for: 4 -> 2; matrix products, arithmetic and copies ran while one was open for 0% -> 0% of each run, Pallas kernels for 34% -> 41%
where the time goes in v4:
time: 39.8 us; the launch traced here: 39.6 us
  Pallas kernels  19.9 us (50%)
  starting transfers between devices  12.4 us (31%)
  waiting for transfers between devices  5.85 us (15%)
  between operations  1.02 us (3%)
    pallas_call x2, Pallas kernels, edge(): pl.pallas_call(functools.partial(edge_kernel, own), name='edge_own' if ow...  6.29 us
    pallas_call x2, Pallas kernels, middle(): pl.pallas_call(functools.partial(middle_kernel, own), name='middle_own' i...  6.04 us
    ppermute x1, starting transfers between devices, shards(): far_b = lax.ppermute(far_b, 'ty', pairs(1))  4.93 us
    ppermute x2, waiting for transfers between devices, over_chips(): got = lax.ppermute(part, 'cond', [(i, i ^ reach) for i in range(nc)])  4.66 us
    ppermute x2, starting transfers between devices, over_chips(): got = lax.ppermute(part, 'cond', [(i, i ^ reach) for i in range(nc)])  2.5 us
    ppermute x2, starting transfers between devices, shards(): got = lax.ppermute(pay, 'cond', swap)  2.15 us
    pallas_call x1, Pallas kernels, bed_middle(): pl.pallas_call(bed_middle_kernel, name='bed_middle', out_shape=[pltpu.HBM...  2.03 us
    pallas_call x1, Pallas kernels, bed_edge(): pl.pallas_call(bed_edge_kernel, name='bed_edge', out_shape=[pltpu.HBM(bed...  1.95 us
  transfers between devices with their start and end apart: 9, of which 2 were waited for; matrix products, arithmetic and copies ran while one was open for 0% of the time, Pallas kernels for 41%

profile of v4, /device:TPU:9, one launch (start us, length us, event | category | flops | bytes accessed | tf_op | source)
XLA Modules:
  0.0 39.6 jit_solution(14408828883644589591)
XLA Ops:
  0.6 1.7 %pack_side.1 = f32[64,128]{1,0:T(8,128)S(1)} custom-call(f32[256,1024]{1,0:T(8,128)} %bed.15, s32[256,1024]{1,0:T(8,128)} %mask.11, s32[256,1024]{1,0:T(8,128)} %kind.11, f32[1,2,256,1024]{3,2,1,0:T(8,128)} %stress.11, f32[1,3,256,1024]{3,2,1,0:T(8,128)} %hydro.11), custom_call_target="tpu_custom_call" | custom-call | flops 2000000000 | tf_op jit(solution)/shard_map/pack_side/pallas_call | solution.py:97
  2.4 0.0 copy-start
  2.4 0.0 copy-start.2
  2.4 0.0 copy-start.3
  2.4 0.0 copy-start.6
  2.4 1.3 %collective-permute-start = (f32[64,128]{1,0:T(8,128)S(1)}, f32[64,128]{1,0:T(8,128)S(1)}, u32[]{:S(2)}, u32[]{:S(2)}) collective-permute-start(f32[64,128]{1,0:T(8,128)S(1)} %pack_side.1), channel_id=1, source_target_pairs={{0,1},{1,0},{2,3},{3,2},{4,5},{5,4},{6,7},{7,6},{8,9},{9,8},{10,11... | collective-permute-start | bytes 98312 | tf_op jit(solution)/shard_map/ppermute | solution.py:640
  3.7 1.8 %pack_rows.1 = (f32[264,128]{1,0:T(8,128)S(1)}, f32[264,128]{1,0:T(8,128)S(1)}) custom-call(f32[256,1024]{1,0:T(8,128)} %bed.15, s32[256,1024]{1,0:T(8,128)} %mask.11, s32[256,1024]{1,0:T(8,128)} %kind.11, f32[1,2,256,1024]{3,2,1,0:T(8,128)} %stress.11, f32[1,3,256,1024]{3,2,1,0:T(8,128)} %hydro.11), custom_call_target="tpu_custom_call" | custom-call | flops 2000000000 | tf_op jit(solution)/shard_map/pack_rows/pallas_call | solution.py:146
  5.6 0.1 collective-permute-start.1
  5.7 0.3 copy-done.4
  6.0 3.0 %middle_other.1 = (f32[1,3,256,1024]{3,2,1,0:T(8,128)S(1)}, f32[520,128]{1,0:T(8,128)S(1)}) custom-call(s32[4]{0:T(128)S(1)} %copy-done.5, f32[1,4]{1,0:T(1,128)S(1)} %copy-done.6, f32[256,1024]{1,0:T(8,128)S(1)} %copy-done.4, s32[256,1024]{1,0:T(8,128)S(1)} %copy-done.2, s32[256,1024]{1,0:T(8,128)S(1)} %copy-done.3, f32[1,2,256,1024]{3,2,1,0:T(8,128)S(1)} %copy-done.1, ...), custom_call_target="tpu_custom_call" | custom-call | flops 4000000000 | tf_op jit(solution)/shard_map/middle_other/pallas_call | solution.py:364
  9.0 1.2 %collective-permute-start.3 = (f32[520,128]{1,0:T(8,128)S(1)}, f32[520,128]{1,0:T(8,128)S(1)}, u32[]{:S(2)}, u32[]{:S(2)}) collective-permute-start(f32[520,128]{1,0:T(8,128)S(1)} %get-tuple-element.41), channel_id=1, source_target_pairs={{0,8},{8,0},{16,24},{24,16},{1,9},{9,1},{17,25},{25,17},{2,10},{10... | collective-permute-start | bytes 798728 | tf_op jit(solution)/shard_map/ppermute | solution.py:646
  10.3 4.9 %collective-permute-start.2 = (f32[264,128]{1,0:T(8,128)S(1)}, f32[264,128]{1,0:T(8,128)S(1)}, u32[]{:S(2)}, u32[]{:S(2)}) collective-permute-start(f32[264,128]{1,0:T(8,128)S(1)} %get-tuple-element.37), channel_id=1, source_target_pairs={{2,4},{4,2},{3,5},{5,3},{10,12},{12,10},{11,13},{13,11},{18,20},{2... | collective-permute-start | bytes 405512 | tf_op jit(solution)/shard_map/ppermute | solution.py:645
  15.2 3.0 %middle_own.1 = (f32[1,3,256,1024]{3,2,1,0:T(8,128)S(1)}, f32[520,128]{1,0:T(8,128)S(1)}) custom-call(s32[4]{0:T(128)S(1)} %copy-done.5, f32[1,4]{1,0:T(1,128)S(1)} %copy-done.6, f32[256,1024]{1,0:T(8,128)S(1)} %copy-done.4, s32[256,1024]{1,0:T(8,128)S(1)} %copy-done.2, s32[256,1024]{1,0:T(8,128)S(1)} %copy-done.3, ...), custom_call_target="tpu_custom_call", output_to_operand_aliasing={{0}: (8, {})} | custom-call | flops 4000000000 | tf_op jit(solution)/shard_map/middle_own/pallas_call | solution.py:364
  18.3 1.3 %collective-permute-start.4 = (f32[520,128]{1,0:T(8,128)S(1)}, f32[520,128]{1,0:T(8,128)S(1)}, u32[]{:S(2)}, u32[]{:S(2)}) collective-permute-start(f32[520,128]{1,0:T(8,128)S(1)} %add.12), channel_id=1, source_target_pairs={{0,16},{8,24},{16,0},{24,8},{1,17},{9,25},{17,1},{25,9},{2,18},{10... | collective-permute-start | bytes 798728 | tf_op jit(solution)/shard_map/ppermute | solution.py:634
  19.6 3.1 %edge_other.1 = (f32[1,3,256,1024]{3,2,1,0:T(8,128)S(1)}, f32[528,128]{1,0:T(8,128)S(1)}) custom-call(s32[4]{0:T(128)S(1)} %copy-done.5, f32[1,4]{1,0:T(1,128)S(1)} %copy-done.6, f32[256,1024]{1,0:T(8,128)S(1)} %copy-done.4, s32[256,1024]{1,0:T(8,128)S(1)} %copy-done.2, s32[256,1024]{1,0:T(8,128)S(1)} %copy-done.3, ...), custom_call_target="tpu_custom_call", output_to_operand_aliasing={{0}: (10, {})} | custom-call | flops 3000000000 | tf_op jit(solution)/shard_map/edge_other/pallas_call | solution.py:444
  22.7 0.9 %collective-permute-start.5 = (f32[528,128]{1,0:T(8,128)S(1)}, f32[528,128]{1,0:T(8,128)S(1)}, u32[]{:S(2)}, u32[]{:S(2)}) collective-permute-start(f32[528,128]{1,0:T(8,128)S(1)} %get-tuple-element.48), channel_id=1, source_target_pairs={{0,8},{8,0},{16,24},{24,16},{1,9},{9,1},{17,25},{25,17},{2,10},{10... | collective-permute-start | bytes 811016 | tf_op jit(solution)/shard_map/ppermute | solution.py:651
  23.6 3.1 %edge_own.1 = (f32[1,3,256,1024]{3,2,1,0:T(8,128)S(1)}, f32[528,128]{1,0:T(8,128)S(1)}) custom-call(s32[4]{0:T(128)S(1)} %copy-done.5, f32[1,4]{1,0:T(1,128)S(1)} %copy-done.6, f32[256,1024]{1,0:T(8,128)S(1)} %copy-done.4, s32[256,1024]{1,0:T(8,128)S(1)} %copy-done.2, s32[256,1024]{1,0:T(8,128)S(1)} %copy-done.3, ...), custom_call_target="tpu_custom_call", output_to_operand_aliasing={{0}: (10, {})} | custom-call | flops 3000000000 | tf_op jit(solution)/shard_map/edge_own/pallas_call | solution.py:444
  26.9 0.4 %collective-permute-start.6 = (f32[520,128]{1,0:T(8,128)S(1)}, f32[520,128]{1,0:T(8,128)S(1)}, u32[]{:S(2)}, u32[]{:S(2)}) collective-permute-start(f32[520,128]{1,0:T(8,128)S(1)} %add.13.own_m), channel_id=1, source_target_pairs={{0,8},{8,0},{16,24},{24,16},{1,9},{9,1},{17,25},{25,17},{2,10},{10... | collective-permute-start | bytes 798728 | tf_op jit(solution)/shard_map/ppermute | solution.py:656
  27.3 1.2 %collective-permute-start.7 = (f32[528,128]{1,0:T(8,128)S(1)}, f32[528,128]{1,0:T(8,128)S(1)}, u32[]{:S(2)}, u32[]{:S(2)}) collective-permute-start(f32[528,128]{1,0:T(8,128)S(1)} %add.14), channel_id=1, source_target_pairs={{0,16},{8,24},{16,0},{24,8},{1,17},{9,25},{17,1},{25,9},{2,18},{10... | collective-permute-start | bytes 811016 | tf_op jit(solution)/shard_map/ppermute | solution.py:634
  28.5 2.0 %bed_middle.1 = (f32[256,1024]{1,0:T(8,128)}, f32[256,1024]{1,0:T(8,128)}, f32[1,3,256,1024]{3,2,1,0:T(8,128)}) custom-call(f32[256,1024]{1,0:T(8,128)S(1)} %copy-done.4, f32[64,128]{1,0:T(8,128)S(1)} %collective-permute-done.side, f32[264,128]{1,0:T(8,128)S(1)} %collective-permute-done.1.far_a, f32[264,128]{1,0:T(8,128)S(1)} %collective-permute-done.2.far_b, ...), custom_call_target="tpu_custom_call" | custom-call | flops 4000000000 | tf_op jit(solution)/shard_map/bed_middle/pallas_call | solution.py:593
  30.6 4.7 %collective-permute-done.7 = f32[528,128]{1,0:T(8,128)S(1)} collective-permute-done((f32[528,128]{1,0:T(8,128)S(1)}, f32[528,128]{1,0:T(8,128)S(1)}, u32[]{:S(2)}, u32[]{:S(2)}) %collective-permute-start.7) | collective-permute-done | bytes 270368 | tf_op jit(solution)/shard_map/ppermute | solution.py:634
  35.3 1.0 %collective-permute-start.8 = (f32[528,128]{1,0:T(8,128)S(1)}, f32[528,128]{1,0:T(8,128)S(1)}, u32[]{:S(2)}, u32[]{:S(2)}) collective-permute-start(f32[528,128]{1,0:T(8,128)S(1)} %add.15.own_e), channel_id=1, source_target_pairs={{0,8},{8,0},{16,24},{24,16},{1,9},{9,1},{17,25},{25,17},{2,10},{10... | collective-permute-start | bytes 811016 | tf_op jit(solution)/shard_map/ppermute | solution.py:659
  36.3 1.2 %collective-permute-done.8.got_e = f32[528,128]{1,0:T(8,128)S(1)} collective-permute-done((f32[528,128]{1,0:T(8,128)S(1)}, f32[528,128]{1,0:T(8,128)S(1)}, u32[]{:S(2)}, u32[]{:S(2)}) %collective-permute-start.8) | collective-permute-done | bytes 270368 | tf_op jit(solution)/shard_map/ppermute | solution.py:659
  37.5 2.0 %bed_edge.1 = (f32[256,1024]{1,0:T(8,128)}, f32[256,1024]{1,0:T(8,128)}) custom-call(f32[256,1024]{1,0:T(8,128)S(1)} %copy-done.4, f32[64,128]{1,0:T(8,128)S(1)} %collective-permute-done.side, f32[264,128]{1,0:T(8,128)S(1)} %collective-permute-done.1.far_a, ...), custom_call_target="tpu_custom_call", output_to_operand_aliasing={{0}: (8, {}), {1}: (9, {})} | custom-call | flops 2000000000 | tf_op jit(solution)/shard_map/bed_edge/pallas_call | solution.py:606
  (21 shorter events, 0.2 us)
Async XLA Ops:
  2.4 3.3 %copy-start = (f32[1,3,256,1024]{3,2,1,0:T(8,128)S(1)}, f32[1,3,256,1024]{3,2,1,0:T(8,128)}, u32[]{:S(2)}) copy-start(f32[1,3,256,1024]{3,2,1,0:T(8,128)} %hydro.11) | copy-start | bytes 9437188
  2.4 3.3 %copy-start.1 = (f32[1,2,256,1024]{3,2,1,0:T(8,128)S(1)}, f32[1,2,256,1024]{3,2,1,0:T(8,128)}, u32[]{:S(2)}) copy-start(f32[1,2,256,1024]{3,2,1,0:T(8,128)} %stress.11) | copy-start | bytes 6291460
  2.4 3.3 %copy-start.2 = (s32[256,1024]{1,0:T(8,128)S(1)}, s32[256,1024]{1,0:T(8,128)}, u32[]{:S(2)}) copy-start(s32[256,1024]{1,0:T(8,128)} %mask.11) | copy-start | bytes 3145732
  2.4 3.3 %copy-start.3 = (s32[256,1024]{1,0:T(8,128)S(1)}, s32[256,1024]{1,0:T(8,128)}, u32[]{:S(2)}) copy-start(s32[256,1024]{1,0:T(8,128)} %kind.11) | copy-start | bytes 3145732
  2.4 3.6 %copy-start.4 = (f32[256,1024]{1,0:T(8,128)S(1)}, f32[256,1024]{1,0:T(8,128)}, u32[]{:S(2)}) copy-start(f32[256,1024]{1,0:T(8,128)} %bed.15) | copy-start | bytes 3145732
  2.4 3.6 %copy-start.5 = (s32[4]{0:T(128)S(1)}, s32[4]{0:T(128)}, u32[]{:S(2)}) copy-start(s32[4]{0:T(128)} %weights.7) | copy-start | bytes 52
  2.4 3.6 %copy-start.6 = (f32[1,4]{1,0:T(1,128)S(1)}, f32[1,4]{1,0:T(1,128)}, u32[]{:S(2)}) copy-start(f32[1,4]{1,0:T(1,128)} %params.7) | copy-start | bytes 52
  2.4 3.1 %collective-permute-start = (f32[64,128]{1,0:T(8,128)S(1)}, f32[64,128]{1,0:T(8,128)S(1)}, u32[]{:S(2)}, u32[]{:S(2)}) collective-permute-start(f32[64,128]{1,0:T(8,128)S(1)} %pack_side.1), channel_id=1, source_target_pairs={{0,1},{1,0},{2,3},{3,2},{4,5},{5,4},{6,7},{7,6},{8,9},{9,8},{10,11... | collective-permute-start | bytes 98312 | tf_op jit(solution)/shard_map/ppermute | solution.py:640
  5.6 4.7 %collective-permute-start.1 = (f32[264,128]{1,0:T(8,128)S(1)}, f32[264,128]{1,0:T(8,128)S(1)}, u32[]{:S(2)}, u32[]{:S(2)}) collective-permute-start(f32[264,128]{1,0:T(8,128)S(1)} %get-tuple-element.34), channel_id=1, source_target_pairs={{0,2},{2,0},{4,6},{6,4},{1,3},{3,1},{5,7},{7,5},{8,10},{10,8},{12,... | collective-permute-start | bytes 405512 | tf_op jit(solution)/shard_map/ppermute | solution.py:642
  9.0 9.2 %collective-permute-start.3 = (f32[520,128]{1,0:T(8,128)S(1)}, f32[520,128]{1,0:T(8,128)S(1)}, u32[]{:S(2)}, u32[]{:S(2)}) collective-permute-start(f32[520,128]{1,0:T(8,128)S(1)} %get-tuple-element.41), channel_id=1, source_target_pairs={{0,8},{8,0},{16,24},{24,16},{1,9},{9,1},{17,25},{25,17},{2,10},{10... | collective-permute-start | bytes 798728 | tf_op jit(solution)/shard_map/ppermute | solution.py:646
  10.3 9.3 %collective-permute-start.2 = (f32[264,128]{1,0:T(8,128)S(1)}, f32[264,128]{1,0:T(8,128)S(1)}, u32[]{:S(2)}, u32[]{:S(2)}) collective-permute-start(f32[264,128]{1,0:T(8,128)S(1)} %get-tuple-element.37), channel_id=1, source_target_pairs={{2,4},{4,2},{3,5},{5,3},{10,12},{12,10},{11,13},{13,11},{18,20},{2... | collective-permute-start | bytes 405512 | tf_op jit(solution)/shard_map/ppermute | solution.py:645
  18.3 8.5 %collective-permute-start.4 = (f32[520,128]{1,0:T(8,128)S(1)}, f32[520,128]{1,0:T(8,128)S(1)}, u32[]{:S(2)}, u32[]{:S(2)}) collective-permute-start(f32[520,128]{1,0:T(8,128)S(1)} %add.12), channel_id=1, source_target_pairs={{0,16},{8,24},{16,0},{24,8},{1,17},{9,25},{17,1},{25,9},{2,18},{10... | collective-permute-start | bytes 798728 | tf_op jit(solution)/shard_map/ppermute | solution.py:634
  22.7 4.1 %collective-permute-start.5 = (f32[528,128]{1,0:T(8,128)S(1)}, f32[528,128]{1,0:T(8,128)S(1)}, u32[]{:S(2)}, u32[]{:S(2)}) collective-permute-start(f32[528,128]{1,0:T(8,128)S(1)} %get-tuple-element.48), channel_id=1, source_target_pairs={{0,8},{8,0},{16,24},{24,16},{1,9},{9,1},{17,25},{25,17},{2,10},{10... | collective-permute-start | bytes 811016 | tf_op jit(solution)/shard_map/ppermute | solution.py:651
  26.9 1.7 %collective-permute-start.6 = (f32[520,128]{1,0:T(8,128)S(1)}, f32[520,128]{1,0:T(8,128)S(1)}, u32[]{:S(2)}, u32[]{:S(2)}) collective-permute-start(f32[520,128]{1,0:T(8,128)S(1)} %add.13.own_m), channel_id=1, source_target_pairs={{0,8},{8,0},{16,24},{24,16},{1,9},{9,1},{17,25},{25,17},{2,10},{10... | collective-permute-start | bytes 798728 | tf_op jit(solution)/shard_map/ppermute | solution.py:656
  27.3 7.9 %collective-permute-start.7 = (f32[528,128]{1,0:T(8,128)S(1)}, f32[528,128]{1,0:T(8,128)S(1)}, u32[]{:S(2)}, u32[]{:S(2)}) collective-permute-start(f32[528,128]{1,0:T(8,128)S(1)} %add.14), channel_id=1, source_target_pairs={{0,16},{8,24},{16,0},{24,8},{1,17},{9,25},{17,1},{25,9},{2,18},{10... | collective-permute-start | bytes 811016 | tf_op jit(solution)/shard_map/ppermute | solution.py:634
  35.3 2.2 %collective-permute-start.8 = (f32[528,128]{1,0:T(8,128)S(1)}, f32[528,128]{1,0:T(8,128)S(1)}, u32[]{:S(2)}, u32[]{:S(2)}) collective-permute-start(f32[528,128]{1,0:T(8,128)S(1)} %add.15.own_e), channel_id=1, source_target_pairs={{0,8},{8,0},{16,24},{24,16},{1,9},{9,1},{17,25},{25,17},{2,10},{10... | collective-permute-start | bytes 811016 | tf_op jit(solution)/shard_map/ppermute | solution.py:659

commit v5 on v4

--- a/solution.py
+++ b/solution.py
@@ -59,113 +59,174 @@
     return pl.CostEstimate(flops=int(micros * 10**9), bytes_accessed=0, transcendentals=0)
 
 
-def raw_fields(bed, mask, kind, stress, hydro):
-    return [bed, mask, kind] + [stress.at[0, k] for k in range(2)] + [hydro.at[0, k] for k in range(3)]
-
-
-SPOTS = [(0, 0), (1, 0), (1, 1)] + [(0, k) for k in range(1, 6)]
-
-
-def pack_side_kernel(bed, mask, kind, stress, hydro, side, reals, ints, sems):
+def level_terms(params):
+    return params[0, 0] - 1.0, 0.3 * params[0, 3]
+
+
+def coefficients(bed, mask, kind, tide, flow_in):
+    depth = mask.astype(jnp.float32) * (1.0 - 0.5 * jnp.tanh(bed))
+    root = depth * lax.rsqrt(jnp.maximum(depth, 1e-12))
+    relax = jnp.where(kind == 1, 0.5 * depth, 0.0)
+    return root, 1.0 - relax, 0.3 * (relax * tide + jnp.where(kind == 2, flow_in * depth, 0.0))
+
+
+def moving(stress, hydro):
+    return [stress.at[0, k] for k in range(2)] + [hydro.at[0, k] for k in range(3)]
+
+
+def pack_side_kernel(params_in, bed, mask, kind, stress, hydro, side, reals, ints, params, sems):
     rows, cols = bed.shape
     at_left = lax.axis_index("tx") == 0
     off = pl.multiple_of(jnp.where(at_left, cols - LANE, 0), LANE)
-    strips = [(reals, ints)[which].at[k] for which, k in SPOTS]
+    strips = [reals.at[0], ints.at[0], ints.at[1]] + [reals.at[k] for k in range(1, 6)]
     copies = [
         pltpu.make_async_copy(src.at[:, pl.ds(off, LANE)], strip, sems.at[f])
-        for f, (src, strip) in enumerate(zip(raw_fields(bed, mask, kind, stress, hydro), strips))
-    ]
+        for f, (src, strip) in enumerate(zip([bed, mask, kind] + moving(stress, hydro), strips))
+    ] + [pltpu.make_async_copy(params_in, params, sems.at[FIELDS])]
     for copy in copies:
         copy.start()
     for copy in copies:
         copy.wait()
+    tide, flow_in = level_terms(params)
     lift = jnp.where(at_left, HALO, 0)
+    lift_bed = jnp.where(at_left, 1, 0)
     lane = lanes_of((SUB, LANE))
     span = rows // FOLD // SUB
+    beds = jnp.zeros((SUB, LANE), jnp.float32)
     for i in range(span):
         total = jnp.zeros((SUB, LANE), jnp.float32)
         for g in range(FOLD):
-            for f in range(FIELDS):
+            at = tile_at(g * span + i)
+            first = strips[0][at, :]
+            fields = list(coefficients(first, strips[1][at, :], strips[2][at, :], tide, flow_in))
+            fields += [strip[at, :] for strip in strips[3:]]
+            for f, part in enumerate(fields):
                 place = g * FIELDS + f
-                part = strips[f][tile_at(g * span + i), :].astype(jnp.float32)
                 total = jnp.where(lane // HALO == place, pltpu.roll(part, lift + place * HALO, 1), total)
+            block = g * span + i
+            beds = jnp.where(lane == block, pltpu.roll(first, lift_bed + block, 1), beds)
         side[tile_at(i), :] = total
-
-
-def pack_side(*raw):
+    side[tile_at(span), :] = beds
+
+
+def pack_side(params, *raw):
     rows, cols = raw[0].shape
     return pl.pallas_call(
         pack_side_kernel,
         name="pack_side",
-        out_shape=pltpu.VMEM((rows // FOLD, LANE), jnp.float32),
-        in_specs=[ANY] * 5,
+        out_shape=pltpu.VMEM((rows // FOLD + SUB, LANE), jnp.float32),
+        in_specs=[ANY] * 6,
         out_specs=VMEM,
         scratch_shapes=[
             pltpu.VMEM((6, rows, LANE), jnp.float32),
             pltpu.VMEM((2, rows, LANE), jnp.int32),
-            pltpu.SemaphoreType.DMA((FIELDS,)),
+            pltpu.SMEM(params.shape, jnp.float32),
+            pltpu.SemaphoreType.DMA((FIELDS + 1,)),
         ],
         compiler_params=pltpu.CompilerParams(vmem_limit_bytes=4 * MIB),
         cost_estimate=cost(2),
-    )(*held(*raw, space=pltpu.HBM))
-
-
-def pack_rows_kernel(bed, mask, kind, stress, hydro, pay_a, pay_b, reals, ints, sems):
+    )(*held(params, *raw, space=pltpu.HBM))
+
+
+PARTS = 4
+
+
+def prepare_kernel(
+    params_in, bed, mask, kind, stress, hydro, bed_v, root, a, b, pay_a, pay_b,
+    mask_v, kind_v, ends, params, load_sems, end_sems, params_sem,
+):
     rows, cols = bed.shape
-    copies = []
-    for f, src in enumerate(raw_fields(bed, mask, kind, stress, hydro)):
-        which, k = SPOTS[f]
+    lanes = cols // LANE
+    chunk = rows // PARTS
+    loads, copies = [], []
+    for c in range(PARTS):
+        at = pl.ds(c * chunk, chunk)
+        loads.append([
+            pltpu.make_async_copy(src.at[at], dst.at[at], load_sems.at[f, c])
+            for f, (src, dst) in enumerate(((bed, bed_v), (mask, mask_v), (kind, kind_v)))
+        ])
+    for f, src in enumerate(moving(stress, hydro)):
         for end, start in enumerate((0, rows - SUB)):
-            copies.append(
-                pltpu.make_async_copy(src.at[pl.ds(start, SUB)], (reals, ints)[which].at[end, k], sems.at[f, end])
-            )
-    for copy in copies:
-        copy.start()
+            copies.append(pltpu.make_async_copy(src.at[pl.ds(start, SUB)], ends.at[end, f], end_sems.at[f, end]))
+    loads[0].append(pltpu.make_async_copy(params_in, params, params_sem))
+    for group in loads + [copies]:
+        for copy in group:
+            copy.start()
+    for copy in loads[0]:
+        copy.wait()
+    tide, flow_in = level_terms(params)
+    for c in range(PARTS):
+        for copy in loads[c] if c else ():
+            copy.wait()
+        for i in range(c * chunk // SUB, (c + 1) * chunk // SUB):
+            at = tile_at(i)
+            root[at, :], a[at, :], b[at, :] = coefficients(bed_v[at, :], mask_v[at, :], kind_v[at, :], tide, flow_in)
     for copy in copies:
         copy.wait()
     low = rows_of((SUB, cols)) < HALO
     odd = lax.axis_index("ty") % 2 == 1
+
+    def edge_rows(f, end):
+        if f < 3:
+            return (root, a, b)[f][tile_at(0 if end == 0 else rows // SUB - 1), :]
+        return ends[end, f - 3]
+
     for p in range(FIELDS // 2):
         pairs = []
         for end in range(2):
-            both = []
-            for f in (2 * p, 2 * p + 1):
-                which, k = SPOTS[f]
-                both.append((reals, ints)[which][end, k].astype(jnp.float32))
+            both = [edge_rows(f, end) for f in (2 * p, 2 * p + 1)]
             both[1 - end] = pltpu.roll(both[1 - end], HALO, 0)
             pairs.append(jnp.where(low, *both))
-        for k in range(cols // LANE):
-            at, lanes = pl.ds(k * GROUP + p * SUB, SUB), slice(k * LANE, (k + 1) * LANE)
-            top, bottom = pairs[0][:, lanes], pairs[1][:, lanes]
+        for k in range(lanes):
+            at, part = pl.ds(k * GROUP + p * SUB, SUB), slice(k * LANE, (k + 1) * LANE)
+            top, bottom = pairs[0][:, part], pairs[1][:, part]
             pay_a[at, :] = jnp.where(odd, top, bottom)
             pay_b[at, :] = jnp.where(odd, bottom, top)
-
-
-def pack_rows(*raw):
+    top = fold_row(bed_v[tile_at(0), :])
+    bottom = fold_row(pltpu.roll(bed_v[tile_at(rows // SUB - 1), :], 1, 0))
+    at = pl.ds(lanes * GROUP + SUB, SUB)
+    pay_a[at, :] = jnp.where(odd, top, bottom)
+    pay_b[at, :] = jnp.where(odd, bottom, top)
+
+
+def fold_row(x):
+    row = rows_of((SUB, LANE))
+    total = x[:, :LANE]
+    for k in range(1, x.shape[1] // LANE):
+        total = jnp.where(row == k, pltpu.roll(x[:, k * LANE : (k + 1) * LANE], k, 0), total)
+    return total
+
+
+def prepare(params, *raw):
     rows, cols = raw[0].shape
+    tile = pltpu.VMEM((rows, cols), jnp.float32)
     return pl.pallas_call(
-        pack_rows_kernel,
-        name="pack_rows",
-        out_shape=[pltpu.VMEM((cols // LANE * GROUP + SUB, LANE), jnp.float32)] * 2,
-        in_specs=[ANY] * 5,
-        out_specs=[VMEM] * 2,
+        prepare_kernel,
+        name="prepare",
+        out_shape=[tile] * 4 + [pltpu.VMEM((cols // LANE * GROUP + 2 * SUB, LANE), jnp.float32)] * 2,
+        in_specs=[ANY] * 6,
+        out_specs=[VMEM] * 6,
         scratch_shapes=[
-            pltpu.VMEM((2, 6, SUB, cols), jnp.float32),
-            pltpu.VMEM((2, 2, SUB, cols), jnp.int32),
-            pltpu.SemaphoreType.DMA((FIELDS, 2)),
+            pltpu.VMEM((rows, cols), jnp.int32),
+            pltpu.VMEM((rows, cols), jnp.int32),
+            pltpu.VMEM((2, 5, SUB, cols), jnp.float32),
+            pltpu.SMEM(params.shape, jnp.float32),
+            pltpu.SemaphoreType.DMA((3, PARTS)),
+            pltpu.SemaphoreType.DMA((5, 2)),
+            pltpu.SemaphoreType.DMA,
         ],
-        compiler_params=pltpu.CompilerParams(vmem_limit_bytes=4 * MIB),
+        compiler_params=pltpu.CompilerParams(vmem_limit_bytes=5 * MIB),
         cost_estimate=cost(2),
-    )(*held(*raw, space=pltpu.HBM))
+    )(*held(params, *raw, space=pltpu.HBM))
 
 
 def corner_kernel(side, in_a, in_b, pay_a, pay_b):
-    tall = pay_a.shape[0]
+    at = pl.ds(pay_a.shape[0] - 2 * SUB, SUB)
     odd = lax.axis_index("ty") % 2 == 1
     top = side[pl.ds(0, SUB), :]
-    bottom = side[pl.ds(side.shape[0] - SUB, SUB), :]
-    pay_a[pl.ds(tall - SUB, SUB), :] = jnp.where(odd, top, bottom)
-    pay_b[pl.ds(tall - SUB, SUB), :] = jnp.where(odd, bottom, top)
+    bottom = side[pl.ds(side.shape[0] - 2 * SUB, SUB), :]
+    pay_a[at, :] = jnp.where(odd, top, bottom)
+    pay_b[at, :] = jnp.where(odd, bottom, top)
 
 
 def add_corners(side, pay_a, pay_b):
@@ -194,17 +255,15 @@
 
 class Sweep:
     NAMES = (
-        ["s", "a", "b", "fc", "fr", "wc", "wr", "e1", "u1"]
+        ["fc", "fr", "wc", "wr", "e1", "u1"]
         + ["v1", "e2", "u2", "v2", "qc1", "qr1", "qc2", "qr2"]
     )
 
-    def __init__(self, count, wide, get, emit, weights, params, refs):
-        self.count, self.wide, self.get, self.emit = count, wide, get, emit
+    def __init__(self, count, wide, get, emit, weights, params, refs, trim):
+        self.count, self.wide, self.get, self.emit, self.trim = count, wide, get, emit, trim
         self.__dict__.update(zip(self.NAMES + ["fr_last", "qr_last"], refs))
         cond = lax.axis_index("cond")
-        self.tide = params[0, 0] - 1.0
         self.slow = 1.0 - 0.2 * params[0, 1]
-        self.flow_in = 0.3 * params[0, 3]
         total = weights[0]
         for k in range(1, weights.shape[0]):
             total = total + weights[k]
@@ -220,32 +279,30 @@
             pltpu.VMEM((SUB, wide), jnp.float32),
         ]
 
-    def prepare(self, i):
-        at = tile_at(i)
-        depth = self.get(1, i).astype(jnp.float32) * (1.0 - 0.5 * jnp.tanh(self.get(0, i)))
-        kinds = self.get(2, i)
-        self.s[at, :] = depth * lax.rsqrt(jnp.maximum(depth, 1e-12))
-        relax = jnp.where(kinds == 1, 0.5 * depth, 0.0)
-        self.a[at, :] = 1.0 - relax
-        self.b[at, :] = 0.3 * (relax * self.tide + jnp.where(kinds == 2, self.flow_in * depth, 0.0))
+    def speed_c(self, i, level, u, wc):
+        return (self.slow * u - (east(level) - level) + self.get(3, i)) * wc
+
+    def speed_r(self, i, level, lower, v, wr):
+        return (self.slow * v - (south(level, lower) - level) + self.get(4, i)) * wr
 
     def move(self, n, i, level, lower, u, v, fc, fr, wc, wr):
-        at = tile_at(i)
-        u = (self.slow * u - (east(level) - level) + self.get(3, i)) * wc
-        v = (self.slow * v - (south(level, lower) - level) + self.get(4, i)) * wr
+        u = self.speed_c(i, level, u, wc)
+        v = self.speed_r(i, level, lower, v, wr)
         flux_c = fc * u
         flux_r = fr * v
-        out = self.a[at, :] * level + self.b[at, :] - (
+        out = self.get(1, i) * level + self.get(2, i) - (
             flux_c - west(flux_c) + flux_r - north(flux_r, self.fr_last[n])
         )
         self.fr_last[n] = flux_r
-        return out, u, v, u * jnp.abs(u), v * jnp.abs(v)
+        return out, u, v
 
     def step_one(self, i):
-        at, after = tile_at(i), tile_at(i + 1)
-        s = self.s[at, :]
+        at = tile_at(i)
+        s = self.get(0, i)
+        level = 0.3 * self.get(5, i)
+        inside = i + 1 < self.count
         face_c = s * east(s)
-        face_r = s * south(s, self.s[after, :])
+        face_r = s * south(s, self.get(0, i + 1) if inside else s)
         ratios = []
         for face in (face_c, face_r):
             base = face + 0.1
@@ -258,36 +315,45 @@
         self.fr[at, :] = fr
         self.wc[at, :] = wc
         self.wr[at, :] = wr
-        level = 0.3 * self.get(5, i)
-        lower = 0.3 * self.get(5, i + 1) if i + 1 < self.count else level
-        e, u, v, qc, qr = self.move(0, i, level, lower, self.get(6, i), self.get(7, i), fc, fr, wc, wr)
+        lower = 0.3 * self.get(5, i + 1) if inside else level
+        e, u, v = self.move(0, i, level, lower, self.get(6, i), self.get(7, i), fc, fr, wc, wr)
         self.e1[at, :] = e
         self.u1[at, :] = u
         self.v1[at, :] = v
-        self.qc1[at, :] = qc
-        self.qr1[at, :] = qr
-
-    def later(self, n, i, e, u, v):
+        self.qc1[at, :] = u * jnp.abs(u)
+        self.qr1[at, :] = v * jnp.abs(v)
+
+    def step_two(self, i):
         at, after = tile_at(i), tile_at(i + 1)
-        return self.move(
-            n, i, e[at, :], e[after, :], u[at, :], v[at, :],
+        e, u, v = self.move(
+            1, i, self.e1[at, :], self.e1[after, :], self.u1[at, :], self.v1[at, :],
             self.fc[at, :], self.fr[at, :], self.wc[at, :], self.wr[at, :],
         )
-
-    def step_two(self, i):
-        at = tile_at(i)
-        e, u, v, qc, qr = self.later(1, i, self.e1, self.u1, self.v1)
         self.e2[at, :] = e
+        if self.trim and i == self.count - 1:
+            return
         self.u2[at, :] = u
         self.v2[at, :] = v
-        self.qc2[at, :] = self.qc1[at, :] + qc
-        self.qr2[at, :] = self.qr1[at, :] + qr
+        self.qc2[at, :] = self.qc1[at, :] + u * jnp.abs(u)
+        self.qr2[at, :] = self.qr1[at, :] + v * jnp.abs(v)
 
     def step_three(self, i):
-        at = tile_at(i)
-        e, u, v, qc, qr = self.later(2, i, self.e2, self.u2, self.v2)
-        qc = self.wc[at, :] * (self.qc2[at, :] + qc)
-        qr = self.wr[at, :] * (self.qr2[at, :] + qr)
+        at, after = tile_at(i), tile_at(i + 1)
+        if self.trim and i == self.count - 1:
+            return
+        if self.trim and i == 0:
+            wr = self.wr[at, :]
+            v = self.speed_r(i, self.e2[at, :], self.e2[after, :], self.v2[at, :], wr)
+            self.fr_last[2] = self.fr[at, :] * v
+            self.qr_last[...] = wr * (self.qr2[at, :] + v * jnp.abs(v))
+            return
+        wc, wr = self.wc[at, :], self.wr[at, :]
+        e, u, v = self.move(
+            2, i, self.e2[at, :], self.e2[after, :], self.u2[at, :], self.v2[at, :],
+            self.fc[at, :], self.fr[at, :], wc, wr,
+        )
+        qc = wc * (self.qc2[at, :] + u * jnp.abs(u))
+        qr = wr * (self.qr2[at, :] + v * jnp.abs(v))
         change = (qc - west(qc) + qr - north(qr, self.qr_last[...])) * self.scale
         self.qr_last[...] = qr
         self.emit(i, e * (1.0 / 0.3), u, v, change)
@@ -295,48 +361,28 @@
     def run(self):
         self.fr_last[...] = jnp.zeros_like(self.fr_last)
         self.qr_last[...] = jnp.zeros_like(self.qr_last)
-        for ref in (self.s, self.e1, self.e2):
+        for ref in (self.e1, self.e2):
             ref[tile_at(self.count), :] = jnp.zeros((SUB, self.wide), jnp.float32)
-        stages = (self.step_three, self.step_two, self.step_one, self.prepare)
-        for t in range(self.count + LAG * STEPS):
+        stages = (self.step_three, self.step_two, self.step_one)
+        for t in range(self.count + LAG * (STEPS - 1)):
             for k, stage in enumerate(stages):
-                i = t - LAG * (STEPS - k)
+                i = t - LAG * (STEPS - 1 - k)
                 if 0 <= i < self.count:
                     stage(i)
 
 
-def raw_reader(bed, mask, kind, stress, hydro, side, unfold, valid):
-    rows = bed.shape[0]
+def reader(root, a, b, stress, hydro, side, unfold, valid):
+    rows = root.shape[0]
     span = rows // FOLD // SUB
-    fields = raw_fields(bed, mask, kind, stress, hydro)
+    fields = [root, a, b] + moving(stress, hydro)
 
     def read(f, block):
-        strip = side[tile_at(block % span), :]
-        part = unfold(strip, (block // span) * FIELDS + f)
-        if f == 1:
+        part = unfold(side[tile_at(block % span), :], (block // span) * FIELDS + f)
+        if f == 0:
             part = jnp.where(valid, part, 0.0)
-        main = fields[f][tile_at(block), :]
-        return jnp.concatenate([main, part.astype(main.dtype)], axis=1)
+        return jnp.concatenate([fields[f][tile_at(block), :], part], axis=1)
 
     return read
-
-
-def middle_kernel(own, weights, params, bed, mask, kind, stress, hydro, side, *refs):
-    hydro_out, pay, *refs = refs[1:] if own else refs
-    rows, cols = bed.shape
-    quarter = rows // SUB // 4
-    unfold, valid = side_lanes(lax.axis_index("tx") == 0)
-    read = raw_reader(bed, mask, kind, stress, hydro, side, unfold, valid)
-    mine = lax.axis_index("cond") % 2
-    lower_half = mine == (1 if own else 0)
-    first = jnp.where(lower_half, 2 * quarter, quarter) - 1
-    emit = quarter_writer(first, quarter, cols, hydro_out, pay)
-
-    def finish(i, e, u, v, change):
-        if 1 <= i <= quarter:
-            emit(i, e, u, v, change)
-
-    Sweep(quarter + 2, cols + LANE, lambda f, i: read(f, first + i), finish, weights, params, refs).run()
 
 
 def quarter_writer(first, quarter, cols, hydro_out, pay):
@@ -358,14 +404,28 @@
     return emit
 
 
-def middle(own, weights, params, raw, side, hydro=None):
-    rows, cols = raw[0].shape
+def middle_kernel(own, weights, params, root, a, b, stress, hydro, side, *refs):
+    hydro_out, pay, *refs = refs[1:] if own else refs
+    rows, cols = root.shape
+    quarter = rows // SUB // 4
+    read = reader(root, a, b, stress, hydro, side, *side_lanes(lax.axis_index("tx") == 0))
+    mine = lax.axis_index("cond") % 2
+    lower_half = mine == (1 if own else 0)
+    first = jnp.where(lower_half, 2 * quarter, quarter) - 1
+    emit = quarter_writer(first, quarter, cols, hydro_out, pay)
+    Sweep(
+        quarter + 2, cols + LANE, lambda f, i: read(f, first + i), emit, weights, params, refs, True
+    ).run()
+
+
+def middle(own, weights, params, fields, side, hydro=None):
+    rows, cols = fields[0].shape
     given = (hydro,) if own else ()
     return pl.pallas_call(
         functools.partial(middle_kernel, own),
         name="middle_own" if own else "middle_other",
         out_shape=[
-            pltpu.VMEM(raw[4].shape, jnp.float32),
+            pltpu.VMEM(fields[4].shape, jnp.float32),
             pltpu.VMEM((cols // LANE * rows // 4 + SUB, LANE), jnp.float32),
         ],
         in_specs=[SMEM, SMEM] + [VMEM] * (6 + own),
@@ -374,26 +434,26 @@
         input_output_aliases={8: 0} if own else {},
         compiler_params=pltpu.CompilerParams(vmem_limit_bytes=10 * MIB),
         cost_estimate=cost(4),
-    )(weights, params, *held(*raw, side, *given))
+    )(weights, params, *held(*fields, side, *given))
 
 
 def edge_kernel(
-    own, weights, params, bed, mask, kind, stress, hydro, side, far_a, far_b, hydro_in,
-    hydro_out, pay, ends_r, ends_i, *refs,
+    own, weights, params, root, a, b, stress, hydro, side, far_a, far_b, hydro_in,
+    hydro_out, pay, ends, *refs,
 ):
-    rows, cols = bed.shape
+    rows, cols = root.shape
     blocks = rows // SUB
     quarter = blocks // 4
-    wide = cols + LANE
     lanes = cols // LANE
     unfold, valid = side_lanes(lax.axis_index("tx") == 0)
-    read = raw_reader(bed, mask, kind, stress, hydro, side, unfold, valid)
+    read = reader(root, a, b, stress, hydro, side, unfold, valid)
     mine = lax.axis_index("cond") % 2
     top = mine == (0 if own else 1)
     from_a = top == (lax.axis_index("ty") % 2 == 1)
     first = jnp.where(top, -1, blocks - quarter - 1)
 
     inner = jnp.where(top, quarter, blocks - quarter - 1)
+    corners = pl.ds(lanes * GROUP, SUB)
     for f in range(FIELDS):
         body = read(f, inner)
         parts = []
@@ -402,44 +462,35 @@
             part = jnp.where(from_a, far_a[at, :], far_b[at, :])
             moved = pltpu.roll(part, HALO, 0)
             parts.append(jnp.where(top, moved, part) if f % 2 == 0 else jnp.where(top, part, moved))
-        at = pl.ds(lanes * GROUP, SUB)
-        corner = jnp.where(from_a, far_a[at, :], far_b[at, :])
+        corner = jnp.where(from_a, far_a[corners, :], far_b[corners, :])
         corner = jnp.where(top, unfold(corner, (FOLD - 1) * FIELDS + f), unfold(corner, f))
-        if f == 1:
+        if f == 0:
             corner = jnp.where(valid, corner, 0.0)
-        outer = jnp.concatenate(parts + [corner], axis=1).astype(body.dtype)
-        which, k = SPOTS[f]
-        ref = (ends_r, ends_i)[which]
-        ref[0, k] = jnp.where(top, outer, body)
-        ref[1, k] = jnp.where(top, body, outer)
+        outer = jnp.concatenate(parts + [corner], axis=1)
+        ends[0, f] = jnp.where(top, outer, body)
+        ends[1, f] = jnp.where(top, body, outer)
 
     def get(f, i):
         if i == 0 or i == quarter + 1:
-            which, k = SPOTS[f]
-            return (ends_r, ends_i)[which][0 if i == 0 else 1, k]
+            return ends[0 if i == 0 else 1, f]
         return read(f, first + i)
 
-    row = rows_of((SUB, LANE))
     emit = quarter_writer(first, quarter, cols, hydro_out, pay)
     outside = []
 
     def finish(i, e, u, v, change):
         if i == 0:
-            outside.append(pltpu.roll(change, 1, 0))
+            outside.append(pltpu.roll(change[:, :cols], 1, 0))
         elif i == quarter + 1:
-            rim = jnp.where(top, outside[0], change)
-            total = rim[:, :LANE]
-            for k in range(1, lanes):
-                total = jnp.where(row == k, pltpu.roll(rim[:, k * LANE : (k + 1) * LANE], k, 0), total)
-            pay[tile_at(lanes * quarter + 1), :] = total
+            pay[tile_at(lanes * quarter + 1), :] = fold_row(jnp.where(top, outside[0], change[:, :cols]))
         else:
             emit(i, e, u, v, change)
 
-    Sweep(quarter + 2, wide, get, finish, weights, params, refs).run()
-
-
-def edge(own, weights, params, raw, side, far_a, far_b, hydro):
-    rows, cols = raw[0].shape
+    Sweep(quarter + 2, cols + LANE, get, finish, weights, params, refs, False).run()
+
+
+def edge(own, weights, params, fields, side, far_a, far_b, hydro):
+    rows, cols = fields[0].shape
     wide = cols + LANE
     return pl.pallas_call(
         functools.partial(edge_kernel, own),
@@ -450,12 +501,12 @@
         ],
         in_specs=[SMEM, SMEM] + [VMEM] * 9,
         out_specs=[VMEM, VMEM],
-        scratch_shapes=[pltpu.VMEM((2, 6, SUB, wide), jnp.float32), pltpu.VMEM((2, 2, SUB, wide), jnp.int32)]
+        scratch_shapes=[pltpu.VMEM((2, FIELDS, SUB, wide), jnp.float32)]
         + Sweep.scratch(rows // SUB // 4 + 2, wide),
         input_output_aliases={10: 0},
         compiler_params=pltpu.CompilerParams(vmem_limit_bytes=12 * MIB),
         cost_estimate=cost(3),
-    )(weights, params, *held(*raw, side, far_a, far_b, hydro))
+    )(weights, params, *held(*fields, side, far_a, far_b, hydro))
 
 
 class Update:
@@ -468,7 +519,8 @@
         self.quarter = self.blocks // 4
         self.lanes = self.cols // LANE
         self.wide = self.cols + LANE
-        self.unfold, _ = side_lanes(lax.axis_index("tx") == 0)
+        self.side_bed = side[pl.ds(side.shape[0] - SUB, SUB), :]
+        self.drop_bed = jnp.where(lax.axis_index("tx") == 0, 0, 1)
         self.mine = lax.axis_index("cond") % 2
         self.odd = lax.axis_index("ty") % 2 == 1
         col = lanes_of((SUB, self.wide))
@@ -484,16 +536,12 @@
         return jnp.where(self.mine == q // 2, own[at, :], got[at, :])
 
     def outside(self, q):
-        rim = self.merged(q, self.lanes * self.quarter + 1)
-        parts = []
-        for k in range(self.lanes):
-            at = tile_at(k * GROUP // SUB)
-            a, b = self.far_a[at, :], self.far_b[at, :]
-            if q == 0:
-                z = jnp.where(self.odd, a, b) + pltpu.roll(rim, (2 * SUB + HALO - 1 - k) % SUB, 0)
-                parts.append(pltpu.roll(z, HALO, 0))
-            else:
-                parts.append(jnp.where(self.odd, b, a) + pltpu.roll(rim, (SUB - k) % SUB, 0))
+        at = pl.ds(self.lanes * GROUP + SUB, SUB)
+        a, b = self.far_a[at, :], self.far_b[at, :]
+        bed = jnp.where(self.odd, a, b) if q == 0 else jnp.where(self.odd, b, a)
+        z = bed + self.merged(q, self.lanes * self.quarter + 1)
+        target = SUB - 1 if q == 0 else 0
+        parts = [pltpu.roll(z, (SUB + target - k) % SUB, 0) if (target - k) % SUB else z for k in range(self.lanes)]
         return jnp.concatenate(parts + [jnp.zeros((SUB, LANE), jnp.float32)], axis=1)
 
     def level(self, b, keep):
@@ -507,8 +555,7 @@
             self.change_v[tile_at(b), :] = change
         if q not in self.rims:
             self.rims[q] = self.merged(q, self.lanes * self.quarter)
-        span = self.blocks // FOLD
-        cols_bed = self.unfold(self.side[tile_at(b % span), :], b // span * FIELDS)
+        cols_bed = pltpu.roll(self.side_bed, 2 * LANE - self.drop_bed - b, 1)
         cols_change = pltpu.roll(self.rims[q], LANE - 1 - 2 * g, 1)
         return jnp.concatenate([self.bed[tile_at(b), :] + change, cols_bed + cols_change], axis=1)
 
@@ -637,19 +684,21 @@
             reach = 2 * reach
         return part, beside
 
-    side = lax.ppermute(pack_side(*raw), "tx", [(0, 1), (1, 0)])
-    far_a, far_b = add_corners(side, *pack_rows(*raw))
+    side = lax.ppermute(pack_side(cond_params, *raw), "tx", [(0, 1), (1, 0)])
+    bed, *terms, far_a, far_b = prepare(cond_params, *raw)
+    fields = (*terms, wave_stress, hydro_state)
+    far_a, far_b = add_corners(side, far_a, far_b)
     far_a = lax.ppermute(far_a, "ty", pairs(0))
-    hydro, pay = middle(False, weights, cond_params, raw, side)
+    hydro, pay = middle(False, weights, cond_params, fields, side)
     hydro, far_a, far_b = lax.optimization_barrier((hydro, far_a, far_b))
     far_b = lax.ppermute(far_b, "ty", pairs(1))
     got = lax.ppermute(pay, "cond", swap)
-    hydro, pay = middle(True, weights, cond_params, raw, side, hydro)
+    hydro, pay = middle(True, weights, cond_params, fields, side, hydro)
     part_m = pay + got
     hydro, part_m = lax.optimization_barrier((hydro, part_m))
-    hydro, pay = edge(False, weights, cond_params, raw, side, far_a, far_b, hydro)
+    hydro, pay = edge(False, weights, cond_params, fields, side, far_a, far_b, hydro)
     got = lax.ppermute(pay, "cond", swap)
-    hydro, pay = edge(True, weights, cond_params, raw, side, far_a, far_b, hydro)
+    hydro, pay = edge(True, weights, cond_params, fields, side, far_a, far_b, hydro)
     own_m, hydro = over_chips(part_m, hydro)
     part_e = pay + got
     own_m, _ = lax.optimization_barrier((own_m, part_e))

time: 39.8 us -> 40.1 us (level)
  Pallas kernels: 19.9 us -> 21.1 us
    pallas_call x1, Pallas kernels: 1.8 us -> 2.58 us  [prepare(): pl.pallas_call(prepare_kernel, name='prepare', out_shape=[tile] * 4 + [pl...]
    ppermute x2, waiting for transfers between devices: 4.66 us -> 3.92 us  [over_chips(): got = lax.ppermute(part, 'cond', [(i, i ^ reach) for i in range(nc)])]
    ppermute x1, starting transfers between devices: 4.93 us -> 4.39 us  [shards(): far_b = lax.ppermute(far_b, 'ty', pairs(1))]
  transfers between devices with their start and end apart: 9 -> 9, of which waited for: 2 -> 4; matrix products, arithmetic and copies ran while one was open for 0% -> 0% of each run, Pallas kernels for 41% -> 44%
where the time goes in v5:
time: 40.1 us; the launch traced here: 39.9 us
  Pallas kernels  21.1 us (53%)
  starting transfers between devices  12.1 us (30%)
  waiting for transfers between devices  5.53 us (14%)
  between operations  0.98 us (2%)
    pallas_call x2, Pallas kernels, edge(): pl.pallas_call(functools.partial(edge_kernel, own), name='edge_own' if ow...  6.35 us
    pallas_call x2, Pallas kernels, middle(): pl.pallas_call(functools.partial(middle_kernel, own), name='middle_own' i...  6.22 us
    ppermute x1, starting transfers between devices, shards(): far_b = lax.ppermute(far_b, 'ty', pairs(1))  4.39 us
    ppermute x2, waiting for transfers between devices, over_chips(): got = lax.ppermute(part, 'cond', [(i, i ^ reach) for i in range(nc)])  3.92 us
    pallas_call x1, Pallas kernels, prepare(): pl.pallas_call(prepare_kernel, name='prepare', out_shape=[tile] * 4 + [pl...  2.58 us
    ppermute x2, starting transfers between devices, over_chips(): got = lax.ppermute(part, 'cond', [(i, i ^ reach) for i in range(nc)])  2.48 us
    ppermute x2, starting transfers between devices, shards(): got = lax.ppermute(pay, 'cond', swap)  2.41 us
    pallas_call x1, Pallas kernels, bed_middle(): pl.pallas_call(bed_middle_kernel, name='bed_middle', out_shape=[pltpu.HBM...  2.24 us
  transfers between devices with their start and end apart: 9, of which 4 were waited for; matrix products, arithmetic and copies ran while one was open for 0% of the time, Pallas kernels for 44%

profile of v5, /device:TPU:9, one launch (start us, length us, event | category | flops | bytes accessed | tf_op | source)
XLA Modules:
  0.0 39.9 jit_solution(2596468890836243141)
XLA Ops:
  0.6 1.8 %pack_side.1 = f32[72,128]{1,0:T(8,128)S(1)} custom-call(f32[1,4]{1,0:T(1,128)} %params.7, f32[256,1024]{1,0:T(8,128)} %bed.3, s32[256,1024]{1,0:T(8,128)} %mask.3, s32[256,1024]{1,0:T(8,128)} %kind.3, f32[1,2,256,1024]{3,2,1,0:T(8,128)} %stress.11, f32[1,3,256,1024]{3,2,1,0:T(8,128)} %hydro.11), custom_call_target="tpu_custom_call" | custom-call | flops 2000000000 | tf_op jit(solution)/shard_map/pack_side/pallas_call | solution.py:114
  2.4 0.0 copy-start
  2.4 0.0 copy-start.1
  2.4 0.0 copy-start.2
  2.5 1.3 %collective-permute-start = (f32[72,128]{1,0:T(8,128)S(1)}, f32[72,128]{1,0:T(8,128)S(1)}, u32[]{:S(2)}, u32[]{:S(2)}) collective-permute-start(f32[72,128]{1,0:T(8,128)S(1)} %pack_side.1), channel_id=1, source_target_pairs={{0,1},{1,0},{2,3},{3,2},{4,5},{5,4},{6,7},{7,6},{8,9},{9,8},{10,11... | collective-permute-start | bytes 110600 | tf_op jit(solution)/shard_map/ppermute | solution.py:687
  3.8 2.6 %prepare.1 = (f32[256,1024]{1,0:T(8,128)S(1)}, f32[256,1024]{1,0:T(8,128)S(1)}, f32[256,1024]{1,0:T(8,128)S(1)}, f32[256,1024]{1,0:T(8,128)S(1)}, f32[272,128]{1,0:T(8,128)S(1)}, /*index=5*/f32[272,128]{1,0:T(8,128)S(1)}) custom-call(f32[1,4]{1,0:T(1,128)} %params.7, f32[256,1024]{1,0:T(8,128)} %bed.3, s32[256,1024]{1,0:T(8,128)} %mask.3, s32[256,1024]{1,0:T(8,128)} %kind.3, ...), custom_call_target="tpu_custom_call" | custom-call | flops 2000000000 | tf_op jit(solution)/shard_map/prepare/pallas_call | solution.py:203
  6.4 0.1 collective-permute-start.1
  6.5 3.1 %middle_other.1 = (f32[1,3,256,1024]{3,2,1,0:T(8,128)S(1)}, f32[520,128]{1,0:T(8,128)S(1)}) custom-call(s32[4]{0:T(128)S(1)} %copy-done.3, f32[1,4]{1,0:T(1,128)S(1)} %copy-done.2, f32[256,1024]{1,0:T(8,128)S(1)} %get-tuple-element.36.root, f32[256,1024]{1,0:T(8,128)S(1)} %get-tuple-element.37.a, f32[256,1024]{1,0:T(8,128)S(1)} %get-tuple-element.38.b, ...), custom_call_target="tpu_custom_call" | custom-call | flops 4000000000 | tf_op jit(solution)/shard_map/middle_other/pallas_call | solution.py:424
  9.6 1.2 %collective-permute-start.3 = (f32[520,128]{1,0:T(8,128)S(1)}, f32[520,128]{1,0:T(8,128)S(1)}, u32[]{:S(2)}, u32[]{:S(2)}) collective-permute-start(f32[520,128]{1,0:T(8,128)S(1)} %get-tuple-element.49), channel_id=1, source_target_pairs={{0,8},{8,0},{16,24},{24,16},{1,9},{9,1},{17,25},{25,17},{2,10},{10... | collective-permute-start | bytes 798728 | tf_op jit(solution)/shard_map/ppermute | solution.py:695
  10.8 0.1 collective-permute-done.1.far_a
  10.9 4.4 %collective-permute-start.2 = (f32[272,128]{1,0:T(8,128)S(1)}, f32[272,128]{1,0:T(8,128)S(1)}, u32[]{:S(2)}, u32[]{:S(2)}) collective-permute-start(f32[272,128]{1,0:T(8,128)S(1)} %get-tuple-element.45), channel_id=1, source_target_pairs={{2,4},{4,2},{3,5},{5,3},{10,12},{12,10},{11,13},{13,11},{18,20},{2... | collective-permute-start | bytes 417800 | tf_op jit(solution)/shard_map/ppermute | solution.py:694
  15.3 3.1 %middle_own.1 = (f32[1,3,256,1024]{3,2,1,0:T(8,128)S(1)}, f32[520,128]{1,0:T(8,128)S(1)}) custom-call(s32[4]{0:T(128)S(1)} %copy-done.3, f32[1,4]{1,0:T(1,128)S(1)} %copy-done.2, f32[256,1024]{1,0:T(8,128)S(1)} %get-tuple-element.36.root, f32[256,1024]{1,0:T(8,128)S(1)} %get-tuple-element.37.a, ...), custom_call_target="tpu_custom_call", output_to_operand_aliasing={{0}: (8, {})} | custom-call | flops 4000000000 | tf_op jit(solution)/shard_map/middle_own/pallas_call | solution.py:424
  18.5 1.3 %collective-permute-start.4 = (f32[520,128]{1,0:T(8,128)S(1)}, f32[520,128]{1,0:T(8,128)S(1)}, u32[]{:S(2)}, u32[]{:S(2)}) collective-permute-start(f32[520,128]{1,0:T(8,128)S(1)} %add.12), channel_id=1, source_target_pairs={{0,16},{8,24},{16,0},{24,8},{1,17},{9,25},{17,1},{25,9},{2,18},{10... | collective-permute-start | bytes 798728 | tf_op jit(solution)/shard_map/ppermute | solution.py:681
  19.8 3.2 %edge_other.1 = (f32[1,3,256,1024]{3,2,1,0:T(8,128)S(1)}, f32[528,128]{1,0:T(8,128)S(1)}) custom-call(s32[4]{0:T(128)S(1)} %copy-done.3, f32[1,4]{1,0:T(1,128)S(1)} %copy-done.2, f32[256,1024]{1,0:T(8,128)S(1)} %get-tuple-element.36.root, f32[256,1024]{1,0:T(8,128)S(1)} %get-tuple-element.37.a, ...), custom_call_target="tpu_custom_call", output_to_operand_aliasing={{0}: (10, {})} | custom-call | flops 3000000000 | tf_op jit(solution)/shard_map/edge_other/pallas_call | solution.py:495
  23.0 1.2 %collective-permute-start.5 = (f32[528,128]{1,0:T(8,128)S(1)}, f32[528,128]{1,0:T(8,128)S(1)}, u32[]{:S(2)}, u32[]{:S(2)}) collective-permute-start(f32[528,128]{1,0:T(8,128)S(1)} %get-tuple-element.56), channel_id=1, source_target_pairs={{0,8},{8,0},{16,24},{24,16},{1,9},{9,1},{17,25},{25,17},{2,10},{10... | collective-permute-start | bytes 811016 | tf_op jit(solution)/shard_map/ppermute | solution.py:700
  24.2 3.2 %edge_own.1 = (f32[1,3,256,1024]{3,2,1,0:T(8,128)S(1)}, f32[528,128]{1,0:T(8,128)S(1)}) custom-call(s32[4]{0:T(128)S(1)} %copy-done.3, f32[1,4]{1,0:T(1,128)S(1)} %copy-done.2, f32[256,1024]{1,0:T(8,128)S(1)} %get-tuple-element.36.root, f32[256,1024]{1,0:T(8,128)S(1)} %get-tuple-element.37.a, ...), custom_call_target="tpu_custom_call", output_to_operand_aliasing={{0}: (10, {})} | custom-call | flops 3000000000 | tf_op jit(solution)/shard_map/edge_own/pallas_call | solution.py:495
  27.5 0.1 collective-permute-start.6
  27.6 1.2 %collective-permute-start.7 = (f32[528,128]{1,0:T(8,128)S(1)}, f32[528,128]{1,0:T(8,128)S(1)}, u32[]{:S(2)}, u32[]{:S(2)}) collective-permute-start(f32[528,128]{1,0:T(8,128)S(1)} %add.14), channel_id=1, source_target_pairs={{0,16},{8,24},{16,0},{24,8},{1,17},{9,25},{17,1},{25,9},{2,18},{10... | collective-permute-start | bytes 811016 | tf_op jit(solution)/shard_map/ppermute | solution.py:681
  28.8 0.3 collective-permute-done.6.got_m
  29.1 2.2 %bed_middle.1 = (f32[256,1024]{1,0:T(8,128)}, f32[256,1024]{1,0:T(8,128)}, f32[1,3,256,1024]{3,2,1,0:T(8,128)}) custom-call(f32[256,1024]{1,0:T(8,128)S(1)} %get-tuple-element.35.bed, f32[72,128]{1,0:T(8,128)S(1)} %collective-permute-done.side, f32[272,128]{1,0:T(8,128)S(1)} %collective-permute-done.1.far_a, f32[272,128]{1,0:T(8,128)S(1)} %collective-permute-done.2.far_b, ...), custom_call_target="tpu_custom_call" | custom-call | flops 4000000000 | tf_op jit(solution)/shard_map/bed_middle/pallas_call | solution.py:640
  31.3 3.9 %collective-permute-done.7 = f32[528,128]{1,0:T(8,128)S(1)} collective-permute-done((f32[528,128]{1,0:T(8,128)S(1)}, f32[528,128]{1,0:T(8,128)S(1)}, u32[]{:S(2)}, u32[]{:S(2)}) %collective-permute-start.7) | collective-permute-done | bytes 270368 | tf_op jit(solution)/shard_map/ppermute | solution.py:681
  35.3 1.3 %collective-permute-start.8 = (f32[528,128]{1,0:T(8,128)S(1)}, f32[528,128]{1,0:T(8,128)S(1)}, u32[]{:S(2)}, u32[]{:S(2)}) collective-permute-start(f32[528,128]{1,0:T(8,128)S(1)} %add.15.own_e), channel_id=1, source_target_pairs={{0,8},{8,0},{16,24},{24,16},{1,9},{9,1},{17,25},{25,17},{2,10},{10... | collective-permute-start | bytes 811016 | tf_op jit(solution)/shard_map/ppermute | solution.py:708
  36.6 1.2 %collective-permute-done.8.got_e = f32[528,128]{1,0:T(8,128)S(1)} collective-permute-done((f32[528,128]{1,0:T(8,128)S(1)}, f32[528,128]{1,0:T(8,128)S(1)}, u32[]{:S(2)}, u32[]{:S(2)}) %collective-permute-start.8) | collective-permute-done | bytes 270368 | tf_op jit(solution)/shard_map/ppermute | solution.py:708
  37.8 1.9 %bed_edge.1 = (f32[256,1024]{1,0:T(8,128)}, f32[256,1024]{1,0:T(8,128)}) custom-call(f32[256,1024]{1,0:T(8,128)S(1)} %get-tuple-element.35.bed, f32[72,128]{1,0:T(8,128)S(1)} %collective-permute-done.side, f32[272,128]{1,0:T(8,128)S(1)} %collective-permute-done.1.far_a, ...), custom_call_target="tpu_custom_call", output_to_operand_aliasing={{0}: (8, {}), {1}: (9, {})} | custom-call | flops 2000000000 | tf_op jit(solution)/shard_map/bed_edge/pallas_call | solution.py:653
  (15 shorter events, 0.2 us)
Async XLA Ops:
  2.4 4.1 %copy-start = (f32[1,3,256,1024]{3,2,1,0:T(8,128)S(1)}, f32[1,3,256,1024]{3,2,1,0:T(8,128)}, u32[]{:S(2)}) copy-start(f32[1,3,256,1024]{3,2,1,0:T(8,128)} %hydro.11) | copy-start | bytes 9437188
  2.4 4.1 %copy-start.1 = (f32[1,2,256,1024]{3,2,1,0:T(8,128)S(1)}, f32[1,2,256,1024]{3,2,1,0:T(8,128)}, u32[]{:S(2)}) copy-start(f32[1,2,256,1024]{3,2,1,0:T(8,128)} %stress.11) | copy-start | bytes 6291460
  2.4 4.1 %copy-start.2 = (f32[1,4]{1,0:T(1,128)S(1)}, f32[1,4]{1,0:T(1,128)}, u32[]{:S(2)}) copy-start(f32[1,4]{1,0:T(1,128)} %params.7) | copy-start | bytes 52
  2.4 4.1 %copy-start.3 = (s32[4]{0:T(128)S(1)}, s32[4]{0:T(128)}, u32[]{:S(2)}) copy-start(s32[4]{0:T(128)} %weights.7) | copy-start | bytes 52
  2.5 3.9 %collective-permute-start = (f32[72,128]{1,0:T(8,128)S(1)}, f32[72,128]{1,0:T(8,128)S(1)}, u32[]{:S(2)}, u32[]{:S(2)}) collective-permute-start(f32[72,128]{1,0:T(8,128)S(1)} %pack_side.1), channel_id=1, source_target_pairs={{0,1},{1,0},{2,3},{3,2},{4,5},{5,4},{6,7},{7,6},{8,9},{9,8},{10,11... | collective-permute-start | bytes 110600 | tf_op jit(solution)/shard_map/ppermute | solution.py:687
  6.4 4.6 %collective-permute-start.1 = (f32[272,128]{1,0:T(8,128)S(1)}, f32[272,128]{1,0:T(8,128)S(1)}, u32[]{:S(2)}, u32[]{:S(2)}) collective-permute-start(f32[272,128]{1,0:T(8,128)S(1)} %get-tuple-element.42), channel_id=1, source_target_pairs={{0,2},{2,0},{4,6},{6,4},{1,3},{3,1},{5,7},{7,5},{8,10},{10,8},{12,... | collective-permute-start | bytes 417800 | tf_op jit(solution)/shard_map/ppermute | solution.py:691
  9.6 8.8 %collective-permute-start.3 = (f32[520,128]{1,0:T(8,128)S(1)}, f32[520,128]{1,0:T(8,128)S(1)}, u32[]{:S(2)}, u32[]{:S(2)}) collective-permute-start(f32[520,128]{1,0:T(8,128)S(1)} %get-tuple-element.49), channel_id=1, source_target_pairs={{0,8},{8,0},{16,24},{24,16},{1,9},{9,1},{17,25},{25,17},{2,10},{10... | collective-permute-start | bytes 798728 | tf_op jit(solution)/shard_map/ppermute | solution.py:695
  10.9 8.8 %collective-permute-start.2 = (f32[272,128]{1,0:T(8,128)S(1)}, f32[272,128]{1,0:T(8,128)S(1)}, u32[]{:S(2)}, u32[]{:S(2)}) collective-permute-start(f32[272,128]{1,0:T(8,128)S(1)} %get-tuple-element.45), channel_id=1, source_target_pairs={{2,4},{4,2},{3,5},{5,3},{10,12},{12,10},{11,13},{13,11},{18,20},{2... | collective-permute-start | bytes 417800 | tf_op jit(solution)/shard_map/ppermute | solution.py:694
  18.5 8.9 %collective-permute-start.4 = (f32[520,128]{1,0:T(8,128)S(1)}, f32[520,128]{1,0:T(8,128)S(1)}, u32[]{:S(2)}, u32[]{:S(2)}) collective-permute-start(f32[520,128]{1,0:T(8,128)S(1)} %add.12), channel_id=1, source_target_pairs={{0,16},{8,24},{16,0},{24,8},{1,17},{9,25},{17,1},{25,9},{2,18},{10... | collective-permute-start | bytes 798728 | tf_op jit(solution)/shard_map/ppermute | solution.py:681
  23.0 4.4 %collective-permute-start.5 = (f32[528,128]{1,0:T(8,128)S(1)}, f32[528,128]{1,0:T(8,128)S(1)}, u32[]{:S(2)}, u32[]{:S(2)}) collective-permute-start(f32[528,128]{1,0:T(8,128)S(1)} %get-tuple-element.56), channel_id=1, source_target_pairs={{0,8},{8,0},{16,24},{24,16},{1,9},{9,1},{17,25},{25,17},{2,10},{10... | collective-permute-start | bytes 811016 | tf_op jit(solution)/shard_map/ppermute | solution.py:700
  27.5 1.6 %collective-permute-start.6 = (f32[520,128]{1,0:T(8,128)S(1)}, f32[520,128]{1,0:T(8,128)S(1)}, u32[]{:S(2)}, u32[]{:S(2)}) collective-permute-start(f32[520,128]{1,0:T(8,128)S(1)} %add.13.own_m), channel_id=1, source_target_pairs={{0,8},{8,0},{16,24},{24,16},{1,9},{9,1},{17,25},{25,17},{2,10},{10... | collective-permute-start | bytes 798728 | tf_op jit(solution)/shard_map/ppermute | solution.py:705
  27.6 7.7 %collective-permute-start.7 = (f32[528,128]{1,0:T(8,128)S(1)}, f32[528,128]{1,0:T(8,128)S(1)}, u32[]{:S(2)}, u32[]{:S(2)}) collective-permute-start(f32[528,128]{1,0:T(8,128)S(1)} %add.14), channel_id=1, source_target_pairs={{0,16},{8,24},{16,0},{24,8},{1,17},{9,25},{17,1},{25,9},{2,18},{10... | collective-permute-start | bytes 811016 | tf_op jit(solution)/shard_map/ppermute | solution.py:681
  35.3 2.5 %collective-permute-start.8 = (f32[528,128]{1,0:T(8,128)S(1)}, f32[528,128]{1,0:T(8,128)S(1)}, u32[]{:S(2)}, u32[]{:S(2)}) collective-permute-start(f32[528,128]{1,0:T(8,128)S(1)} %add.15.own_e), channel_id=1, source_target_pairs={{0,8},{8,0},{16,24},{24,16},{1,9},{9,1},{17,25},{25,17},{2,10},{10... | collective-permute-start | bytes 811016 | tf_op jit(solution)/shard_map/ppermute | solution.py:708

commit v6 on v5

--- a/solution.py
+++ b/solution.py
@@ -182,8 +182,8 @@
             top, bottom = pairs[0][:, part], pairs[1][:, part]
             pay_a[at, :] = jnp.where(odd, top, bottom)
             pay_b[at, :] = jnp.where(odd, bottom, top)
-    top = fold_row(bed_v[tile_at(0), :])
-    bottom = fold_row(pltpu.roll(bed_v[tile_at(rows // SUB - 1), :], 1, 0))
+    top = fold_row([bed_v[tile_at(0), lanes_at(k)] for k in range(lanes)])
+    bottom = fold_row([pltpu.roll(bed_v[tile_at(rows // SUB - 1), lanes_at(k)], 1, 0) for k in range(lanes)])
     at = pl.ds(lanes * GROUP + SUB, SUB)
     pay_a[at, :] = jnp.where(odd, top, bottom)
     pay_b[at, :] = jnp.where(odd, bottom, top)
@@ -191,9 +191,9 @@
 
 def fold_row(x):
     row = rows_of((SUB, LANE))
-    total = x[:, :LANE]
-    for k in range(1, x.shape[1] // LANE):
-        total = jnp.where(row == k, pltpu.roll(x[:, k * LANE : (k + 1) * LANE], k, 0), total)
+    total = x[0]
+    for k in range(1, len(x)):
+        total = jnp.where(row == k, pltpu.roll(x[k], k, 0), total)
     return total
 
 
@@ -259,8 +259,8 @@
         + ["v1", "e2", "u2", "v2", "qc1", "qr1", "qc2", "qr2"]
     )
 
-    def __init__(self, count, wide, get, emit, weights, params, refs, trim):
-        self.count, self.wide, self.get, self.emit, self.trim = count, wide, get, emit, trim
+    def __init__(self, count, tiles, get, emit, weights, params, refs, trim):
+        self.count, self.tiles, self.get, self.emit, self.trim = count, tiles, get, emit, trim
         self.__dict__.update(zip(self.NAMES + ["fr_last", "qr_last"], refs))
         cond = lax.axis_index("cond")
         self.slow = 1.0 - 0.2 * params[0, 1]
@@ -269,100 +269,150 @@
             total = total + weights[k]
         ones = jnp.ones((SUB, LANE), jnp.float32)
         share = weights[cond].astype(jnp.float32) * ones / (total.astype(jnp.float32) * ones)
-        self.scale = jnp.concatenate([-4.0 * params[0, 2] * share] * (wide // LANE), axis=1)
+        self.scale = -4.0 * params[0, 2] * share
+        lane, row = lanes_of((SUB, LANE)), rows_of((SUB, LANE))
+        self.last_lane, self.first_lane = lane == LANE - 1, lane == 0
+        self.last_row, self.first_row = row == SUB - 1, row == 0
 
     @classmethod
-    def scratch(cls, count, wide):
-        block = pltpu.VMEM(((count + 1) * SUB, wide), jnp.float32)
+    def scratch(cls, count, tiles):
+        block = pltpu.VMEM((tiles, (count + 1) * SUB, LANE), jnp.float32)
         return [block] * len(cls.NAMES) + [
-            pltpu.VMEM((STEPS, SUB, wide), jnp.float32),
-            pltpu.VMEM((SUB, wide), jnp.float32),
+            pltpu.VMEM((STEPS, tiles, SUB, LANE), jnp.float32),
+            pltpu.VMEM((tiles, SUB, LANE), jnp.float32),
         ]
 
-    def speed_c(self, i, level, u, wc):
-        return (self.slow * u - (east(level) - level) + self.get(3, i)) * wc
-
-    def speed_r(self, i, level, lower, v, wr):
-        return (self.slow * v - (south(level, lower) - level) + self.get(4, i)) * wr
-
-    def move(self, n, i, level, lower, u, v, fc, fr, wc, wr):
-        u = self.speed_c(i, level, u, wc)
-        v = self.speed_r(i, level, lower, v, wr)
-        flux_c = fc * u
-        flux_r = fr * v
-        out = self.get(1, i) * level + self.get(2, i) - (
-            flux_c - west(flux_c) + flux_r - north(flux_r, self.fr_last[n])
-        )
-        self.fr_last[n] = flux_r
-        return out, u, v
+    def south(self, x, below):
+        return pltpu.roll(jnp.where(self.first_row, below, x), SUB - 1, 0)
+
+    def north(self, x, above):
+        return pltpu.roll(jnp.where(self.last_row, above, x), 1, 0)
+
+    def easts(self, values):
+        first = value = values(0)
+        first_rolled = rolled = pltpu.roll(first, LANE - 1, 1)
+        for k in range(self.tiles):
+            if k + 1 < self.tiles:
+                after = values(k + 1)
+                after_rolled = pltpu.roll(after, LANE - 1, 1)
+            else:
+                after, after_rolled = first, first_rolled
+            yield k, value, jnp.where(self.last_lane, after_rolled, rolled)
+            value, rolled = after, after_rolled
+
+    def wests(self, values):
+        before = pltpu.roll(values[-1], 1, 1)
+        for k, value in enumerate(values):
+            rolled = pltpu.roll(value, 1, 1)
+            yield k, value, jnp.where(self.first_lane, before, rolled)
+            before = rolled
+
+    def move(self, n, i, level, lower, speeds, faces, wets, keep):
+        flux, part = [], []
+        for k, here, right in self.easts(level):
+            wc, wr = wets(k)
+            fc, fr = faces(k)
+            u, v = speeds(k)
+            u = (self.slow * u - (right - here) + self.get(3, i, k)) * wc
+            v = (self.slow * v - (self.south(here, lower(k)) - here) + self.get(4, i, k)) * wr
+            flux_r = fr * v
+            part.append(
+                self.get(1, i, k) * here + self.get(2, i, k) - flux_r + self.north(flux_r, self.fr_last[n, k])
+            )
+            self.fr_last[n, k] = flux_r
+            flux.append(fc * u)
+            keep(k, u, v)
+        for k, value, left in self.wests(flux):
+            yield k, part[k] - value + left
 
     def step_one(self, i):
         at = tile_at(i)
-        s = self.get(0, i)
-        level = 0.3 * self.get(5, i)
         inside = i + 1 < self.count
-        face_c = s * east(s)
-        face_r = s * south(s, self.get(0, i + 1) if inside else s)
-        ratios = []
-        for face in (face_c, face_r):
-            base = face + 0.1
-            inverse = pl.reciprocal(base, approx=True)
-            ratios.append(face * (inverse * (2.0 - base * inverse)))
-        wc, wr = ratios
-        fc = 0.3 * face_c
-        fr = 0.3 * face_r
-        self.fc[at, :] = fc
-        self.fr[at, :] = fr
-        self.wc[at, :] = wc
-        self.wr[at, :] = wr
-        lower = 0.3 * self.get(5, i + 1) if inside else level
-        e, u, v = self.move(0, i, level, lower, self.get(6, i), self.get(7, i), fc, fr, wc, wr)
-        self.e1[at, :] = e
-        self.u1[at, :] = u
-        self.v1[at, :] = v
-        self.qc1[at, :] = u * jnp.abs(u)
-        self.qr1[at, :] = v * jnp.abs(v)
+        for k, s, right in self.easts(lambda k: self.get(0, i, k)):
+            below = self.get(0, i + 1, k) if inside else s
+            for other, face_ref, wet_ref in ((right, self.fc, self.wc), (self.south(s, below), self.fr, self.wr)):
+                face = s * other
+                base = face + 0.1
+                inverse = pl.reciprocal(base, approx=True)
+                wet_ref[k, at, :] = face * (inverse * (2.0 - base * inverse))
+                face_ref[k, at, :] = 0.3 * face
+
+        def level(k):
+            return 0.3 * self.get(5, i, k)
+
+        def lower(k):
+            return 0.3 * self.get(5, i + 1 if inside else i, k)
+
+        def keep(k, u, v):
+            self.u1[k, at, :] = u
+            self.v1[k, at, :] = v
+            self.qc1[k, at, :] = u * jnp.abs(u)
+            self.qr1[k, at, :] = v * jnp.abs(v)
+
+        speeds = lambda k: (self.get(6, i, k), self.get(7, i, k))
+        for k, e in self.move(0, i, level, lower, speeds, self.faces(at), self.wets(at), keep):
+            self.e1[k, at, :] = e
+
+    def faces(self, at):
+        return lambda k: (self.fc[k, at, :], self.fr[k, at, :])
+
+    def wets(self, at):
+        return lambda k: (self.wc[k, at, :], self.wr[k, at, :])
+
+    def later(self, n, i, e, u, v, keep):
+        at, after = tile_at(i), tile_at(i + 1)
+        return self.move(
+            n, i, lambda k: e[k, at, :], lambda k: e[k, after, :], lambda k: (u[k, at, :], v[k, at, :]),
+            self.faces(at), self.wets(at), keep,
+        )
 
     def step_two(self, i):
-        at, after = tile_at(i), tile_at(i + 1)
-        e, u, v = self.move(
-            1, i, self.e1[at, :], self.e1[after, :], self.u1[at, :], self.v1[at, :],
-            self.fc[at, :], self.fr[at, :], self.wc[at, :], self.wr[at, :],
-        )
-        self.e2[at, :] = e
-        if self.trim and i == self.count - 1:
-            return
-        self.u2[at, :] = u
-        self.v2[at, :] = v
-        self.qc2[at, :] = self.qc1[at, :] + u * jnp.abs(u)
-        self.qr2[at, :] = self.qr1[at, :] + v * jnp.abs(v)
+        at = tile_at(i)
+        last = self.trim and i == self.count - 1
+
+        def keep(k, u, v):
+            if not last:
+                self.u2[k, at, :] = u
+                self.v2[k, at, :] = v
+                self.qc2[k, at, :] = self.qc1[k, at, :] + u * jnp.abs(u)
+                self.qr2[k, at, :] = self.qr1[k, at, :] + v * jnp.abs(v)
+
+        for k, e in self.later(1, i, self.e1, self.u1, self.v1, keep):
+            self.e2[k, at, :] = e
 
     def step_three(self, i):
         at, after = tile_at(i), tile_at(i + 1)
         if self.trim and i == self.count - 1:
             return
         if self.trim and i == 0:
-            wr = self.wr[at, :]
-            v = self.speed_r(i, self.e2[at, :], self.e2[after, :], self.v2[at, :], wr)
-            self.fr_last[2] = self.fr[at, :] * v
-            self.qr_last[...] = wr * (self.qr2[at, :] + v * jnp.abs(v))
+            for k in range(self.tiles):
+                here, wr = self.e2[k, at, :], self.wr[k, at, :]
+                lower = self.e2[k, after, :]
+                v = (self.slow * self.v2[k, at, :] - (self.south(here, lower) - here) + self.get(4, i, k)) * wr
+                self.fr_last[2, k] = self.fr[k, at, :] * v
+                self.qr_last[k] = wr * (self.qr2[k, at, :] + v * jnp.abs(v))
             return
-        wc, wr = self.wc[at, :], self.wr[at, :]
-        e, u, v = self.move(
-            2, i, self.e2[at, :], self.e2[after, :], self.u2[at, :], self.v2[at, :],
-            self.fc[at, :], self.fr[at, :], wc, wr,
-        )
-        qc = wc * (self.qc2[at, :] + u * jnp.abs(u))
-        qr = wr * (self.qr2[at, :] + v * jnp.abs(v))
-        change = (qc - west(qc) + qr - north(qr, self.qr_last[...])) * self.scale
-        self.qr_last[...] = qr
-        self.emit(i, e * (1.0 / 0.3), u, v, change)
+        qcs, parts = [], []
+
+        def keep(k, u, v):
+            wc, wr = self.wets(at)(k)
+            self.emit(i, 1, k, u)
+            self.emit(i, 2, k, v)
+            qr = wr * (self.qr2[k, at, :] + v * jnp.abs(v))
+            qcs.append(wc * (self.qc2[k, at, :] + u * jnp.abs(u)))
+            parts.append(qr - self.north(qr, self.qr_last[k]))
+            self.qr_last[k] = qr
+
+        for k, e in self.later(2, i, self.e2, self.u2, self.v2, keep):
+            self.emit(i, 0, k, e * (1.0 / 0.3))
+        for k, qc, left in self.wests(qcs):
+            self.emit(i, 3, k, (qc - left + parts[k]) * self.scale)
 
     def run(self):
         self.fr_last[...] = jnp.zeros_like(self.fr_last)
         self.qr_last[...] = jnp.zeros_like(self.qr_last)
         for ref in (self.e1, self.e2):
-            ref[tile_at(self.count), :] = jnp.zeros((SUB, self.wide), jnp.float32)
+            ref[:, tile_at(self.count), :] = jnp.zeros((self.tiles, SUB, LANE), jnp.float32)
         stages = (self.step_three, self.step_two, self.step_one)
         for t in range(self.count + LAG * (STEPS - 1)):
             for k, stage in enumerate(stages):
@@ -371,35 +421,41 @@
                     stage(i)
 
 
+def lanes_at(k):
+    return slice(k * LANE, (k + 1) * LANE)
+
+
 def reader(root, a, b, stress, hydro, side, unfold, valid):
-    rows = root.shape[0]
+    rows, cols = root.shape
     span = rows // FOLD // SUB
+    tiles = cols // LANE
     fields = [root, a, b] + moving(stress, hydro)
 
-    def read(f, block):
+    def read(f, block, k):
+        if k < tiles:
+            return fields[f][tile_at(block), lanes_at(k)]
         part = unfold(side[tile_at(block % span), :], (block // span) * FIELDS + f)
-        if f == 0:
-            part = jnp.where(valid, part, 0.0)
-        return jnp.concatenate([fields[f][tile_at(block), :], part], axis=1)
+        return jnp.where(valid, part, 0.0) if f == 0 else part
 
     return read
 
 
 def quarter_writer(first, quarter, cols, hydro_out, pay):
     lane = lanes_of((SUB, LANE))
-    lanes = cols // LANE
+    tiles = cols // LANE
     rims = [jnp.zeros((SUB, LANE), jnp.float32)]
 
-    def emit(i, e, u, v, change):
-        at = tile_at(first + i)
-        for k, value in enumerate((e, u, v)):
-            hydro_out[0, k, at, :] = value[:, :cols]
+    def emit(i, what, k, value):
         g = i - 1
-        for k in range(lanes):
-            pay[tile_at(k * quarter + g), :] = change[:, k * LANE : (k + 1) * LANE]
-        rims[0] = jnp.where(lane // 2 == g, pltpu.roll(change[:, cols:], 1 + 2 * g, 1), rims[0])
-        if g == quarter - 1:
-            pay[tile_at(lanes * quarter), :] = rims[0]
+        if what < 3:
+            if k < tiles:
+                hydro_out[0, what, tile_at(first + i), lanes_at(k)] = value
+        elif k < tiles:
+            pay[tile_at(k * quarter + g), :] = value
+        else:
+            rims[0] = jnp.where(lane // 2 == g, pltpu.roll(value, 1 + 2 * g, 1), rims[0])
+            if g == quarter - 1:
+                pay[tile_at(tiles * quarter), :] = rims[0]
 
     return emit
 
@@ -414,7 +470,7 @@
     first = jnp.where(lower_half, 2 * quarter, quarter) - 1
     emit = quarter_writer(first, quarter, cols, hydro_out, pay)
     Sweep(
-        quarter + 2, cols + LANE, lambda f, i: read(f, first + i), emit, weights, params, refs, True
+        quarter + 2, cols // LANE + 1, lambda f, i, k: read(f, first + i, k), emit, weights, params, refs, True
     ).run()
 
 
@@ -430,7 +486,7 @@
         ],
         in_specs=[SMEM, SMEM] + [VMEM] * (6 + own),
         out_specs=[VMEM, VMEM],
-        scratch_shapes=Sweep.scratch(rows // SUB // 4 + 2, cols + LANE),
+        scratch_shapes=Sweep.scratch(rows // SUB // 4 + 2, cols // LANE + 1),
         input_output_aliases={8: 0} if own else {},
         compiler_params=pltpu.CompilerParams(vmem_limit_bytes=10 * MIB),
         cost_estimate=cost(4),
@@ -455,43 +511,43 @@
     inner = jnp.where(top, quarter, blocks - quarter - 1)
     corners = pl.ds(lanes * GROUP, SUB)
     for f in range(FIELDS):
-        body = read(f, inner)
-        parts = []
-        for k in range(lanes):
-            at = pl.ds(k * GROUP + f // 2 * SUB, SUB)
-            part = jnp.where(from_a, far_a[at, :], far_b[at, :])
-            moved = pltpu.roll(part, HALO, 0)
-            parts.append(jnp.where(top, moved, part) if f % 2 == 0 else jnp.where(top, part, moved))
-        corner = jnp.where(from_a, far_a[corners, :], far_b[corners, :])
-        corner = jnp.where(top, unfold(corner, (FOLD - 1) * FIELDS + f), unfold(corner, f))
-        if f == 0:
-            corner = jnp.where(valid, corner, 0.0)
-        outer = jnp.concatenate(parts + [corner], axis=1)
-        ends[0, f] = jnp.where(top, outer, body)
-        ends[1, f] = jnp.where(top, body, outer)
-
-    def get(f, i):
+        for k in range(lanes + 1):
+            body = read(f, inner, k)
+            if k < lanes:
+                at = pl.ds(k * GROUP + f // 2 * SUB, SUB)
+                part = jnp.where(from_a, far_a[at, :], far_b[at, :])
+                moved = pltpu.roll(part, HALO, 0)
+                outer = jnp.where(top, moved, part) if f % 2 == 0 else jnp.where(top, part, moved)
+            else:
+                corner = jnp.where(from_a, far_a[corners, :], far_b[corners, :])
+                outer = jnp.where(top, unfold(corner, (FOLD - 1) * FIELDS + f), unfold(corner, f))
+                if f == 0:
+                    outer = jnp.where(valid, outer, 0.0)
+            ends[0, f, k] = jnp.where(top, outer, body)
+            ends[1, f, k] = jnp.where(top, body, outer)
+
+    def get(f, i, k):
         if i == 0 or i == quarter + 1:
-            return ends[0 if i == 0 else 1, f]
-        return read(f, first + i)
+            return ends[0 if i == 0 else 1, f, k]
+        return read(f, first + i, k)
 
     emit = quarter_writer(first, quarter, cols, hydro_out, pay)
-    outside = []
-
-    def finish(i, e, u, v, change):
-        if i == 0:
-            outside.append(pltpu.roll(change[:, :cols], 1, 0))
-        elif i == quarter + 1:
-            pay[tile_at(lanes * quarter + 1), :] = fold_row(jnp.where(top, outside[0], change[:, :cols]))
-        else:
-            emit(i, e, u, v, change)
-
-    Sweep(quarter + 2, cols + LANE, get, finish, weights, params, refs, False).run()
+    outside = {0: [], quarter + 1: []}
+
+    def finish(i, what, k, value):
+        if i not in outside:
+            emit(i, what, k, value)
+        elif what == 3 and k < lanes:
+            outside[i].append(value)
+            if i and k == lanes - 1:
+                rim = [jnp.where(top, pltpu.roll(x, 1, 0), y) for x, y in zip(outside[0], outside[i])]
+                pay[tile_at(lanes * quarter + 1), :] = fold_row(rim)
+
+    Sweep(quarter + 2, lanes + 1, get, finish, weights, params, refs, False).run()
 
 
 def edge(own, weights, params, fields, side, far_a, far_b, hydro):
     rows, cols = fields[0].shape
-    wide = cols + LANE
     return pl.pallas_call(
         functools.partial(edge_kernel, own),
         name="edge_own" if own else "edge_other",
@@ -501,8 +557,8 @@
         ],
         in_specs=[SMEM, SMEM] + [VMEM] * 9,
         out_specs=[VMEM, VMEM],
-        scratch_shapes=[pltpu.VMEM((2, FIELDS, SUB, wide), jnp.float32)]
-        + Sweep.scratch(rows // SUB // 4 + 2, wide),
+        scratch_shapes=[pltpu.VMEM((2, FIELDS, cols // LANE + 1, SUB, LANE), jnp.float32)]
+        + Sweep.scratch(rows // SUB // 4 + 2, cols // LANE + 1),
         input_output_aliases={10: 0},
         compiler_params=pltpu.CompilerParams(vmem_limit_bytes=12 * MIB),
         cost_estimate=cost(3),

time: 40.1 us -> 41 us (1.022)
  Pallas kernels: 21.1 us -> 22.4 us
  starting transfers between devices: 12.1 us -> 11.5 us
    pallas_call x2, Pallas kernels: 6.35 us -> 7 us  [edge(): pl.pallas_call(functools.partial(edge_kernel, own), name='edge_own' if ow...]
    pallas_call x2, Pallas kernels: 6.22 us -> 6.83 us  [middle(): pl.pallas_call(functools.partial(middle_kernel, own), name='middle_own' i...]
  transfers between devices with their start and end apart: 9 -> 9, of which waited for: 4 -> 3; matrix products, arithmetic and copies ran while one was open for 0% -> 0% of each run, Pallas kernels for 44% -> 46%
where the time goes in v6:
time: 41 us; the launch traced here: 40.9 us
  Pallas kernels  22.4 us (55%)
  starting transfers between devices  11.5 us (28%)
  waiting for transfers between devices  5.76 us (14%)
  between operations  0.98 us (2%)
    pallas_call x2, Pallas kernels, edge(): pl.pallas_call(functools.partial(edge_kernel, own), name='edge_own' if ow...  7 us
    pallas_call x2, Pallas kernels, middle(): pl.pallas_call(functools.partial(middle_kernel, own), name='middle_own' i...  6.83 us
    ppermute x1, starting transfers between devices, shards(): far_b = lax.ppermute(far_b, 'ty', pairs(1))  4.5 us
    ppermute x2, waiting for transfers between devices, over_chips(): got = lax.ppermute(part, 'cond', [(i, i ^ reach) for i in range(nc)])  3.92 us
    pallas_call x1, Pallas kernels, prepare(): pl.pallas_call(prepare_kernel, name='prepare', out_shape=[tile] * 4 + [pl...  2.58 us
    pallas_call x1, Pallas kernels, bed_middle(): pl.pallas_call(bed_middle_kernel, name='bed_middle', out_shape=[pltpu.HBM...  2.24 us
    ppermute x2, starting transfers between devices, over_chips(): got = lax.ppermute(part, 'cond', [(i, i ^ reach) for i in range(nc)])  2.14 us
    ppermute x2, starting transfers between devices, shards(): got = lax.ppermute(pay, 'cond', swap)  2.11 us
  transfers between devices with their start and end apart: 9, of which 3 were waited for; matrix products, arithmetic and copies ran while one was open for 0% of the time, Pallas kernels for 46%

profile of v6, /device:TPU:9, one launch (start us, length us, event | category | flops | bytes accessed | tf_op | source)
XLA Modules:
  0.0 40.9 jit_solution(6190815105480124475)
XLA Ops:
  0.6 1.8 %pack_side.1 = f32[72,128]{1,0:T(8,128)S(1)} custom-call(f32[1,4]{1,0:T(1,128)} %params.7, f32[256,1024]{1,0:T(8,128)} %bed.3, s32[256,1024]{1,0:T(8,128)} %mask.3, s32[256,1024]{1,0:T(8,128)} %kind.3, f32[1,2,256,1024]{3,2,1,0:T(8,128)} %stress.11, f32[1,3,256,1024]{3,2,1,0:T(8,128)} %hydro.11), custom_call_target="tpu_custom_call" | custom-call | flops 2000000000 | tf_op jit(solution)/shard_map/pack_side/pallas_call | solution.py:114
  2.4 0.0 copy-start
  2.4 0.0 copy-start.1
  2.4 0.0 copy-start.2
  2.4 0.0 copy-start.3
  2.5 1.3 %collective-permute-start = (f32[72,128]{1,0:T(8,128)S(1)}, f32[72,128]{1,0:T(8,128)S(1)}, u32[]{:S(2)}, u32[]{:S(2)}) collective-permute-start(f32[72,128]{1,0:T(8,128)S(1)} %pack_side.1), channel_id=1, source_target_pairs={{0,1},{1,0},{2,3},{3,2},{4,5},{5,4},{6,7},{7,6},{8,9},{9,8},{10,11... | collective-permute-start | bytes 110600 | tf_op jit(solution)/shard_map/ppermute | solution.py:743
  3.8 2.6 %prepare.1 = (f32[256,1024]{1,0:T(8,128)S(1)}, f32[256,1024]{1,0:T(8,128)S(1)}, f32[256,1024]{1,0:T(8,128)S(1)}, f32[256,1024]{1,0:T(8,128)S(1)}, f32[272,128]{1,0:T(8,128)S(1)}, /*index=5*/f32[272,128]{1,0:T(8,128)S(1)}) custom-call(f32[1,4]{1,0:T(1,128)} %params.7, f32[256,1024]{1,0:T(8,128)} %bed.3, s32[256,1024]{1,0:T(8,128)} %mask.3, s32[256,1024]{1,0:T(8,128)} %kind.3, ...), custom_call_target="tpu_custom_call" | custom-call | flops 2000000000 | tf_op jit(solution)/shard_map/prepare/pallas_call | solution.py:203
  6.4 0.1 collective-permute-start.1
  6.5 3.4 %middle_other.1 = (f32[1,3,256,1024]{3,2,1,0:T(8,128)S(1)}, f32[520,128]{1,0:T(8,128)S(1)}) custom-call(s32[4]{0:T(128)S(1)} %copy-done.3, f32[1,4]{1,0:T(1,128)S(1)} %copy-done.2, f32[256,1024]{1,0:T(8,128)S(1)} %get-tuple-element.36.root, f32[256,1024]{1,0:T(8,128)S(1)} %get-tuple-element.37.a, f32[256,1024]{1,0:T(8,128)S(1)} %get-tuple-element.38.b, ...), custom_call_target="tpu_custom_call" | custom-call | flops 4000000000 | tf_op jit(solution)/shard_map/middle_other/pallas_call | solution.py:480
  9.9 1.2 %collective-permute-start.3 = (f32[520,128]{1,0:T(8,128)S(1)}, f32[520,128]{1,0:T(8,128)S(1)}, u32[]{:S(2)}, u32[]{:S(2)}) collective-permute-start(f32[520,128]{1,0:T(8,128)S(1)} %get-tuple-element.49), channel_id=1, source_target_pairs={{0,8},{8,0},{16,24},{24,16},{1,9},{9,1},{17,25},{25,17},{2,10},{10... | collective-permute-start | bytes 798728 | tf_op jit(solution)/shard_map/ppermute | solution.py:751
  11.1 4.5 %collective-permute-start.2 = (f32[272,128]{1,0:T(8,128)S(1)}, f32[272,128]{1,0:T(8,128)S(1)}, u32[]{:S(2)}, u32[]{:S(2)}) collective-permute-start(f32[272,128]{1,0:T(8,128)S(1)} %get-tuple-element.45), channel_id=1, source_target_pairs={{2,4},{4,2},{3,5},{5,3},{10,12},{12,10},{11,13},{13,11},{18,20},{2... | collective-permute-start | bytes 417800 | tf_op jit(solution)/shard_map/ppermute | solution.py:750
  15.6 3.4 %middle_own.1 = (f32[1,3,256,1024]{3,2,1,0:T(8,128)S(1)}, f32[520,128]{1,0:T(8,128)S(1)}) custom-call(s32[4]{0:T(128)S(1)} %copy-done.3, f32[1,4]{1,0:T(1,128)S(1)} %copy-done.2, f32[256,1024]{1,0:T(8,128)S(1)} %get-tuple-element.36.root, f32[256,1024]{1,0:T(8,128)S(1)} %get-tuple-element.37.a, ...), custom_call_target="tpu_custom_call", output_to_operand_aliasing={{0}: (8, {})} | custom-call | flops 4000000000 | tf_op jit(solution)/shard_map/middle_own/pallas_call | solution.py:480
  19.1 1.3 %collective-permute-start.4 = (f32[520,128]{1,0:T(8,128)S(1)}, f32[520,128]{1,0:T(8,128)S(1)}, u32[]{:S(2)}, u32[]{:S(2)}) collective-permute-start(f32[520,128]{1,0:T(8,128)S(1)} %add.12), channel_id=1, source_target_pairs={{0,16},{8,24},{16,0},{24,8},{1,17},{9,25},{17,1},{25,9},{2,18},{10... | collective-permute-start | bytes 798728 | tf_op jit(solution)/shard_map/ppermute | solution.py:737
  20.4 3.5 %edge_other.1 = (f32[1,3,256,1024]{3,2,1,0:T(8,128)S(1)}, f32[528,128]{1,0:T(8,128)S(1)}) custom-call(s32[4]{0:T(128)S(1)} %copy-done.3, f32[1,4]{1,0:T(1,128)S(1)} %copy-done.2, f32[256,1024]{1,0:T(8,128)S(1)} %get-tuple-element.36.root, f32[256,1024]{1,0:T(8,128)S(1)} %get-tuple-element.37.a, ...), custom_call_target="tpu_custom_call", output_to_operand_aliasing={{0}: (10, {})} | custom-call | flops 3000000000 | tf_op jit(solution)/shard_map/edge_other/pallas_call | solution.py:551
  23.9 0.9 %collective-permute-start.5 = (f32[528,128]{1,0:T(8,128)S(1)}, f32[528,128]{1,0:T(8,128)S(1)}, u32[]{:S(2)}, u32[]{:S(2)}) collective-permute-start(f32[528,128]{1,0:T(8,128)S(1)} %get-tuple-element.56), channel_id=1, source_target_pairs={{0,8},{8,0},{16,24},{24,16},{1,9},{9,1},{17,25},{25,17},{2,10},{10... | collective-permute-start | bytes 811016 | tf_op jit(solution)/shard_map/ppermute | solution.py:756
  24.8 3.5 %edge_own.1 = (f32[1,3,256,1024]{3,2,1,0:T(8,128)S(1)}, f32[528,128]{1,0:T(8,128)S(1)}) custom-call(s32[4]{0:T(128)S(1)} %copy-done.3, f32[1,4]{1,0:T(1,128)S(1)} %copy-done.2, f32[256,1024]{1,0:T(8,128)S(1)} %get-tuple-element.36.root, f32[256,1024]{1,0:T(8,128)S(1)} %get-tuple-element.37.a, ...), custom_call_target="tpu_custom_call", output_to_operand_aliasing={{0}: (10, {})} | custom-call | flops 3000000000 | tf_op jit(solution)/shard_map/edge_own/pallas_call | solution.py:551
  28.4 0.1 collective-permute-start.6
  28.5 0.9 %collective-permute-start.7 = (f32[528,128]{1,0:T(8,128)S(1)}, f32[528,128]{1,0:T(8,128)S(1)}, u32[]{:S(2)}, u32[]{:S(2)}) collective-permute-start(f32[528,128]{1,0:T(8,128)S(1)} %add.14), channel_id=1, source_target_pairs={{0,16},{8,24},{16,0},{24,8},{1,17},{9,25},{17,1},{25,9},{2,18},{10... | collective-permute-start | bytes 811016 | tf_op jit(solution)/shard_map/ppermute | solution.py:737
  29.4 0.7 %collective-permute-done.6.got_m = f32[520,128]{1,0:T(8,128)S(1)} collective-permute-done((f32[520,128]{1,0:T(8,128)S(1)}, f32[520,128]{1,0:T(8,128)S(1)}, u32[]{:S(2)}, u32[]{:S(2)}) %collective-permute-start.6) | collective-permute-done | bytes 266272 | tf_op jit(solution)/shard_map/ppermute | solution.py:761
  30.0 2.2 %bed_middle.1 = (f32[256,1024]{1,0:T(8,128)}, f32[256,1024]{1,0:T(8,128)}, f32[1,3,256,1024]{3,2,1,0:T(8,128)}) custom-call(f32[256,1024]{1,0:T(8,128)S(1)} %get-tuple-element.35.bed, f32[72,128]{1,0:T(8,128)S(1)} %collective-permute-done.side, f32[272,128]{1,0:T(8,128)S(1)} %collective-permute-done.1.far_a, f32[272,128]{1,0:T(8,128)S(1)} %collective-permute-done.2.far_b, ...), custom_call_target="tpu_custom_call" | custom-call | flops 4000000000 | tf_op jit(solution)/shard_map/bed_middle/pallas_call | solution.py:696
  32.3 3.9 %collective-permute-done.7 = f32[528,128]{1,0:T(8,128)S(1)} collective-permute-done((f32[528,128]{1,0:T(8,128)S(1)}, f32[528,128]{1,0:T(8,128)S(1)}, u32[]{:S(2)}, u32[]{:S(2)}) %collective-permute-start.7) | collective-permute-done | bytes 270368 | tf_op jit(solution)/shard_map/ppermute | solution.py:737
  36.2 1.3 %collective-permute-start.8 = (f32[528,128]{1,0:T(8,128)S(1)}, f32[528,128]{1,0:T(8,128)S(1)}, u32[]{:S(2)}, u32[]{:S(2)}) collective-permute-start(f32[528,128]{1,0:T(8,128)S(1)} %add.15.own_e), channel_id=1, source_target_pairs={{0,8},{8,0},{16,24},{24,16},{1,9},{9,1},{17,25},{25,17},{2,10},{10... | collective-permute-start | bytes 811016 | tf_op jit(solution)/shard_map/ppermute | solution.py:764
  37.6 1.2 %collective-permute-done.8.got_e = f32[528,128]{1,0:T(8,128)S(1)} collective-permute-done((f32[528,128]{1,0:T(8,128)S(1)}, f32[528,128]{1,0:T(8,128)S(1)}, u32[]{:S(2)}, u32[]{:S(2)}) %collective-permute-start.8) | collective-permute-done | bytes 270368 | tf_op jit(solution)/shard_map/ppermute | solution.py:764
  38.7 1.9 %bed_edge.1 = (f32[256,1024]{1,0:T(8,128)}, f32[256,1024]{1,0:T(8,128)}) custom-call(f32[256,1024]{1,0:T(8,128)S(1)} %get-tuple-element.35.bed, f32[72,128]{1,0:T(8,128)S(1)} %collective-permute-done.side, f32[272,128]{1,0:T(8,128)S(1)} %collective-permute-done.1.far_a, ...), custom_call_target="tpu_custom_call", output_to_operand_aliasing={{0}: (8, {}), {1}: (9, {})} | custom-call | flops 2000000000 | tf_op jit(solution)/shard_map/bed_edge/pallas_call | solution.py:709
  (15 shorter events, 0.2 us)
Async XLA Ops:
  2.4 4.1 %copy-start = (f32[1,3,256,1024]{3,2,1,0:T(8,128)S(1)}, f32[1,3,256,1024]{3,2,1,0:T(8,128)}, u32[]{:S(2)}) copy-start(f32[1,3,256,1024]{3,2,1,0:T(8,128)} %hydro.11) | copy-start | bytes 9437188
  2.4 4.1 %copy-start.1 = (f32[1,2,256,1024]{3,2,1,0:T(8,128)S(1)}, f32[1,2,256,1024]{3,2,1,0:T(8,128)}, u32[]{:S(2)}) copy-start(f32[1,2,256,1024]{3,2,1,0:T(8,128)} %stress.11) | copy-start | bytes 6291460
  2.4 4.1 %copy-start.2 = (f32[1,4]{1,0:T(1,128)S(1)}, f32[1,4]{1,0:T(1,128)}, u32[]{:S(2)}) copy-start(f32[1,4]{1,0:T(1,128)} %params.7) | copy-start | bytes 52
  2.4 4.1 %copy-start.3 = (s32[4]{0:T(128)S(1)}, s32[4]{0:T(128)}, u32[]{:S(2)}) copy-start(s32[4]{0:T(128)} %weights.7) | copy-start | bytes 52
  2.5 3.9 %collective-permute-start = (f32[72,128]{1,0:T(8,128)S(1)}, f32[72,128]{1,0:T(8,128)S(1)}, u32[]{:S(2)}, u32[]{:S(2)}) collective-permute-start(f32[72,128]{1,0:T(8,128)S(1)} %pack_side.1), channel_id=1, source_target_pairs={{0,1},{1,0},{2,3},{3,2},{4,5},{5,4},{6,7},{7,6},{8,9},{9,8},{10,11... | collective-permute-start | bytes 110600 | tf_op jit(solution)/shard_map/ppermute | solution.py:743
  6.4 4.7 %collective-permute-start.1 = (f32[272,128]{1,0:T(8,128)S(1)}, f32[272,128]{1,0:T(8,128)S(1)}, u32[]{:S(2)}, u32[]{:S(2)}) collective-permute-start(f32[272,128]{1,0:T(8,128)S(1)} %get-tuple-element.42), channel_id=1, source_target_pairs={{0,2},{2,0},{4,6},{6,4},{1,3},{3,1},{5,7},{7,5},{8,10},{10,8},{12,... | collective-permute-start | bytes 417800 | tf_op jit(solution)/shard_map/ppermute | solution.py:747
  9.9 9.1 %collective-permute-start.3 = (f32[520,128]{1,0:T(8,128)S(1)}, f32[520,128]{1,0:T(8,128)S(1)}, u32[]{:S(2)}, u32[]{:S(2)}) collective-permute-start(f32[520,128]{1,0:T(8,128)S(1)} %get-tuple-element.49), channel_id=1, source_target_pairs={{0,8},{8,0},{16,24},{24,16},{1,9},{9,1},{17,25},{25,17},{2,10},{10... | collective-permute-start | bytes 798728 | tf_op jit(solution)/shard_map/ppermute | solution.py:751
  11.1 9.3 %collective-permute-start.2 = (f32[272,128]{1,0:T(8,128)S(1)}, f32[272,128]{1,0:T(8,128)S(1)}, u32[]{:S(2)}, u32[]{:S(2)}) collective-permute-start(f32[272,128]{1,0:T(8,128)S(1)} %get-tuple-element.45), channel_id=1, source_target_pairs={{2,4},{4,2},{3,5},{5,3},{10,12},{12,10},{11,13},{13,11},{18,20},{2... | collective-permute-start | bytes 417800 | tf_op jit(solution)/shard_map/ppermute | solution.py:750
  19.1 9.2 %collective-permute-start.4 = (f32[520,128]{1,0:T(8,128)S(1)}, f32[520,128]{1,0:T(8,128)S(1)}, u32[]{:S(2)}, u32[]{:S(2)}) collective-permute-start(f32[520,128]{1,0:T(8,128)S(1)} %add.12), channel_id=1, source_target_pairs={{0,16},{8,24},{16,0},{24,8},{1,17},{9,25},{17,1},{25,9},{2,18},{10... | collective-permute-start | bytes 798728 | tf_op jit(solution)/shard_map/ppermute | solution.py:737
  23.9 4.5 %collective-permute-start.5 = (f32[528,128]{1,0:T(8,128)S(1)}, f32[528,128]{1,0:T(8,128)S(1)}, u32[]{:S(2)}, u32[]{:S(2)}) collective-permute-start(f32[528,128]{1,0:T(8,128)S(1)} %get-tuple-element.56), channel_id=1, source_target_pairs={{0,8},{8,0},{16,24},{24,16},{1,9},{9,1},{17,25},{25,17},{2,10},{10... | collective-permute-start | bytes 811016 | tf_op jit(solution)/shard_map/ppermute | solution.py:756
  28.4 1.6 %collective-permute-start.6 = (f32[520,128]{1,0:T(8,128)S(1)}, f32[520,128]{1,0:T(8,128)S(1)}, u32[]{:S(2)}, u32[]{:S(2)}) collective-permute-start(f32[520,128]{1,0:T(8,128)S(1)} %add.13.own_m), channel_id=1, source_target_pairs={{0,8},{8,0},{16,24},{24,16},{1,9},{9,1},{17,25},{25,17},{2,10},{10... | collective-permute-start | bytes 798728 | tf_op jit(solution)/shard_map/ppermute | solution.py:761
  28.5 7.7 %collective-permute-start.7 = (f32[528,128]{1,0:T(8,128)S(1)}, f32[528,128]{1,0:T(8,128)S(1)}, u32[]{:S(2)}, u32[]{:S(2)}) collective-permute-start(f32[528,128]{1,0:T(8,128)S(1)} %add.14), channel_id=1, source_target_pairs={{0,16},{8,24},{16,0},{24,8},{1,17},{9,25},{17,1},{25,9},{2,18},{10... | collective-permute-start | bytes 811016 | tf_op jit(solution)/shard_map/ppermute | solution.py:737
  36.2 2.5 %collective-permute-start.8 = (f32[528,128]{1,0:T(8,128)S(1)}, f32[528,128]{1,0:T(8,128)S(1)}, u32[]{:S(2)}, u32[]{:S(2)}) collective-permute-start(f32[528,128]{1,0:T(8,128)S(1)} %add.15.own_e), channel_id=1, source_target_pairs={{0,8},{8,0},{16,24},{24,16},{1,9},{9,1},{17,25},{25,17},{2,10},{10... | collective-permute-start | bytes 811016 | tf_op jit(solution)/shard_map/ppermute | solution.py:764

commit v7 on v5

--- a/solution.py
+++ b/solution.py
@@ -7,14 +7,12 @@
 from jax.experimental.pallas import tpu as pltpu
 from jax.sharding import PartitionSpec as P
 
-STEPS = 3
-HALO = STEPS + 1
+HALO = 4
 SUB = 8
 LANE = 128
 FIELDS = 8
 GROUP = HALO * FIELDS
 FOLD = LANE // GROUP
-LAG = 2
 MIB = 2**20
 ANY = pl.BlockSpec(memory_space=pl.ANY)
 VMEM = pl.BlockSpec(memory_space=pltpu.VMEM)
@@ -49,6 +47,10 @@
     if isinstance(index, int):
         return pl.ds(index * SUB, SUB)
     return pl.ds(pl.multiple_of(index * SUB, SUB), SUB)
+
+
+def lanes_at(k):
+    return slice(k * LANE, (k + 1) * LANE)
 
 
 def held(*arrays, space=pltpu.VMEM):
@@ -160,7 +162,10 @@
             copy.wait()
         for i in range(c * chunk // SUB, (c + 1) * chunk // SUB):
             at = tile_at(i)
-            root[at, :], a[at, :], b[at, :] = coefficients(bed_v[at, :], mask_v[at, :], kind_v[at, :], tide, flow_in)
+            values = coefficients(bed_v[at, :], mask_v[at, :], kind_v[at, :], tide, flow_in)
+            for ref, value in zip((root, a, b), values):
+                for k in range(lanes):
+                    ref[k, at, :] = value[:, lanes_at(k)]
     for copy in copies:
         copy.wait()
     low = rows_of((SUB, cols)) < HALO
@@ -168,7 +173,8 @@
 
     def edge_rows(f, end):
         if f < 3:
-            return (root, a, b)[f][tile_at(0 if end == 0 else rows // SUB - 1), :]
+            at = tile_at(0 if end == 0 else rows // SUB - 1)
+            return jnp.concatenate([(root, a, b)[f][k, at, :] for k in range(lanes)], axis=1)
         return ends[end, f - 3]
 
     for p in range(FIELDS // 2):
@@ -182,8 +188,8 @@
             top, bottom = pairs[0][:, part], pairs[1][:, part]
             pay_a[at, :] = jnp.where(odd, top, bottom)
             pay_b[at, :] = jnp.where(odd, bottom, top)
-    top = fold_row(bed_v[tile_at(0), :])
-    bottom = fold_row(pltpu.roll(bed_v[tile_at(rows // SUB - 1), :], 1, 0))
+    top = fold_row([bed_v[tile_at(0), lanes_at(k)] for k in range(lanes)])
+    bottom = fold_row([pltpu.roll(bed_v[tile_at(rows // SUB - 1), lanes_at(k)], 1, 0) for k in range(lanes)])
     at = pl.ds(lanes * GROUP + SUB, SUB)
     pay_a[at, :] = jnp.where(odd, top, bottom)
     pay_b[at, :] = jnp.where(odd, bottom, top)
@@ -191,19 +197,20 @@
 
 def fold_row(x):
     row = rows_of((SUB, LANE))
-    total = x[:, :LANE]
-    for k in range(1, x.shape[1] // LANE):
-        total = jnp.where(row == k, pltpu.roll(x[:, k * LANE : (k + 1) * LANE], k, 0), total)
+    total = x[0]
+    for k in range(1, len(x)):
+        total = jnp.where(row == k, pltpu.roll(x[k], k, 0), total)
     return total
 
 
 def prepare(params, *raw):
     rows, cols = raw[0].shape
     tile = pltpu.VMEM((rows, cols), jnp.float32)
+    planes = pltpu.VMEM((cols // LANE, rows, LANE), jnp.float32)
     return pl.pallas_call(
         prepare_kernel,
         name="prepare",
-        out_shape=[tile] * 4 + [pltpu.VMEM((cols // LANE * GROUP + 2 * SUB, LANE), jnp.float32)] * 2,
+        out_shape=[tile] + [planes] * 3 + [pltpu.VMEM((cols // LANE * GROUP + 2 * SUB, LANE), jnp.float32)] * 2,
         in_specs=[ANY] * 6,
         out_specs=[VMEM] * 6,
         scratch_shapes=[
@@ -255,13 +262,13 @@
 
 class Sweep:
     NAMES = (
-        ["fc", "fr", "wc", "wr", "e1", "u1"]
-        + ["v1", "e2", "u2", "v2", "qc1", "qr1", "qc2", "qr2"]
+        ["s", "e0", "fc", "fr", "wc", "wr", "e1", "u1", "v1"]
+        + ["e2", "u2", "v2", "qc1", "qr1", "qc2", "qr2", "flux", "load"]
     )
 
-    def __init__(self, count, wide, get, emit, weights, params, refs, trim):
-        self.count, self.wide, self.get, self.emit, self.trim = count, wide, get, emit, trim
-        self.__dict__.update(zip(self.NAMES + ["fr_last", "qr_last"], refs))
+    def __init__(self, count, tiles, get, weights, params, refs):
+        self.count, self.tiles, self.get = count, tiles, get
+        self.__dict__.update(zip(self.NAMES + ["results"], refs))
         cond = lax.axis_index("cond")
         self.slow = 1.0 - 0.2 * params[0, 1]
         total = weights[0]
@@ -269,242 +276,252 @@
             total = total + weights[k]
         ones = jnp.ones((SUB, LANE), jnp.float32)
         share = weights[cond].astype(jnp.float32) * ones / (total.astype(jnp.float32) * ones)
-        self.scale = jnp.concatenate([-4.0 * params[0, 2] * share] * (wide // LANE), axis=1)
+        self.scale = jnp.concatenate([-4.0 * params[0, 2] * share] * tiles, axis=1)
 
     @classmethod
-    def scratch(cls, count, wide):
-        block = pltpu.VMEM(((count + 1) * SUB, wide), jnp.float32)
-        return [block] * len(cls.NAMES) + [
-            pltpu.VMEM((STEPS, SUB, wide), jnp.float32),
-            pltpu.VMEM((SUB, wide), jnp.float32),
-        ]
-
-    def speed_c(self, i, level, u, wc):
-        return (self.slow * u - (east(level) - level) + self.get(3, i)) * wc
-
-    def speed_r(self, i, level, lower, v, wr):
-        return (self.slow * v - (south(level, lower) - level) + self.get(4, i)) * wr
-
-    def move(self, n, i, level, lower, u, v, fc, fr, wc, wr):
-        u = self.speed_c(i, level, u, wc)
-        v = self.speed_r(i, level, lower, v, wr)
-        flux_c = fc * u
-        flux_r = fr * v
-        out = self.get(1, i) * level + self.get(2, i) - (
-            flux_c - west(flux_c) + flux_r - north(flux_r, self.fr_last[n])
-        )
-        self.fr_last[n] = flux_r
-        return out, u, v
-
-    def step_one(self, i):
-        at = tile_at(i)
-        s = self.get(0, i)
-        level = 0.3 * self.get(5, i)
-        inside = i + 1 < self.count
-        face_c = s * east(s)
-        face_r = s * south(s, self.get(0, i + 1) if inside else s)
-        ratios = []
-        for face in (face_c, face_r):
-            base = face + 0.1
-            inverse = pl.reciprocal(base, approx=True)
-            ratios.append(face * (inverse * (2.0 - base * inverse)))
-        wc, wr = ratios
-        fc = 0.3 * face_c
-        fr = 0.3 * face_r
-        self.fc[at, :] = fc
-        self.fr[at, :] = fr
-        self.wc[at, :] = wc
-        self.wr[at, :] = wr
-        lower = 0.3 * self.get(5, i + 1) if inside else level
-        e, u, v = self.move(0, i, level, lower, self.get(6, i), self.get(7, i), fc, fr, wc, wr)
-        self.e1[at, :] = e
-        self.u1[at, :] = u
-        self.v1[at, :] = v
-        self.qc1[at, :] = u * jnp.abs(u)
-        self.qr1[at, :] = v * jnp.abs(v)
-
-    def step_two(self, i):
-        at, after = tile_at(i), tile_at(i + 1)
-        e, u, v = self.move(
-            1, i, self.e1[at, :], self.e1[after, :], self.u1[at, :], self.v1[at, :],
-            self.fc[at, :], self.fr[at, :], self.wc[at, :], self.wr[at, :],
-        )
-        self.e2[at, :] = e
-        if self.trim and i == self.count - 1:
-            return
-        self.u2[at, :] = u
-        self.v2[at, :] = v
-        self.qc2[at, :] = self.qc1[at, :] + u * jnp.abs(u)
-        self.qr2[at, :] = self.qr1[at, :] + v * jnp.abs(v)
-
-    def step_three(self, i):
-        at, after = tile_at(i), tile_at(i + 1)
-        if self.trim and i == self.count - 1:
-            return
-        if self.trim and i == 0:
-            wr = self.wr[at, :]
-            v = self.speed_r(i, self.e2[at, :], self.e2[after, :], self.v2[at, :], wr)
-            self.fr_last[2] = self.fr[at, :] * v
-            self.qr_last[...] = wr * (self.qr2[at, :] + v * jnp.abs(v))
-            return
-        wc, wr = self.wc[at, :], self.wr[at, :]
-        e, u, v = self.move(
-            2, i, self.e2[at, :], self.e2[after, :], self.u2[at, :], self.v2[at, :],
-            self.fc[at, :], self.fr[at, :], wc, wr,
-        )
-        qc = wc * (self.qc2[at, :] + u * jnp.abs(u))
-        qr = wr * (self.qr2[at, :] + v * jnp.abs(v))
-        change = (qc - west(qc) + qr - north(qr, self.qr_last[...])) * self.scale
-        self.qr_last[...] = qr
-        self.emit(i, e * (1.0 / 0.3), u, v, change)
+    def scratch(cls, count, tiles):
+        block = pltpu.VMEM((count * SUB, tiles * LANE), jnp.float32)
+        return [block] * len(cls.NAMES) + [pltpu.VMEM((4, tiles, count * SUB, LANE), jnp.float32)]
+
+    def below(self, ref, j):
+        if j + 1 < self.count:
+            return ref[tile_at(j + 1), :]
+        return pltpu.roll(ref[tile_at(0), :], SUB - 1, 0)
+
+    def above(self, ref, j):
+        if j > 0:
+            return ref[tile_at(j - 1), :]
+        return pltpu.roll(ref[tile_at(self.count - 1), :], 1, 0)
+
+    def put(self, what, j, value):
+        for k in range(self.tiles):
+            self.results[what, k, pl.ds(j, SUB, stride=self.count), :] = value[:, lanes_at(k)]
+
+    def step(self, e, u, v, after):
+        rest = []
+        for j in range(self.count):
+            at = tile_at(j)
+            level = e[at, :]
+            new_u = (self.slow * u(j) - (east(level) - level) + self.get(3, j)) * self.wc[at, :]
+            new_v = (self.slow * v(j) - (self.below(e, j) - level) + self.get(4, j)) * self.wr[at, :]
+            flux_c = self.fc[at, :] * new_u
+            flux_r = self.fr[at, :] * new_v
+            self.flux[at, :] = flux_r
+            part = self.get(1, j) * level + self.get(2, j) - (flux_c - west(flux_c) + flux_r)
+            if j == 0:
+                rest.append(part)
+            after(j, new_u, new_v)
+            if j:
+                yield j, part + self.above(self.flux, j)
+        yield 0, rest[0] + self.above(self.flux, 0)
 
     def run(self):
-        self.fr_last[...] = jnp.zeros_like(self.fr_last)
-        self.qr_last[...] = jnp.zeros_like(self.qr_last)
-        for ref in (self.e1, self.e2):
-            ref[tile_at(self.count), :] = jnp.zeros((SUB, self.wide), jnp.float32)
-        stages = (self.step_three, self.step_two, self.step_one)
-        for t in range(self.count + LAG * (STEPS - 1)):
-            for k, stage in enumerate(stages):
-                i = t - LAG * (STEPS - 1 - k)
-                if 0 <= i < self.count:
-                    stage(i)
-
-
-def reader(root, a, b, stress, hydro, side, unfold, valid):
-    rows = root.shape[0]
-    span = rows // FOLD // SUB
-    fields = [root, a, b] + moving(stress, hydro)
-
-    def read(f, block):
-        part = unfold(side[tile_at(block % span), :], (block // span) * FIELDS + f)
-        if f == 0:
-            part = jnp.where(valid, part, 0.0)
-        return jnp.concatenate([fields[f][tile_at(block), :], part], axis=1)
-
-    return read
-
-
-def quarter_writer(first, quarter, cols, hydro_out, pay):
-    lane = lanes_of((SUB, LANE))
-    lanes = cols // LANE
-    rims = [jnp.zeros((SUB, LANE), jnp.float32)]
-
-    def emit(i, e, u, v, change):
-        at = tile_at(first + i)
-        for k, value in enumerate((e, u, v)):
-            hydro_out[0, k, at, :] = value[:, :cols]
-        g = i - 1
-        for k in range(lanes):
-            pay[tile_at(k * quarter + g), :] = change[:, k * LANE : (k + 1) * LANE]
-        rims[0] = jnp.where(lane // 2 == g, pltpu.roll(change[:, cols:], 1 + 2 * g, 1), rims[0])
-        if g == quarter - 1:
-            pay[tile_at(lanes * quarter), :] = rims[0]
-
-    return emit
+        for j in range(self.count):
+            at = tile_at(j)
+            self.s[at, :] = self.get(0, j)
+            self.e0[at, :] = 0.3 * self.get(5, j)
+        for j in range(self.count):
+            at = tile_at(j)
+            s = self.s[at, :]
+            for other, face_ref, wet_ref in (
+                (east(s), self.fc, self.wc),
+                (self.below(self.s, j), self.fr, self.wr),
+            ):
+                face = s * other
+                base = face + 0.1
+                inverse = pl.reciprocal(base, approx=True)
+                wet_ref[at, :] = face * (inverse * (2.0 - base * inverse))
+                face_ref[at, :] = 0.3 * face
+
+        def first(j, u, v):
+            at = tile_at(j)
+            self.u1[at, :] = u
+            self.v1[at, :] = v
+            self.qc1[at, :] = u * jnp.abs(u)
+            self.qr1[at, :] = v * jnp.abs(v)
+
+        for j, e in self.step(self.e0, lambda j: self.get(6, j), lambda j: self.get(7, j), first):
+            self.e1[tile_at(j), :] = e
+
+        def second(j, u, v):
+            at = tile_at(j)
+            self.u2[at, :] = u
+            self.v2[at, :] = v
+            self.qc2[at, :] = self.qc1[at, :] + u * jnp.abs(u)
+            self.qr2[at, :] = self.qr1[at, :] + v * jnp.abs(v)
+
+        u, v = self.u1, self.v1
+        for j, e in self.step(self.e1, lambda j: u[tile_at(j), :], lambda j: v[tile_at(j), :], second):
+            self.e2[tile_at(j), :] = e
+
+        rest = []
+
+        def third(j, u, v):
+            at = tile_at(j)
+            self.put(1, j, u)
+            self.put(2, j, v)
+            qc = self.wc[at, :] * (self.qc2[at, :] + u * jnp.abs(u))
+            qr = self.wr[at, :] * (self.qr2[at, :] + v * jnp.abs(v))
+            self.load[at, :] = qr
+            part = qc - west(qc) + qr
+            if j == 0:
+                rest.append(part)
+            else:
+                self.put(3, j, (part - self.above(self.load, j)) * self.scale)
+
+        u2, v2 = self.u2, self.v2
+        for j, e in self.step(self.e2, lambda j: u2[tile_at(j), :], lambda j: v2[tile_at(j), :], third):
+            self.put(0, j, e * (1.0 / 0.3))
+        self.put(3, 0, (rest[0] - self.above(self.load, 0)) * self.scale)
+        return self.results
+
+
+class Region:
+    def __init__(self, fields, side, stage, first, quarter):
+        self.fields, self.side, self.stage, self.first = fields, side, stage, first
+        self.count = quarter + 2
+        _, rows, _ = fields[0].shape
+        self.span = rows // FOLD // SUB
+        self.tiles = fields[0].shape[0]
+        self.unfold, self.valid = side_lanes(lax.axis_index("tx") == 0)
+
+    def main(self, f, block, k):
+        if f < 3:
+            return self.fields[f][k, tile_at(block), :]
+        return self.fields[f][tile_at(block), lanes_at(k)]
+
+    def lanes(self, f, block):
+        part = self.unfold(self.side[tile_at(block % self.span), :], (block // self.span) * FIELDS + f)
+        return jnp.where(self.valid, part, 0.0) if f == 0 else part
+
+    def fill(self, spots, direct):
+        for i in spots:
+            for f in range(FIELDS):
+                for k in range(self.tiles):
+                    if not (direct and f < 3):
+                        self.stage[f, k, tile_at(i), :] = self.main(f, self.first + i, k)
+                self.stage[f, self.tiles, tile_at(i), :] = self.lanes(f, self.first + i)
+
+    def get(self, direct):
+        start = pl.multiple_of(self.first * SUB, SUB)
+
+        def get(f, j):
+            parts = []
+            for k in range(self.tiles + 1):
+                if direct and f < 3 and k < self.tiles:
+                    parts.append(self.fields[f][k, pl.ds(start + j, SUB, stride=self.count), :])
+                else:
+                    parts.append(self.stage[f, k, pl.ds(j, SUB, stride=self.count), :])
+            return jnp.concatenate(parts, axis=1)
+
+        return get
+
+    def write(self, results, hydro_out, pay):
+        lane = lanes_of((SUB, LANE))
+        quarter = self.count - 2
+        rim = jnp.zeros((SUB, LANE), jnp.float32)
+        for g in range(quarter):
+            for k in range(self.tiles):
+                for what in range(3):
+                    hydro_out[0, what, tile_at(self.first + g + 1), lanes_at(k)] = results[what, k, tile_at(g + 1), :]
+                pay[tile_at(k * quarter + g), :] = results[3, k, tile_at(g + 1), :]
+            rim = jnp.where(lane // 2 == g, pltpu.roll(results[3, self.tiles, tile_at(g + 1), :], 1 + 2 * g, 1), rim)
+        pay[tile_at(self.tiles * quarter), :] = rim
 
 
 def middle_kernel(own, weights, params, root, a, b, stress, hydro, side, *refs):
-    hydro_out, pay, *refs = refs[1:] if own else refs
-    rows, cols = root.shape
+    hydro_out, pay, stage, *refs = refs[1:] if own else refs
+    tiles, rows, _ = root.shape
     quarter = rows // SUB // 4
-    read = reader(root, a, b, stress, hydro, side, *side_lanes(lax.axis_index("tx") == 0))
     mine = lax.axis_index("cond") % 2
     lower_half = mine == (1 if own else 0)
     first = jnp.where(lower_half, 2 * quarter, quarter) - 1
-    emit = quarter_writer(first, quarter, cols, hydro_out, pay)
-    Sweep(
-        quarter + 2, cols + LANE, lambda f, i: read(f, first + i), emit, weights, params, refs, True
-    ).run()
+    region = Region([root, a, b] + moving(stress, hydro), side, stage, first, quarter)
+    region.fill(range(quarter + 2), True)
+    results = Sweep(quarter + 2, tiles + 1, region.get(True), weights, params, refs).run()
+    region.write(results, hydro_out, pay)
+
+
+def flow_scratch(rows, tiles):
+    count = rows // SUB // 4 + 2
+    return [pltpu.VMEM((FIELDS, tiles + 1, count * SUB, LANE), jnp.float32)] + Sweep.scratch(count, tiles + 1)
 
 
 def middle(own, weights, params, fields, side, hydro=None):
-    rows, cols = fields[0].shape
+    tiles, rows, _ = fields[0].shape
     given = (hydro,) if own else ()
     return pl.pallas_call(
         functools.partial(middle_kernel, own),
         name="middle_own" if own else "middle_other",
         out_shape=[
             pltpu.VMEM(fields[4].shape, jnp.float32),
-            pltpu.VMEM((cols // LANE * rows // 4 + SUB, LANE), jnp.float32),
+            pltpu.VMEM((tiles * rows // 4 + SUB, LANE), jnp.float32),
         ],
         in_specs=[SMEM, SMEM] + [VMEM] * (6 + own),
         out_specs=[VMEM, VMEM],
-        scratch_shapes=Sweep.scratch(rows // SUB // 4 + 2, cols + LANE),
+        scratch_shapes=flow_scratch(rows, tiles),
         input_output_aliases={8: 0} if own else {},
-        compiler_params=pltpu.CompilerParams(vmem_limit_bytes=10 * MIB),
+        compiler_params=pltpu.CompilerParams(vmem_limit_bytes=16 * MIB),
         cost_estimate=cost(4),
     )(weights, params, *held(*fields, side, *given))
 
 
 def edge_kernel(
     own, weights, params, root, a, b, stress, hydro, side, far_a, far_b, hydro_in,
-    hydro_out, pay, ends, *refs,
+    hydro_out, pay, stage, *refs,
 ):
-    rows, cols = root.shape
+    tiles, rows, _ = root.shape
     blocks = rows // SUB
     quarter = blocks // 4
-    lanes = cols // LANE
-    unfold, valid = side_lanes(lax.axis_index("tx") == 0)
-    read = reader(root, a, b, stress, hydro, side, unfold, valid)
     mine = lax.axis_index("cond") % 2
     top = mine == (0 if own else 1)
     from_a = top == (lax.axis_index("ty") % 2 == 1)
     first = jnp.where(top, -1, blocks - quarter - 1)
+    region = Region([root, a, b] + moving(stress, hydro), side, stage, first, quarter)
+    region.fill(range(1, quarter + 1), False)
 
     inner = jnp.where(top, quarter, blocks - quarter - 1)
-    corners = pl.ds(lanes * GROUP, SUB)
+    corners = pl.ds(tiles * GROUP, SUB)
     for f in range(FIELDS):
-        body = read(f, inner)
-        parts = []
-        for k in range(lanes):
-            at = pl.ds(k * GROUP + f // 2 * SUB, SUB)
-            part = jnp.where(from_a, far_a[at, :], far_b[at, :])
-            moved = pltpu.roll(part, HALO, 0)
-            parts.append(jnp.where(top, moved, part) if f % 2 == 0 else jnp.where(top, part, moved))
-        corner = jnp.where(from_a, far_a[corners, :], far_b[corners, :])
-        corner = jnp.where(top, unfold(corner, (FOLD - 1) * FIELDS + f), unfold(corner, f))
-        if f == 0:
-            corner = jnp.where(valid, corner, 0.0)
-        outer = jnp.concatenate(parts + [corner], axis=1)
-        ends[0, f] = jnp.where(top, outer, body)
-        ends[1, f] = jnp.where(top, body, outer)
-
-    def get(f, i):
-        if i == 0 or i == quarter + 1:
-            return ends[0 if i == 0 else 1, f]
-        return read(f, first + i)
-
-    emit = quarter_writer(first, quarter, cols, hydro_out, pay)
-    outside = []
-
-    def finish(i, e, u, v, change):
-        if i == 0:
-            outside.append(pltpu.roll(change[:, :cols], 1, 0))
-        elif i == quarter + 1:
-            pay[tile_at(lanes * quarter + 1), :] = fold_row(jnp.where(top, outside[0], change[:, :cols]))
-        else:
-            emit(i, e, u, v, change)
-
-    Sweep(quarter + 2, cols + LANE, get, finish, weights, params, refs, False).run()
+        for k in range(tiles + 1):
+            if k < tiles:
+                body = region.main(f, inner, k)
+                at = pl.ds(k * GROUP + f // 2 * SUB, SUB)
+                part = jnp.where(from_a, far_a[at, :], far_b[at, :])
+                moved = pltpu.roll(part, HALO, 0)
+                outer = jnp.where(top, moved, part) if f % 2 == 0 else jnp.where(top, part, moved)
+            else:
+                body = region.lanes(f, inner)
+                corner = jnp.where(from_a, far_a[corners, :], far_b[corners, :])
+                outer = region.unfold(corner, jnp.where(top, (FOLD - 1) * FIELDS, 0) + f)
+                if f == 0:
+                    outer = jnp.where(region.valid, outer, 0.0)
+            stage[f, k, tile_at(0), :] = jnp.where(top, outer, body)
+            stage[f, k, tile_at(quarter + 1), :] = jnp.where(top, body, outer)
+
+    results = Sweep(quarter + 2, tiles + 1, region.get(False), weights, params, refs).run()
+    region.write(results, hydro_out, pay)
+    rim = [
+        jnp.where(top, pltpu.roll(results[3, k, tile_at(0), :], 1, 0), results[3, k, tile_at(quarter + 1), :])
+        for k in range(tiles)
+    ]
+    pay[tile_at(tiles * quarter + 1), :] = fold_row(rim)
 
 
 def edge(own, weights, params, fields, side, far_a, far_b, hydro):
-    rows, cols = fields[0].shape
-    wide = cols + LANE
+    tiles, rows, _ = fields[0].shape
     return pl.pallas_call(
         functools.partial(edge_kernel, own),
         name="edge_own" if own else "edge_other",
         out_shape=[
             pltpu.VMEM(hydro.shape, jnp.float32),
-            pltpu.VMEM((cols // LANE * rows // 4 + 2 * SUB, LANE), jnp.float32),
+            pltpu.VMEM((tiles * rows // 4 + 2 * SUB, LANE), jnp.float32),
         ],
         in_specs=[SMEM, SMEM] + [VMEM] * 9,
         out_specs=[VMEM, VMEM],
-        scratch_shapes=[pltpu.VMEM((2, FIELDS, SUB, wide), jnp.float32)]
-        + Sweep.scratch(rows // SUB // 4 + 2, wide),
+        scratch_shapes=flow_scratch(rows, tiles),
         input_output_aliases={10: 0},
-        compiler_params=pltpu.CompilerParams(vmem_limit_bytes=12 * MIB),
+        compiler_params=pltpu.CompilerParams(vmem_limit_bytes=16 * MIB),
         cost_estimate=cost(3),
     )(weights, params, *held(*fields, side, far_a, far_b, hydro))
 

time: 40.1 us -> 41.4 us (1.032)
  Pallas kernels: 21.1 us -> 22.9 us
  starting transfers between devices: 12.1 us -> 11.3 us
    pallas_call x2, Pallas kernels: 6.22 us -> 7.09 us  [middle(): pl.pallas_call(functools.partial(middle_kernel, own), name='middle_own' i...]
    pallas_call x2, Pallas kernels: 6.35 us -> 7.22 us  [edge(): pl.pallas_call(functools.partial(edge_kernel, own), name='edge_own' if ow...]
    ppermute x2, starting transfers between devices: 2.48 us -> 2.03 us  [over_chips(): got = lax.ppermute(part, 'cond', [(i, i ^ reach) for i in range(nc)])]
    ppermute x1, waiting for transfers between devices: 0.31 us -> 0.76 us  [shards(): got_m = lax.ppermute(own_m, 'cond', swap)]
    ppermute x2, starting transfers between devices: 2.41 us -> 1.99 us  [shards(): got = lax.ppermute(pay, 'cond', swap)]
  transfers between devices with their start and end apart: 9 -> 9, of which waited for: 4 -> 3; matrix products, arithmetic and copies ran while one was open for 0% -> 0% of each run, Pallas kernels for 44% -> 46%
where the time goes in v7:
time: 41.4 us; the launch traced here: 41.2 us
  Pallas kernels  22.9 us (55%)
  starting transfers between devices  11.3 us (27%)
  waiting for transfers between devices  5.87 us (14%)
  between operations  0.98 us (2%)
    pallas_call x2, Pallas kernels, edge(): pl.pallas_call(functools.partial(edge_kernel, own), name='edge_own' if ow...  7.22 us
    pallas_call x2, Pallas kernels, middle(): pl.pallas_call(functools.partial(middle_kernel, own), name='middle_own' i...  7.09 us
    ppermute x1, starting transfers between devices, shards(): far_b = lax.ppermute(far_b, 'ty', pairs(1))  4.5 us
    ppermute x2, waiting for transfers between devices, over_chips(): got = lax.ppermute(part, 'cond', [(i, i ^ reach) for i in range(nc)])  3.92 us
    pallas_call x1, Pallas kernels, prepare(): pl.pallas_call(prepare_kernel, name='prepare', out_shape=[tile] + [planes...  2.59 us
    pallas_call x1, Pallas kernels, bed_middle(): pl.pallas_call(bed_middle_kernel, name='bed_middle', out_shape=[pltpu.HBM...  2.24 us
    ppermute x2, starting transfers between devices, over_chips(): got = lax.ppermute(part, 'cond', [(i, i ^ reach) for i in range(nc)])  2.03 us
    ppermute x2, starting transfers between devices, shards(): got = lax.ppermute(pay, 'cond', swap)  1.99 us
  transfers between devices with their start and end apart: 9, of which 3 were waited for; matrix products, arithmetic and copies ran while one was open for 0% of the time, Pallas kernels for 46%

profile of v7, /device:TPU:9, one launch (start us, length us, event | category | flops | bytes accessed | tf_op | source)
XLA Modules:
  0.0 41.2 jit_solution(7047814637601293839)
XLA Ops:
  0.6 1.8 %pack_side.1 = f32[72,128]{1,0:T(8,128)S(1)} custom-call(f32[1,4]{1,0:T(1,128)} %params.7, f32[256,1024]{1,0:T(8,128)} %bed.3, s32[256,1024]{1,0:T(8,128)} %mask.3, s32[256,1024]{1,0:T(8,128)} %kind.3, f32[1,2,256,1024]{3,2,1,0:T(8,128)} %stress.11, f32[1,3,256,1024]{3,2,1,0:T(8,128)} %hydro.11), custom_call_target="tpu_custom_call" | custom-call | flops 2000000000 | tf_op jit(solution)/shard_map/pack_side/pallas_call | solution.py:116
  2.4 0.0 copy-start
  2.4 0.0 copy-start.1
  2.4 0.0 copy-start.2
  2.4 0.0 copy-start.3
  2.5 1.3 %collective-permute-start = (f32[72,128]{1,0:T(8,128)S(1)}, f32[72,128]{1,0:T(8,128)S(1)}, u32[]{:S(2)}, u32[]{:S(2)}) collective-permute-start(f32[72,128]{1,0:T(8,128)S(1)} %pack_side.1), channel_id=1, source_target_pairs={{0,1},{1,0},{2,3},{3,2},{4,5},{5,4},{6,7},{7,6},{8,9},{9,8},{10,11... | collective-permute-start | bytes 110600 | tf_op jit(solution)/shard_map/ppermute | solution.py:704
  3.8 2.6 %prepare.1 = (f32[256,1024]{1,0:T(8,128)S(1)}, f32[8,256,128]{2,1,0:T(8,128)S(1)}, f32[8,256,128]{2,1,0:T(8,128)S(1)}, f32[8,256,128]{2,1,0:T(8,128)S(1)}, f32[2...) custom-call(f32[1,4]{1,0:T(1,128)} %params.7, f32[256,1024]{1,0:T(8,128)} %bed.3, s32[256,1024]{1,0:T(8,128)} %mask.3, ...), custom_call_target="tpu_custom_call" | custom-call | flops 2000000000 | tf_op jit(solution)/shard_map/prepare/pallas_call | solution.py:210
  6.4 0.1 collective-permute-start.1
  6.5 3.5 %middle_other.1 = (f32[1,3,256,1024]{3,2,1,0:T(8,128)S(1)}, f32[520,128]{1,0:T(8,128)S(1)}) custom-call(s32[4]{0:T(128)S(1)} %copy-done.3, f32[1,4]{1,0:T(1,128)S(1)} %copy-done.2, f32[8,256,128]{2,1,0:T(8,128)S(1)} %get-tuple-element.36.root, f32[8,256,128]{2,1,0:T(8,128)S(1)} %get-tuple-element.37.a, f32[8,256,128]{2,1,0:T(8,128)S(1)} %get-tuple-element.38.b, ...), custom_call_target="tpu_custom_call" | custom-call | flops 4000000000 | tf_op jit(solution)/shard_map/middle_other/pallas_call | solution.py:453
  10.1 1.2 %collective-permute-start.3 = (f32[520,128]{1,0:T(8,128)S(1)}, f32[520,128]{1,0:T(8,128)S(1)}, u32[]{:S(2)}, u32[]{:S(2)}) collective-permute-start(f32[520,128]{1,0:T(8,128)S(1)} %get-tuple-element.49), channel_id=1, source_target_pairs={{0,8},{8,0},{16,24},{24,16},{1,9},{9,1},{17,25},{25,17},{2,10},{10... | collective-permute-start | bytes 798728 | tf_op jit(solution)/shard_map/ppermute | solution.py:712
  11.3 4.5 %collective-permute-start.2 = (f32[272,128]{1,0:T(8,128)S(1)}, f32[272,128]{1,0:T(8,128)S(1)}, u32[]{:S(2)}, u32[]{:S(2)}) collective-permute-start(f32[272,128]{1,0:T(8,128)S(1)} %get-tuple-element.45), channel_id=1, source_target_pairs={{2,4},{4,2},{3,5},{5,3},{10,12},{12,10},{11,13},{13,11},{18,20},{2... | collective-permute-start | bytes 417800 | tf_op jit(solution)/shard_map/ppermute | solution.py:711
  15.8 3.5 %middle_own.1 = (f32[1,3,256,1024]{3,2,1,0:T(8,128)S(1)}, f32[520,128]{1,0:T(8,128)S(1)}) custom-call(s32[4]{0:T(128)S(1)} %copy-done.3, f32[1,4]{1,0:T(1,128)S(1)} %copy-done.2, f32[8,256,128]{2,1,0:T(8,128)S(1)} %get-tuple-element.36.root, f32[8,256,128]{2,1,0:T(8,128)S(1)} %get-tuple-element.37.a, ...), custom_call_target="tpu_custom_call", output_to_operand_aliasing={{0}: (8, {})} | custom-call | flops 4000000000 | tf_op jit(solution)/shard_map/middle_own/pallas_call | solution.py:453
  19.4 1.3 %collective-permute-start.4 = (f32[520,128]{1,0:T(8,128)S(1)}, f32[520,128]{1,0:T(8,128)S(1)}, u32[]{:S(2)}, u32[]{:S(2)}) collective-permute-start(f32[520,128]{1,0:T(8,128)S(1)} %add.12), channel_id=1, source_target_pairs={{0,16},{8,24},{16,0},{24,8},{1,17},{9,25},{17,1},{25,9},{2,18},{10... | collective-permute-start | bytes 798728 | tf_op jit(solution)/shard_map/ppermute | solution.py:698
  20.7 3.6 %edge_other.1 = (f32[1,3,256,1024]{3,2,1,0:T(8,128)S(1)}, f32[528,128]{1,0:T(8,128)S(1)}) custom-call(s32[4]{0:T(128)S(1)} %copy-done.3, f32[1,4]{1,0:T(1,128)S(1)} %copy-done.2, f32[8,256,128]{2,1,0:T(8,128)S(1)} %get-tuple-element.36.root, f32[8,256,128]{2,1,0:T(8,128)S(1)} %get-tuple-element.37.a, ...), custom_call_target="tpu_custom_call", output_to_operand_aliasing={{0}: (10, {})} | custom-call | flops 3000000000 | tf_op jit(solution)/shard_map/edge_other/pallas_call | solution.py:513
  24.3 0.8 %collective-permute-start.5 = (f32[528,128]{1,0:T(8,128)S(1)}, f32[528,128]{1,0:T(8,128)S(1)}, u32[]{:S(2)}, u32[]{:S(2)}) collective-permute-start(f32[528,128]{1,0:T(8,128)S(1)} %get-tuple-element.56), channel_id=1, source_target_pairs={{0,8},{8,0},{16,24},{24,16},{1,9},{9,1},{17,25},{25,17},{2,10},{10... | collective-permute-start | bytes 811016 | tf_op jit(solution)/shard_map/ppermute | solution.py:717
  25.1 3.6 %edge_own.1 = (f32[1,3,256,1024]{3,2,1,0:T(8,128)S(1)}, f32[528,128]{1,0:T(8,128)S(1)}) custom-call(s32[4]{0:T(128)S(1)} %copy-done.3, f32[1,4]{1,0:T(1,128)S(1)} %copy-done.2, f32[8,256,128]{2,1,0:T(8,128)S(1)} %get-tuple-element.36.root, f32[8,256,128]{2,1,0:T(8,128)S(1)} %get-tuple-element.37.a, ...), custom_call_target="tpu_custom_call", output_to_operand_aliasing={{0}: (10, {})} | custom-call | flops 3000000000 | tf_op jit(solution)/shard_map/edge_own/pallas_call | solution.py:513
  28.8 0.1 collective-permute-start.6
  28.9 0.8 %collective-permute-start.7 = (f32[528,128]{1,0:T(8,128)S(1)}, f32[528,128]{1,0:T(8,128)S(1)}, u32[]{:S(2)}, u32[]{:S(2)}) collective-permute-start(f32[528,128]{1,0:T(8,128)S(1)} %add.14), channel_id=1, source_target_pairs={{0,16},{8,24},{16,0},{24,8},{1,17},{9,25},{17,1},{25,9},{2,18},{10... | collective-permute-start | bytes 811016 | tf_op jit(solution)/shard_map/ppermute | solution.py:698
  29.6 0.8 %collective-permute-done.6.got_m = f32[520,128]{1,0:T(8,128)S(1)} collective-permute-done((f32[520,128]{1,0:T(8,128)S(1)}, f32[520,128]{1,0:T(8,128)S(1)}, u32[]{:S(2)}, u32[]{:S(2)}) %collective-permute-start.6) | collective-permute-done | bytes 266272 | tf_op jit(solution)/shard_map/ppermute | solution.py:722
  30.4 2.2 %bed_middle.1 = (f32[256,1024]{1,0:T(8,128)}, f32[256,1024]{1,0:T(8,128)}, f32[1,3,256,1024]{3,2,1,0:T(8,128)}) custom-call(f32[256,1024]{1,0:T(8,128)S(1)} %get-tuple-element.35.bed, f32[72,128]{1,0:T(8,128)S(1)} %collective-permute-done.side, f32[272,128]{1,0:T(8,128)S(1)} %collective-permute-done.1.far_a, f32[272,128]{1,0:T(8,128)S(1)} %collective-permute-done.2.far_b, ...), custom_call_target="tpu_custom_call" | custom-call | flops 4000000000 | tf_op jit(solution)/shard_map/bed_middle/pallas_call | solution.py:657
  32.6 3.9 %collective-permute-done.7 = f32[528,128]{1,0:T(8,128)S(1)} collective-permute-done((f32[528,128]{1,0:T(8,128)S(1)}, f32[528,128]{1,0:T(8,128)S(1)}, u32[]{:S(2)}, u32[]{:S(2)}) %collective-permute-start.7) | collective-permute-done | bytes 270368 | tf_op jit(solution)/shard_map/ppermute | solution.py:698
  36.6 1.3 %collective-permute-start.8 = (f32[528,128]{1,0:T(8,128)S(1)}, f32[528,128]{1,0:T(8,128)S(1)}, u32[]{:S(2)}, u32[]{:S(2)}) collective-permute-start(f32[528,128]{1,0:T(8,128)S(1)} %add.15.own_e), channel_id=1, source_target_pairs={{0,8},{8,0},{16,24},{24,16},{1,9},{9,1},{17,25},{25,17},{2,10},{10... | collective-permute-start | bytes 811016 | tf_op jit(solution)/shard_map/ppermute | solution.py:725
  37.9 1.2 %collective-permute-done.8.got_e = f32[528,128]{1,0:T(8,128)S(1)} collective-permute-done((f32[528,128]{1,0:T(8,128)S(1)}, f32[528,128]{1,0:T(8,128)S(1)}, u32[]{:S(2)}, u32[]{:S(2)}) %collective-permute-start.8) | collective-permute-done | bytes 270368 | tf_op jit(solution)/shard_map/ppermute | solution.py:725
  39.1 1.9 %bed_edge.1 = (f32[256,1024]{1,0:T(8,128)}, f32[256,1024]{1,0:T(8,128)}) custom-call(f32[256,1024]{1,0:T(8,128)S(1)} %get-tuple-element.35.bed, f32[72,128]{1,0:T(8,128)S(1)} %collective-permute-done.side, f32[272,128]{1,0:T(8,128)S(1)} %collective-permute-done.1.far_a, ...), custom_call_target="tpu_custom_call", output_to_operand_aliasing={{0}: (8, {}), {1}: (9, {})} | custom-call | flops 2000000000 | tf_op jit(solution)/shard_map/bed_edge/pallas_call | solution.py:670
  (15 shorter events, 0.2 us)
Async XLA Ops:
  2.4 4.1 %copy-start = (f32[1,3,256,1024]{3,2,1,0:T(8,128)S(1)}, f32[1,3,256,1024]{3,2,1,0:T(8,128)}, u32[]{:S(2)}) copy-start(f32[1,3,256,1024]{3,2,1,0:T(8,128)} %hydro.11) | copy-start | bytes 9437188
  2.4 4.1 %copy-start.1 = (f32[1,2,256,1024]{3,2,1,0:T(8,128)S(1)}, f32[1,2,256,1024]{3,2,1,0:T(8,128)}, u32[]{:S(2)}) copy-start(f32[1,2,256,1024]{3,2,1,0:T(8,128)} %stress.11) | copy-start | bytes 6291460
  2.4 4.1 %copy-start.2 = (f32[1,4]{1,0:T(1,128)S(1)}, f32[1,4]{1,0:T(1,128)}, u32[]{:S(2)}) copy-start(f32[1,4]{1,0:T(1,128)} %params.7) | copy-start | bytes 52
  2.4 4.1 %copy-start.3 = (s32[4]{0:T(128)S(1)}, s32[4]{0:T(128)}, u32[]{:S(2)}) copy-start(s32[4]{0:T(128)} %weights.7) | copy-start | bytes 52
  2.5 3.9 %collective-permute-start = (f32[72,128]{1,0:T(8,128)S(1)}, f32[72,128]{1,0:T(8,128)S(1)}, u32[]{:S(2)}, u32[]{:S(2)}) collective-permute-start(f32[72,128]{1,0:T(8,128)S(1)} %pack_side.1), channel_id=1, source_target_pairs={{0,1},{1,0},{2,3},{3,2},{4,5},{5,4},{6,7},{7,6},{8,9},{9,8},{10,11... | collective-permute-start | bytes 110600 | tf_op jit(solution)/shard_map/ppermute | solution.py:704
  6.4 4.9 %collective-permute-start.1 = (f32[272,128]{1,0:T(8,128)S(1)}, f32[272,128]{1,0:T(8,128)S(1)}, u32[]{:S(2)}, u32[]{:S(2)}) collective-permute-start(f32[272,128]{1,0:T(8,128)S(1)} %get-tuple-element.42), channel_id=1, source_target_pairs={{0,2},{2,0},{4,6},{6,4},{1,3},{3,1},{5,7},{7,5},{8,10},{10,8},{12,... | collective-permute-start | bytes 417800 | tf_op jit(solution)/shard_map/ppermute | solution.py:708
  10.1 9.3 %collective-permute-start.3 = (f32[520,128]{1,0:T(8,128)S(1)}, f32[520,128]{1,0:T(8,128)S(1)}, u32[]{:S(2)}, u32[]{:S(2)}) collective-permute-start(f32[520,128]{1,0:T(8,128)S(1)} %get-tuple-element.49), channel_id=1, source_target_pairs={{0,8},{8,0},{16,24},{24,16},{1,9},{9,1},{17,25},{25,17},{2,10},{10... | collective-permute-start | bytes 798728 | tf_op jit(solution)/shard_map/ppermute | solution.py:712
  11.3 9.4 %collective-permute-start.2 = (f32[272,128]{1,0:T(8,128)S(1)}, f32[272,128]{1,0:T(8,128)S(1)}, u32[]{:S(2)}, u32[]{:S(2)}) collective-permute-start(f32[272,128]{1,0:T(8,128)S(1)} %get-tuple-element.45), channel_id=1, source_target_pairs={{2,4},{4,2},{3,5},{5,3},{10,12},{12,10},{11,13},{13,11},{18,20},{2... | collective-permute-start | bytes 417800 | tf_op jit(solution)/shard_map/ppermute | solution.py:711
  19.4 9.3 %collective-permute-start.4 = (f32[520,128]{1,0:T(8,128)S(1)}, f32[520,128]{1,0:T(8,128)S(1)}, u32[]{:S(2)}, u32[]{:S(2)}) collective-permute-start(f32[520,128]{1,0:T(8,128)S(1)} %add.12), channel_id=1, source_target_pairs={{0,16},{8,24},{16,0},{24,8},{1,17},{9,25},{17,1},{25,9},{2,18},{10... | collective-permute-start | bytes 798728 | tf_op jit(solution)/shard_map/ppermute | solution.py:698
  24.3 4.5 %collective-permute-start.5 = (f32[528,128]{1,0:T(8,128)S(1)}, f32[528,128]{1,0:T(8,128)S(1)}, u32[]{:S(2)}, u32[]{:S(2)}) collective-permute-start(f32[528,128]{1,0:T(8,128)S(1)} %get-tuple-element.56), channel_id=1, source_target_pairs={{0,8},{8,0},{16,24},{24,16},{1,9},{9,1},{17,25},{25,17},{2,10},{10... | collective-permute-start | bytes 811016 | tf_op jit(solution)/shard_map/ppermute | solution.py:717
  28.8 1.6 %collective-permute-start.6 = (f32[520,128]{1,0:T(8,128)S(1)}, f32[520,128]{1,0:T(8,128)S(1)}, u32[]{:S(2)}, u32[]{:S(2)}) collective-permute-start(f32[520,128]{1,0:T(8,128)S(1)} %add.13.own_m), channel_id=1, source_target_pairs={{0,8},{8,0},{16,24},{24,16},{1,9},{9,1},{17,25},{25,17},{2,10},{10... | collective-permute-start | bytes 798728 | tf_op jit(solution)/shard_map/ppermute | solution.py:722
  28.9 7.7 %collective-permute-start.7 = (f32[528,128]{1,0:T(8,128)S(1)}, f32[528,128]{1,0:T(8,128)S(1)}, u32[]{:S(2)}, u32[]{:S(2)}) collective-permute-start(f32[528,128]{1,0:T(8,128)S(1)} %add.14), channel_id=1, source_target_pairs={{0,16},{8,24},{16,0},{24,8},{1,17},{9,25},{17,1},{25,9},{2,18},{10... | collective-permute-start | bytes 811016 | tf_op jit(solution)/shard_map/ppermute | solution.py:698
  36.6 2.5 %collective-permute-start.8 = (f32[528,128]{1,0:T(8,128)S(1)}, f32[528,128]{1,0:T(8,128)S(1)}, u32[]{:S(2)}, u32[]{:S(2)}) collective-permute-start(f32[528,128]{1,0:T(8,128)S(1)} %add.15.own_e), channel_id=1, source_target_pairs={{0,8},{8,0},{16,24},{24,16},{1,9},{9,1},{17,25},{25,17},{2,10},{10... | collective-permute-start | bytes 811016 | tf_op jit(solution)/shard_map/ppermute | solution.py:725

commit v8 on v5

--- a/solution.py
+++ b/solution.py
@@ -53,6 +53,9 @@
 
 def held(*arrays, space=pltpu.VMEM):
     return [pltpu.with_memory_space_constraint(x, space) for x in arrays]
+
+
+MIDDLE, EDGE_FIRST, EDGE_SECOND = 5, 3, 3
 
 
 def cost(micros):
@@ -182,8 +185,9 @@
             top, bottom = pairs[0][:, part], pairs[1][:, part]
             pay_a[at, :] = jnp.where(odd, top, bottom)
             pay_b[at, :] = jnp.where(odd, bottom, top)
-    top = fold_row(bed_v[tile_at(0), :])
-    bottom = fold_row(pltpu.roll(bed_v[tile_at(rows // SUB - 1), :], 1, 0))
+    parts = [slice(k * LANE, (k + 1) * LANE) for k in range(lanes)]
+    top = fold_row([bed_v[tile_at(0), part] for part in parts])
+    bottom = fold_row([pltpu.roll(bed_v[tile_at(rows // SUB - 1), part], 1, 0) for part in parts])
     at = pl.ds(lanes * GROUP + SUB, SUB)
     pay_a[at, :] = jnp.where(odd, top, bottom)
     pay_b[at, :] = jnp.where(odd, bottom, top)
@@ -191,9 +195,9 @@
 
 def fold_row(x):
     row = rows_of((SUB, LANE))
-    total = x[:, :LANE]
-    for k in range(1, x.shape[1] // LANE):
-        total = jnp.where(row == k, pltpu.roll(x[:, k * LANE : (k + 1) * LANE], k, 0), total)
+    total = x[0]
+    for k in range(1, len(x)):
+        total = jnp.where(row == k, pltpu.roll(x[k], k, 0), total)
     return total
 
 
@@ -256,7 +260,7 @@
 class Sweep:
     NAMES = (
         ["fc", "fr", "wc", "wr", "e1", "u1"]
-        + ["v1", "e2", "u2", "v2", "qc1", "qr1", "qc2", "qr2"]
+        + ["v1", "e2", "u2", "v2"]
     )
 
     def __init__(self, count, wide, get, emit, weights, params, refs, trim):
@@ -320,8 +324,6 @@
         self.e1[at, :] = e
         self.u1[at, :] = u
         self.v1[at, :] = v
-        self.qc1[at, :] = u * jnp.abs(u)
-        self.qr1[at, :] = v * jnp.abs(v)
 
     def step_two(self, i):
         at, after = tile_at(i), tile_at(i + 1)
@@ -330,12 +332,14 @@
             self.fc[at, :], self.fr[at, :], self.wc[at, :], self.wr[at, :],
         )
         self.e2[at, :] = e
-        if self.trim and i == self.count - 1:
-            return
         self.u2[at, :] = u
         self.v2[at, :] = v
-        self.qc2[at, :] = self.qc1[at, :] + u * jnp.abs(u)
-        self.qr2[at, :] = self.qr1[at, :] + v * jnp.abs(v)
+
+    def transport(self, *speeds):
+        total = speeds[0] * jnp.abs(speeds[0])
+        for speed in speeds[1:]:
+            total = total + speed * jnp.abs(speed)
+        return total
 
     def step_three(self, i):
         at, after = tile_at(i), tile_at(i + 1)
@@ -345,15 +349,15 @@
             wr = self.wr[at, :]
             v = self.speed_r(i, self.e2[at, :], self.e2[after, :], self.v2[at, :], wr)
             self.fr_last[2] = self.fr[at, :] * v
-            self.qr_last[...] = wr * (self.qr2[at, :] + v * jnp.abs(v))
+            self.qr_last[...] = wr * self.transport(self.v1[at, :], self.v2[at, :], v)
             return
         wc, wr = self.wc[at, :], self.wr[at, :]
+        u2, v2 = self.u2[at, :], self.v2[at, :]
         e, u, v = self.move(
-            2, i, self.e2[at, :], self.e2[after, :], self.u2[at, :], self.v2[at, :],
-            self.fc[at, :], self.fr[at, :], wc, wr,
+            2, i, self.e2[at, :], self.e2[after, :], u2, v2, self.fc[at, :], self.fr[at, :], wc, wr
         )
-        qc = wc * (self.qc2[at, :] + u * jnp.abs(u))
-        qr = wr * (self.qr2[at, :] + v * jnp.abs(v))
+        qc = wc * self.transport(self.u1[at, :], u2, u)
+        qr = wr * self.transport(self.v1[at, :], v2, v)
         change = (qc - west(qc) + qr - north(qr, self.qr_last[...])) * self.scale
         self.qr_last[...] = qr
         self.emit(i, e * (1.0 / 0.3), u, v, change)
@@ -385,61 +389,58 @@
     return read
 
 
-def quarter_writer(first, quarter, cols, hydro_out, pay):
+def chunk_writer(first, count, cols, hydro_out, pay):
     lane = lanes_of((SUB, LANE))
     lanes = cols // LANE
-    rims = [jnp.zeros((SUB, LANE), jnp.float32)]
+    half = count // 2
+    mine = lax.axis_index("cond") % 2
+    rims = [jnp.zeros((SUB, LANE), jnp.float32)] * 2
 
     def emit(i, e, u, v, change):
         at = tile_at(first + i)
         for k, value in enumerate((e, u, v)):
             hydro_out[0, k, at, :] = value[:, :cols]
-        g = i - 1
+        which, g = divmod(i - 1, half)
+        slot = jnp.where(mine == which, 1, 0)
         for k in range(lanes):
-            pay[tile_at(k * quarter + g), :] = change[:, k * LANE : (k + 1) * LANE]
-        rims[0] = jnp.where(lane // 2 == g, pltpu.roll(change[:, cols:], 1 + 2 * g, 1), rims[0])
-        if g == quarter - 1:
-            pay[tile_at(lanes * quarter), :] = rims[0]
+            pay[slot, tile_at(k * half + g), :] = change[:, k * LANE : (k + 1) * LANE]
+        rims[which] = jnp.where(lane // 2 == g, pltpu.roll(change[:, cols:], 1 + 2 * g, 1), rims[which])
+        if g == half - 1:
+            pay[slot, tile_at(lanes * half), :] = rims[which]
 
     return emit
 
 
-def middle_kernel(own, weights, params, root, a, b, stress, hydro, side, *refs):
-    hydro_out, pay, *refs = refs[1:] if own else refs
+def middle_kernel(weights, params, root, a, b, stress, hydro, side, hydro_out, pay, *refs):
     rows, cols = root.shape
-    quarter = rows // SUB // 4
+    blocks = rows // SUB
     read = reader(root, a, b, stress, hydro, side, *side_lanes(lax.axis_index("tx") == 0))
-    mine = lax.axis_index("cond") % 2
-    lower_half = mine == (1 if own else 0)
-    first = jnp.where(lower_half, 2 * quarter, quarter) - 1
-    emit = quarter_writer(first, quarter, cols, hydro_out, pay)
+    first = blocks // 4 - 1
+    write = chunk_writer(first, blocks // 2, cols, hydro_out, pay)
     Sweep(
-        quarter + 2, cols + LANE, lambda f, i: read(f, first + i), emit, weights, params, refs, True
+        blocks // 2 + 2, cols + LANE, lambda f, i: read(f, first + i), write, weights, params, refs, True
     ).run()
 
 
-def middle(own, weights, params, fields, side, hydro=None):
+def middle(weights, params, fields, side):
     rows, cols = fields[0].shape
-    given = (hydro,) if own else ()
     return pl.pallas_call(
-        functools.partial(middle_kernel, own),
-        name="middle_own" if own else "middle_other",
+        middle_kernel,
+        name="middle",
         out_shape=[
             pltpu.VMEM(fields[4].shape, jnp.float32),
-            pltpu.VMEM((cols // LANE * rows // 4 + SUB, LANE), jnp.float32),
+            pltpu.VMEM((2, cols // LANE * rows // 4 + SUB, LANE), jnp.float32),
         ],
-        in_specs=[SMEM, SMEM] + [VMEM] * (6 + own),
+        in_specs=[SMEM, SMEM] + [VMEM] * 6,
         out_specs=[VMEM, VMEM],
-        scratch_shapes=Sweep.scratch(rows // SUB // 4 + 2, cols + LANE),
-        input_output_aliases={8: 0} if own else {},
-        compiler_params=pltpu.CompilerParams(vmem_limit_bytes=10 * MIB),
-        cost_estimate=cost(4),
-    )(weights, params, *held(*fields, side, *given))
+        scratch_shapes=Sweep.scratch(rows // SUB // 2 + 2, cols + LANE),
+        compiler_params=pltpu.CompilerParams(vmem_limit_bytes=12 * MIB),
+        cost_estimate=cost(MIDDLE),
+    )(weights, params, *held(*fields, side))
 
 
 def edge_kernel(
-    own, weights, params, root, a, b, stress, hydro, side, far_a, far_b, hydro_in,
-    hydro_out, pay, ends, *refs,
+    second, weights, params, root, a, b, stress, hydro, side, far, hydro_in, hydro_out, pay, ends, *refs
 ):
     rows, cols = root.shape
     blocks = rows // SUB
@@ -447,9 +448,7 @@
     lanes = cols // LANE
     unfold, valid = side_lanes(lax.axis_index("tx") == 0)
     read = reader(root, a, b, stress, hydro, side, unfold, valid)
-    mine = lax.axis_index("cond") % 2
-    top = mine == (0 if own else 1)
-    from_a = top == (lax.axis_index("ty") % 2 == 1)
+    top = lax.axis_index("ty") % 2 == (0 if second else 1)
     first = jnp.where(top, -1, blocks - quarter - 1)
 
     inner = jnp.where(top, quarter, blocks - quarter - 1)
@@ -458,12 +457,10 @@
         body = read(f, inner)
         parts = []
         for k in range(lanes):
-            at = pl.ds(k * GROUP + f // 2 * SUB, SUB)
-            part = jnp.where(from_a, far_a[at, :], far_b[at, :])
+            part = far[pl.ds(k * GROUP + f // 2 * SUB, SUB), :]
             moved = pltpu.roll(part, HALO, 0)
             parts.append(jnp.where(top, moved, part) if f % 2 == 0 else jnp.where(top, part, moved))
-        corner = jnp.where(from_a, far_a[corners, :], far_b[corners, :])
-        corner = jnp.where(top, unfold(corner, (FOLD - 1) * FIELDS + f), unfold(corner, f))
+        corner = unfold(far[corners, :], jnp.where(top, (FOLD - 1) * FIELDS, 0) + f)
         if f == 0:
             corner = jnp.where(valid, corner, 0.0)
         outer = jnp.concatenate(parts + [corner], axis=1)
@@ -475,44 +472,48 @@
             return ends[0 if i == 0 else 1, f]
         return read(f, first + i)
 
-    emit = quarter_writer(first, quarter, cols, hydro_out, pay)
+    write = chunk_writer(first, quarter, cols, hydro_out, pay)
     outside = []
 
     def finish(i, e, u, v, change):
         if i == 0:
             outside.append(pltpu.roll(change[:, :cols], 1, 0))
         elif i == quarter + 1:
-            pay[tile_at(lanes * quarter + 1), :] = fold_row(jnp.where(top, outside[0], change[:, :cols]))
+            rim = jnp.where(top, outside[0], change[:, :cols])
+            rim = fold_row([rim[:, k * LANE : (k + 1) * LANE] for k in range(lanes)])
+            for slot in range(2):
+                pay[slot, tile_at(lanes * quarter // 2 + 1), :] = rim
         else:
-            emit(i, e, u, v, change)
+            write(i, e, u, v, change)
 
     Sweep(quarter + 2, cols + LANE, get, finish, weights, params, refs, False).run()
 
 
-def edge(own, weights, params, fields, side, far_a, far_b, hydro):
+def edge(second, weights, params, fields, side, far, hydro):
     rows, cols = fields[0].shape
     wide = cols + LANE
     return pl.pallas_call(
-        functools.partial(edge_kernel, own),
-        name="edge_own" if own else "edge_other",
+        functools.partial(edge_kernel, second),
+        name="edge_second" if second else "edge_first",
         out_shape=[
             pltpu.VMEM(hydro.shape, jnp.float32),
-            pltpu.VMEM((cols // LANE * rows // 4 + 2 * SUB, LANE), jnp.float32),
+            pltpu.VMEM((2, cols // LANE * rows // 8 + 2 * SUB, LANE), jnp.float32),
         ],
-        in_specs=[SMEM, SMEM] + [VMEM] * 9,
+        in_specs=[SMEM, SMEM] + [VMEM] * 8,
         out_specs=[VMEM, VMEM],
         scratch_shapes=[pltpu.VMEM((2, FIELDS, SUB, wide), jnp.float32)]
         + Sweep.scratch(rows // SUB // 4 + 2, wide),
-        input_output_aliases={10: 0},
+        input_output_aliases={9: 0},
         compiler_params=pltpu.CompilerParams(vmem_limit_bytes=12 * MIB),
-        cost_estimate=cost(3),
-    )(weights, params, *held(*fields, side, far_a, far_b, hydro))
+        cost_estimate=cost(EDGE_SECOND if second else EDGE_FIRST),
+    )(weights, params, *held(*fields, side, far, hydro))
 
 
 class Update:
-    def __init__(self, bed, side, far_a, far_b, own_m, got_m, own_e, got_e, change_v, next_v):
-        self.bed, self.side, self.far_a, self.far_b = bed, side, far_a, far_b
-        self.parts = {"m": (own_m, got_m), "e": (own_e, got_e)}
+    def __init__(self, odd, bed, side, far_a, far_b, middle, first, second, change_v, next_v):
+        self.bed, self.side = bed, side
+        self.far = (far_a, far_b) if odd else (far_b, far_a)
+        self.parts = [first if odd else second, middle, second if odd else first]
         self.change_v, self.next_v = change_v, next_v
         rows, self.cols = bed.shape
         self.blocks = rows // SUB
@@ -522,7 +523,6 @@
         self.side_bed = side[pl.ds(side.shape[0] - SUB, SUB), :]
         self.drop_bed = jnp.where(lax.axis_index("tx") == 0, 0, 1)
         self.mine = lax.axis_index("cond") % 2
-        self.odd = lax.axis_index("ty") % 2 == 1
         col = lanes_of((SUB, self.wide))
         last_c = lax.axis_index("tx") == lax.axis_size("tx") - 1
         first_c = lax.axis_index("tx") == 0
@@ -530,17 +530,15 @@
         self.last_row = rows_of((SUB, self.wide)) == SUB - 1
         self.rims = {}
 
-    def merged(self, q, block):
-        own, got = self.parts["e" if q in (0, 3) else "m"]
+    def merged(self, chunk, half, block):
+        own, got = self.parts[chunk]
         at = tile_at(block)
-        return jnp.where(self.mine == q // 2, own[at, :], got[at, :])
-
-    def outside(self, q):
-        at = pl.ds(self.lanes * GROUP + SUB, SUB)
-        a, b = self.far_a[at, :], self.far_b[at, :]
-        bed = jnp.where(self.odd, a, b) if q == 0 else jnp.where(self.odd, b, a)
-        z = bed + self.merged(q, self.lanes * self.quarter + 1)
-        target = SUB - 1 if q == 0 else 0
+        return jnp.where(self.mine == half, own[at, :], got[at, :])
+
+    def outside(self, chunk):
+        bed = self.far[0 if chunk == 0 else 1][pl.ds(self.lanes * GROUP + SUB, SUB), :]
+        z = bed + self.merged(chunk, 0, self.lanes * self.quarter // 2 + 1)
+        target = SUB - 1 if chunk == 0 else 0
         parts = [pltpu.roll(z, (SUB + target - k) % SUB, 0) if (target - k) % SUB else z for k in range(self.lanes)]
         return jnp.concatenate(parts + [jnp.zeros((SUB, LANE), jnp.float32)], axis=1)
 
@@ -548,15 +546,20 @@
         if b == -1:
             return self.outside(0)
         if b == self.blocks:
-            return self.outside(3)
-        q, g = divmod(b, self.quarter)
-        change = jnp.concatenate([self.merged(q, k * self.quarter + g) for k in range(self.lanes)], axis=1)
-        if keep:
+            return self.outside(2)
+        q = b // self.quarter
+        chunk = (0, 1, 1, 2)[q]
+        start, count = ((0, self.quarter), (self.quarter, 2 * self.quarter), (3 * self.quarter, self.quarter))[chunk]
+        half, g = divmod(b - start, count // 2)
+        change = jnp.concatenate(
+            [self.merged(chunk, half, k * (count // 2) + g) for k in range(self.lanes)], axis=1
+        )
+        if keep(q):
             self.change_v[tile_at(b), :] = change
-        if q not in self.rims:
-            self.rims[q] = self.merged(q, self.lanes * self.quarter)
+        if (chunk, half) not in self.rims:
+            self.rims[chunk, half] = self.merged(chunk, half, self.lanes * count // 2)
         cols_bed = pltpu.roll(self.side_bed, 2 * LANE - self.drop_bed - b, 1)
-        cols_change = pltpu.roll(self.rims[q], LANE - 1 - 2 * g, 1)
+        cols_change = pltpu.roll(self.rims[chunk, half], LANE - 1 - 2 * g, 1)
         return jnp.concatenate([self.bed[tile_at(b), :] + change, cols_bed + cols_change], axis=1)
 
     def spill(self, slope):
@@ -570,7 +573,7 @@
             return jnp.where((lax.axis_index("ty") == lax.axis_size("ty") - 1) & self.last_row, 0.0, out)
         return out
 
-    def run(self, first, stop, keep, after=lambda b: None):
+    def run(self, first, stop, keep):
         z = self.level(first - 1, keep)
         lower = self.level(first, keep)
         gr = self.south_face(z, lower, first - 1)
@@ -580,79 +583,90 @@
             gc = jnp.where(self.shut_c, 0.0, self.spill(east(z) - z))
             out = z + gc - west(gc) + gr - north(gr, gr_above)
             self.next_v[tile_at(b), :] = out[:, : self.cols]
-            after(b)
-
-
-def bed_middle_kernel(
-    bed, side, far_a, far_b, own_m, got_m, hydro, bed_next, bed_change, hydro_out, change_v, next_v, sems
-):
-    rows = bed.shape[0]
-    quarter = rows // SUB // 4
-    copies = [pltpu.make_async_copy(hydro, hydro_out, sems.at[0])]
-    copies[0].start()
-    update = Update(bed, side, far_a, far_b, own_m, got_m, None, None, change_v, next_v)
-    update.run(quarter + 1, 3 * quarter - 1, True)
-    for src, dst, low, high in (
-        (change_v, bed_change, quarter, 3 * quarter),
-        (next_v, bed_next, quarter + 1, 3 * quarter - 1),
-    ):
+
+
+def by_row(run):
+    odd = lax.axis_index("ty") % 2 == 1
+    pl.when(odd)(lambda: run(True))
+    pl.when(jnp.logical_not(odd))(lambda: run(False))
+
+
+def send_rows(copies, sems):
+    started = []
+    for n, (src, dst, low, high) in enumerate(copies):
         at = pl.ds(low * SUB, (high - low) * SUB)
-        copies.append(pltpu.make_async_copy(src.at[at], dst.at[at], sems.at[len(copies)]))
-        copies[-1].start()
-    for copy in copies:
+        started.append(pltpu.make_async_copy(src.at[at], dst.at[at], sems.at[n]))
+        started[-1].start()
+    for copy in started:
         copy.wait()
 
 
-def bed_edge_kernel(
-    bed, side, far_a, far_b, own_m, got_m, own_e, got_e, next_in, change_in, bed_next, bed_change,
+def bed_early_kernel(
+    bed, side, far_a, far_b, own_m, got_m, own_a, got_a, hydro, bed_next, bed_change, hydro_out,
     change_v, next_v, sems,
 ):
-    rows = bed.shape[0]
-    blocks = rows // SUB
+    blocks = bed.shape[0] // SUB
     quarter = blocks // 4
-    update = Update(bed, side, far_a, far_b, own_m, got_m, own_e, got_e, change_v, next_v)
-    copies = []
-
-    def send(src, dst, low, high):
-        at = pl.ds(low * SUB, (high - low) * SUB)
-        copies.append(pltpu.make_async_copy(src.at[at], dst.at[at], sems.at[len(copies)]))
-        copies[-1].start()
-
-    update.run(0, quarter + 1, True)
-    send(change_v, bed_change, 0, quarter)
-    send(next_v, bed_next, 0, quarter + 1)
-    update.run(blocks - quarter - 1, blocks, True)
-    send(change_v, bed_change, blocks - quarter, blocks)
-    send(next_v, bed_next, blocks - quarter - 1, blocks)
-    for copy in copies:
-        copy.wait()
+    state = pltpu.make_async_copy(hydro, hydro_out, sems.at[2])
+    state.start()
+
+    def run(odd):
+        update = Update(
+            odd, bed, side, far_a, far_b, (own_m, got_m), (own_a, got_a), None, change_v, next_v
+        )
+        rows = (0, 3 * quarter - 1) if odd else (quarter + 1, blocks)
+        changes = (0, 3 * quarter) if odd else (quarter, blocks)
+        update.run(*rows, lambda q: True)
+        send_rows([(change_v, bed_change, *changes), (next_v, bed_next, *rows)], sems)
+
+    by_row(run)
+    state.wait()
+
+
+def bed_late_kernel(
+    bed, side, far_a, far_b, own_m, got_m, own_b, got_b, next_in, change_in, bed_next, bed_change,
+    change_v, next_v, sems,
+):
+    blocks = bed.shape[0] // SUB
+    quarter = blocks // 4
+
+    def run(odd):
+        update = Update(
+            odd, bed, side, far_a, far_b, (own_m, got_m), None, (own_b, got_b), change_v, next_v
+        )
+        rows = (3 * quarter - 1, blocks) if odd else (0, quarter + 1)
+        changes = (3 * quarter, blocks) if odd else (0, quarter)
+        update.run(*rows, lambda q: q in (0, 3))
+        send_rows([(change_v, bed_change, *changes), (next_v, bed_next, *rows)], sems)
+
+    by_row(run)
 
 
 def bed_scratch(rows, cols):
     return [
         pltpu.VMEM((rows, cols), jnp.float32),
         pltpu.VMEM((rows, cols), jnp.float32),
-        pltpu.SemaphoreType.DMA((4,)),
+        pltpu.SemaphoreType.DMA((3,)),
     ]
 
 
-def bed_middle(bed, side, far_a, far_b, own_m, got_m, hydro):
+def bed_early(bed, side, far_a, far_b, merged_m, merged_a, hydro):
     return pl.pallas_call(
-        bed_middle_kernel,
-        name="bed_middle",
+        bed_early_kernel,
+        name="bed_early",
         out_shape=[pltpu.HBM(x.shape, jnp.float32) for x in (bed, bed, hydro)],
-        in_specs=[VMEM] * 7,
+        in_specs=[VMEM] * 9,
         out_specs=[ANY] * 3,
         scratch_shapes=bed_scratch(*bed.shape),
         compiler_params=pltpu.CompilerParams(vmem_limit_bytes=6 * MIB),
         cost_estimate=cost(4),
-    )(*held(bed, side, far_a, far_b, own_m, got_m, hydro))
-
-
-def bed_edge(bed, side, far_a, far_b, own_m, got_m, own_e, got_e, bed_next, bed_change):
+    )(*held(bed, side, far_a, far_b, *merged_m, *merged_a, hydro))
+
+
+def bed_late(bed, side, far_a, far_b, merged_m, merged_b, bed_next, bed_change):
     return pl.pallas_call(
-        bed_edge_kernel,
-        name="bed_edge",
+        bed_late_kernel,
+        name="bed_late",
         out_shape=[pltpu.HBM(bed.shape, jnp.float32)] * 2,
         in_specs=[VMEM] * 8 + [ANY] * 2,
         out_specs=[ANY] * 2,
@@ -661,7 +675,7 @@
         compiler_params=pltpu.CompilerParams(vmem_limit_bytes=6 * MIB),
         cost_estimate=cost(2),
     )(
-        *held(bed, side, far_a, far_b, own_m, got_m, own_e, got_e),
+        *held(bed, side, far_a, far_b, *merged_m, *merged_b),
         *held(bed_next, bed_change, space=pltpu.HBM),
     )
 
@@ -689,26 +703,27 @@
     fields = (*terms, wave_stress, hydro_state)
     far_a, far_b = add_corners(side, far_a, far_b)
     far_a = lax.ppermute(far_a, "ty", pairs(0))
-    hydro, pay = middle(False, weights, cond_params, fields, side)
-    hydro, far_a, far_b = lax.optimization_barrier((hydro, far_a, far_b))
+    hydro, pay_m = middle(weights, cond_params, fields, side)
+    hydro, pay_m, far_a, far_b = lax.optimization_barrier((hydro, pay_m, far_a, far_b))
+    got_m = lax.ppermute(pay_m[0], "cond", swap)
     far_b = lax.ppermute(far_b, "ty", pairs(1))
-    got = lax.ppermute(pay, "cond", swap)
-    hydro, pay = middle(True, weights, cond_params, fields, side, hydro)
-    part_m = pay + got
+    part_m = pay_m[1] + got_m
     hydro, part_m = lax.optimization_barrier((hydro, part_m))
-    hydro, pay = edge(False, weights, cond_params, fields, side, far_a, far_b, hydro)
-    got = lax.ppermute(pay, "cond", swap)
-    hydro, pay = edge(True, weights, cond_params, fields, side, far_a, far_b, hydro)
+    hydro, pay_a = edge(False, weights, cond_params, fields, side, far_a, hydro)
+    got_a = lax.ppermute(pay_a[0], "cond", swap)
+    hydro, pay_b = edge(True, weights, cond_params, fields, side, far_b, hydro)
     own_m, hydro = over_chips(part_m, hydro)
-    part_e = pay + got
-    own_m, _ = lax.optimization_barrier((own_m, part_e))
-    got_m = lax.ppermute(own_m, "cond", swap)
-    bed_next, bed_change, hydro = bed_middle(bed, side, far_a, far_b, own_m, got_m, hydro)
-    own_e, (bed_next, bed_change) = over_chips(part_e, (bed_next, bed_change))
-    got_e = lax.ppermute(own_e, "cond", swap)
-    bed_next, bed_change = bed_edge(
-        bed, side, far_a, far_b, own_m, got_m, own_e, got_e, bed_next, bed_change
-    )
+    own_m, got_a = lax.optimization_barrier((own_m, got_a))
+    part_a = pay_a[1] + got_a
+    got_b = lax.ppermute(pay_b[0], "cond", swap)
+    part_b = pay_b[1] + got_b
+    merged_m = (own_m, lax.ppermute(own_m, "cond", swap))
+    own_a, _ = over_chips(part_a, part_b)
+    merged_a = (own_a, lax.ppermute(own_a, "cond", swap))
+    bed_next, bed_change, hydro = bed_early(bed, side, far_a, far_b, merged_m, merged_a, hydro)
+    own_b, (bed_next, bed_change) = over_chips(part_b, (bed_next, bed_change))
+    merged_b = (own_b, lax.ppermute(own_b, "cond", swap))
+    bed_next, bed_change = bed_late(bed, side, far_a, far_b, merged_m, merged_b, bed_next, bed_change)
     return bed_next, bed_change, hydro
 
 

time: 40.1 us -> 42 us (1.047)
  starting transfers between devices: 12.1 us -> 13.7 us
    ppermute x4 -> x6, starting transfers between devices: 3.84 us -> 5.55 us  [the longest x1 1.39 us: shards(): merged_a = (own_a, lax.ppermute(own_a, 'cond', swap))]
    ppermute x2 -> x3, waiting for transfers between devices: 3.92 us -> 4.46 us  [over_chips(): got = lax.ppermute(part, 'cond', [(i, i ^ reach) for i in range(nc)])]
    ppermute x4 -> x6, waiting for transfers between devices: 1.49 us -> 1.41 us  [the longest x1 1 us: shards(): merged_b = (own_b, lax.ppermute(own_b, 'cond', swap))]
    pallas_call x6 -> x5, Pallas kernels: 16.8 us -> 16.7 us  [the longest x1 6.5 us: middle(): pl.pallas_call(middle_kernel, name='middle', out_shape=[pltpu.VMEM(fields...]
    ppermute x2 -> x3, starting transfers between devices: 2.48 us -> 2.5 us  [over_chips(): got = lax.ppermute(part, 'cond', [(i, i ^ reach) for i in range(nc)])]
  transfers between devices with their start and end apart: 9 -> 12, of which waited for: 4 -> 4; matrix products, arithmetic and copies ran while one was open for 0% -> 0% of each run, Pallas kernels for 44% -> 43%
where the time goes in v8:
time: 42 us; the launch traced here: 41.8 us
  Pallas kernels  21.1 us (50%)
  starting transfers between devices  13.7 us (33%)
  waiting for transfers between devices  5.88 us (14%)
  between operations  0.84 us (2%)
    pallas_call x1, Pallas kernels, middle(): pl.pallas_call(middle_kernel, name='middle', out_shape=[pltpu.VMEM(fields...  6.5 us
    pallas_call x2, Pallas kernels, edge(): pl.pallas_call(functools.partial(edge_kernel, second), name='edge_second'...  6.41 us
    ppermute x3, waiting for transfers between devices, over_chips(): got = lax.ppermute(part, 'cond', [(i, i ^ reach) for i in range(nc)])  4.46 us
    ppermute x1, starting transfers between devices, shards(): far_b = lax.ppermute(far_b, 'ty', pairs(1))  4.32 us
    pallas_call x1, Pallas kernels, bed_early(): pl.pallas_call(bed_early_kernel, name='bed_early', out_shape=[pltpu.HBM(x...  2.65 us
    pallas_call x1, Pallas kernels, prepare(): pl.pallas_call(prepare_kernel, name='prepare', out_shape=[tile] * 4 + [pl...  2.58 us
    ppermute x3, starting transfers between devices, over_chips(): got = lax.ppermute(part, 'cond', [(i, i ^ reach) for i in range(nc)])  2.5 us
    pallas_call x1, Pallas kernels, pack_side(): pl.pallas_call(pack_side_kernel, name='pack_side', out_shape=pltpu.VMEM((...  1.77 us
  transfers between devices with their start and end apart: 12, of which 4 were waited for; matrix products, arithmetic and copies ran while one was open for 0% of the time, Pallas kernels for 43%

profile of v8, /device:TPU:9, one launch (start us, length us, event | category | flops | bytes accessed | tf_op | source)
XLA Modules:
  0.0 41.8 jit_solution(9493745829923360192)
XLA Ops:
  0.6 1.8 %pack_side.1 = f32[72,128]{1,0:T(8,128)S(1)} custom-call(f32[1,4]{1,0:T(1,128)} %params.5, f32[256,1024]{1,0:T(8,128)} %bed.3, s32[256,1024]{1,0:T(8,128)} %mask.3, s32[256,1024]{1,0:T(8,128)} %kind.3, f32[1,2,256,1024]{3,2,1,0:T(8,128)} %stress.9, f32[1,3,256,1024]{3,2,1,0:T(8,128)} %hydro.9), custom_call_target="tpu_custom_call" | custom-call | flops 2000000000 | tf_op jit(solution)/shard_map/pack_side/pallas_call | solution.py:117
  2.5 1.3 %collective-permute-start = (f32[72,128]{1,0:T(8,128)S(1)}, f32[72,128]{1,0:T(8,128)S(1)}, u32[]{:S(2)}, u32[]{:S(2)}) collective-permute-start(f32[72,128]{1,0:T(8,128)S(1)} %pack_side.1), channel_id=1, source_target_pairs={{0,1},{1,0},{2,3},{3,2},{4,5},{5,4},{6,7},{7,6},{8,9},{9,8},{10,11... | collective-permute-start | bytes 110600 | tf_op jit(solution)/shard_map/ppermute | solution.py:701
  3.8 2.6 %prepare.1 = (f32[256,1024]{1,0:T(8,128)S(1)}, f32[256,1024]{1,0:T(8,128)S(1)}, f32[256,1024]{1,0:T(8,128)S(1)}, f32[256,1024]{1,0:T(8,128)S(1)}, f32[272,128]{1,0:T(8,128)S(1)}, /*index=5*/f32[272,128]{1,0:T(8,128)S(1)}) custom-call(f32[1,4]{1,0:T(1,128)} %params.5, f32[256,1024]{1,0:T(8,128)} %bed.3, s32[256,1024]{1,0:T(8,128)} %mask.3, s32[256,1024]{1,0:T(8,128)} %kind.3, ...), custom_call_target="tpu_custom_call" | custom-call | flops 2000000000 | tf_op jit(solution)/shard_map/prepare/pallas_call | solution.py:207
  6.4 0.1 collective-permute-start.1
  6.5 6.5 %middle.1 = (f32[1,3,256,1024]{3,2,1,0:T(8,128)S(1)}, f32[2,520,128]{2,1,0:T(8,128)S(1)}) custom-call(s32[4]{0:T(128)S(1)} %copy-done.3, f32[1,4]{1,0:T(1,128)S(1)} %copy-done.2, f32[256,1024]{1,0:T(8,128)S(1)} %get-tuple-element.37.root, f32[256,1024]{1,0:T(8,128)S(1)} %get-tuple-element.38.a, f32[256,1024]{1,0:T(8,128)S(1)} %get-tuple-element.39.b, ...), custom_call_target="tpu_custom_call" | custom-call | flops 5000000000 | tf_op jit(solution)/shard_map/middle/pallas_call | solution.py:427
  13.1 1.2 %collective-permute-start.3 = (f32[520,128]{1,0:T(8,128)S(1)}, f32[520,128]{1,0:T(8,128)S(1)}, u32[]{:S(2)}, u32[]{:S(2)}) collective-permute-start(f32[520,128]{1,0:T(8,128)S(1)} %slice_bitcast_fusion), channel_id=1, source_target_pairs={{0,8},{8,0},{16,24},{24,16},{1,9},{9,1},{17,25},{25,17},{2,10},{10... | collective-permute-start | bytes 798728 | tf_op jit(solution)/shard_map/ppermute | solution.py:708
  14.3 4.3 %collective-permute-start.2 = (f32[272,128]{1,0:T(8,128)S(1)}, f32[272,128]{1,0:T(8,128)S(1)}, u32[]{:S(2)}, u32[]{:S(2)}) collective-permute-start(f32[272,128]{1,0:T(8,128)S(1)} %get-tuple-element.47), channel_id=1, source_target_pairs={{2,4},{4,2},{3,5},{5,3},{10,12},{12,10},{11,13},{13,11},{18,20},{2... | collective-permute-start | bytes 417800 | tf_op jit(solution)/shard_map/ppermute | solution.py:709
  18.6 0.1 bitcast_add_fusion
  18.6 1.3 %collective-permute-start.4 = (f32[520,128]{1,0:T(8,128)S(1)}, f32[520,128]{1,0:T(8,128)S(1)}, u32[]{:S(2)}, u32[]{:S(2)}) collective-permute-start(f32[520,128]{1,0:T(8,128)S(1)} %bitcast_add_fusion), channel_id=1, source_target_pairs={{0,16},{8,24},{16,0},{24,8},{1,17},{9,25},{17,1},{25,9},{2,18},{10... | collective-permute-start | bytes 798728 | tf_op jit(solution)/shard_map/ppermute | solution.py:695
  19.9 3.2 %edge_first.1 = (f32[1,3,256,1024]{3,2,1,0:T(8,128)S(1)}, f32[2,272,128]{2,1,0:T(8,128)S(1)}) custom-call(s32[4]{0:T(128)S(1)} %copy-done.3, f32[1,4]{1,0:T(1,128)S(1)} %copy-done.2, f32[256,1024]{1,0:T(8,128)S(1)} %get-tuple-element.37.root, f32[256,1024]{1,0:T(8,128)S(1)} %get-tuple-element.38.a, ...), custom_call_target="tpu_custom_call", output_to_operand_aliasing={{0}: (9, {})} | custom-call | flops 3000000000 | tf_op jit(solution)/shard_map/edge_first/pallas_call | solution.py:495
  23.1 0.7 %collective-permute-start.5 = (f32[272,128]{1,0:T(8,128)S(1)}, f32[272,128]{1,0:T(8,128)S(1)}, u32[]{:S(2)}, u32[]{:S(2)}) collective-permute-start(f32[272,128]{1,0:T(8,128)S(1)} %slice_bitcast_fusion.2), channel_id=1, source_target_pairs={{0,8},{8,0},{16,24},{24,16},{1,9},{9,1},{17,25},{25,17},{2,10},{10... | collective-permute-start | bytes 417800 | tf_op jit(solution)/shard_map/ppermute | solution.py:713
  23.8 3.2 %edge_second.1 = (f32[1,3,256,1024]{3,2,1,0:T(8,128)S(1)}, f32[2,272,128]{2,1,0:T(8,128)S(1)}) custom-call(s32[4]{0:T(128)S(1)} %copy-done.3, f32[1,4]{1,0:T(1,128)S(1)} %copy-done.2, f32[256,1024]{1,0:T(8,128)S(1)} %get-tuple-element.37.root, f32[256,1024]{1,0:T(8,128)S(1)} %get-tuple-element.38.a, ...), custom_call_target="tpu_custom_call", output_to_operand_aliasing={{0}: (9, {})} | custom-call | flops 3000000000 | tf_op jit(solution)/shard_map/edge_second/pallas_call | solution.py:495
  27.0 0.1 collective-permute-start.7
  27.2 0.6 %collective-permute-start.9 = (f32[272,128]{1,0:T(8,128)S(1)}, f32[272,128]{1,0:T(8,128)S(1)}, u32[]{:S(2)}, u32[]{:S(2)}) collective-permute-start(f32[272,128]{1,0:T(8,128)S(1)} %bitcast_add_fusion.1), channel_id=1, source_target_pairs={{0,16},{8,24},{16,0},{24,8},{1,17},{9,25},{17,1},{25,9},{2,18},{10... | collective-permute-start | bytes 417800 | tf_op jit(solution)/shard_map/ppermute | solution.py:695
  27.8 1.3 %collective-permute-start.6 = (f32[520,128]{1,0:T(8,128)S(1)}, f32[520,128]{1,0:T(8,128)S(1)}, u32[]{:S(2)}, u32[]{:S(2)}) collective-permute-start(f32[520,128]{1,0:T(8,128)S(1)} %add.19.own_m), channel_id=1, source_target_pairs={{0,8},{8,0},{16,24},{24,16},{1,9},{9,1},{17,25},{25,17},{2,10},{10... | collective-permute-start | bytes 798728 | tf_op jit(solution)/shard_map/ppermute | solution.py:720
  29.2 2.9 %collective-permute-done.9 = f32[272,128]{1,0:T(8,128)S(1)} collective-permute-done((f32[272,128]{1,0:T(8,128)S(1)}, f32[272,128]{1,0:T(8,128)S(1)}, u32[]{:S(2)}, u32[]{:S(2)}) %collective-permute-start.9) | collective-permute-done | bytes 139296 | tf_op jit(solution)/shard_map/ppermute | solution.py:695
  32.0 1.4 %collective-permute-start.10 = (f32[272,128]{1,0:T(8,128)S(1)}, f32[272,128]{1,0:T(8,128)S(1)}, u32[]{:S(2)}, u32[]{:S(2)}) collective-permute-start(f32[272,128]{1,0:T(8,128)S(1)} %add.22.own_a), channel_id=1, source_target_pairs={{0,8},{8,0},{16,24},{24,16},{1,9},{9,1},{17,25},{25,17},{2,10},{10... | collective-permute-start | bytes 417800 | tf_op jit(solution)/shard_map/ppermute | solution.py:722
  33.4 0.6 %collective-permute-start.8 = (f32[272,128]{1,0:T(8,128)S(1)}, f32[272,128]{1,0:T(8,128)S(1)}, u32[]{:S(2)}, u32[]{:S(2)}) collective-permute-start(f32[272,128]{1,0:T(8,128)S(1)} %bitcast_add_fusion.2), channel_id=1, source_target_pairs={{0,16},{8,24},{16,0},{24,8},{1,17},{9,25},{17,1},{25,9},{2,18},{10... | collective-permute-start | bytes 417800 | tf_op jit(solution)/shard_map/ppermute | solution.py:695
  34.0 0.4 collective-permute-done.10.got_a
  34.4 2.6 %bed_early.1 = (f32[256,1024]{1,0:T(8,128)}, f32[256,1024]{1,0:T(8,128)}, f32[1,3,256,1024]{3,2,1,0:T(8,128)}) custom-call(f32[256,1024]{1,0:T(8,128)S(1)} %get-tuple-element.36.bed, f32[72,128]{1,0:T(8,128)S(1)} %collective-permute-done.side, f32[272,128]{1,0:T(8,128)S(1)} %collective-permute-done.1.far.far_a, ...), custom_call_target="tpu_custom_call" | custom-call | flops 4000000000 | tf_op jit(solution)/shard_map/bed_early/pallas_call | solution.py:654
  37.1 1.6 %collective-permute-done.8 = f32[272,128]{1,0:T(8,128)S(1)} collective-permute-done((f32[272,128]{1,0:T(8,128)S(1)}, f32[272,128]{1,0:T(8,128)S(1)}, u32[]{:S(2)}, u32[]{:S(2)}) %collective-permute-start.8) | collective-permute-done | bytes 139296 | tf_op jit(solution)/shard_map/ppermute | solution.py:695
  38.7 0.9 %collective-permute-start.11 = (f32[272,128]{1,0:T(8,128)S(1)}, f32[272,128]{1,0:T(8,128)S(1)}, u32[]{:S(2)}, u32[]{:S(2)}) collective-permute-start(f32[272,128]{1,0:T(8,128)S(1)} %add.23.own_b), channel_id=1, source_target_pairs={{0,8},{8,0},{16,24},{24,16},{1,9},{9,1},{17,25},{25,17},{2,10},{10... | collective-permute-start | bytes 417800 | tf_op jit(solution)/shard_map/ppermute | solution.py:725
  39.6 1.0 %collective-permute-done.11.got_b = f32[272,128]{1,0:T(8,128)S(1)} collective-permute-done((f32[272,128]{1,0:T(8,128)S(1)}, f32[272,128]{1,0:T(8,128)S(1)}, u32[]{:S(2)}, u32[]{:S(2)}) %collective-permute-start.11) | collective-permute-done | bytes 139296 | tf_op jit(solution)/shard_map/ppermute | solution.py:725
  40.6 1.2 %bed_late.1 = (f32[256,1024]{1,0:T(8,128)}, f32[256,1024]{1,0:T(8,128)}) custom-call(f32[256,1024]{1,0:T(8,128)S(1)} %get-tuple-element.36.bed, f32[72,128]{1,0:T(8,128)S(1)} %collective-permute-done.side, f32[272,128]{1,0:T(8,128)S(1)} %collective-permute-done.1.far.far_a, ...), custom_call_target="tpu_custom_call", output_to_operand_aliasing={{0}: (8, {}), {1}: (9, {})} | custom-call | flops 2000000000 | tf_op jit(solution)/shard_map/bed_late/pallas_call | solution.py:667
  (25 shorter events, 0.2 us)
Async XLA Ops:
  2.4 4.1 %copy-start = (f32[1,3,256,1024]{3,2,1,0:T(8,128)S(1)}, f32[1,3,256,1024]{3,2,1,0:T(8,128)}, u32[]{:S(2)}) copy-start(f32[1,3,256,1024]{3,2,1,0:T(8,128)} %hydro.9) | copy-start | bytes 9437188
  2.4 4.1 %copy-start.1 = (f32[1,2,256,1024]{3,2,1,0:T(8,128)S(1)}, f32[1,2,256,1024]{3,2,1,0:T(8,128)}, u32[]{:S(2)}) copy-start(f32[1,2,256,1024]{3,2,1,0:T(8,128)} %stress.9) | copy-start | bytes 6291460
  2.4 4.1 %copy-start.2 = (f32[1,4]{1,0:T(1,128)S(1)}, f32[1,4]{1,0:T(1,128)}, u32[]{:S(2)}) copy-start(f32[1,4]{1,0:T(1,128)} %params.5) | copy-start | bytes 52
  2.4 4.1 %copy-start.3 = (s32[4]{0:T(128)S(1)}, s32[4]{0:T(128)}, u32[]{:S(2)}) copy-start(s32[4]{0:T(128)} %weights.5) | copy-start | bytes 52
  2.5 3.9 %collective-permute-start = (f32[72,128]{1,0:T(8,128)S(1)}, f32[72,128]{1,0:T(8,128)S(1)}, u32[]{:S(2)}, u32[]{:S(2)}) collective-permute-start(f32[72,128]{1,0:T(8,128)S(1)} %pack_side.1), channel_id=1, source_target_pairs={{0,1},{1,0},{2,3},{3,2},{4,5},{5,4},{6,7},{7,6},{8,9},{9,8},{10,11... | collective-permute-start | bytes 110600 | tf_op jit(solution)/shard_map/ppermute | solution.py:701
  6.4 6.6 %collective-permute-start.1 = (f32[272,128]{1,0:T(8,128)S(1)}, f32[272,128]{1,0:T(8,128)S(1)}, u32[]{:S(2)}, u32[]{:S(2)}) collective-permute-start(f32[272,128]{1,0:T(8,128)S(1)} %get-tuple-element.44), channel_id=1, source_target_pairs={{0,2},{2,0},{4,6},{6,4},{1,3},{3,1},{5,7},{7,5},{8,10},{10,8},{12,... | collective-permute-start | bytes 417800 | tf_op jit(solution)/shard_map/ppermute | solution.py:705
  13.1 5.5 %collective-permute-start.3 = (f32[520,128]{1,0:T(8,128)S(1)}, f32[520,128]{1,0:T(8,128)S(1)}, u32[]{:S(2)}, u32[]{:S(2)}) collective-permute-start(f32[520,128]{1,0:T(8,128)S(1)} %slice_bitcast_fusion), channel_id=1, source_target_pairs={{0,8},{8,0},{16,24},{24,16},{1,9},{9,1},{17,25},{25,17},{2,10},{10... | collective-permute-start | bytes 798728 | tf_op jit(solution)/shard_map/ppermute | solution.py:708
  14.3 9.5 %collective-permute-start.2 = (f32[272,128]{1,0:T(8,128)S(1)}, f32[272,128]{1,0:T(8,128)S(1)}, u32[]{:S(2)}, u32[]{:S(2)}) collective-permute-start(f32[272,128]{1,0:T(8,128)S(1)} %get-tuple-element.47), channel_id=1, source_target_pairs={{2,4},{4,2},{3,5},{5,3},{10,12},{12,10},{11,13},{13,11},{18,20},{2... | collective-permute-start | bytes 417800 | tf_op jit(solution)/shard_map/ppermute | solution.py:709
  18.6 8.5 %collective-permute-start.4 = (f32[520,128]{1,0:T(8,128)S(1)}, f32[520,128]{1,0:T(8,128)S(1)}, u32[]{:S(2)}, u32[]{:S(2)}) collective-permute-start(f32[520,128]{1,0:T(8,128)S(1)} %bitcast_add_fusion), channel_id=1, source_target_pairs={{0,16},{8,24},{16,0},{24,8},{1,17},{9,25},{17,1},{25,9},{2,18},{10... | collective-permute-start | bytes 798728 | tf_op jit(solution)/shard_map/ppermute | solution.py:695
  23.1 4.0 %collective-permute-start.5 = (f32[272,128]{1,0:T(8,128)S(1)}, f32[272,128]{1,0:T(8,128)S(1)}, u32[]{:S(2)}, u32[]{:S(2)}) collective-permute-start(f32[272,128]{1,0:T(8,128)S(1)} %slice_bitcast_fusion.2), channel_id=1, source_target_pairs={{0,8},{8,0},{16,24},{24,16},{1,9},{9,1},{17,25},{25,17},{2,10},{10... | collective-permute-start | bytes 417800 | tf_op jit(solution)/shard_map/ppermute | solution.py:713
  27.0 2.1 %collective-permute-start.7 = (f32[272,128]{1,0:T(8,128)S(1)}, f32[272,128]{1,0:T(8,128)S(1)}, u32[]{:S(2)}, u32[]{:S(2)}) collective-permute-start(f32[272,128]{1,0:T(8,128)S(1)} %slice_bitcast_fusion.1), channel_id=1, source_target_pairs={{0,8},{8,0},{16,24},{24,16},{1,9},{9,1},{17,25},{25,17},{2,10},{10... | collective-permute-start | bytes 417800 | tf_op jit(solution)/shard_map/ppermute | solution.py:718
  27.2 4.8 %collective-permute-start.9 = (f32[272,128]{1,0:T(8,128)S(1)}, f32[272,128]{1,0:T(8,128)S(1)}, u32[]{:S(2)}, u32[]{:S(2)}) collective-permute-start(f32[272,128]{1,0:T(8,128)S(1)} %bitcast_add_fusion.1), channel_id=1, source_target_pairs={{0,16},{8,24},{16,0},{24,8},{1,17},{9,25},{17,1},{25,9},{2,18},{10... | collective-permute-start | bytes 417800 | tf_op jit(solution)/shard_map/ppermute | solution.py:695
  27.8 6.2 %collective-permute-start.6 = (f32[520,128]{1,0:T(8,128)S(1)}, f32[520,128]{1,0:T(8,128)S(1)}, u32[]{:S(2)}, u32[]{:S(2)}) collective-permute-start(f32[520,128]{1,0:T(8,128)S(1)} %add.19.own_m), channel_id=1, source_target_pairs={{0,8},{8,0},{16,24},{24,16},{1,9},{9,1},{17,25},{25,17},{2,10},{10... | collective-permute-start | bytes 798728 | tf_op jit(solution)/shard_map/ppermute | solution.py:720
  32.0 2.4 %collective-permute-start.10 = (f32[272,128]{1,0:T(8,128)S(1)}, f32[272,128]{1,0:T(8,128)S(1)}, u32[]{:S(2)}, u32[]{:S(2)}) collective-permute-start(f32[272,128]{1,0:T(8,128)S(1)} %add.22.own_a), channel_id=1, source_target_pairs={{0,8},{8,0},{16,24},{24,16},{1,9},{9,1},{17,25},{25,17},{2,10},{10... | collective-permute-start | bytes 417800 | tf_op jit(solution)/shard_map/ppermute | solution.py:722
  33.4 5.3 %collective-permute-start.8 = (f32[272,128]{1,0:T(8,128)S(1)}, f32[272,128]{1,0:T(8,128)S(1)}, u32[]{:S(2)}, u32[]{:S(2)}) collective-permute-start(f32[272,128]{1,0:T(8,128)S(1)} %bitcast_add_fusion.2), channel_id=1, source_target_pairs={{0,16},{8,24},{16,0},{24,8},{1,17},{9,25},{17,1},{25,9},{2,18},{10... | collective-permute-start | bytes 417800 | tf_op jit(solution)/shard_map/ppermute | solution.py:695
  38.7 1.9 %collective-permute-start.11 = (f32[272,128]{1,0:T(8,128)S(1)}, f32[272,128]{1,0:T(8,128)S(1)}, u32[]{:S(2)}, u32[]{:S(2)}) collective-permute-start(f32[272,128]{1,0:T(8,128)S(1)} %add.23.own_b), channel_id=1, source_target_pairs={{0,8},{8,0},{16,24},{24,16},{1,9},{9,1},{17,25},{25,17},{2,10},{10... | collective-permute-start | bytes 417800 | tf_op jit(solution)/shard_map/ppermute | solution.py:725

commit v9 on v5

--- a/solution.py
+++ b/solution.py
@@ -452,6 +452,8 @@
     from_a = top == (lax.axis_index("ty") % 2 == 1)
     first = jnp.where(top, -1, blocks - quarter - 1)
 
+    ty = lax.axis_index("ty")
+    outside_map = ty == jnp.where(top, 0, lax.axis_size("ty") - 1)
     inner = jnp.where(top, quarter, blocks - quarter - 1)
     corners = pl.ds(lanes * GROUP, SUB)
     for f in range(FIELDS):
@@ -467,6 +469,8 @@
         if f == 0:
             corner = jnp.where(valid, corner, 0.0)
         outer = jnp.concatenate(parts + [corner], axis=1)
+        if f == 0:
+            outer = jnp.where(outside_map, 0.0, outer)
         ends[0, f] = jnp.where(top, outer, body)
         ends[1, f] = jnp.where(top, body, outer)
 
@@ -673,7 +677,10 @@
     swap = [(i, i ^ 1) for i in range(nc)]
 
     def pairs(first):
-        return [p for i in range(first, ny - 1, 2) for p in ((i, i + 1), (i + 1, i))]
+        partner = list(range(ny))
+        for i in range(first, ny - 1, 2):
+            partner[i], partner[i + 1] = i + 1, i
+        return list(enumerate(partner))
 
     def over_chips(part, beside=()):
         reach = 2

time: 40.1 us -> 40 us (level)
  no operation moved by 1% of the time
where the time goes in v9:
time: 40 us; the launch traced here: 39.9 us
  Pallas kernels  21.1 us (53%)
  starting transfers between devices  12.1 us (30%)
  waiting for transfers between devices  5.49 us (14%)
  between operations  0.98 us (2%)
    pallas_call x2, Pallas kernels, edge(): pl.pallas_call(functools.partial(edge_kernel, own), name='edge_own' if ow...  6.31 us
    pallas_call x2, Pallas kernels, middle(): pl.pallas_call(functools.partial(middle_kernel, own), name='middle_own' i...  6.22 us
    ppermute x1, starting transfers between devices, shards(): far_b = lax.ppermute(far_b, 'ty', pairs(1))  4.39 us
    ppermute x2, waiting for transfers between devices, over_chips(): got = lax.ppermute(part, 'cond', [(i, i ^ reach) for i in range(nc)])  3.92 us
    pallas_call x1, Pallas kernels, prepare(): pl.pallas_call(prepare_kernel, name='prepare', out_shape=[tile] * 4 + [pl...  2.58 us
    ppermute x2, starting transfers between devices, over_chips(): got = lax.ppermute(part, 'cond', [(i, i ^ reach) for i in range(nc)])  2.5 us
    ppermute x2, starting transfers between devices, shards(): got = lax.ppermute(pay, 'cond', swap)  2.41 us
    pallas_call x1, Pallas kernels, bed_middle(): pl.pallas_call(bed_middle_kernel, name='bed_middle', out_shape=[pltpu.HBM...  2.24 us
  transfers between devices with their start and end apart: 9, of which 4 were waited for; matrix products, arithmetic and copies ran while one was open for 0% of the time, Pallas kernels for 44%

profile of v9, /device:TPU:9, one launch (start us, length us, event | category | flops | bytes accessed | tf_op | source)
XLA Modules:
  0.0 39.9 jit_solution(12857038968094819026)
XLA Ops:
  0.6 1.8 %pack_side.1 = f32[72,128]{1,0:T(8,128)S(1)} custom-call(f32[1,4]{1,0:T(1,128)} %params.7, f32[256,1024]{1,0:T(8,128)} %bed.3, s32[256,1024]{1,0:T(8,128)} %mask.3, s32[256,1024]{1,0:T(8,128)} %kind.3, f32[1,2,256,1024]{3,2,1,0:T(8,128)} %stress.11, f32[1,3,256,1024]{3,2,1,0:T(8,128)} %hydro.11), custom_call_target="tpu_custom_call" | custom-call | flops 2000000000 | tf_op jit(solution)/shard_map/pack_side/pallas_call | solution.py:114
  2.4 0.0 copy-start
  2.4 0.0 copy-start.1
  2.4 0.0 copy-start.3
  2.5 1.3 %collective-permute-start = (f32[72,128]{1,0:T(8,128)S(1)}, f32[72,128]{1,0:T(8,128)S(1)}, u32[]{:S(2)}, u32[]{:S(2)}) collective-permute-start(f32[72,128]{1,0:T(8,128)S(1)} %pack_side.1), channel_id=1, source_target_pairs={{0,1},{1,0},{2,3},{3,2},{4,5},{5,4},{6,7},{7,6},{8,9},{9,8},{10,11... | collective-permute-start | bytes 110600 | tf_op jit(solution)/shard_map/ppermute | solution.py:694
  3.8 2.6 %prepare.1 = (f32[256,1024]{1,0:T(8,128)S(1)}, f32[256,1024]{1,0:T(8,128)S(1)}, f32[256,1024]{1,0:T(8,128)S(1)}, f32[256,1024]{1,0:T(8,128)S(1)}, f32[272,128]{1,0:T(8,128)S(1)}, /*index=5*/f32[272,128]{1,0:T(8,128)S(1)}) custom-call(f32[1,4]{1,0:T(1,128)} %params.7, f32[256,1024]{1,0:T(8,128)} %bed.3, s32[256,1024]{1,0:T(8,128)} %mask.3, s32[256,1024]{1,0:T(8,128)} %kind.3, ...), custom_call_target="tpu_custom_call" | custom-call | flops 2000000000 | tf_op jit(solution)/shard_map/prepare/pallas_call | solution.py:203
  6.4 0.1 collective-permute-start.1
  6.5 3.1 %middle_other.1 = (f32[1,3,256,1024]{3,2,1,0:T(8,128)S(1)}, f32[520,128]{1,0:T(8,128)S(1)}) custom-call(s32[4]{0:T(128)S(1)} %copy-done.3, f32[1,4]{1,0:T(1,128)S(1)} %copy-done.2, f32[256,1024]{1,0:T(8,128)S(1)} %get-tuple-element.36.root, f32[256,1024]{1,0:T(8,128)S(1)} %get-tuple-element.37.a, f32[256,1024]{1,0:T(8,128)S(1)} %get-tuple-element.38.b, ...), custom_call_target="tpu_custom_call" | custom-call | flops 4000000000 | tf_op jit(solution)/shard_map/middle_other/pallas_call | solution.py:424
  9.6 1.2 %collective-permute-start.3 = (f32[520,128]{1,0:T(8,128)S(1)}, f32[520,128]{1,0:T(8,128)S(1)}, u32[]{:S(2)}, u32[]{:S(2)}) collective-permute-start(f32[520,128]{1,0:T(8,128)S(1)} %get-tuple-element.49), channel_id=1, source_target_pairs={{0,8},{8,0},{16,24},{24,16},{1,9},{9,1},{17,25},{25,17},{2,10},{10... | collective-permute-start | bytes 798728 | tf_op jit(solution)/shard_map/ppermute | solution.py:702
  10.8 0.1 collective-permute-done.1.far_a
  10.9 4.4 %collective-permute-start.2 = (f32[272,128]{1,0:T(8,128)S(1)}, f32[272,128]{1,0:T(8,128)S(1)}, u32[]{:S(2)}, u32[]{:S(2)}) collective-permute-start(f32[272,128]{1,0:T(8,128)S(1)} %get-tuple-element.45), channel_id=1, source_target_pairs={{0,0},{2,4},{4,2},{6,6},{1,1},{3,5},{5,3},{7,7},{8,8},{10,12},{12,... | collective-permute-start | bytes 417800 | tf_op jit(solution)/shard_map/ppermute | solution.py:701
  15.3 3.1 %middle_own.1 = (f32[1,3,256,1024]{3,2,1,0:T(8,128)S(1)}, f32[520,128]{1,0:T(8,128)S(1)}) custom-call(s32[4]{0:T(128)S(1)} %copy-done.3, f32[1,4]{1,0:T(1,128)S(1)} %copy-done.2, f32[256,1024]{1,0:T(8,128)S(1)} %get-tuple-element.36.root, f32[256,1024]{1,0:T(8,128)S(1)} %get-tuple-element.37.a, ...), custom_call_target="tpu_custom_call", output_to_operand_aliasing={{0}: (8, {})} | custom-call | flops 4000000000 | tf_op jit(solution)/shard_map/middle_own/pallas_call | solution.py:424
  18.5 1.3 %collective-permute-start.4 = (f32[520,128]{1,0:T(8,128)S(1)}, f32[520,128]{1,0:T(8,128)S(1)}, u32[]{:S(2)}, u32[]{:S(2)}) collective-permute-start(f32[520,128]{1,0:T(8,128)S(1)} %add.12), channel_id=1, source_target_pairs={{0,16},{8,24},{16,0},{24,8},{1,17},{9,25},{17,1},{25,9},{2,18},{10... | collective-permute-start | bytes 798728 | tf_op jit(solution)/shard_map/ppermute | solution.py:688
  19.8 3.2 %edge_other.1 = (f32[1,3,256,1024]{3,2,1,0:T(8,128)S(1)}, f32[528,128]{1,0:T(8,128)S(1)}) custom-call(s32[4]{0:T(128)S(1)} %copy-done.3, f32[1,4]{1,0:T(1,128)S(1)} %copy-done.2, f32[256,1024]{1,0:T(8,128)S(1)} %get-tuple-element.36.root, f32[256,1024]{1,0:T(8,128)S(1)} %get-tuple-element.37.a, ...), custom_call_target="tpu_custom_call", output_to_operand_aliasing={{0}: (10, {})} | custom-call | flops 3000000000 | tf_op jit(solution)/shard_map/edge_other/pallas_call | solution.py:499
  23.0 1.2 %collective-permute-start.5 = (f32[528,128]{1,0:T(8,128)S(1)}, f32[528,128]{1,0:T(8,128)S(1)}, u32[]{:S(2)}, u32[]{:S(2)}) collective-permute-start(f32[528,128]{1,0:T(8,128)S(1)} %get-tuple-element.56), channel_id=1, source_target_pairs={{0,8},{8,0},{16,24},{24,16},{1,9},{9,1},{17,25},{25,17},{2,10},{10... | collective-permute-start | bytes 811016 | tf_op jit(solution)/shard_map/ppermute | solution.py:707
  24.2 3.2 %edge_own.1 = (f32[1,3,256,1024]{3,2,1,0:T(8,128)S(1)}, f32[528,128]{1,0:T(8,128)S(1)}) custom-call(s32[4]{0:T(128)S(1)} %copy-done.3, f32[1,4]{1,0:T(1,128)S(1)} %copy-done.2, f32[256,1024]{1,0:T(8,128)S(1)} %get-tuple-element.36.root, f32[256,1024]{1,0:T(8,128)S(1)} %get-tuple-element.37.a, ...), custom_call_target="tpu_custom_call", output_to_operand_aliasing={{0}: (10, {})} | custom-call | flops 3000000000 | tf_op jit(solution)/shard_map/edge_own/pallas_call | solution.py:499
  27.4 0.1 collective-permute-start.6
  27.5 1.2 %collective-permute-start.7 = (f32[528,128]{1,0:T(8,128)S(1)}, f32[528,128]{1,0:T(8,128)S(1)}, u32[]{:S(2)}, u32[]{:S(2)}) collective-permute-start(f32[528,128]{1,0:T(8,128)S(1)} %add.14), channel_id=1, source_target_pairs={{0,16},{8,24},{16,0},{24,8},{1,17},{9,25},{17,1},{25,9},{2,18},{10... | collective-permute-start | bytes 811016 | tf_op jit(solution)/shard_map/ppermute | solution.py:688
  28.8 0.3 collective-permute-done.6.got_m
  29.0 2.2 %bed_middle.1 = (f32[256,1024]{1,0:T(8,128)}, f32[256,1024]{1,0:T(8,128)}, f32[1,3,256,1024]{3,2,1,0:T(8,128)}) custom-call(f32[256,1024]{1,0:T(8,128)S(1)} %get-tuple-element.35.bed, f32[72,128]{1,0:T(8,128)S(1)} %collective-permute-done.side, f32[272,128]{1,0:T(8,128)S(1)} %collective-permute-done.1.far_a, f32[272,128]{1,0:T(8,128)S(1)} %collective-permute-done.2.far_b, ...), custom_call_target="tpu_custom_call" | custom-call | flops 4000000000 | tf_op jit(solution)/shard_map/bed_middle/pallas_call | solution.py:644
  31.3 3.9 %collective-permute-done.7 = f32[528,128]{1,0:T(8,128)S(1)} collective-permute-done((f32[528,128]{1,0:T(8,128)S(1)}, f32[528,128]{1,0:T(8,128)S(1)}, u32[]{:S(2)}, u32[]{:S(2)}) %collective-permute-start.7) | collective-permute-done | bytes 270368 | tf_op jit(solution)/shard_map/ppermute | solution.py:688
  35.2 1.3 %collective-permute-start.8 = (f32[528,128]{1,0:T(8,128)S(1)}, f32[528,128]{1,0:T(8,128)S(1)}, u32[]{:S(2)}, u32[]{:S(2)}) collective-permute-start(f32[528,128]{1,0:T(8,128)S(1)} %add.15.own_e), channel_id=1, source_target_pairs={{0,8},{8,0},{16,24},{24,16},{1,9},{9,1},{17,25},{25,17},{2,10},{10... | collective-permute-start | bytes 811016 | tf_op jit(solution)/shard_map/ppermute | solution.py:715
  36.6 1.2 %collective-permute-done.8.got_e = f32[528,128]{1,0:T(8,128)S(1)} collective-permute-done((f32[528,128]{1,0:T(8,128)S(1)}, f32[528,128]{1,0:T(8,128)S(1)}, u32[]{:S(2)}, u32[]{:S(2)}) %collective-permute-start.8) | collective-permute-done | bytes 270368 | tf_op jit(solution)/shard_map/ppermute | solution.py:715
  37.7 1.9 %bed_edge.1 = (f32[256,1024]{1,0:T(8,128)}, f32[256,1024]{1,0:T(8,128)}) custom-call(f32[256,1024]{1,0:T(8,128)S(1)} %get-tuple-element.35.bed, f32[72,128]{1,0:T(8,128)S(1)} %collective-permute-done.side, f32[272,128]{1,0:T(8,128)S(1)} %collective-permute-done.1.far_a, ...), custom_call_target="tpu_custom_call", output_to_operand_aliasing={{0}: (8, {}), {1}: (9, {})} | custom-call | flops 2000000000 | tf_op jit(solution)/shard_map/bed_edge/pallas_call | solution.py:657
  (15 shorter events, 0.2 us)
Async XLA Ops:
  2.4 4.1 %copy-start = (f32[1,3,256,1024]{3,2,1,0:T(8,128)S(1)}, f32[1,3,256,1024]{3,2,1,0:T(8,128)}, u32[]{:S(2)}) copy-start(f32[1,3,256,1024]{3,2,1,0:T(8,128)} %hydro.11) | copy-start | bytes 9437188
  2.4 4.1 %copy-start.1 = (f32[1,2,256,1024]{3,2,1,0:T(8,128)S(1)}, f32[1,2,256,1024]{3,2,1,0:T(8,128)}, u32[]{:S(2)}) copy-start(f32[1,2,256,1024]{3,2,1,0:T(8,128)} %stress.11) | copy-start | bytes 6291460
  2.4 4.1 %copy-start.2 = (f32[1,4]{1,0:T(1,128)S(1)}, f32[1,4]{1,0:T(1,128)}, u32[]{:S(2)}) copy-start(f32[1,4]{1,0:T(1,128)} %params.7) | copy-start | bytes 52
  2.4 4.1 %copy-start.3 = (s32[4]{0:T(128)S(1)}, s32[4]{0:T(128)}, u32[]{:S(2)}) copy-start(s32[4]{0:T(128)} %weights.7) | copy-start | bytes 52
  2.5 3.9 %collective-permute-start = (f32[72,128]{1,0:T(8,128)S(1)}, f32[72,128]{1,0:T(8,128)S(1)}, u32[]{:S(2)}, u32[]{:S(2)}) collective-permute-start(f32[72,128]{1,0:T(8,128)S(1)} %pack_side.1), channel_id=1, source_target_pairs={{0,1},{1,0},{2,3},{3,2},{4,5},{5,4},{6,7},{7,6},{8,9},{9,8},{10,11... | collective-permute-start | bytes 110600 | tf_op jit(solution)/shard_map/ppermute | solution.py:694
  6.4 4.6 %collective-permute-start.1 = (f32[272,128]{1,0:T(8,128)S(1)}, f32[272,128]{1,0:T(8,128)S(1)}, u32[]{:S(2)}, u32[]{:S(2)}) collective-permute-start(f32[272,128]{1,0:T(8,128)S(1)} %get-tuple-element.42), channel_id=1, source_target_pairs={{0,2},{2,0},{4,6},{6,4},{1,3},{3,1},{5,7},{7,5},{8,10},{10,8},{12,... | collective-permute-start | bytes 417800 | tf_op jit(solution)/shard_map/ppermute | solution.py:698
  9.6 8.8 %collective-permute-start.3 = (f32[520,128]{1,0:T(8,128)S(1)}, f32[520,128]{1,0:T(8,128)S(1)}, u32[]{:S(2)}, u32[]{:S(2)}) collective-permute-start(f32[520,128]{1,0:T(8,128)S(1)} %get-tuple-element.49), channel_id=1, source_target_pairs={{0,8},{8,0},{16,24},{24,16},{1,9},{9,1},{17,25},{25,17},{2,10},{10... | collective-permute-start | bytes 798728 | tf_op jit(solution)/shard_map/ppermute | solution.py:702
  10.9 8.8 %collective-permute-start.2 = (f32[272,128]{1,0:T(8,128)S(1)}, f32[272,128]{1,0:T(8,128)S(1)}, u32[]{:S(2)}, u32[]{:S(2)}) collective-permute-start(f32[272,128]{1,0:T(8,128)S(1)} %get-tuple-element.45), channel_id=1, source_target_pairs={{0,0},{2,4},{4,2},{6,6},{1,1},{3,5},{5,3},{7,7},{8,8},{10,12},{12,... | collective-permute-start | bytes 417800 | tf_op jit(solution)/shard_map/ppermute | solution.py:701
  18.5 8.8 %collective-permute-start.4 = (f32[520,128]{1,0:T(8,128)S(1)}, f32[520,128]{1,0:T(8,128)S(1)}, u32[]{:S(2)}, u32[]{:S(2)}) collective-permute-start(f32[520,128]{1,0:T(8,128)S(1)} %add.12), channel_id=1, source_target_pairs={{0,16},{8,24},{16,0},{24,8},{1,17},{9,25},{17,1},{25,9},{2,18},{10... | collective-permute-start | bytes 798728 | tf_op jit(solution)/shard_map/ppermute | solution.py:688
  23.0 4.4 %collective-permute-start.5 = (f32[528,128]{1,0:T(8,128)S(1)}, f32[528,128]{1,0:T(8,128)S(1)}, u32[]{:S(2)}, u32[]{:S(2)}) collective-permute-start(f32[528,128]{1,0:T(8,128)S(1)} %get-tuple-element.56), channel_id=1, source_target_pairs={{0,8},{8,0},{16,24},{24,16},{1,9},{9,1},{17,25},{25,17},{2,10},{10... | collective-permute-start | bytes 811016 | tf_op jit(solution)/shard_map/ppermute | solution.py:707
  27.4 1.6 %collective-permute-start.6 = (f32[520,128]{1,0:T(8,128)S(1)}, f32[520,128]{1,0:T(8,128)S(1)}, u32[]{:S(2)}, u32[]{:S(2)}) collective-permute-start(f32[520,128]{1,0:T(8,128)S(1)} %add.13.own_m), channel_id=1, source_target_pairs={{0,8},{8,0},{16,24},{24,16},{1,9},{9,1},{17,25},{25,17},{2,10},{10... | collective-permute-start | bytes 798728 | tf_op jit(solution)/shard_map/ppermute | solution.py:712
  27.5 7.7 %collective-permute-start.7 = (f32[528,128]{1,0:T(8,128)S(1)}, f32[528,128]{1,0:T(8,128)S(1)}, u32[]{:S(2)}, u32[]{:S(2)}) collective-permute-start(f32[528,128]{1,0:T(8,128)S(1)} %add.14), channel_id=1, source_target_pairs={{0,16},{8,24},{16,0},{24,8},{1,17},{9,25},{17,1},{25,9},{2,18},{10... | collective-permute-start | bytes 811016 | tf_op jit(solution)/shard_map/ppermute | solution.py:688
  35.2 2.5 %collective-permute-start.8 = (f32[528,128]{1,0:T(8,128)S(1)}, f32[528,128]{1,0:T(8,128)S(1)}, u32[]{:S(2)}, u32[]{:S(2)}) collective-permute-start(f32[528,128]{1,0:T(8,128)S(1)} %add.15.own_e), channel_id=1, source_target_pairs={{0,8},{8,0},{16,24},{24,16},{1,9},{9,1},{17,25},{25,17},{2,10},{10... | collective-permute-start | bytes 811016 | tf_op jit(solution)/shard_map/ppermute | solution.py:715

commit v10 on v9

--- a/solution.py
+++ b/solution.py
@@ -279,63 +279,72 @@
             pltpu.VMEM((SUB, wide), jnp.float32),
         ]
 
-    def speed_c(self, i, level, u, wc):
-        return (self.slow * u - (east(level) - level) + self.get(3, i)) * wc
-
     def speed_r(self, i, level, lower, v, wr):
         return (self.slow * v - (south(level, lower) - level) + self.get(4, i)) * wr
 
-    def move(self, n, i, level, lower, u, v, fc, fr, wc, wr):
-        u = self.speed_c(i, level, u, wc)
-        v = self.speed_r(i, level, lower, v, wr)
+    def move(self, n, i, level, lower, u, v, faces, rest):
+        right, down = east(level), south(level, lower)
+        yield
+        fc, fr, wc, wr = faces()
+        u = (self.slow * u() - (right - level) + self.get(3, i)) * wc
+        v = (self.slow * v() - (down - level) + self.get(4, i)) * wr
         flux_c = fc * u
         flux_r = fr * v
-        out = self.get(1, i) * level + self.get(2, i) - (
-            flux_c - west(flux_c) + flux_r - north(flux_r, self.fr_last[n])
-        )
+        left, up = west(flux_c), north(flux_r, self.fr_last[n])
         self.fr_last[n] = flux_r
-        return out, u, v
+        more = rest(u, v)
+        yield
+        out = self.get(1, i) * level + self.get(2, i) - (flux_c - left + flux_r - up)
+        return out, more
 
     def step_one(self, i):
         at = tile_at(i)
         s = self.get(0, i)
+        inside = i + 1 < self.count
         level = 0.3 * self.get(5, i)
-        inside = i + 1 < self.count
-        face_c = s * east(s)
-        face_r = s * south(s, self.get(0, i + 1) if inside else s)
-        ratios = []
-        for face in (face_c, face_r):
-            base = face + 0.1
-            inverse = pl.reciprocal(base, approx=True)
-            ratios.append(face * (inverse * (2.0 - base * inverse)))
-        wc, wr = ratios
-        fc = 0.3 * face_c
-        fr = 0.3 * face_r
-        self.fc[at, :] = fc
-        self.fr[at, :] = fr
-        self.wc[at, :] = wc
-        self.wr[at, :] = wr
         lower = 0.3 * self.get(5, i + 1) if inside else level
-        e, u, v = self.move(0, i, level, lower, self.get(6, i), self.get(7, i), fc, fr, wc, wr)
-        self.e1[at, :] = e
-        self.u1[at, :] = u
-        self.v1[at, :] = v
-        self.qc1[at, :] = u * jnp.abs(u)
-        self.qr1[at, :] = v * jnp.abs(v)
+        right, down = east(s), south(s, self.get(0, i + 1) if inside else s)
+
+        def faces():
+            ratios = []
+            for face in (s * right, s * down):
+                base = face + 0.1
+                inverse = pl.reciprocal(base, approx=True)
+                ratios.append((0.3 * face, face * (inverse * (2.0 - base * inverse))))
+            (fc, wc), (fr, wr) = ratios
+            for ref, value in ((self.fc, fc), (self.fr, fr), (self.wc, wc), (self.wr, wr)):
+                ref[at, :] = value
+            return fc, fr, wc, wr
+
+        def rest(u, v):
+            self.u1[at, :] = u
+            self.v1[at, :] = v
+            self.qc1[at, :] = u * jnp.abs(u)
+            self.qr1[at, :] = v * jnp.abs(v)
+
+        out, _ = yield from self.move(
+            0, i, level, lower, lambda: self.get(6, i), lambda: self.get(7, i), faces, rest
+        )
+        self.e1[at, :] = out
+
+    def faces_at(self, at):
+        return lambda: [ref[at, :] for ref in (self.fc, self.fr, self.wc, self.wr)]
 
     def step_two(self, i):
         at, after = tile_at(i), tile_at(i + 1)
-        e, u, v = self.move(
-            1, i, self.e1[at, :], self.e1[after, :], self.u1[at, :], self.v1[at, :],
-            self.fc[at, :], self.fr[at, :], self.wc[at, :], self.wr[at, :],
+
+        def rest(u, v):
+            if not (self.trim and i == self.count - 1):
+                self.u2[at, :] = u
+                self.v2[at, :] = v
+                self.qc2[at, :] = self.qc1[at, :] + u * jnp.abs(u)
+                self.qr2[at, :] = self.qr1[at, :] + v * jnp.abs(v)
+
+        out, _ = yield from self.move(
+            1, i, self.e1[at, :], self.e1[after, :], lambda: self.u1[at, :], lambda: self.v1[at, :],
+            self.faces_at(at), rest,
         )
-        self.e2[at, :] = e
-        if self.trim and i == self.count - 1:
-            return
-        self.u2[at, :] = u
-        self.v2[at, :] = v
-        self.qc2[at, :] = self.qc1[at, :] + u * jnp.abs(u)
-        self.qr2[at, :] = self.qr1[at, :] + v * jnp.abs(v)
+        self.e2[at, :] = out
 
     def step_three(self, i):
         at, after = tile_at(i), tile_at(i + 1)
@@ -347,16 +356,19 @@
             self.fr_last[2] = self.fr[at, :] * v
             self.qr_last[...] = wr * (self.qr2[at, :] + v * jnp.abs(v))
             return
-        wc, wr = self.wc[at, :], self.wr[at, :]
-        e, u, v = self.move(
-            2, i, self.e2[at, :], self.e2[after, :], self.u2[at, :], self.v2[at, :],
-            self.fc[at, :], self.fr[at, :], wc, wr,
+
+        def rest(u, v):
+            qc = self.wc[at, :] * (self.qc2[at, :] + u * jnp.abs(u))
+            qr = self.wr[at, :] * (self.qr2[at, :] + v * jnp.abs(v))
+            left, up = west(qc), north(qr, self.qr_last[...])
+            self.qr_last[...] = qr
+            return u, v, qc, qr, left, up
+
+        out, (u, v, qc, qr, left, up) = yield from self.move(
+            2, i, self.e2[at, :], self.e2[after, :], lambda: self.u2[at, :], lambda: self.v2[at, :],
+            self.faces_at(at), rest,
         )
-        qc = wc * (self.qc2[at, :] + u * jnp.abs(u))
-        qr = wr * (self.qr2[at, :] + v * jnp.abs(v))
-        change = (qc - west(qc) + qr - north(qr, self.qr_last[...])) * self.scale
-        self.qr_last[...] = qr
-        self.emit(i, e * (1.0 / 0.3), u, v, change)
+        self.emit(i, out * (1.0 / 0.3), u, v, (qc - left + qr - up) * self.scale)
 
     def run(self):
         self.fr_last[...] = jnp.zeros_like(self.fr_last)
@@ -365,10 +377,13 @@
             ref[tile_at(self.count), :] = jnp.zeros((SUB, self.wide), jnp.float32)
         stages = (self.step_three, self.step_two, self.step_one)
         for t in range(self.count + LAG * (STEPS - 1)):
+            turns = []
             for k, stage in enumerate(stages):
                 i = t - LAG * (STEPS - 1 - k)
                 if 0 <= i < self.count:
-                    stage(i)
+                    turns.append(stage(i))
+            while turns:
+                turns = [turn for turn in turns if next(turn, True) is None]
 
 
 def reader(root, a, b, stress, hydro, side, unfold, valid):

time: 40 us -> 39.4 us (0.985)
  Pallas kernels: 21.1 us -> 20.1 us
    pallas_call x2, Pallas kernels: 6.22 us -> 5.61 us  [middle(): pl.pallas_call(functools.partial(middle_kernel, own), name='middle_own' i...]
  transfers between devices with their start and end apart: 9 -> 9, of which waited for: 4 -> 4; matrix products, arithmetic and copies ran while one was open for 0% -> 0% of each run, Pallas kernels for 44% -> 42%
where the time goes in v10:
time: 39.4 us; the launch traced here: 39.2 us
  Pallas kernels  20.1 us (51%)
  starting transfers between devices  12.2 us (31%)
  waiting for transfers between devices  5.76 us (15%)
  between operations  0.98 us (2%)
    pallas_call x2, Pallas kernels, edge(): pl.pallas_call(functools.partial(edge_kernel, own), name='edge_own' if ow...  5.96 us
    pallas_call x2, Pallas kernels, middle(): pl.pallas_call(functools.partial(middle_kernel, own), name='middle_own' i...  5.61 us
    ppermute x1, starting transfers between devices, shards(): far_b = lax.ppermute(far_b, 'ty', pairs(1))  4.08 us
    ppermute x2, waiting for transfers between devices, over_chips(): got = lax.ppermute(part, 'cond', [(i, i ^ reach) for i in range(nc)])  3.93 us
    ppermute x2, starting transfers between devices, shards(): got = lax.ppermute(pay, 'cond', swap)  2.72 us
    pallas_call x1, Pallas kernels, prepare(): pl.pallas_call(prepare_kernel, name='prepare', out_shape=[tile] * 4 + [pl...  2.58 us
    ppermute x2, starting transfers between devices, over_chips(): got = lax.ppermute(part, 'cond', [(i, i ^ reach) for i in range(nc)])  2.5 us
    pallas_call x1, Pallas kernels, bed_middle(): pl.pallas_call(bed_middle_kernel, name='bed_middle', out_shape=[pltpu.HBM...  2.24 us
  transfers between devices with their start and end apart: 9, of which 4 were waited for; matrix products, arithmetic and copies ran while one was open for 0% of the time, Pallas kernels for 42%

profile of v10, /device:TPU:9, one launch (start us, length us, event | category | flops | bytes accessed | tf_op | source)
XLA Modules:
  0.0 39.2 jit_solution(14743105603507214269)
XLA Ops:
  0.6 1.8 %pack_side.1 = f32[72,128]{1,0:T(8,128)S(1)} custom-call(f32[1,4]{1,0:T(1,128)} %params.7, f32[256,1024]{1,0:T(8,128)} %bed.3, s32[256,1024]{1,0:T(8,128)} %mask.3, s32[256,1024]{1,0:T(8,128)} %kind.3, f32[1,2,256,1024]{3,2,1,0:T(8,128)} %stress.11, f32[1,3,256,1024]{3,2,1,0:T(8,128)} %hydro.11), custom_call_target="tpu_custom_call" | custom-call | flops 2000000000 | tf_op jit(solution)/shard_map/pack_side/pallas_call | solution.py:114
  2.4 0.0 copy-start
  2.4 0.0 copy-start.1
  2.4 0.0 copy-start.2
  2.5 1.3 %collective-permute-start = (f32[72,128]{1,0:T(8,128)S(1)}, f32[72,128]{1,0:T(8,128)S(1)}, u32[]{:S(2)}, u32[]{:S(2)}) collective-permute-start(f32[72,128]{1,0:T(8,128)S(1)} %pack_side.1), channel_id=1, source_target_pairs={{0,1},{1,0},{2,3},{3,2},{4,5},{5,4},{6,7},{7,6},{8,9},{9,8},{10,11... | collective-permute-start | bytes 110600 | tf_op jit(solution)/shard_map/ppermute | solution.py:709
  3.8 2.6 %prepare.1 = (f32[256,1024]{1,0:T(8,128)S(1)}, f32[256,1024]{1,0:T(8,128)S(1)}, f32[256,1024]{1,0:T(8,128)S(1)}, f32[256,1024]{1,0:T(8,128)S(1)}, f32[272,128]{1,0:T(8,128)S(1)}, /*index=5*/f32[272,128]{1,0:T(8,128)S(1)}) custom-call(f32[1,4]{1,0:T(1,128)} %params.7, f32[256,1024]{1,0:T(8,128)} %bed.3, s32[256,1024]{1,0:T(8,128)} %mask.3, s32[256,1024]{1,0:T(8,128)} %kind.3, ...), custom_call_target="tpu_custom_call" | custom-call | flops 2000000000 | tf_op jit(solution)/shard_map/prepare/pallas_call | solution.py:203
  6.4 0.1 collective-permute-start.1
  6.5 2.8 %middle_other.1 = (f32[1,3,256,1024]{3,2,1,0:T(8,128)S(1)}, f32[520,128]{1,0:T(8,128)S(1)}) custom-call(s32[4]{0:T(128)S(1)} %copy-done.3, f32[1,4]{1,0:T(1,128)S(1)} %copy-done.2, f32[256,1024]{1,0:T(8,128)S(1)} %get-tuple-element.36.root, f32[256,1024]{1,0:T(8,128)S(1)} %get-tuple-element.37.a, f32[256,1024]{1,0:T(8,128)S(1)} %get-tuple-element.38.b, ...), custom_call_target="tpu_custom_call" | custom-call | flops 4000000000 | tf_op jit(solution)/shard_map/middle_other/pallas_call | solution.py:439
  9.3 1.2 %collective-permute-start.3 = (f32[520,128]{1,0:T(8,128)S(1)}, f32[520,128]{1,0:T(8,128)S(1)}, u32[]{:S(2)}, u32[]{:S(2)}) collective-permute-start(f32[520,128]{1,0:T(8,128)S(1)} %get-tuple-element.49), channel_id=1, source_target_pairs={{0,8},{8,0},{16,24},{24,16},{1,9},{9,1},{17,25},{25,17},{2,10},{10... | collective-permute-start | bytes 798728 | tf_op jit(solution)/shard_map/ppermute | solution.py:717
  10.5 0.4 %collective-permute-done.1.far_a = f32[272,128]{1,0:T(8,128)S(1)} collective-permute-done((f32[272,128]{1,0:T(8,128)S(1)}, f32[272,128]{1,0:T(8,128)S(1)}, u32[]{:S(2)}, u32[]{:S(2)}) %collective-permute-start.1) | collective-permute-done | bytes 139296 | tf_op jit(solution)/shard_map/ppermute | solution.py:713
  10.9 4.1 %collective-permute-start.2 = (f32[272,128]{1,0:T(8,128)S(1)}, f32[272,128]{1,0:T(8,128)S(1)}, u32[]{:S(2)}, u32[]{:S(2)}) collective-permute-start(f32[272,128]{1,0:T(8,128)S(1)} %get-tuple-element.45), channel_id=1, source_target_pairs={{0,0},{2,4},{4,2},{6,6},{1,1},{3,5},{5,3},{7,7},{8,8},{10,12},{12,... | collective-permute-start | bytes 417800 | tf_op jit(solution)/shard_map/ppermute | solution.py:716
  15.0 2.8 %middle_own.1 = (f32[1,3,256,1024]{3,2,1,0:T(8,128)S(1)}, f32[520,128]{1,0:T(8,128)S(1)}) custom-call(s32[4]{0:T(128)S(1)} %copy-done.3, f32[1,4]{1,0:T(1,128)S(1)} %copy-done.2, f32[256,1024]{1,0:T(8,128)S(1)} %get-tuple-element.36.root, f32[256,1024]{1,0:T(8,128)S(1)} %get-tuple-element.37.a, ...), custom_call_target="tpu_custom_call", output_to_operand_aliasing={{0}: (8, {})} | custom-call | flops 4000000000 | tf_op jit(solution)/shard_map/middle_own/pallas_call | solution.py:439
  17.9 1.3 %collective-permute-start.4 = (f32[520,128]{1,0:T(8,128)S(1)}, f32[520,128]{1,0:T(8,128)S(1)}, u32[]{:S(2)}, u32[]{:S(2)}) collective-permute-start(f32[520,128]{1,0:T(8,128)S(1)} %add.12), channel_id=1, source_target_pairs={{0,16},{8,24},{16,0},{24,8},{1,17},{9,25},{17,1},{25,9},{2,18},{10... | collective-permute-start | bytes 798728 | tf_op jit(solution)/shard_map/ppermute | solution.py:703
  19.2 3.0 %edge_other.1 = (f32[1,3,256,1024]{3,2,1,0:T(8,128)S(1)}, f32[528,128]{1,0:T(8,128)S(1)}) custom-call(s32[4]{0:T(128)S(1)} %copy-done.3, f32[1,4]{1,0:T(1,128)S(1)} %copy-done.2, f32[256,1024]{1,0:T(8,128)S(1)} %get-tuple-element.36.root, f32[256,1024]{1,0:T(8,128)S(1)} %get-tuple-element.37.a, ...), custom_call_target="tpu_custom_call", output_to_operand_aliasing={{0}: (10, {})} | custom-call | flops 3000000000 | tf_op jit(solution)/shard_map/edge_other/pallas_call | solution.py:514
  22.2 1.5 %collective-permute-start.5 = (f32[528,128]{1,0:T(8,128)S(1)}, f32[528,128]{1,0:T(8,128)S(1)}, u32[]{:S(2)}, u32[]{:S(2)}) collective-permute-start(f32[528,128]{1,0:T(8,128)S(1)} %get-tuple-element.56), channel_id=1, source_target_pairs={{0,8},{8,0},{16,24},{24,16},{1,9},{9,1},{17,25},{25,17},{2,10},{10... | collective-permute-start | bytes 811016 | tf_op jit(solution)/shard_map/ppermute | solution.py:722
  23.7 3.0 %edge_own.1 = (f32[1,3,256,1024]{3,2,1,0:T(8,128)S(1)}, f32[528,128]{1,0:T(8,128)S(1)}) custom-call(s32[4]{0:T(128)S(1)} %copy-done.3, f32[1,4]{1,0:T(1,128)S(1)} %copy-done.2, f32[256,1024]{1,0:T(8,128)S(1)} %get-tuple-element.36.root, f32[256,1024]{1,0:T(8,128)S(1)} %get-tuple-element.37.a, ...), custom_call_target="tpu_custom_call", output_to_operand_aliasing={{0}: (10, {})} | custom-call | flops 3000000000 | tf_op jit(solution)/shard_map/edge_own/pallas_call | solution.py:514
  26.8 0.1 collective-permute-start.6
  26.9 1.2 %collective-permute-start.7 = (f32[528,128]{1,0:T(8,128)S(1)}, f32[528,128]{1,0:T(8,128)S(1)}, u32[]{:S(2)}, u32[]{:S(2)}) collective-permute-start(f32[528,128]{1,0:T(8,128)S(1)} %add.14), channel_id=1, source_target_pairs={{0,16},{8,24},{16,0},{24,8},{1,17},{9,25},{17,1},{25,9},{2,18},{10... | collective-permute-start | bytes 811016 | tf_op jit(solution)/shard_map/ppermute | solution.py:703
  28.1 0.2 collective-permute-done.6.got_m
  28.4 2.2 %bed_middle.1 = (f32[256,1024]{1,0:T(8,128)}, f32[256,1024]{1,0:T(8,128)}, f32[1,3,256,1024]{3,2,1,0:T(8,128)}) custom-call(f32[256,1024]{1,0:T(8,128)S(1)} %get-tuple-element.35.bed, f32[72,128]{1,0:T(8,128)S(1)} %collective-permute-done.side, f32[272,128]{1,0:T(8,128)S(1)} %collective-permute-done.1.far_a, f32[272,128]{1,0:T(8,128)S(1)} %collective-permute-done.2.far_b, ...), custom_call_target="tpu_custom_call" | custom-call | flops 4000000000 | tf_op jit(solution)/shard_map/bed_middle/pallas_call | solution.py:659
  30.6 3.9 %collective-permute-done.7 = f32[528,128]{1,0:T(8,128)S(1)} collective-permute-done((f32[528,128]{1,0:T(8,128)S(1)}, f32[528,128]{1,0:T(8,128)S(1)}, u32[]{:S(2)}, u32[]{:S(2)}) %collective-permute-start.7) | collective-permute-done | bytes 270368 | tf_op jit(solution)/shard_map/ppermute | solution.py:703
  34.6 1.3 %collective-permute-start.8 = (f32[528,128]{1,0:T(8,128)S(1)}, f32[528,128]{1,0:T(8,128)S(1)}, u32[]{:S(2)}, u32[]{:S(2)}) collective-permute-start(f32[528,128]{1,0:T(8,128)S(1)} %add.15.own_e), channel_id=1, source_target_pairs={{0,8},{8,0},{16,24},{24,16},{1,9},{9,1},{17,25},{25,17},{2,10},{10... | collective-permute-start | bytes 811016 | tf_op jit(solution)/shard_map/ppermute | solution.py:730
  35.9 1.2 %collective-permute-done.8.got_e = f32[528,128]{1,0:T(8,128)S(1)} collective-permute-done((f32[528,128]{1,0:T(8,128)S(1)}, f32[528,128]{1,0:T(8,128)S(1)}, u32[]{:S(2)}, u32[]{:S(2)}) %collective-permute-start.8) | collective-permute-done | bytes 270368 | tf_op jit(solution)/shard_map/ppermute | solution.py:730
  37.1 1.9 %bed_edge.1 = (f32[256,1024]{1,0:T(8,128)}, f32[256,1024]{1,0:T(8,128)}) custom-call(f32[256,1024]{1,0:T(8,128)S(1)} %get-tuple-element.35.bed, f32[72,128]{1,0:T(8,128)S(1)} %collective-permute-done.side, f32[272,128]{1,0:T(8,128)S(1)} %collective-permute-done.1.far_a, ...), custom_call_target="tpu_custom_call", output_to_operand_aliasing={{0}: (8, {}), {1}: (9, {})} | custom-call | flops 2000000000 | tf_op jit(solution)/shard_map/bed_edge/pallas_call | solution.py:672
  (15 shorter events, 0.2 us)
Async XLA Ops:
  2.4 4.1 %copy-start = (f32[1,3,256,1024]{3,2,1,0:T(8,128)S(1)}, f32[1,3,256,1024]{3,2,1,0:T(8,128)}, u32[]{:S(2)}) copy-start(f32[1,3,256,1024]{3,2,1,0:T(8,128)} %hydro.11) | copy-start | bytes 9437188
  2.4 4.1 %copy-start.1 = (f32[1,2,256,1024]{3,2,1,0:T(8,128)S(1)}, f32[1,2,256,1024]{3,2,1,0:T(8,128)}, u32[]{:S(2)}) copy-start(f32[1,2,256,1024]{3,2,1,0:T(8,128)} %stress.11) | copy-start | bytes 6291460
  2.4 4.1 %copy-start.2 = (f32[1,4]{1,0:T(1,128)S(1)}, f32[1,4]{1,0:T(1,128)}, u32[]{:S(2)}) copy-start(f32[1,4]{1,0:T(1,128)} %params.7) | copy-start | bytes 52
  2.4 4.1 %copy-start.3 = (s32[4]{0:T(128)S(1)}, s32[4]{0:T(128)}, u32[]{:S(2)}) copy-start(s32[4]{0:T(128)} %weights.7) | copy-start | bytes 52
  2.5 3.9 %collective-permute-start = (f32[72,128]{1,0:T(8,128)S(1)}, f32[72,128]{1,0:T(8,128)S(1)}, u32[]{:S(2)}, u32[]{:S(2)}) collective-permute-start(f32[72,128]{1,0:T(8,128)S(1)} %pack_side.1), channel_id=1, source_target_pairs={{0,1},{1,0},{2,3},{3,2},{4,5},{5,4},{6,7},{7,6},{8,9},{9,8},{10,11... | collective-permute-start | bytes 110600 | tf_op jit(solution)/shard_map/ppermute | solution.py:709
  6.4 4.6 %collective-permute-start.1 = (f32[272,128]{1,0:T(8,128)S(1)}, f32[272,128]{1,0:T(8,128)S(1)}, u32[]{:S(2)}, u32[]{:S(2)}) collective-permute-start(f32[272,128]{1,0:T(8,128)S(1)} %get-tuple-element.42), channel_id=1, source_target_pairs={{0,2},{2,0},{4,6},{6,4},{1,3},{3,1},{5,7},{7,5},{8,10},{10,8},{12,... | collective-permute-start | bytes 417800 | tf_op jit(solution)/shard_map/ppermute | solution.py:713
  9.3 8.5 %collective-permute-start.3 = (f32[520,128]{1,0:T(8,128)S(1)}, f32[520,128]{1,0:T(8,128)S(1)}, u32[]{:S(2)}, u32[]{:S(2)}) collective-permute-start(f32[520,128]{1,0:T(8,128)S(1)} %get-tuple-element.49), channel_id=1, source_target_pairs={{0,8},{8,0},{16,24},{24,16},{1,9},{9,1},{17,25},{25,17},{2,10},{10... | collective-permute-start | bytes 798728 | tf_op jit(solution)/shard_map/ppermute | solution.py:717
  10.9 8.2 %collective-permute-start.2 = (f32[272,128]{1,0:T(8,128)S(1)}, f32[272,128]{1,0:T(8,128)S(1)}, u32[]{:S(2)}, u32[]{:S(2)}) collective-permute-start(f32[272,128]{1,0:T(8,128)S(1)} %get-tuple-element.45), channel_id=1, source_target_pairs={{0,0},{2,4},{4,2},{6,6},{1,1},{3,5},{5,3},{7,7},{8,8},{10,12},{12,... | collective-permute-start | bytes 417800 | tf_op jit(solution)/shard_map/ppermute | solution.py:716
  17.9 8.8 %collective-permute-start.4 = (f32[520,128]{1,0:T(8,128)S(1)}, f32[520,128]{1,0:T(8,128)S(1)}, u32[]{:S(2)}, u32[]{:S(2)}) collective-permute-start(f32[520,128]{1,0:T(8,128)S(1)} %add.12), channel_id=1, source_target_pairs={{0,16},{8,24},{16,0},{24,8},{1,17},{9,25},{17,1},{25,9},{2,18},{10... | collective-permute-start | bytes 798728 | tf_op jit(solution)/shard_map/ppermute | solution.py:703
  22.2 4.6 %collective-permute-start.5 = (f32[528,128]{1,0:T(8,128)S(1)}, f32[528,128]{1,0:T(8,128)S(1)}, u32[]{:S(2)}, u32[]{:S(2)}) collective-permute-start(f32[528,128]{1,0:T(8,128)S(1)} %get-tuple-element.56), channel_id=1, source_target_pairs={{0,8},{8,0},{16,24},{24,16},{1,9},{9,1},{17,25},{25,17},{2,10},{10... | collective-permute-start | bytes 811016 | tf_op jit(solution)/shard_map/ppermute | solution.py:722
  26.8 1.6 %collective-permute-start.6 = (f32[520,128]{1,0:T(8,128)S(1)}, f32[520,128]{1,0:T(8,128)S(1)}, u32[]{:S(2)}, u32[]{:S(2)}) collective-permute-start(f32[520,128]{1,0:T(8,128)S(1)} %add.13.own_m), channel_id=1, source_target_pairs={{0,8},{8,0},{16,24},{24,16},{1,9},{9,1},{17,25},{25,17},{2,10},{10... | collective-permute-start | bytes 798728 | tf_op jit(solution)/shard_map/ppermute | solution.py:727
  26.9 7.6 %collective-permute-start.7 = (f32[528,128]{1,0:T(8,128)S(1)}, f32[528,128]{1,0:T(8,128)S(1)}, u32[]{:S(2)}, u32[]{:S(2)}) collective-permute-start(f32[528,128]{1,0:T(8,128)S(1)} %add.14), channel_id=1, source_target_pairs={{0,16},{8,24},{16,0},{24,8},{1,17},{9,25},{17,1},{25,9},{2,18},{10... | collective-permute-start | bytes 811016 | tf_op jit(solution)/shard_map/ppermute | solution.py:703
  34.6 2.5 %collective-permute-start.8 = (f32[528,128]{1,0:T(8,128)S(1)}, f32[528,128]{1,0:T(8,128)S(1)}, u32[]{:S(2)}, u32[]{:S(2)}) collective-permute-start(f32[528,128]{1,0:T(8,128)S(1)} %add.15.own_e), channel_id=1, source_target_pairs={{0,8},{8,0},{16,24},{24,16},{1,9},{9,1},{17,25},{25,17},{2,10},{10... | collective-permute-start | bytes 811016 | tf_op jit(solution)/shard_map/ppermute | solution.py:730

commit v11 on v10

--- a/solution.py
+++ b/solution.py
@@ -375,15 +375,22 @@
         self.qr_last[...] = jnp.zeros_like(self.qr_last)
         for ref in (self.e1, self.e2):
             ref[tile_at(self.count), :] = jnp.zeros((SUB, self.wide), jnp.float32)
-        stages = (self.step_three, self.step_two, self.step_one)
+        turns = []
         for t in range(self.count + LAG * (STEPS - 1)):
-            turns = []
-            for k, stage in enumerate(stages):
-                i = t - LAG * (STEPS - 1 - k)
-                if 0 <= i < self.count:
-                    turns.append(stage(i))
-            while turns:
-                turns = [turn for turn in turns if next(turn, True) is None]
+            for k, stage in enumerate((self.step_one, self.step_two, self.step_three)):
+                if 0 <= t - LAG * k < self.count:
+                    turns.append(stage(t - LAG * k))
+        pipeline(turns)
+
+
+def pipeline(turns):
+    active = []
+    for turn in turns:
+        active = [one for one in active if next(one, True) is None]
+        if next(turn, True) is None:
+            active.append(turn)
+    while active:
+        active = [one for one in active if next(one, True) is None]
 
 
 def reader(root, a, b, stress, hydro, side, unfold, valid):
@@ -581,25 +588,32 @@
     def spill(self, slope):
         return 0.25 * (slope - jnp.clip(slope, -1.0, 1.0))
 
-    def south_face(self, z, lower, b):
-        out = self.spill(south(z, lower) - z)
+    def south_face(self, slope, b):
+        out = self.spill(slope)
         if b == -1:
             return jnp.where((lax.axis_index("ty") == 0) & self.last_row, 0.0, out)
         if b == self.blocks - 1:
             return jnp.where((lax.axis_index("ty") == lax.axis_size("ty") - 1) & self.last_row, 0.0, out)
         return out
 
-    def run(self, first, stop, keep, after=lambda b: None):
+    def block(self, b, keep):
+        z, lower = self.ahead, self.level(b + 1, keep)
+        self.ahead = lower
+        right, down = east(z), south(z, lower)
+        yield
+        gc = jnp.where(self.shut_c, 0.0, self.spill(right - z))
+        gr = self.south_face(down - z, b)
+        left, up = west(gc), north(gr, self.gr_above)
+        self.gr_above = gr
+        yield
+        out = z + gc - left + gr - up
+        self.next_v[tile_at(b), :] = out[:, : self.cols]
+
+    def run(self, first, stop, keep):
         z = self.level(first - 1, keep)
-        lower = self.level(first, keep)
-        gr = self.south_face(z, lower, first - 1)
-        for b in range(first, stop):
-            z, lower = lower, self.level(b + 1, keep)
-            gr_above, gr = gr, self.south_face(z, lower, b)
-            gc = jnp.where(self.shut_c, 0.0, self.spill(east(z) - z))
-            out = z + gc - west(gc) + gr - north(gr, gr_above)
-            self.next_v[tile_at(b), :] = out[:, : self.cols]
-            after(b)
+        self.ahead = self.level(first, keep)
+        self.gr_above = self.south_face(south(z, self.ahead) - z, first - 1)
+        pipeline([self.block(b, keep) for b in range(first, stop)])
 
 
 def bed_middle_kernel(

time: 39.4 us -> 40.6 us (1.030)
  Pallas kernels: 20.1 us -> 21.8 us
  starting transfers between devices: 12.2 us -> 11.7 us
    pallas_call x2, Pallas kernels: 5.61 us -> 6.47 us  [middle(): pl.pallas_call(functools.partial(middle_kernel, own), name='middle_own' i...]
    pallas_call x2, Pallas kernels: 5.96 us -> 6.8 us  [edge(): pl.pallas_call(functools.partial(edge_kernel, own), name='edge_own' if ow...]
    ppermute x2, starting transfers between devices: 2.72 us -> 2.29 us  [shards(): got = lax.ppermute(pay, 'cond', swap)]
    ppermute x1, starting transfers between devices: 4.08 us -> 4.5 us  [shards(): far_b = lax.ppermute(far_b, 'ty', pairs(1))]
    ppermute x1, waiting for transfers between devices: 0.42 us -> 0.01 us  [shards(): far_a = lax.ppermute(far_a, 'ty', pairs(0))]
  transfers between devices with their start and end apart: 9 -> 9, of which waited for: 4 -> 3; matrix products, arithmetic and copies ran while one was open for 0% -> 0% of each run, Pallas kernels for 42% -> 45%
where the time goes in v11:
time: 40.6 us; the launch traced here: 40.5 us
  Pallas kernels  21.8 us (54%)
  starting transfers between devices  11.7 us (29%)
  waiting for transfers between devices  5.74 us (14%)
  between operations  0.98 us (2%)
    pallas_call x2, Pallas kernels, edge(): pl.pallas_call(functools.partial(edge_kernel, own), name='edge_own' if ow...  6.8 us
    pallas_call x2, Pallas kernels, middle(): pl.pallas_call(functools.partial(middle_kernel, own), name='middle_own' i...  6.47 us
    ppermute x1, starting transfers between devices, shards(): far_b = lax.ppermute(far_b, 'ty', pairs(1))  4.5 us
    ppermute x2, waiting for transfers between devices, over_chips(): got = lax.ppermute(part, 'cond', [(i, i ^ reach) for i in range(nc)])  3.92 us
    pallas_call x1, Pallas kernels, prepare(): pl.pallas_call(prepare_kernel, name='prepare', out_shape=[tile] * 4 + [pl...  2.58 us
    ppermute x2, starting transfers between devices, shards(): got = lax.ppermute(pay, 'cond', swap)  2.29 us
    pallas_call x1, Pallas kernels, bed_middle(): pl.pallas_call(bed_middle_kernel, name='bed_middle', out_shape=[pltpu.HBM...  2.24 us
    ppermute x2, starting transfers between devices, over_chips(): got = lax.ppermute(part, 'cond', [(i, i ^ reach) for i in range(nc)])  2.16 us
  transfers between devices with their start and end apart: 9, of which 3 were waited for; matrix products, arithmetic and copies ran while one was open for 0% of the time, Pallas kernels for 45%

profile of v11, /device:TPU:9, one launch (start us, length us, event | category | flops | bytes accessed | tf_op | source)
XLA Modules:
  0.0 40.5 jit_solution(15171703682861408829)
XLA Ops:
  0.6 1.8 %pack_side.1 = f32[72,128]{1,0:T(8,128)S(1)} custom-call(f32[1,4]{1,0:T(1,128)} %params.7, f32[256,1024]{1,0:T(8,128)} %bed.3, s32[256,1024]{1,0:T(8,128)} %mask.3, s32[256,1024]{1,0:T(8,128)} %kind.3, f32[1,2,256,1024]{3,2,1,0:T(8,128)} %stress.11, f32[1,3,256,1024]{3,2,1,0:T(8,128)} %hydro.11), custom_call_target="tpu_custom_call" | custom-call | flops 2000000000 | tf_op jit(solution)/shard_map/pack_side/pallas_call | solution.py:114
  2.4 0.0 copy-start
  2.4 0.0 copy-start.1
  2.4 0.0 copy-start.2
  2.4 0.0 copy-start.3
  2.5 1.3 %collective-permute-start = (f32[72,128]{1,0:T(8,128)S(1)}, f32[72,128]{1,0:T(8,128)S(1)}, u32[]{:S(2)}, u32[]{:S(2)}) collective-permute-start(f32[72,128]{1,0:T(8,128)S(1)} %pack_side.1), channel_id=1, source_target_pairs={{0,1},{1,0},{2,3},{3,2},{4,5},{5,4},{6,7},{7,6},{8,9},{9,8},{10,11... | collective-permute-start | bytes 110600 | tf_op jit(solution)/shard_map/ppermute | solution.py:723
  3.8 2.6 %prepare.1 = (f32[256,1024]{1,0:T(8,128)S(1)}, f32[256,1024]{1,0:T(8,128)S(1)}, f32[256,1024]{1,0:T(8,128)S(1)}, f32[256,1024]{1,0:T(8,128)S(1)}, f32[272,128]{1,0:T(8,128)S(1)}, /*index=5*/f32[272,128]{1,0:T(8,128)S(1)}) custom-call(f32[1,4]{1,0:T(1,128)} %params.7, f32[256,1024]{1,0:T(8,128)} %bed.3, s32[256,1024]{1,0:T(8,128)} %mask.3, s32[256,1024]{1,0:T(8,128)} %kind.3, ...), custom_call_target="tpu_custom_call" | custom-call | flops 2000000000 | tf_op jit(solution)/shard_map/prepare/pallas_call | solution.py:203
  6.4 0.1 collective-permute-start.1
  6.5 3.2 %middle_other.1 = (f32[1,3,256,1024]{3,2,1,0:T(8,128)S(1)}, f32[520,128]{1,0:T(8,128)S(1)}) custom-call(s32[4]{0:T(128)S(1)} %copy-done.3, f32[1,4]{1,0:T(1,128)S(1)} %copy-done.2, f32[256,1024]{1,0:T(8,128)S(1)} %get-tuple-element.36.root, f32[256,1024]{1,0:T(8,128)S(1)} %get-tuple-element.37.a, f32[256,1024]{1,0:T(8,128)S(1)} %get-tuple-element.38.b, ...), custom_call_target="tpu_custom_call" | custom-call | flops 4000000000 | tf_op jit(solution)/shard_map/middle_other/pallas_call | solution.py:446
  9.8 1.2 %collective-permute-start.3 = (f32[520,128]{1,0:T(8,128)S(1)}, f32[520,128]{1,0:T(8,128)S(1)}, u32[]{:S(2)}, u32[]{:S(2)}) collective-permute-start(f32[520,128]{1,0:T(8,128)S(1)} %get-tuple-element.49), channel_id=1, source_target_pairs={{0,8},{8,0},{16,24},{24,16},{1,9},{9,1},{17,25},{25,17},{2,10},{10... | collective-permute-start | bytes 798728 | tf_op jit(solution)/shard_map/ppermute | solution.py:731
  11.0 4.5 %collective-permute-start.2 = (f32[272,128]{1,0:T(8,128)S(1)}, f32[272,128]{1,0:T(8,128)S(1)}, u32[]{:S(2)}, u32[]{:S(2)}) collective-permute-start(f32[272,128]{1,0:T(8,128)S(1)} %get-tuple-element.45), channel_id=1, source_target_pairs={{0,0},{2,4},{4,2},{6,6},{1,1},{3,5},{5,3},{7,7},{8,8},{10,12},{12,... | collective-permute-start | bytes 417800 | tf_op jit(solution)/shard_map/ppermute | solution.py:730
  15.5 3.2 %middle_own.1 = (f32[1,3,256,1024]{3,2,1,0:T(8,128)S(1)}, f32[520,128]{1,0:T(8,128)S(1)}) custom-call(s32[4]{0:T(128)S(1)} %copy-done.3, f32[1,4]{1,0:T(1,128)S(1)} %copy-done.2, f32[256,1024]{1,0:T(8,128)S(1)} %get-tuple-element.36.root, f32[256,1024]{1,0:T(8,128)S(1)} %get-tuple-element.37.a, ...), custom_call_target="tpu_custom_call", output_to_operand_aliasing={{0}: (8, {})} | custom-call | flops 4000000000 | tf_op jit(solution)/shard_map/middle_own/pallas_call | solution.py:446
  18.8 1.3 %collective-permute-start.4 = (f32[520,128]{1,0:T(8,128)S(1)}, f32[520,128]{1,0:T(8,128)S(1)}, u32[]{:S(2)}, u32[]{:S(2)}) collective-permute-start(f32[520,128]{1,0:T(8,128)S(1)} %add.12), channel_id=1, source_target_pairs={{0,16},{8,24},{16,0},{24,8},{1,17},{9,25},{17,1},{25,9},{2,18},{10... | collective-permute-start | bytes 798728 | tf_op jit(solution)/shard_map/ppermute | solution.py:717
  20.0 3.4 %edge_other.1 = (f32[1,3,256,1024]{3,2,1,0:T(8,128)S(1)}, f32[528,128]{1,0:T(8,128)S(1)}) custom-call(s32[4]{0:T(128)S(1)} %copy-done.3, f32[1,4]{1,0:T(1,128)S(1)} %copy-done.2, f32[256,1024]{1,0:T(8,128)S(1)} %get-tuple-element.36.root, f32[256,1024]{1,0:T(8,128)S(1)} %get-tuple-element.37.a, ...), custom_call_target="tpu_custom_call", output_to_operand_aliasing={{0}: (10, {})} | custom-call | flops 3000000000 | tf_op jit(solution)/shard_map/edge_other/pallas_call | solution.py:521
  23.4 1.1 %collective-permute-start.5 = (f32[528,128]{1,0:T(8,128)S(1)}, f32[528,128]{1,0:T(8,128)S(1)}, u32[]{:S(2)}, u32[]{:S(2)}) collective-permute-start(f32[528,128]{1,0:T(8,128)S(1)} %get-tuple-element.56), channel_id=1, source_target_pairs={{0,8},{8,0},{16,24},{24,16},{1,9},{9,1},{17,25},{25,17},{2,10},{10... | collective-permute-start | bytes 811016 | tf_op jit(solution)/shard_map/ppermute | solution.py:736
  24.5 3.4 %edge_own.1 = (f32[1,3,256,1024]{3,2,1,0:T(8,128)S(1)}, f32[528,128]{1,0:T(8,128)S(1)}) custom-call(s32[4]{0:T(128)S(1)} %copy-done.3, f32[1,4]{1,0:T(1,128)S(1)} %copy-done.2, f32[256,1024]{1,0:T(8,128)S(1)} %get-tuple-element.36.root, f32[256,1024]{1,0:T(8,128)S(1)} %get-tuple-element.37.a, ...), custom_call_target="tpu_custom_call", output_to_operand_aliasing={{0}: (10, {})} | custom-call | flops 3000000000 | tf_op jit(solution)/shard_map/edge_own/pallas_call | solution.py:521
  28.0 0.1 collective-permute-start.6
  28.1 0.9 %collective-permute-start.7 = (f32[528,128]{1,0:T(8,128)S(1)}, f32[528,128]{1,0:T(8,128)S(1)}, u32[]{:S(2)}, u32[]{:S(2)}) collective-permute-start(f32[528,128]{1,0:T(8,128)S(1)} %add.14), channel_id=1, source_target_pairs={{0,16},{8,24},{16,0},{24,8},{1,17},{9,25},{17,1},{25,9},{2,18},{10... | collective-permute-start | bytes 811016 | tf_op jit(solution)/shard_map/ppermute | solution.py:717
  29.0 0.6 %collective-permute-done.6.got_m = f32[520,128]{1,0:T(8,128)S(1)} collective-permute-done((f32[520,128]{1,0:T(8,128)S(1)}, f32[520,128]{1,0:T(8,128)S(1)}, u32[]{:S(2)}, u32[]{:S(2)}) %collective-permute-start.6) | collective-permute-done | bytes 266272 | tf_op jit(solution)/shard_map/ppermute | solution.py:741
  29.6 2.2 %bed_middle.1 = (f32[256,1024]{1,0:T(8,128)}, f32[256,1024]{1,0:T(8,128)}, f32[1,3,256,1024]{3,2,1,0:T(8,128)}) custom-call(f32[256,1024]{1,0:T(8,128)S(1)} %get-tuple-element.35.bed, f32[72,128]{1,0:T(8,128)S(1)} %collective-permute-done.side, f32[272,128]{1,0:T(8,128)S(1)} %collective-permute-done.1.far_a, f32[272,128]{1,0:T(8,128)S(1)} %collective-permute-done.2.far_b, ...), custom_call_target="tpu_custom_call" | custom-call | flops 4000000000 | tf_op jit(solution)/shard_map/bed_middle/pallas_call | solution.py:673
  31.9 3.9 %collective-permute-done.7 = f32[528,128]{1,0:T(8,128)S(1)} collective-permute-done((f32[528,128]{1,0:T(8,128)S(1)}, f32[528,128]{1,0:T(8,128)S(1)}, u32[]{:S(2)}, u32[]{:S(2)}) %collective-permute-start.7) | collective-permute-done | bytes 270368 | tf_op jit(solution)/shard_map/ppermute | solution.py:717
  35.8 1.3 %collective-permute-start.8 = (f32[528,128]{1,0:T(8,128)S(1)}, f32[528,128]{1,0:T(8,128)S(1)}, u32[]{:S(2)}, u32[]{:S(2)}) collective-permute-start(f32[528,128]{1,0:T(8,128)S(1)} %add.15.own_e), channel_id=1, source_target_pairs={{0,8},{8,0},{16,24},{24,16},{1,9},{9,1},{17,25},{25,17},{2,10},{10... | collective-permute-start | bytes 811016 | tf_op jit(solution)/shard_map/ppermute | solution.py:744
  37.2 1.2 %collective-permute-done.8.got_e = f32[528,128]{1,0:T(8,128)S(1)} collective-permute-done((f32[528,128]{1,0:T(8,128)S(1)}, f32[528,128]{1,0:T(8,128)S(1)}, u32[]{:S(2)}, u32[]{:S(2)}) %collective-permute-start.8) | collective-permute-done | bytes 270368 | tf_op jit(solution)/shard_map/ppermute | solution.py:744
  38.4 1.9 %bed_edge.1 = (f32[256,1024]{1,0:T(8,128)}, f32[256,1024]{1,0:T(8,128)}) custom-call(f32[256,1024]{1,0:T(8,128)S(1)} %get-tuple-element.35.bed, f32[72,128]{1,0:T(8,128)S(1)} %collective-permute-done.side, f32[272,128]{1,0:T(8,128)S(1)} %collective-permute-done.1.far_a, ...), custom_call_target="tpu_custom_call", output_to_operand_aliasing={{0}: (8, {}), {1}: (9, {})} | custom-call | flops 2000000000 | tf_op jit(solution)/shard_map/bed_edge/pallas_call | solution.py:686
  (15 shorter events, 0.2 us)
Async XLA Ops:
  2.4 4.1 %copy-start = (f32[1,3,256,1024]{3,2,1,0:T(8,128)S(1)}, f32[1,3,256,1024]{3,2,1,0:T(8,128)}, u32[]{:S(2)}) copy-start(f32[1,3,256,1024]{3,2,1,0:T(8,128)} %hydro.11) | copy-start | bytes 9437188
  2.4 4.1 %copy-start.1 = (f32[1,2,256,1024]{3,2,1,0:T(8,128)S(1)}, f32[1,2,256,1024]{3,2,1,0:T(8,128)}, u32[]{:S(2)}) copy-start(f32[1,2,256,1024]{3,2,1,0:T(8,128)} %stress.11) | copy-start | bytes 6291460
  2.4 4.1 %copy-start.2 = (f32[1,4]{1,0:T(1,128)S(1)}, f32[1,4]{1,0:T(1,128)}, u32[]{:S(2)}) copy-start(f32[1,4]{1,0:T(1,128)} %params.7) | copy-start | bytes 52
  2.4 4.1 %copy-start.3 = (s32[4]{0:T(128)S(1)}, s32[4]{0:T(128)}, u32[]{:S(2)}) copy-start(s32[4]{0:T(128)} %weights.7) | copy-start | bytes 52
  2.5 3.9 %collective-permute-start = (f32[72,128]{1,0:T(8,128)S(1)}, f32[72,128]{1,0:T(8,128)S(1)}, u32[]{:S(2)}, u32[]{:S(2)}) collective-permute-start(f32[72,128]{1,0:T(8,128)S(1)} %pack_side.1), channel_id=1, source_target_pairs={{0,1},{1,0},{2,3},{3,2},{4,5},{5,4},{6,7},{7,6},{8,9},{9,8},{10,11... | collective-permute-start | bytes 110600 | tf_op jit(solution)/shard_map/ppermute | solution.py:723
  6.4 4.6 %collective-permute-start.1 = (f32[272,128]{1,0:T(8,128)S(1)}, f32[272,128]{1,0:T(8,128)S(1)}, u32[]{:S(2)}, u32[]{:S(2)}) collective-permute-start(f32[272,128]{1,0:T(8,128)S(1)} %get-tuple-element.42), channel_id=1, source_target_pairs={{0,2},{2,0},{4,6},{6,4},{1,3},{3,1},{5,7},{7,5},{8,10},{10,8},{12,... | collective-permute-start | bytes 417800 | tf_op jit(solution)/shard_map/ppermute | solution.py:727
  9.8 9.0 %collective-permute-start.3 = (f32[520,128]{1,0:T(8,128)S(1)}, f32[520,128]{1,0:T(8,128)S(1)}, u32[]{:S(2)}, u32[]{:S(2)}) collective-permute-start(f32[520,128]{1,0:T(8,128)S(1)} %get-tuple-element.49), channel_id=1, source_target_pairs={{0,8},{8,0},{16,24},{24,16},{1,9},{9,1},{17,25},{25,17},{2,10},{10... | collective-permute-start | bytes 798728 | tf_op jit(solution)/shard_map/ppermute | solution.py:731
  11.0 9.1 %collective-permute-start.2 = (f32[272,128]{1,0:T(8,128)S(1)}, f32[272,128]{1,0:T(8,128)S(1)}, u32[]{:S(2)}, u32[]{:S(2)}) collective-permute-start(f32[272,128]{1,0:T(8,128)S(1)} %get-tuple-element.45), channel_id=1, source_target_pairs={{0,0},{2,4},{4,2},{6,6},{1,1},{3,5},{5,3},{7,7},{8,8},{10,12},{12,... | collective-permute-start | bytes 417800 | tf_op jit(solution)/shard_map/ppermute | solution.py:730
  18.8 9.2 %collective-permute-start.4 = (f32[520,128]{1,0:T(8,128)S(1)}, f32[520,128]{1,0:T(8,128)S(1)}, u32[]{:S(2)}, u32[]{:S(2)}) collective-permute-start(f32[520,128]{1,0:T(8,128)S(1)} %add.12), channel_id=1, source_target_pairs={{0,16},{8,24},{16,0},{24,8},{1,17},{9,25},{17,1},{25,9},{2,18},{10... | collective-permute-start | bytes 798728 | tf_op jit(solution)/shard_map/ppermute | solution.py:717
  23.4 4.5 %collective-permute-start.5 = (f32[528,128]{1,0:T(8,128)S(1)}, f32[528,128]{1,0:T(8,128)S(1)}, u32[]{:S(2)}, u32[]{:S(2)}) collective-permute-start(f32[528,128]{1,0:T(8,128)S(1)} %get-tuple-element.56), channel_id=1, source_target_pairs={{0,8},{8,0},{16,24},{24,16},{1,9},{9,1},{17,25},{25,17},{2,10},{10... | collective-permute-start | bytes 811016 | tf_op jit(solution)/shard_map/ppermute | solution.py:736
  28.0 1.6 %collective-permute-start.6 = (f32[520,128]{1,0:T(8,128)S(1)}, f32[520,128]{1,0:T(8,128)S(1)}, u32[]{:S(2)}, u32[]{:S(2)}) collective-permute-start(f32[520,128]{1,0:T(8,128)S(1)} %add.13.own_m), channel_id=1, source_target_pairs={{0,8},{8,0},{16,24},{24,16},{1,9},{9,1},{17,25},{25,17},{2,10},{10... | collective-permute-start | bytes 798728 | tf_op jit(solution)/shard_map/ppermute | solution.py:741
  28.1 7.7 %collective-permute-start.7 = (f32[528,128]{1,0:T(8,128)S(1)}, f32[528,128]{1,0:T(8,128)S(1)}, u32[]{:S(2)}, u32[]{:S(2)}) collective-permute-start(f32[528,128]{1,0:T(8,128)S(1)} %add.14), channel_id=1, source_target_pairs={{0,16},{8,24},{16,0},{24,8},{1,17},{9,25},{17,1},{25,9},{2,18},{10... | collective-permute-start | bytes 811016 | tf_op jit(solution)/shard_map/ppermute | solution.py:717
  35.8 2.5 %collective-permute-start.8 = (f32[528,128]{1,0:T(8,128)S(1)}, f32[528,128]{1,0:T(8,128)S(1)}, u32[]{:S(2)}, u32[]{:S(2)}) collective-permute-start(f32[528,128]{1,0:T(8,128)S(1)} %add.15.own_e), channel_id=1, source_target_pairs={{0,8},{8,0},{16,24},{24,16},{1,9},{9,1},{17,25},{25,17},{2,10},{10... | collective-permute-start | bytes 811016 | tf_op jit(solution)/shard_map/ppermute | solution.py:744

commit v12 on v6

--- a/solution.py
+++ b/solution.py
@@ -15,6 +15,7 @@
 GROUP = HALO * FIELDS
 FOLD = LANE // GROUP
 LAG = 2
+GROUP_TILES = 4
 MIB = 2**20
 ANY = pl.BlockSpec(memory_space=pl.ANY)
 VMEM = pl.BlockSpec(memory_space=pltpu.VMEM)
@@ -254,10 +255,7 @@
 
 
 class Sweep:
-    NAMES = (
-        ["fc", "fr", "wc", "wr", "e1", "u1"]
-        + ["v1", "e2", "u2", "v2", "qc1", "qr1", "qc2", "qr2"]
-    )
+    NAMES = ["fc", "fr", "wc", "wr", "e1", "u1"] + ["v1", "e2", "u2", "v2"] + ["qc1", "qr1", "qc2", "qr2"]
 
     def __init__(self, count, tiles, get, emit, weights, params, refs, trim):
         self.count, self.tiles, self.get, self.emit, self.trim = count, tiles, get, emit, trim
@@ -273,6 +271,8 @@
         lane, row = lanes_of((SUB, LANE)), rows_of((SUB, LANE))
         self.last_lane, self.first_lane = lane == LANE - 1, lane == 0
         self.last_row, self.first_row = row == SUB - 1, row == 0
+        own = list(range(tiles - 1))
+        self.groups = [[tiles - 1]] + [own[k : k + GROUP_TILES] for k in range(0, tiles - 1, GROUP_TILES)]
 
     @classmethod
     def scratch(cls, count, tiles):
@@ -288,60 +288,75 @@
     def north(self, x, above):
         return pltpu.roll(jnp.where(self.last_row, above, x), 1, 0)
 
-    def easts(self, values):
-        first = value = values(0)
-        first_rolled = rolled = pltpu.roll(first, LANE - 1, 1)
-        for k in range(self.tiles):
-            if k + 1 < self.tiles:
-                after = values(k + 1)
-                after_rolled = pltpu.roll(after, LANE - 1, 1)
-            else:
-                after, after_rolled = first, first_rolled
-            yield k, value, jnp.where(self.last_lane, after_rolled, rolled)
-            value, rolled = after, after_rolled
-
-    def wests(self, values):
-        before = pltpu.roll(values[-1], 1, 1)
-        for k, value in enumerate(values):
-            rolled = pltpu.roll(value, 1, 1)
-            yield k, value, jnp.where(self.first_lane, before, rolled)
-            before = rolled
-
-    def move(self, n, i, level, lower, speeds, faces, wets, keep):
-        flux, part = [], []
-        for k, here, right in self.easts(level):
-            wc, wr = wets(k)
-            fc, fr = faces(k)
-            u, v = speeds(k)
-            u = (self.slow * u - (right - here) + self.get(3, i, k)) * wc
-            v = (self.slow * v - (self.south(here, lower(k)) - here) + self.get(4, i, k)) * wr
-            flux_r = fr * v
-            part.append(
-                self.get(1, i, k) * here + self.get(2, i, k) - flux_r + self.north(flux_r, self.fr_last[n, k])
-            )
-            self.fr_last[n, k] = flux_r
-            flux.append(fc * u)
-            keep(k, u, v)
-        for k, value, left in self.wests(flux):
-            yield k, part[k] - value + left
+    def eastward(self, values):
+        kept = {}
+
+        def one(k):
+            if k not in kept:
+                value = values(k)
+                kept[k] = value, pltpu.roll(value, LANE - 1, 1)
+            return kept[k]
+
+        def both(k):
+            value, rolled = one(k)
+            return value, jnp.where(self.last_lane, one((k + 1) % self.tiles)[1], rolled)
+
+        return both
+
+    def west(self, rolled, k):
+        return jnp.where(self.first_lane, rolled[(k - 1) % self.tiles], rolled[k])
+
+    def move(self, n, i, level, lower, speeds, start, faces, keep, done):
+        levels = self.eastward(level)
+        flux, rolled, base, ups = {}, {}, {}, {}
+
+        def close(k):
+            done(k, base[k] + ups[k] - flux[k] + self.west(rolled, k))
+
+        for group in self.groups:
+            opened = []
+            for k in group:
+                here, right = levels(k)
+                opened.append((k, here, right, self.south(here, lower(k)), start(k)))
+            yield
+            for k, here, right, down, begun in opened:
+                fc, fr, wc, wr = faces(k, begun)
+                u, v = speeds(k)
+                u = (self.slow * u - (right - here) + self.get(3, i, k)) * wc
+                v = (self.slow * v - (down - here) + self.get(4, i, k)) * wr
+                flux[k] = fc * u
+                rolled[k] = pltpu.roll(flux[k], 1, 1)
+                flux_r = fr * v
+                ups[k] = self.north(flux_r, self.fr_last[n, k])
+                self.fr_last[n, k] = flux_r
+                base[k] = self.get(1, i, k) * here + self.get(2, i, k) - flux_r
+                keep(k, u, v)
+            yield
+            for k in group:
+                if k < self.tiles - 1:
+                    close(k)
+        close(self.tiles - 1)
 
     def step_one(self, i):
         at = tile_at(i)
         inside = i + 1 < self.count
-        for k, s, right in self.easts(lambda k: self.get(0, i, k)):
-            below = self.get(0, i + 1, k) if inside else s
-            for other, face_ref, wet_ref in ((right, self.fc, self.wc), (self.south(s, below), self.fr, self.wr)):
+        roots = self.eastward(lambda k: self.get(0, i, k))
+
+        def start(k):
+            s, right = roots(k)
+            return s, right, self.south(s, self.get(0, i + 1, k) if inside else s)
+
+        def faces(k, begun):
+            s, right, down = begun
+            out = []
+            for other, face_ref, wet_ref in ((right, self.fc, self.wc), (down, self.fr, self.wr)):
                 face = s * other
                 base = face + 0.1
                 inverse = pl.reciprocal(base, approx=True)
-                wet_ref[k, at, :] = face * (inverse * (2.0 - base * inverse))
-                face_ref[k, at, :] = 0.3 * face
-
-        def level(k):
-            return 0.3 * self.get(5, i, k)
-
-        def lower(k):
-            return 0.3 * self.get(5, i + 1 if inside else i, k)
+                out.append((0.3 * face, face * (inverse * (2.0 - base * inverse))))
+                face_ref[k, at, :], wet_ref[k, at, :] = out[-1]
+            (fc, wc), (fr, wr) = out
+            return fc, fr, wc, wr
 
         def keep(k, u, v):
             self.u1[k, at, :] = u
@@ -349,41 +364,41 @@
             self.qc1[k, at, :] = u * jnp.abs(u)
             self.qr1[k, at, :] = v * jnp.abs(v)
 
+        def done(k, e):
+            self.e1[k, at, :] = e
+
+        level = lambda k: 0.3 * self.get(5, i, k)
+        lower = lambda k: 0.3 * self.get(5, i + 1 if inside else i, k)
         speeds = lambda k: (self.get(6, i, k), self.get(7, i, k))
-        for k, e in self.move(0, i, level, lower, speeds, self.faces(at), self.wets(at), keep):
-            self.e1[k, at, :] = e
-
-    def faces(self, at):
-        return lambda k: (self.fc[k, at, :], self.fr[k, at, :])
-
-    def wets(self, at):
-        return lambda k: (self.wc[k, at, :], self.wr[k, at, :])
-
-    def later(self, n, i, e, u, v, keep):
+        return self.move(0, i, level, lower, speeds, start, faces, keep, done)
+
+    def later(self, n, i, e, u, v, keep, done):
         at, after = tile_at(i), tile_at(i + 1)
+        faces = lambda k, _: [ref[k, at, :] for ref in (self.fc, self.fr, self.wc, self.wr)]
+        speeds = lambda k: (u[k, at, :], v[k, at, :])
         return self.move(
-            n, i, lambda k: e[k, at, :], lambda k: e[k, after, :], lambda k: (u[k, at, :], v[k, at, :]),
-            self.faces(at), self.wets(at), keep,
+            n, i, lambda k: e[k, at, :], lambda k: e[k, after, :], speeds, lambda k: None, faces, keep, done
         )
 
     def step_two(self, i):
         at = tile_at(i)
-        last = self.trim and i == self.count - 1
 
         def keep(k, u, v):
-            if not last:
+            if not (self.trim and i == self.count - 1):
                 self.u2[k, at, :] = u
                 self.v2[k, at, :] = v
                 self.qc2[k, at, :] = self.qc1[k, at, :] + u * jnp.abs(u)
                 self.qr2[k, at, :] = self.qr1[k, at, :] + v * jnp.abs(v)
 
-        for k, e in self.later(1, i, self.e1, self.u1, self.v1, keep):
+        def done(k, e):
             self.e2[k, at, :] = e
+
+        return self.later(1, i, self.e1, self.u1, self.v1, keep, done)
 
     def step_three(self, i):
         at, after = tile_at(i), tile_at(i + 1)
         if self.trim and i == self.count - 1:
-            return
+            return iter(())
         if self.trim and i == 0:
             for k in range(self.tiles):
                 here, wr = self.e2[k, at, :], self.wr[k, at, :]
@@ -391,22 +406,24 @@
                 v = (self.slow * self.v2[k, at, :] - (self.south(here, lower) - here) + self.get(4, i, k)) * wr
                 self.fr_last[2, k] = self.fr[k, at, :] * v
                 self.qr_last[k] = wr * (self.qr2[k, at, :] + v * jnp.abs(v))
-            return
-        qcs, parts = [], []
+            return iter(())
+        rolled, parts = {}, {}
 
         def keep(k, u, v):
-            wc, wr = self.wets(at)(k)
             self.emit(i, 1, k, u)
             self.emit(i, 2, k, v)
-            qr = wr * (self.qr2[k, at, :] + v * jnp.abs(v))
-            qcs.append(wc * (self.qc2[k, at, :] + u * jnp.abs(u)))
-            parts.append(qr - self.north(qr, self.qr_last[k]))
+            qc = self.wc[k, at, :] * (self.qc2[k, at, :] + u * jnp.abs(u))
+            qr = self.wr[k, at, :] * (self.qr2[k, at, :] + v * jnp.abs(v))
+            rolled[k] = pltpu.roll(qc, 1, 1)
+            parts[k] = qc + qr, self.north(qr, self.qr_last[k])
             self.qr_last[k] = qr
 
-        for k, e in self.later(2, i, self.e2, self.u2, self.v2, keep):
+        def done(k, e):
             self.emit(i, 0, k, e * (1.0 / 0.3))
-        for k, qc, left in self.wests(qcs):
-            self.emit(i, 3, k, (qc - left + parts[k]) * self.scale)
+            part, up = parts[k]
+            self.emit(i, 3, k, (part - up - self.west(rolled, k)) * self.scale)
+
+        return self.later(2, i, self.e2, self.u2, self.v2, keep, done)
 
     def run(self):
         self.fr_last[...] = jnp.zeros_like(self.fr_last)
@@ -415,10 +432,13 @@
             ref[:, tile_at(self.count), :] = jnp.zeros((self.tiles, SUB, LANE), jnp.float32)
         stages = (self.step_three, self.step_two, self.step_one)
         for t in range(self.count + LAG * (STEPS - 1)):
+            turns = []
             for k, stage in enumerate(stages):
                 i = t - LAG * (STEPS - 1 - k)
                 if 0 <= i < self.count:
-                    stage(i)
+                    turns.append(stage(i))
+            while turns:
+                turns = [turn for turn in turns if next(turn, True) is None]
 
 
 def lanes_at(k):
@@ -508,6 +528,8 @@
     from_a = top == (lax.axis_index("ty") % 2 == 1)
     first = jnp.where(top, -1, blocks - quarter - 1)
 
+    ty = lax.axis_index("ty")
+    outside_map = ty == jnp.where(top, 0, lax.axis_size("ty") - 1)
     inner = jnp.where(top, quarter, blocks - quarter - 1)
     corners = pl.ds(lanes * GROUP, SUB)
     for f in range(FIELDS):
@@ -523,6 +545,8 @@
                 outer = jnp.where(top, unfold(corner, (FOLD - 1) * FIELDS + f), unfold(corner, f))
                 if f == 0:
                     outer = jnp.where(valid, outer, 0.0)
+            if f == 0:
+                outer = jnp.where(outside_map, 0.0, outer)
             ends[0, f, k] = jnp.where(top, outer, body)
             ends[1, f, k] = jnp.where(top, body, outer)
 
@@ -729,7 +753,10 @@
     swap = [(i, i ^ 1) for i in range(nc)]
 
     def pairs(first):
-        return [p for i in range(first, ny - 1, 2) for p in ((i, i + 1), (i + 1, i))]
+        partner = list(range(ny))
+        for i in range(first, ny - 1, 2):
+            partner[i], partner[i + 1] = i + 1, i
+        return list(enumerate(partner))
 
     def over_chips(part, beside=()):
         reach = 2

time: 41 us -> 43.3 us (1.056)
  Pallas kernels: 22.4 us -> 25 us
  starting transfers between devices: 11.5 us -> 10.7 us
  waiting for transfers between devices: 5.76 us -> 6.31 us
    pallas_call x2, Pallas kernels: 7 us -> 8.32 us  [edge(): pl.pallas_call(functools.partial(edge_kernel, own), name='edge_own' if ow...]
    pallas_call x2, Pallas kernels: 6.83 us -> 8.08 us  [middle(): pl.pallas_call(functools.partial(middle_kernel, own), name='middle_own' i...]
    ppermute x1, waiting for transfers between devices: 0.66 us -> 1.21 us  [shards(): got_m = lax.ppermute(own_m, 'cond', swap)]
    ppermute x2, starting transfers between devices: 2.14 us -> 1.59 us  [over_chips(): got = lax.ppermute(part, 'cond', [(i, i ^ reach) for i in range(nc)])]
  transfers between devices with their start and end apart: 9 -> 9, of which waited for: 3 -> 3; matrix products, arithmetic and copies ran while one was open for 0% -> 0% of each run, Pallas kernels for 46% -> 49%
where the time goes in v12:
time: 43.3 us; the launch traced here: 43.2 us
  Pallas kernels  25 us (58%)
  starting transfers between devices  10.7 us (25%)
  waiting for transfers between devices  6.31 us (15%)
  between operations  0.98 us (2%)
    pallas_call x2, Pallas kernels, edge(): pl.pallas_call(functools.partial(edge_kernel, own), name='edge_own' if ow...  8.32 us
    pallas_call x2, Pallas kernels, middle(): pl.pallas_call(functools.partial(middle_kernel, own), name='middle_own' i...  8.08 us
    ppermute x1, starting transfers between devices, shards(): far_b = lax.ppermute(far_b, 'ty', pairs(1))  4.5 us
    ppermute x2, waiting for transfers between devices, over_chips(): got = lax.ppermute(part, 'cond', [(i, i ^ reach) for i in range(nc)])  3.92 us
    pallas_call x1, Pallas kernels, prepare(): pl.pallas_call(prepare_kernel, name='prepare', out_shape=[tile] * 4 + [pl...  2.58 us
    pallas_call x1, Pallas kernels, bed_middle(): pl.pallas_call(bed_middle_kernel, name='bed_middle', out_shape=[pltpu.HBM...  2.24 us
    pallas_call x1, Pallas kernels, bed_edge(): pl.pallas_call(bed_edge_kernel, name='bed_edge', out_shape=[pltpu.HBM(bed...  1.95 us
    ppermute x2, starting transfers between devices, shards(): got = lax.ppermute(pay, 'cond', swap)  1.85 us
  transfers between devices with their start and end apart: 9, of which 3 were waited for; matrix products, arithmetic and copies ran while one was open for 0% of the time, Pallas kernels for 49%

profile of v12, /device:TPU:9, one launch (start us, length us, event | category | flops | bytes accessed | tf_op | source)
XLA Modules:
  0.0 43.2 jit_solution(13664833710643834301)
XLA Ops:
  0.6 1.8 %pack_side.1 = f32[72,128]{1,0:T(8,128)S(1)} custom-call(f32[1,4]{1,0:T(1,128)} %params.7, f32[256,1024]{1,0:T(8,128)} %bed.3, s32[256,1024]{1,0:T(8,128)} %mask.3, s32[256,1024]{1,0:T(8,128)} %kind.3, f32[1,2,256,1024]{3,2,1,0:T(8,128)} %stress.11, f32[1,3,256,1024]{3,2,1,0:T(8,128)} %hydro.11), custom_call_target="tpu_custom_call" | custom-call | flops 2000000000 | tf_op jit(solution)/shard_map/pack_side/pallas_call | solution.py:115
  2.4 0.0 copy-start
  2.4 0.0 copy-start.1
  2.4 0.0 copy-start.2
  2.4 0.0 copy-start.3
  2.5 1.3 %collective-permute-start = (f32[72,128]{1,0:T(8,128)S(1)}, f32[72,128]{1,0:T(8,128)S(1)}, u32[]{:S(2)}, u32[]{:S(2)}) collective-permute-start(f32[72,128]{1,0:T(8,128)S(1)} %pack_side.1), channel_id=1, source_target_pairs={{0,1},{1,0},{2,3},{3,2},{4,5},{5,4},{6,7},{7,6},{8,9},{9,8},{10,11... | collective-permute-start | bytes 110600 | tf_op jit(solution)/shard_map/ppermute | solution.py:770
  3.8 2.6 %prepare.1 = (f32[256,1024]{1,0:T(8,128)S(1)}, f32[256,1024]{1,0:T(8,128)S(1)}, f32[256,1024]{1,0:T(8,128)S(1)}, f32[256,1024]{1,0:T(8,128)S(1)}, f32[272,128]{1,0:T(8,128)S(1)}, /*index=5*/f32[272,128]{1,0:T(8,128)S(1)}) custom-call(f32[1,4]{1,0:T(1,128)} %params.7, f32[256,1024]{1,0:T(8,128)} %bed.3, s32[256,1024]{1,0:T(8,128)} %mask.3, s32[256,1024]{1,0:T(8,128)} %kind.3, ...), custom_call_target="tpu_custom_call" | custom-call | flops 2000000000 | tf_op jit(solution)/shard_map/prepare/pallas_call | solution.py:204
  6.4 0.1 collective-permute-start.1
  6.5 4.0 %middle_other.1 = (f32[1,3,256,1024]{3,2,1,0:T(8,128)S(1)}, f32[520,128]{1,0:T(8,128)S(1)}) custom-call(s32[4]{0:T(128)S(1)} %copy-done.3, f32[1,4]{1,0:T(1,128)S(1)} %copy-done.2, f32[256,1024]{1,0:T(8,128)S(1)} %get-tuple-element.36.root, f32[256,1024]{1,0:T(8,128)S(1)} %get-tuple-element.37.a, f32[256,1024]{1,0:T(8,128)S(1)} %get-tuple-element.38.b, ...), custom_call_target="tpu_custom_call" | custom-call | flops 4000000000 | tf_op jit(solution)/shard_map/middle_other/pallas_call | solution.py:500
  10.6 1.2 %collective-permute-start.3 = (f32[520,128]{1,0:T(8,128)S(1)}, f32[520,128]{1,0:T(8,128)S(1)}, u32[]{:S(2)}, u32[]{:S(2)}) collective-permute-start(f32[520,128]{1,0:T(8,128)S(1)} %get-tuple-element.49), channel_id=1, source_target_pairs={{0,8},{8,0},{16,24},{24,16},{1,9},{9,1},{17,25},{25,17},{2,10},{10... | collective-permute-start | bytes 798728 | tf_op jit(solution)/shard_map/ppermute | solution.py:778
  11.8 4.5 %collective-permute-start.2 = (f32[272,128]{1,0:T(8,128)S(1)}, f32[272,128]{1,0:T(8,128)S(1)}, u32[]{:S(2)}, u32[]{:S(2)}) collective-permute-start(f32[272,128]{1,0:T(8,128)S(1)} %get-tuple-element.45), channel_id=1, source_target_pairs={{0,0},{2,4},{4,2},{6,6},{1,1},{3,5},{5,3},{7,7},{8,8},{10,12},{12,... | collective-permute-start | bytes 417800 | tf_op jit(solution)/shard_map/ppermute | solution.py:777
  16.3 4.0 %middle_own.1 = (f32[1,3,256,1024]{3,2,1,0:T(8,128)S(1)}, f32[520,128]{1,0:T(8,128)S(1)}) custom-call(s32[4]{0:T(128)S(1)} %copy-done.3, f32[1,4]{1,0:T(1,128)S(1)} %copy-done.2, f32[256,1024]{1,0:T(8,128)S(1)} %get-tuple-element.36.root, f32[256,1024]{1,0:T(8,128)S(1)} %get-tuple-element.37.a, ...), custom_call_target="tpu_custom_call", output_to_operand_aliasing={{0}: (8, {})} | custom-call | flops 4000000000 | tf_op jit(solution)/shard_map/middle_own/pallas_call | solution.py:500
  20.4 1.3 %collective-permute-start.4 = (f32[520,128]{1,0:T(8,128)S(1)}, f32[520,128]{1,0:T(8,128)S(1)}, u32[]{:S(2)}, u32[]{:S(2)}) collective-permute-start(f32[520,128]{1,0:T(8,128)S(1)} %add.12), channel_id=1, source_target_pairs={{0,16},{8,24},{16,0},{24,8},{1,17},{9,25},{17,1},{25,9},{2,18},{10... | collective-permute-start | bytes 798728 | tf_op jit(solution)/shard_map/ppermute | solution.py:764
  21.6 4.2 %edge_other.1 = (f32[1,3,256,1024]{3,2,1,0:T(8,128)S(1)}, f32[528,128]{1,0:T(8,128)S(1)}) custom-call(s32[4]{0:T(128)S(1)} %copy-done.3, f32[1,4]{1,0:T(1,128)S(1)} %copy-done.2, f32[256,1024]{1,0:T(8,128)S(1)} %get-tuple-element.36.root, f32[256,1024]{1,0:T(8,128)S(1)} %get-tuple-element.37.a, ...), custom_call_target="tpu_custom_call", output_to_operand_aliasing={{0}: (10, {})} | custom-call | flops 3000000000 | tf_op jit(solution)/shard_map/edge_other/pallas_call | solution.py:575
  25.8 0.7 %collective-permute-start.5 = (f32[528,128]{1,0:T(8,128)S(1)}, f32[528,128]{1,0:T(8,128)S(1)}, u32[]{:S(2)}, u32[]{:S(2)}) collective-permute-start(f32[528,128]{1,0:T(8,128)S(1)} %get-tuple-element.56), channel_id=1, source_target_pairs={{0,8},{8,0},{16,24},{24,16},{1,9},{9,1},{17,25},{25,17},{2,10},{10... | collective-permute-start | bytes 811016 | tf_op jit(solution)/shard_map/ppermute | solution.py:783
  26.5 4.2 %edge_own.1 = (f32[1,3,256,1024]{3,2,1,0:T(8,128)S(1)}, f32[528,128]{1,0:T(8,128)S(1)}) custom-call(s32[4]{0:T(128)S(1)} %copy-done.3, f32[1,4]{1,0:T(1,128)S(1)} %copy-done.2, f32[256,1024]{1,0:T(8,128)S(1)} %get-tuple-element.36.root, f32[256,1024]{1,0:T(8,128)S(1)} %get-tuple-element.37.a, ...), custom_call_target="tpu_custom_call", output_to_operand_aliasing={{0}: (10, {})} | custom-call | flops 3000000000 | tf_op jit(solution)/shard_map/edge_own/pallas_call | solution.py:575
  30.7 0.1 collective-permute-start.6
  30.8 0.3 collective-permute-start.7
  31.1 1.2 %collective-permute-done.6.got_m = f32[520,128]{1,0:T(8,128)S(1)} collective-permute-done((f32[520,128]{1,0:T(8,128)S(1)}, f32[520,128]{1,0:T(8,128)S(1)}, u32[]{:S(2)}, u32[]{:S(2)}) %collective-permute-start.6) | collective-permute-done | bytes 266272 | tf_op jit(solution)/shard_map/ppermute | solution.py:788
  32.3 2.2 %bed_middle.1 = (f32[256,1024]{1,0:T(8,128)}, f32[256,1024]{1,0:T(8,128)}, f32[1,3,256,1024]{3,2,1,0:T(8,128)}) custom-call(f32[256,1024]{1,0:T(8,128)S(1)} %get-tuple-element.35.bed, f32[72,128]{1,0:T(8,128)S(1)} %collective-permute-done.side, f32[272,128]{1,0:T(8,128)S(1)} %collective-permute-done.1.far_a, f32[272,128]{1,0:T(8,128)S(1)} %collective-permute-done.2.far_b, ...), custom_call_target="tpu_custom_call" | custom-call | flops 4000000000 | tf_op jit(solution)/shard_map/bed_middle/pallas_call | solution.py:720
  34.6 3.9 %collective-permute-done.7 = f32[528,128]{1,0:T(8,128)S(1)} collective-permute-done((f32[528,128]{1,0:T(8,128)S(1)}, f32[528,128]{1,0:T(8,128)S(1)}, u32[]{:S(2)}, u32[]{:S(2)}) %collective-permute-start.7) | collective-permute-done | bytes 270368 | tf_op jit(solution)/shard_map/ppermute | solution.py:764
  38.5 1.3 %collective-permute-start.8 = (f32[528,128]{1,0:T(8,128)S(1)}, f32[528,128]{1,0:T(8,128)S(1)}, u32[]{:S(2)}, u32[]{:S(2)}) collective-permute-start(f32[528,128]{1,0:T(8,128)S(1)} %add.15.own_e), channel_id=1, source_target_pairs={{0,8},{8,0},{16,24},{24,16},{1,9},{9,1},{17,25},{25,17},{2,10},{10... | collective-permute-start | bytes 811016 | tf_op jit(solution)/shard_map/ppermute | solution.py:791
  39.9 1.2 %collective-permute-done.8.got_e = f32[528,128]{1,0:T(8,128)S(1)} collective-permute-done((f32[528,128]{1,0:T(8,128)S(1)}, f32[528,128]{1,0:T(8,128)S(1)}, u32[]{:S(2)}, u32[]{:S(2)}) %collective-permute-start.8) | collective-permute-done | bytes 270368 | tf_op jit(solution)/shard_map/ppermute | solution.py:791
  41.1 1.9 %bed_edge.1 = (f32[256,1024]{1,0:T(8,128)}, f32[256,1024]{1,0:T(8,128)}) custom-call(f32[256,1024]{1,0:T(8,128)S(1)} %get-tuple-element.35.bed, f32[72,128]{1,0:T(8,128)S(1)} %collective-permute-done.side, f32[272,128]{1,0:T(8,128)S(1)} %collective-permute-done.1.far_a, ...), custom_call_target="tpu_custom_call", output_to_operand_aliasing={{0}: (8, {}), {1}: (9, {})} | custom-call | flops 2000000000 | tf_op jit(solution)/shard_map/bed_edge/pallas_call | solution.py:733
  (15 shorter events, 0.2 us)
Async XLA Ops:
  2.4 4.1 %copy-start = (f32[1,3,256,1024]{3,2,1,0:T(8,128)S(1)}, f32[1,3,256,1024]{3,2,1,0:T(8,128)}, u32[]{:S(2)}) copy-start(f32[1,3,256,1024]{3,2,1,0:T(8,128)} %hydro.11) | copy-start | bytes 9437188
  2.4 4.1 %copy-start.1 = (f32[1,2,256,1024]{3,2,1,0:T(8,128)S(1)}, f32[1,2,256,1024]{3,2,1,0:T(8,128)}, u32[]{:S(2)}) copy-start(f32[1,2,256,1024]{3,2,1,0:T(8,128)} %stress.11) | copy-start | bytes 6291460
  2.4 4.1 %copy-start.2 = (f32[1,4]{1,0:T(1,128)S(1)}, f32[1,4]{1,0:T(1,128)}, u32[]{:S(2)}) copy-start(f32[1,4]{1,0:T(1,128)} %params.7) | copy-start | bytes 52
  2.4 4.1 %copy-start.3 = (s32[4]{0:T(128)S(1)}, s32[4]{0:T(128)}, u32[]{:S(2)}) copy-start(s32[4]{0:T(128)} %weights.7) | copy-start | bytes 52
  2.5 3.9 %collective-permute-start = (f32[72,128]{1,0:T(8,128)S(1)}, f32[72,128]{1,0:T(8,128)S(1)}, u32[]{:S(2)}, u32[]{:S(2)}) collective-permute-start(f32[72,128]{1,0:T(8,128)S(1)} %pack_side.1), channel_id=1, source_target_pairs={{0,1},{1,0},{2,3},{3,2},{4,5},{5,4},{6,7},{7,6},{8,9},{9,8},{10,11... | collective-permute-start | bytes 110600 | tf_op jit(solution)/shard_map/ppermute | solution.py:770
  6.4 5.4 %collective-permute-start.1 = (f32[272,128]{1,0:T(8,128)S(1)}, f32[272,128]{1,0:T(8,128)S(1)}, u32[]{:S(2)}, u32[]{:S(2)}) collective-permute-start(f32[272,128]{1,0:T(8,128)S(1)} %get-tuple-element.42), channel_id=1, source_target_pairs={{0,2},{2,0},{4,6},{6,4},{1,3},{3,1},{5,7},{7,5},{8,10},{10,8},{12,... | collective-permute-start | bytes 417800 | tf_op jit(solution)/shard_map/ppermute | solution.py:774
  10.6 9.8 %collective-permute-start.3 = (f32[520,128]{1,0:T(8,128)S(1)}, f32[520,128]{1,0:T(8,128)S(1)}, u32[]{:S(2)}, u32[]{:S(2)}) collective-permute-start(f32[520,128]{1,0:T(8,128)S(1)} %get-tuple-element.49), channel_id=1, source_target_pairs={{0,8},{8,0},{16,24},{24,16},{1,9},{9,1},{17,25},{25,17},{2,10},{10... | collective-permute-start | bytes 798728 | tf_op jit(solution)/shard_map/ppermute | solution.py:778
  11.8 9.9 %collective-permute-start.2 = (f32[272,128]{1,0:T(8,128)S(1)}, f32[272,128]{1,0:T(8,128)S(1)}, u32[]{:S(2)}, u32[]{:S(2)}) collective-permute-start(f32[272,128]{1,0:T(8,128)S(1)} %get-tuple-element.45), channel_id=1, source_target_pairs={{0,0},{2,4},{4,2},{6,6},{1,1},{3,5},{5,3},{7,7},{8,8},{10,12},{12,... | collective-permute-start | bytes 417800 | tf_op jit(solution)/shard_map/ppermute | solution.py:777
  20.4 10.3 %collective-permute-start.4 = (f32[520,128]{1,0:T(8,128)S(1)}, f32[520,128]{1,0:T(8,128)S(1)}, u32[]{:S(2)}, u32[]{:S(2)}) collective-permute-start(f32[520,128]{1,0:T(8,128)S(1)} %add.12), channel_id=1, source_target_pairs={{0,16},{8,24},{16,0},{24,8},{1,17},{9,25},{17,1},{25,9},{2,18},{10... | collective-permute-start | bytes 798728 | tf_op jit(solution)/shard_map/ppermute | solution.py:764
  25.8 4.9 %collective-permute-start.5 = (f32[528,128]{1,0:T(8,128)S(1)}, f32[528,128]{1,0:T(8,128)S(1)}, u32[]{:S(2)}, u32[]{:S(2)}) collective-permute-start(f32[528,128]{1,0:T(8,128)S(1)} %get-tuple-element.56), channel_id=1, source_target_pairs={{0,8},{8,0},{16,24},{24,16},{1,9},{9,1},{17,25},{25,17},{2,10},{10... | collective-permute-start | bytes 811016 | tf_op jit(solution)/shard_map/ppermute | solution.py:783
  30.7 1.6 %collective-permute-start.6 = (f32[520,128]{1,0:T(8,128)S(1)}, f32[520,128]{1,0:T(8,128)S(1)}, u32[]{:S(2)}, u32[]{:S(2)}) collective-permute-start(f32[520,128]{1,0:T(8,128)S(1)} %add.13.own_m), channel_id=1, source_target_pairs={{0,8},{8,0},{16,24},{24,16},{1,9},{9,1},{17,25},{25,17},{2,10},{10... | collective-permute-start | bytes 798728 | tf_op jit(solution)/shard_map/ppermute | solution.py:788
  30.8 7.7 %collective-permute-start.7 = (f32[528,128]{1,0:T(8,128)S(1)}, f32[528,128]{1,0:T(8,128)S(1)}, u32[]{:S(2)}, u32[]{:S(2)}) collective-permute-start(f32[528,128]{1,0:T(8,128)S(1)} %add.14), channel_id=1, source_target_pairs={{0,16},{8,24},{16,0},{24,8},{1,17},{9,25},{17,1},{25,9},{2,18},{10... | collective-permute-start | bytes 811016 | tf_op jit(solution)/shard_map/ppermute | solution.py:764
  38.5 2.5 %collective-permute-start.8 = (f32[528,128]{1,0:T(8,128)S(1)}, f32[528,128]{1,0:T(8,128)S(1)}, u32[]{:S(2)}, u32[]{:S(2)}) collective-permute-start(f32[528,128]{1,0:T(8,128)S(1)} %add.15.own_e), channel_id=1, source_target_pairs={{0,8},{8,0},{16,24},{24,16},{1,9},{9,1},{17,25},{25,17},{2,10},{10... | collective-permute-start | bytes 811016 | tf_op jit(solution)/shard_map/ppermute | solution.py:791

commit v13 on v10

--- a/solution.py
+++ b/solution.py
@@ -242,15 +242,21 @@
     )(*held(side, pay_a, pay_b))
 
 
-def side_lanes(at_left):
+def side_lanes():
+    at_left = lax.axis_index("tx") == 0
     drop = jnp.where(at_left, 0, HALO)
     lane = lanes_of((SUB, LANE))
     valid = jnp.where(at_left, lane, LANE - 1 - lane) < HALO
-
-    def unfold(strip, place):
-        return pltpu.roll(strip, 2 * LANE - drop - place * HALO, 1)
-
-    return unfold, valid
+    return lambda strip: pltpu.roll(strip, LANE - drop, 1), valid
+
+
+def unfold(strip, place):
+    return pltpu.roll(strip, (LANE - place * HALO) % LANE, 1) if place else strip
+
+
+def by_flag(flag, run):
+    pl.when(flag)(lambda: run(True))
+    pl.when(jnp.logical_not(flag))(lambda: run(False))
 
 
 class Sweep:
@@ -386,13 +392,16 @@
                 turns = [turn for turn in turns if next(turn, True) is None]
 
 
-def reader(root, a, b, stress, hydro, side, unfold, valid):
+def reader(root, a, b, stress, hydro, side, side_x):
     rows = root.shape[0]
     span = rows // FOLD // SUB
     fields = [root, a, b] + moving(stress, hydro)
+    turn, valid = side_lanes()
+    for g in range(span):
+        side_x[tile_at(g), :] = turn(side[tile_at(g), :])
 
     def read(f, block):
-        part = unfold(side[tile_at(block % span), :], (block // span) * FIELDS + f)
+        part = unfold(side_x[tile_at(block % span), :], (block // span) * FIELDS + f)
         if f == 0:
             part = jnp.where(valid, part, 0.0)
         return jnp.concatenate([fields[f][tile_at(block), :], part], axis=1)
@@ -420,17 +429,18 @@
 
 
 def middle_kernel(own, weights, params, root, a, b, stress, hydro, side, *refs):
-    hydro_out, pay, *refs = refs[1:] if own else refs
+    hydro_out, pay, side_x, *refs = refs[1:] if own else refs
     rows, cols = root.shape
     quarter = rows // SUB // 4
-    read = reader(root, a, b, stress, hydro, side, *side_lanes(lax.axis_index("tx") == 0))
-    mine = lax.axis_index("cond") % 2
-    lower_half = mine == (1 if own else 0)
-    first = jnp.where(lower_half, 2 * quarter, quarter) - 1
-    emit = quarter_writer(first, quarter, cols, hydro_out, pay)
-    Sweep(
-        quarter + 2, cols + LANE, lambda f, i: read(f, first + i), emit, weights, params, refs, True
-    ).run()
+    read = reader(root, a, b, stress, hydro, side, side_x)
+
+    def run(lower_half):
+        first = (2 * quarter if lower_half else quarter) - 1
+        emit = quarter_writer(first, quarter, cols, hydro_out, pay)
+        get = lambda f, i: read(f, first + i)
+        Sweep(quarter + 2, cols + LANE, get, emit, weights, params, refs, True).run()
+
+    by_flag(lax.axis_index("cond") % 2 == (1 if own else 0), run)
 
 
 def middle(own, weights, params, fields, side, hydro=None):
@@ -445,7 +455,7 @@
         ],
         in_specs=[SMEM, SMEM] + [VMEM] * (6 + own),
         out_specs=[VMEM, VMEM],
-        scratch_shapes=Sweep.scratch(rows // SUB // 4 + 2, cols + LANE),
+        scratch_shapes=[pltpu.VMEM(side.shape, jnp.float32)] + Sweep.scratch(rows // SUB // 4 + 2, cols + LANE),
         input_output_aliases={8: 0} if own else {},
         compiler_params=pltpu.CompilerParams(vmem_limit_bytes=10 * MIB),
         cost_estimate=cost(4),
@@ -454,58 +464,55 @@
 
 def edge_kernel(
     own, weights, params, root, a, b, stress, hydro, side, far_a, far_b, hydro_in,
-    hydro_out, pay, ends, *refs,
+    hydro_out, pay, ends, side_x, *refs,
 ):
     rows, cols = root.shape
     blocks = rows // SUB
     quarter = blocks // 4
     lanes = cols // LANE
-    unfold, valid = side_lanes(lax.axis_index("tx") == 0)
-    read = reader(root, a, b, stress, hydro, side, unfold, valid)
-    mine = lax.axis_index("cond") % 2
-    top = mine == (0 if own else 1)
-    from_a = top == (lax.axis_index("ty") % 2 == 1)
-    first = jnp.where(top, -1, blocks - quarter - 1)
-
+    read = reader(root, a, b, stress, hydro, side, side_x)
+    turn, valid = side_lanes()
     ty = lax.axis_index("ty")
-    outside_map = ty == jnp.where(top, 0, lax.axis_size("ty") - 1)
-    inner = jnp.where(top, quarter, blocks - quarter - 1)
     corners = pl.ds(lanes * GROUP, SUB)
-    for f in range(FIELDS):
-        body = read(f, inner)
-        parts = []
-        for k in range(lanes):
-            at = pl.ds(k * GROUP + f // 2 * SUB, SUB)
-            part = jnp.where(from_a, far_a[at, :], far_b[at, :])
-            moved = pltpu.roll(part, HALO, 0)
-            parts.append(jnp.where(top, moved, part) if f % 2 == 0 else jnp.where(top, part, moved))
-        corner = jnp.where(from_a, far_a[corners, :], far_b[corners, :])
-        corner = jnp.where(top, unfold(corner, (FOLD - 1) * FIELDS + f), unfold(corner, f))
-        if f == 0:
-            corner = jnp.where(valid, corner, 0.0)
-        outer = jnp.concatenate(parts + [corner], axis=1)
-        if f == 0:
-            outer = jnp.where(outside_map, 0.0, outer)
-        ends[0, f] = jnp.where(top, outer, body)
-        ends[1, f] = jnp.where(top, body, outer)
-
-    def get(f, i):
-        if i == 0 or i == quarter + 1:
-            return ends[0 if i == 0 else 1, f]
-        return read(f, first + i)
-
-    emit = quarter_writer(first, quarter, cols, hydro_out, pay)
-    outside = []
-
-    def finish(i, e, u, v, change):
-        if i == 0:
-            outside.append(pltpu.roll(change[:, :cols], 1, 0))
-        elif i == quarter + 1:
-            pay[tile_at(lanes * quarter + 1), :] = fold_row(jnp.where(top, outside[0], change[:, :cols]))
-        else:
-            emit(i, e, u, v, change)
-
-    Sweep(quarter + 2, cols + LANE, get, finish, weights, params, refs, False).run()
+
+    def run(top):
+        from_a = ty % 2 == (1 if top else 0)
+        first = -1 if top else blocks - quarter - 1
+        outside_map = ty == (0 if top else lax.axis_size("ty") - 1)
+        inner = quarter if top else blocks - quarter - 1
+        corner = turn(jnp.where(from_a, far_a[corners, :], far_b[corners, :]))
+        for f in range(FIELDS):
+            body = read(f, inner)
+            parts = []
+            for k in range(lanes):
+                at = pl.ds(k * GROUP + f // 2 * SUB, SUB)
+                part = jnp.where(from_a, far_a[at, :], far_b[at, :])
+                parts.append(pltpu.roll(part, HALO, 0) if top == (f % 2 == 0) else part)
+            end = unfold(corner, ((FOLD - 1) * FIELDS if top else 0) + f)
+            if f == 0:
+                end = jnp.where(valid, end, 0.0)
+            outer = jnp.concatenate(parts + [end], axis=1)
+            if f == 0:
+                outer = jnp.where(outside_map, 0.0, outer)
+            ends[0, f], ends[1, f] = (outer, body) if top else (body, outer)
+
+        def get(f, i):
+            if i == 0 or i == quarter + 1:
+                return ends[0 if i == 0 else 1, f]
+            return read(f, first + i)
+
+        emit = quarter_writer(first, quarter, cols, hydro_out, pay)
+
+        def finish(i, e, u, v, change):
+            if 1 <= i <= quarter:
+                emit(i, e, u, v, change)
+            elif i == (0 if top else quarter + 1):
+                rim = change[:, :cols]
+                pay[tile_at(lanes * quarter + 1), :] = fold_row(pltpu.roll(rim, 1, 0) if top else rim)
+
+        Sweep(quarter + 2, cols + LANE, get, finish, weights, params, refs, False).run()
+
+    by_flag(lax.axis_index("cond") % 2 == (0 if own else 1), run)
 
 
 def edge(own, weights, params, fields, side, far_a, far_b, hydro):
@@ -520,7 +527,7 @@
         ],
         in_specs=[SMEM, SMEM] + [VMEM] * 9,
         out_specs=[VMEM, VMEM],
-        scratch_shapes=[pltpu.VMEM((2, FIELDS, SUB, wide), jnp.float32)]
+        scratch_shapes=[pltpu.VMEM((2, FIELDS, SUB, wide), jnp.float32), pltpu.VMEM(side.shape, jnp.float32)]
         + Sweep.scratch(rows // SUB // 4 + 2, wide),
         input_output_aliases={10: 0},
         compiler_params=pltpu.CompilerParams(vmem_limit_bytes=12 * MIB),

time: 39.4 us -> 39.2 us (level)
  no operation moved by 1% of the time
where the time goes in v13:
time: 39.2 us; the launch traced here: 39.1 us
  Pallas kernels  20.1 us (51%)
  starting transfers between devices  12 us (31%)
  waiting for transfers between devices  5.83 us (15%)
  between operations  0.98 us (2%)
    pallas_call x2, Pallas kernels, edge(): pl.pallas_call(functools.partial(edge_kernel, own), name='edge_own' if ow...  5.93 us
    pallas_call x2, Pallas kernels, middle(): pl.pallas_call(functools.partial(middle_kernel, own), name='middle_own' i...  5.61 us
    ppermute x2, waiting for transfers between devices, over_chips(): got = lax.ppermute(part, 'cond', [(i, i ^ reach) for i in range(nc)])  4.08 us
    ppermute x1, starting transfers between devices, shards(): far_b = lax.ppermute(far_b, 'ty', pairs(1))  3.91 us
    ppermute x2, starting transfers between devices, shards(): got = lax.ppermute(pay, 'cond', swap)  2.7 us
    pallas_call x1, Pallas kernels, prepare(): pl.pallas_call(prepare_kernel, name='prepare', out_shape=[tile] * 4 + [pl...  2.58 us
    ppermute x2, starting transfers between devices, over_chips(): got = lax.ppermute(part, 'cond', [(i, i ^ reach) for i in range(nc)])  2.5 us
    pallas_call x1, Pallas kernels, bed_middle(): pl.pallas_call(bed_middle_kernel, name='bed_middle', out_shape=[pltpu.HBM...  2.24 us
  transfers between devices with their start and end apart: 9, of which 4 were waited for; matrix products, arithmetic and copies ran while one was open for 0% of the time, Pallas kernels for 42%

profile of v13, /device:TPU:9, one launch (start us, length us, event | category | flops | bytes accessed | tf_op | source)
XLA Modules:
  0.0 39.1 jit_solution(13393062189285191330)
XLA Ops:
  0.6 1.8 %pack_side.1 = f32[72,128]{1,0:T(8,128)S(1)} custom-call(f32[1,4]{1,0:T(1,128)} %params.7, f32[256,1024]{1,0:T(8,128)} %bed.3, s32[256,1024]{1,0:T(8,128)} %mask.3, s32[256,1024]{1,0:T(8,128)} %kind.3, f32[1,2,256,1024]{3,2,1,0:T(8,128)} %stress.11, f32[1,3,256,1024]{3,2,1,0:T(8,128)} %hydro.11), custom_call_target="tpu_custom_call" | custom-call | flops 2000000000 | tf_op jit(solution)/shard_map/pack_side/pallas_call | solution.py:114
  2.4 0.0 copy-start
  2.4 0.0 copy-start.1
  2.4 0.0 copy-start.2
  2.5 1.3 %collective-permute-start = (f32[72,128]{1,0:T(8,128)S(1)}, f32[72,128]{1,0:T(8,128)S(1)}, u32[]{:S(2)}, u32[]{:S(2)}) collective-permute-start(f32[72,128]{1,0:T(8,128)S(1)} %pack_side.1), channel_id=1, source_target_pairs={{0,1},{1,0},{2,3},{3,2},{4,5},{5,4},{6,7},{7,6},{8,9},{9,8},{10,11... | collective-permute-start | bytes 110600 | tf_op jit(solution)/shard_map/ppermute | solution.py:716
  3.8 2.6 %prepare.1 = (f32[256,1024]{1,0:T(8,128)S(1)}, f32[256,1024]{1,0:T(8,128)S(1)}, f32[256,1024]{1,0:T(8,128)S(1)}, f32[256,1024]{1,0:T(8,128)S(1)}, f32[272,128]{1,0:T(8,128)S(1)}, /*index=5*/f32[272,128]{1,0:T(8,128)S(1)}) custom-call(f32[1,4]{1,0:T(1,128)} %params.7, f32[256,1024]{1,0:T(8,128)} %bed.3, s32[256,1024]{1,0:T(8,128)} %mask.3, s32[256,1024]{1,0:T(8,128)} %kind.3, ...), custom_call_target="tpu_custom_call" | custom-call | flops 2000000000 | tf_op jit(solution)/shard_map/prepare/pallas_call | solution.py:203
  6.4 0.1 collective-permute-start.1
  6.5 2.8 %middle_other.1 = (f32[1,3,256,1024]{3,2,1,0:T(8,128)S(1)}, f32[520,128]{1,0:T(8,128)S(1)}) custom-call(s32[4]{0:T(128)S(1)} %copy-done.3, f32[1,4]{1,0:T(1,128)S(1)} %copy-done.2, f32[256,1024]{1,0:T(8,128)S(1)} %get-tuple-element.36.root, f32[256,1024]{1,0:T(8,128)S(1)} %get-tuple-element.37.a, f32[256,1024]{1,0:T(8,128)S(1)} %get-tuple-element.38.b, ...), custom_call_target="tpu_custom_call" | custom-call | flops 4000000000 | tf_op jit(solution)/shard_map/middle_other/pallas_call | solution.py:449
  9.3 1.2 %collective-permute-start.3 = (f32[520,128]{1,0:T(8,128)S(1)}, f32[520,128]{1,0:T(8,128)S(1)}, u32[]{:S(2)}, u32[]{:S(2)}) collective-permute-start(f32[520,128]{1,0:T(8,128)S(1)} %get-tuple-element.49), channel_id=1, source_target_pairs={{0,8},{8,0},{16,24},{24,16},{1,9},{9,1},{17,25},{25,17},{2,10},{10... | collective-permute-start | bytes 798728 | tf_op jit(solution)/shard_map/ppermute | solution.py:724
  10.5 0.4 %collective-permute-done.1.far_a = f32[272,128]{1,0:T(8,128)S(1)} collective-permute-done((f32[272,128]{1,0:T(8,128)S(1)}, f32[272,128]{1,0:T(8,128)S(1)}, u32[]{:S(2)}, u32[]{:S(2)}) %collective-permute-start.1) | collective-permute-done | bytes 139296 | tf_op jit(solution)/shard_map/ppermute | solution.py:720
  10.9 3.9 %collective-permute-start.2 = (f32[272,128]{1,0:T(8,128)S(1)}, f32[272,128]{1,0:T(8,128)S(1)}, u32[]{:S(2)}, u32[]{:S(2)}) collective-permute-start(f32[272,128]{1,0:T(8,128)S(1)} %get-tuple-element.45), channel_id=1, source_target_pairs={{0,0},{2,4},{4,2},{6,6},{1,1},{3,5},{5,3},{7,7},{8,8},{10,12},{12,... | collective-permute-start | bytes 417800 | tf_op jit(solution)/shard_map/ppermute | solution.py:723
  14.9 2.8 %middle_own.1 = (f32[1,3,256,1024]{3,2,1,0:T(8,128)S(1)}, f32[520,128]{1,0:T(8,128)S(1)}) custom-call(s32[4]{0:T(128)S(1)} %copy-done.3, f32[1,4]{1,0:T(1,128)S(1)} %copy-done.2, f32[256,1024]{1,0:T(8,128)S(1)} %get-tuple-element.36.root, f32[256,1024]{1,0:T(8,128)S(1)} %get-tuple-element.37.a, ...), custom_call_target="tpu_custom_call", output_to_operand_aliasing={{0}: (8, {})} | custom-call | flops 4000000000 | tf_op jit(solution)/shard_map/middle_own/pallas_call | solution.py:449
  17.7 1.3 %collective-permute-start.4 = (f32[520,128]{1,0:T(8,128)S(1)}, f32[520,128]{1,0:T(8,128)S(1)}, u32[]{:S(2)}, u32[]{:S(2)}) collective-permute-start(f32[520,128]{1,0:T(8,128)S(1)} %add.12), channel_id=1, source_target_pairs={{0,16},{8,24},{16,0},{24,8},{1,17},{9,25},{17,1},{25,9},{2,18},{10... | collective-permute-start | bytes 798728 | tf_op jit(solution)/shard_map/ppermute | solution.py:710
  19.0 3.0 %edge_other.1 = (f32[1,3,256,1024]{3,2,1,0:T(8,128)S(1)}, f32[528,128]{1,0:T(8,128)S(1)}) custom-call(s32[4]{0:T(128)S(1)} %copy-done.3, f32[1,4]{1,0:T(1,128)S(1)} %copy-done.2, f32[256,1024]{1,0:T(8,128)S(1)} %get-tuple-element.36.root, f32[256,1024]{1,0:T(8,128)S(1)} %get-tuple-element.37.a, ...), custom_call_target="tpu_custom_call", output_to_operand_aliasing={{0}: (10, {})} | custom-call | flops 3000000000 | tf_op jit(solution)/shard_map/edge_other/pallas_call | solution.py:521
  22.1 1.5 %collective-permute-start.5 = (f32[528,128]{1,0:T(8,128)S(1)}, f32[528,128]{1,0:T(8,128)S(1)}, u32[]{:S(2)}, u32[]{:S(2)}) collective-permute-start(f32[528,128]{1,0:T(8,128)S(1)} %get-tuple-element.56), channel_id=1, source_target_pairs={{0,8},{8,0},{16,24},{24,16},{1,9},{9,1},{17,25},{25,17},{2,10},{10... | collective-permute-start | bytes 811016 | tf_op jit(solution)/shard_map/ppermute | solution.py:729
  23.5 2.9 %edge_own.1 = (f32[1,3,256,1024]{3,2,1,0:T(8,128)S(1)}, f32[528,128]{1,0:T(8,128)S(1)}) custom-call(s32[4]{0:T(128)S(1)} %copy-done.3, f32[1,4]{1,0:T(1,128)S(1)} %copy-done.2, f32[256,1024]{1,0:T(8,128)S(1)} %get-tuple-element.36.root, f32[256,1024]{1,0:T(8,128)S(1)} %get-tuple-element.37.a, ...), custom_call_target="tpu_custom_call", output_to_operand_aliasing={{0}: (10, {})} | custom-call | flops 3000000000 | tf_op jit(solution)/shard_map/edge_own/pallas_call | solution.py:521
  26.5 0.2 collective-permute-start.6
  26.8 1.2 %collective-permute-start.7 = (f32[528,128]{1,0:T(8,128)S(1)}, f32[528,128]{1,0:T(8,128)S(1)}, u32[]{:S(2)}, u32[]{:S(2)}) collective-permute-start(f32[528,128]{1,0:T(8,128)S(1)} %add.14), channel_id=1, source_target_pairs={{0,16},{8,24},{16,0},{24,8},{1,17},{9,25},{17,1},{25,9},{2,18},{10... | collective-permute-start | bytes 811016 | tf_op jit(solution)/shard_map/ppermute | solution.py:710
  28.0 0.2 collective-permute-done.6.got_m
  28.2 2.2 %bed_middle.1 = (f32[256,1024]{1,0:T(8,128)}, f32[256,1024]{1,0:T(8,128)}, f32[1,3,256,1024]{3,2,1,0:T(8,128)}) custom-call(f32[256,1024]{1,0:T(8,128)S(1)} %get-tuple-element.35.bed, f32[72,128]{1,0:T(8,128)S(1)} %collective-permute-done.side, f32[272,128]{1,0:T(8,128)S(1)} %collective-permute-done.1.far_a, f32[272,128]{1,0:T(8,128)S(1)} %collective-permute-done.2.far_b, ...), custom_call_target="tpu_custom_call" | custom-call | flops 4000000000 | tf_op jit(solution)/shard_map/bed_middle/pallas_call | solution.py:666
  30.4 4.1 %collective-permute-done.7 = f32[528,128]{1,0:T(8,128)S(1)} collective-permute-done((f32[528,128]{1,0:T(8,128)S(1)}, f32[528,128]{1,0:T(8,128)S(1)}, u32[]{:S(2)}, u32[]{:S(2)}) %collective-permute-start.7) | collective-permute-done | bytes 270368 | tf_op jit(solution)/shard_map/ppermute | solution.py:710
  34.5 1.2 %collective-permute-start.8 = (f32[528,128]{1,0:T(8,128)S(1)}, f32[528,128]{1,0:T(8,128)S(1)}, u32[]{:S(2)}, u32[]{:S(2)}) collective-permute-start(f32[528,128]{1,0:T(8,128)S(1)} %add.15.own_e), channel_id=1, source_target_pairs={{0,8},{8,0},{16,24},{24,16},{1,9},{9,1},{17,25},{25,17},{2,10},{10... | collective-permute-start | bytes 811016 | tf_op jit(solution)/shard_map/ppermute | solution.py:737
  35.8 1.2 %collective-permute-done.8.got_e = f32[528,128]{1,0:T(8,128)S(1)} collective-permute-done((f32[528,128]{1,0:T(8,128)S(1)}, f32[528,128]{1,0:T(8,128)S(1)}, u32[]{:S(2)}, u32[]{:S(2)}) %collective-permute-start.8) | collective-permute-done | bytes 270368 | tf_op jit(solution)/shard_map/ppermute | solution.py:737
  36.9 1.9 %bed_edge.1 = (f32[256,1024]{1,0:T(8,128)}, f32[256,1024]{1,0:T(8,128)}) custom-call(f32[256,1024]{1,0:T(8,128)S(1)} %get-tuple-element.35.bed, f32[72,128]{1,0:T(8,128)S(1)} %collective-permute-done.side, f32[272,128]{1,0:T(8,128)S(1)} %collective-permute-done.1.far_a, ...), custom_call_target="tpu_custom_call", output_to_operand_aliasing={{0}: (8, {}), {1}: (9, {})} | custom-call | flops 2000000000 | tf_op jit(solution)/shard_map/bed_edge/pallas_call | solution.py:679
  (15 shorter events, 0.2 us)
Async XLA Ops:
  2.4 4.1 %copy-start = (f32[1,3,256,1024]{3,2,1,0:T(8,128)S(1)}, f32[1,3,256,1024]{3,2,1,0:T(8,128)}, u32[]{:S(2)}) copy-start(f32[1,3,256,1024]{3,2,1,0:T(8,128)} %hydro.11) | copy-start | bytes 9437188
  2.4 4.1 %copy-start.1 = (f32[1,2,256,1024]{3,2,1,0:T(8,128)S(1)}, f32[1,2,256,1024]{3,2,1,0:T(8,128)}, u32[]{:S(2)}) copy-start(f32[1,2,256,1024]{3,2,1,0:T(8,128)} %stress.11) | copy-start | bytes 6291460
  2.4 4.1 %copy-start.2 = (f32[1,4]{1,0:T(1,128)S(1)}, f32[1,4]{1,0:T(1,128)}, u32[]{:S(2)}) copy-start(f32[1,4]{1,0:T(1,128)} %params.7) | copy-start | bytes 52
  2.4 4.1 %copy-start.3 = (s32[4]{0:T(128)S(1)}, s32[4]{0:T(128)}, u32[]{:S(2)}) copy-start(s32[4]{0:T(128)} %weights.7) | copy-start | bytes 52
  2.5 3.9 %collective-permute-start = (f32[72,128]{1,0:T(8,128)S(1)}, f32[72,128]{1,0:T(8,128)S(1)}, u32[]{:S(2)}, u32[]{:S(2)}) collective-permute-start(f32[72,128]{1,0:T(8,128)S(1)} %pack_side.1), channel_id=1, source_target_pairs={{0,1},{1,0},{2,3},{3,2},{4,5},{5,4},{6,7},{7,6},{8,9},{9,8},{10,11... | collective-permute-start | bytes 110600 | tf_op jit(solution)/shard_map/ppermute | solution.py:716
  6.4 4.6 %collective-permute-start.1 = (f32[272,128]{1,0:T(8,128)S(1)}, f32[272,128]{1,0:T(8,128)S(1)}, u32[]{:S(2)}, u32[]{:S(2)}) collective-permute-start(f32[272,128]{1,0:T(8,128)S(1)} %get-tuple-element.42), channel_id=1, source_target_pairs={{0,2},{2,0},{4,6},{6,4},{1,3},{3,1},{5,7},{7,5},{8,10},{10,8},{12,... | collective-permute-start | bytes 417800 | tf_op jit(solution)/shard_map/ppermute | solution.py:720
  9.3 8.4 %collective-permute-start.3 = (f32[520,128]{1,0:T(8,128)S(1)}, f32[520,128]{1,0:T(8,128)S(1)}, u32[]{:S(2)}, u32[]{:S(2)}) collective-permute-start(f32[520,128]{1,0:T(8,128)S(1)} %get-tuple-element.49), channel_id=1, source_target_pairs={{0,8},{8,0},{16,24},{24,16},{1,9},{9,1},{17,25},{25,17},{2,10},{10... | collective-permute-start | bytes 798728 | tf_op jit(solution)/shard_map/ppermute | solution.py:724
  10.9 8.1 %collective-permute-start.2 = (f32[272,128]{1,0:T(8,128)S(1)}, f32[272,128]{1,0:T(8,128)S(1)}, u32[]{:S(2)}, u32[]{:S(2)}) collective-permute-start(f32[272,128]{1,0:T(8,128)S(1)} %get-tuple-element.45), channel_id=1, source_target_pairs={{0,0},{2,4},{4,2},{6,6},{1,1},{3,5},{5,3},{7,7},{8,8},{10,12},{12,... | collective-permute-start | bytes 417800 | tf_op jit(solution)/shard_map/ppermute | solution.py:723
  17.7 8.7 %collective-permute-start.4 = (f32[520,128]{1,0:T(8,128)S(1)}, f32[520,128]{1,0:T(8,128)S(1)}, u32[]{:S(2)}, u32[]{:S(2)}) collective-permute-start(f32[520,128]{1,0:T(8,128)S(1)} %add.12), channel_id=1, source_target_pairs={{0,16},{8,24},{16,0},{24,8},{1,17},{9,25},{17,1},{25,9},{2,18},{10... | collective-permute-start | bytes 798728 | tf_op jit(solution)/shard_map/ppermute | solution.py:710
  22.1 4.4 %collective-permute-start.5 = (f32[528,128]{1,0:T(8,128)S(1)}, f32[528,128]{1,0:T(8,128)S(1)}, u32[]{:S(2)}, u32[]{:S(2)}) collective-permute-start(f32[528,128]{1,0:T(8,128)S(1)} %get-tuple-element.56), channel_id=1, source_target_pairs={{0,8},{8,0},{16,24},{24,16},{1,9},{9,1},{17,25},{25,17},{2,10},{10... | collective-permute-start | bytes 811016 | tf_op jit(solution)/shard_map/ppermute | solution.py:729
  26.5 1.6 %collective-permute-start.6 = (f32[520,128]{1,0:T(8,128)S(1)}, f32[520,128]{1,0:T(8,128)S(1)}, u32[]{:S(2)}, u32[]{:S(2)}) collective-permute-start(f32[520,128]{1,0:T(8,128)S(1)} %add.13.own_m), channel_id=1, source_target_pairs={{0,8},{8,0},{16,24},{24,16},{1,9},{9,1},{17,25},{25,17},{2,10},{10... | collective-permute-start | bytes 798728 | tf_op jit(solution)/shard_map/ppermute | solution.py:734
  26.8 7.7 %collective-permute-start.7 = (f32[528,128]{1,0:T(8,128)S(1)}, f32[528,128]{1,0:T(8,128)S(1)}, u32[]{:S(2)}, u32[]{:S(2)}) collective-permute-start(f32[528,128]{1,0:T(8,128)S(1)} %add.14), channel_id=1, source_target_pairs={{0,16},{8,24},{16,0},{24,8},{1,17},{9,25},{17,1},{25,9},{2,18},{10... | collective-permute-start | bytes 811016 | tf_op jit(solution)/shard_map/ppermute | solution.py:710
  34.5 2.4 %collective-permute-start.8 = (f32[528,128]{1,0:T(8,128)S(1)}, f32[528,128]{1,0:T(8,128)S(1)}, u32[]{:S(2)}, u32[]{:S(2)}) collective-permute-start(f32[528,128]{1,0:T(8,128)S(1)} %add.15.own_e), channel_id=1, source_target_pairs={{0,8},{8,0},{16,24},{24,16},{1,9},{9,1},{17,25},{25,17},{2,10},{10... | collective-permute-start | bytes 811016 | tf_op jit(solution)/shard_map/ppermute | solution.py:737

commit v14 on v13

--- a/solution.py
+++ b/solution.py
@@ -630,28 +630,26 @@
 
 
 def bed_edge_kernel(
-    bed, side, far_a, far_b, own_m, got_m, own_e, got_e, next_in, change_in, bed_next, bed_change,
+    own, bed, side, far_a, far_b, own_m, got_m, part_e, next_in, change_in, bed_next, bed_change,
     change_v, next_v, sems,
 ):
-    rows = bed.shape[0]
-    blocks = rows // SUB
+    blocks = bed.shape[0] // SUB
     quarter = blocks // 4
-    update = Update(bed, side, far_a, far_b, own_m, got_m, own_e, got_e, change_v, next_v)
-    copies = []
-
-    def send(src, dst, low, high):
-        at = pl.ds(low * SUB, (high - low) * SUB)
-        copies.append(pltpu.make_async_copy(src.at[at], dst.at[at], sems.at[len(copies)]))
-        copies[-1].start()
-
-    update.run(0, quarter + 1, True)
-    send(change_v, bed_change, 0, quarter)
-    send(next_v, bed_next, 0, quarter + 1)
-    update.run(blocks - quarter - 1, blocks, True)
-    send(change_v, bed_change, blocks - quarter, blocks)
-    send(next_v, bed_next, blocks - quarter - 1, blocks)
-    for copy in copies:
-        copy.wait()
+    update = Update(bed, side, far_a, far_b, own_m, got_m, part_e, part_e, change_v, next_v)
+
+    def run(top):
+        rows = (0, quarter + 1) if top else (blocks - quarter - 1, blocks)
+        changes = (0, quarter) if top else (blocks - quarter, blocks)
+        update.run(*rows, True)
+        copies = []
+        for n, (src, dst, (low, high)) in enumerate(((change_v, bed_change, changes), (next_v, bed_next, rows))):
+            at = pl.ds(low * SUB, (high - low) * SUB)
+            copies.append(pltpu.make_async_copy(src.at[at], dst.at[at], sems.at[n]))
+            copies[-1].start()
+        for copy in copies:
+            copy.wait()
+
+    by_flag(lax.axis_index("cond") % 2 == (0 if own else 1), run)
 
 
 def bed_scratch(rows, cols):
@@ -675,19 +673,19 @@
     )(*held(bed, side, far_a, far_b, own_m, got_m, hydro))
 
 
-def bed_edge(bed, side, far_a, far_b, own_m, got_m, own_e, got_e, bed_next, bed_change):
+def bed_edge(own, bed, side, far_a, far_b, own_m, got_m, part_e, bed_next, bed_change):
     return pl.pallas_call(
-        bed_edge_kernel,
-        name="bed_edge",
+        functools.partial(bed_edge_kernel, own),
+        name="bed_own" if own else "bed_other",
         out_shape=[pltpu.HBM(bed.shape, jnp.float32)] * 2,
-        in_specs=[VMEM] * 8 + [ANY] * 2,
+        in_specs=[VMEM] * 7 + [ANY] * 2,
         out_specs=[ANY] * 2,
         scratch_shapes=bed_scratch(*bed.shape),
-        input_output_aliases={8: 0, 9: 1},
+        input_output_aliases={7: 0, 8: 1},
         compiler_params=pltpu.CompilerParams(vmem_limit_bytes=6 * MIB),
-        cost_estimate=cost(2),
+        cost_estimate=cost(3),
     )(
-        *held(bed, side, far_a, far_b, own_m, got_m, own_e, got_e),
+        *held(bed, side, far_a, far_b, own_m, got_m, part_e),
         *held(bed_next, bed_change, space=pltpu.HBM),
     )
 
@@ -735,9 +733,9 @@
     bed_next, bed_change, hydro = bed_middle(bed, side, far_a, far_b, own_m, got_m, hydro)
     own_e, (bed_next, bed_change) = over_chips(part_e, (bed_next, bed_change))
     got_e = lax.ppermute(own_e, "cond", swap)
-    bed_next, bed_change = bed_edge(
-        bed, side, far_a, far_b, own_m, got_m, own_e, got_e, bed_next, bed_change
-    )
+    given = (bed, side, far_a, far_b, own_m, got_m)
+    bed_next, bed_change = bed_edge(True, *given, own_e, bed_next, bed_change)
+    bed_next, bed_change = bed_edge(False, *given, got_e, bed_next, bed_change)
     return bed_next, bed_change, hydro
 
 

time: 39.2 us -> 38.5 us (0.982)
  waiting for transfers between devices: 5.83 us -> 4.65 us
  Pallas kernels: 20.1 us -> 20.5 us
    ppermute x1, waiting for transfers between devices: 1.17 us -> 0.01 us  [shards(): got_e = lax.ppermute(own_e, 'cond', swap)]
    pallas_call x1 -> x2, Pallas kernels: 1.95 us -> 2.38 us  [bed_edge(): pl.pallas_call(functools.partial(bed_edge_kernel, own), name='bed_own' if...]
  transfers between devices with their start and end apart: 9 -> 9, of which waited for: 4 -> 3; matrix products, arithmetic and copies ran while one was open for 0% -> 0% of each run, Pallas kernels for 42% -> 46%
where the time goes in v14:
time: 38.5 us; the launch traced here: 38.3 us
  Pallas kernels  20.5 us (53%)
  starting transfers between devices  12 us (31%)
  waiting for transfers between devices  4.65 us (12%)
  between operations  1 us (3%)
    pallas_call x2, Pallas kernels, edge(): pl.pallas_call(functools.partial(edge_kernel, own), name='edge_own' if ow...  5.93 us
    pallas_call x2, Pallas kernels, middle(): pl.pallas_call(functools.partial(middle_kernel, own), name='middle_own' i...  5.61 us
    ppermute x2, waiting for transfers between devices, over_chips(): got = lax.ppermute(part, 'cond', [(i, i ^ reach) for i in range(nc)])  4.07 us
    ppermute x1, starting transfers between devices, shards(): far_b = lax.ppermute(far_b, 'ty', pairs(1))  3.91 us
    ppermute x2, starting transfers between devices, shards(): got = lax.ppermute(pay, 'cond', swap)  2.7 us
    pallas_call x1, Pallas kernels, prepare(): pl.pallas_call(prepare_kernel, name='prepare', out_shape=[tile] * 4 + [pl...  2.58 us
    ppermute x2, starting transfers between devices, over_chips(): got = lax.ppermute(part, 'cond', [(i, i ^ reach) for i in range(nc)])  2.5 us
    pallas_call x2, Pallas kernels, bed_edge(): pl.pallas_call(functools.partial(bed_edge_kernel, own), name='bed_own' if...  2.38 us
  transfers between devices with their start and end apart: 9, of which 3 were waited for; matrix products, arithmetic and copies ran while one was open for 0% of the time, Pallas kernels for 46%

profile of v14, /device:TPU:9, one launch (start us, length us, event | category | flops | bytes accessed | tf_op | source)
XLA Modules:
  0.0 38.3 jit_solution(15326835102806890319)
XLA Ops:
  0.6 1.8 %pack_side.1 = f32[72,128]{1,0:T(8,128)S(1)} custom-call(f32[1,4]{1,0:T(1,128)} %params.7, f32[256,1024]{1,0:T(8,128)} %bed.3, s32[256,1024]{1,0:T(8,128)} %mask.3, s32[256,1024]{1,0:T(8,128)} %kind.3, f32[1,2,256,1024]{3,2,1,0:T(8,128)} %stress.11, f32[1,3,256,1024]{3,2,1,0:T(8,128)} %hydro.11), custom_call_target="tpu_custom_call" | custom-call | flops 2000000000 | tf_op jit(solution)/shard_map/pack_side/pallas_call | solution.py:114
  2.4 0.0 copy-start
  2.4 0.0 copy-start.1
  2.4 0.0 copy-start.2
  2.5 1.3 %collective-permute-start = (f32[72,128]{1,0:T(8,128)S(1)}, f32[72,128]{1,0:T(8,128)S(1)}, u32[]{:S(2)}, u32[]{:S(2)}) collective-permute-start(f32[72,128]{1,0:T(8,128)S(1)} %pack_side.1), channel_id=1, source_target_pairs={{0,1},{1,0},{2,3},{3,2},{4,5},{5,4},{6,7},{7,6},{8,9},{9,8},{10,11... | collective-permute-start | bytes 110600 | tf_op jit(solution)/shard_map/ppermute | solution.py:714
  3.8 2.6 %prepare.1 = (f32[256,1024]{1,0:T(8,128)S(1)}, f32[256,1024]{1,0:T(8,128)S(1)}, f32[256,1024]{1,0:T(8,128)S(1)}, f32[256,1024]{1,0:T(8,128)S(1)}, f32[272,128]{1,0:T(8,128)S(1)}, /*index=5*/f32[272,128]{1,0:T(8,128)S(1)}) custom-call(f32[1,4]{1,0:T(1,128)} %params.7, f32[256,1024]{1,0:T(8,128)} %bed.3, s32[256,1024]{1,0:T(8,128)} %mask.3, s32[256,1024]{1,0:T(8,128)} %kind.3, ...), custom_call_target="tpu_custom_call" | custom-call | flops 2000000000 | tf_op jit(solution)/shard_map/prepare/pallas_call | solution.py:203
  6.4 0.1 collective-permute-start.1
  6.5 2.8 %middle_other.1 = (f32[1,3,256,1024]{3,2,1,0:T(8,128)S(1)}, f32[520,128]{1,0:T(8,128)S(1)}) custom-call(s32[4]{0:T(128)S(1)} %copy-done.3, f32[1,4]{1,0:T(1,128)S(1)} %copy-done.2, f32[256,1024]{1,0:T(8,128)S(1)} %get-tuple-element.38.root, f32[256,1024]{1,0:T(8,128)S(1)} %get-tuple-element.39.a, f32[256,1024]{1,0:T(8,128)S(1)} %get-tuple-element.40.b, ...), custom_call_target="tpu_custom_call" | custom-call | flops 4000000000 | tf_op jit(solution)/shard_map/middle_other/pallas_call | solution.py:449
  9.3 1.2 %collective-permute-start.3 = (f32[520,128]{1,0:T(8,128)S(1)}, f32[520,128]{1,0:T(8,128)S(1)}, u32[]{:S(2)}, u32[]{:S(2)}) collective-permute-start(f32[520,128]{1,0:T(8,128)S(1)} %get-tuple-element.51), channel_id=1, source_target_pairs={{0,8},{8,0},{16,24},{24,16},{1,9},{9,1},{17,25},{25,17},{2,10},{10... | collective-permute-start | bytes 798728 | tf_op jit(solution)/shard_map/ppermute | solution.py:722
  10.5 0.4 %collective-permute-done.1.far_a = f32[272,128]{1,0:T(8,128)S(1)} collective-permute-done((f32[272,128]{1,0:T(8,128)S(1)}, f32[272,128]{1,0:T(8,128)S(1)}, u32[]{:S(2)}, u32[]{:S(2)}) %collective-permute-start.1) | collective-permute-done | bytes 139296 | tf_op jit(solution)/shard_map/ppermute | solution.py:718
  10.9 3.9 %collective-permute-start.2 = (f32[272,128]{1,0:T(8,128)S(1)}, f32[272,128]{1,0:T(8,128)S(1)}, u32[]{:S(2)}, u32[]{:S(2)}) collective-permute-start(f32[272,128]{1,0:T(8,128)S(1)} %get-tuple-element.47), channel_id=1, source_target_pairs={{0,0},{2,4},{4,2},{6,6},{1,1},{3,5},{5,3},{7,7},{8,8},{10,12},{12,... | collective-permute-start | bytes 417800 | tf_op jit(solution)/shard_map/ppermute | solution.py:721
  14.9 2.8 %middle_own.1 = (f32[1,3,256,1024]{3,2,1,0:T(8,128)S(1)}, f32[520,128]{1,0:T(8,128)S(1)}) custom-call(s32[4]{0:T(128)S(1)} %copy-done.3, f32[1,4]{1,0:T(1,128)S(1)} %copy-done.2, f32[256,1024]{1,0:T(8,128)S(1)} %get-tuple-element.38.root, f32[256,1024]{1,0:T(8,128)S(1)} %get-tuple-element.39.a, ...), custom_call_target="tpu_custom_call", output_to_operand_aliasing={{0}: (8, {})} | custom-call | flops 4000000000 | tf_op jit(solution)/shard_map/middle_own/pallas_call | solution.py:449
  17.7 1.3 %collective-permute-start.4 = (f32[520,128]{1,0:T(8,128)S(1)}, f32[520,128]{1,0:T(8,128)S(1)}, u32[]{:S(2)}, u32[]{:S(2)}) collective-permute-start(f32[520,128]{1,0:T(8,128)S(1)} %add.12), channel_id=1, source_target_pairs={{0,16},{8,24},{16,0},{24,8},{1,17},{9,25},{17,1},{25,9},{2,18},{10... | collective-permute-start | bytes 798728 | tf_op jit(solution)/shard_map/ppermute | solution.py:708
  19.0 3.0 %edge_other.1 = (f32[1,3,256,1024]{3,2,1,0:T(8,128)S(1)}, f32[528,128]{1,0:T(8,128)S(1)}) custom-call(s32[4]{0:T(128)S(1)} %copy-done.3, f32[1,4]{1,0:T(1,128)S(1)} %copy-done.2, f32[256,1024]{1,0:T(8,128)S(1)} %get-tuple-element.38.root, f32[256,1024]{1,0:T(8,128)S(1)} %get-tuple-element.39.a, ...), custom_call_target="tpu_custom_call", output_to_operand_aliasing={{0}: (10, {})} | custom-call | flops 3000000000 | tf_op jit(solution)/shard_map/edge_other/pallas_call | solution.py:521
  22.1 1.5 %collective-permute-start.5 = (f32[528,128]{1,0:T(8,128)S(1)}, f32[528,128]{1,0:T(8,128)S(1)}, u32[]{:S(2)}, u32[]{:S(2)}) collective-permute-start(f32[528,128]{1,0:T(8,128)S(1)} %get-tuple-element.58), channel_id=1, source_target_pairs={{0,8},{8,0},{16,24},{24,16},{1,9},{9,1},{17,25},{25,17},{2,10},{10... | collective-permute-start | bytes 811016 | tf_op jit(solution)/shard_map/ppermute | solution.py:727
  23.5 2.9 %edge_own.1 = (f32[1,3,256,1024]{3,2,1,0:T(8,128)S(1)}, f32[528,128]{1,0:T(8,128)S(1)}) custom-call(s32[4]{0:T(128)S(1)} %copy-done.3, f32[1,4]{1,0:T(1,128)S(1)} %copy-done.2, f32[256,1024]{1,0:T(8,128)S(1)} %get-tuple-element.38.root, f32[256,1024]{1,0:T(8,128)S(1)} %get-tuple-element.39.a, ...), custom_call_target="tpu_custom_call", output_to_operand_aliasing={{0}: (10, {})} | custom-call | flops 3000000000 | tf_op jit(solution)/shard_map/edge_own/pallas_call | solution.py:521
  26.5 0.2 collective-permute-start.6
  26.8 1.2 %collective-permute-start.7 = (f32[528,128]{1,0:T(8,128)S(1)}, f32[528,128]{1,0:T(8,128)S(1)}, u32[]{:S(2)}, u32[]{:S(2)}) collective-permute-start(f32[528,128]{1,0:T(8,128)S(1)} %add.14), channel_id=1, source_target_pairs={{0,16},{8,24},{16,0},{24,8},{1,17},{9,25},{17,1},{25,9},{2,18},{10... | collective-permute-start | bytes 811016 | tf_op jit(solution)/shard_map/ppermute | solution.py:708
  28.0 0.2 collective-permute-done.6.got_m
  28.2 2.2 %bed_middle.1 = (f32[256,1024]{1,0:T(8,128)}, f32[256,1024]{1,0:T(8,128)}, f32[1,3,256,1024]{3,2,1,0:T(8,128)}) custom-call(f32[256,1024]{1,0:T(8,128)S(1)} %get-tuple-element.37.bed, f32[72,128]{1,0:T(8,128)S(1)} %collective-permute-done.side, f32[272,128]{1,0:T(8,128)S(1)} %collective-permute-done.1.far_a, f32[272,128]{1,0:T(8,128)S(1)} %collective-permute-done.2.far_b, ...), custom_call_target="tpu_custom_call" | custom-call | flops 4000000000 | tf_op jit(solution)/shard_map/bed_middle/pallas_call | solution.py:664
  30.4 4.1 %collective-permute-done.7 = f32[528,128]{1,0:T(8,128)S(1)} collective-permute-done((f32[528,128]{1,0:T(8,128)S(1)}, f32[528,128]{1,0:T(8,128)S(1)}, u32[]{:S(2)}, u32[]{:S(2)}) %collective-permute-start.7) | collective-permute-done | bytes 270368 | tf_op jit(solution)/shard_map/ppermute | solution.py:708
  34.5 1.2 %collective-permute-start.8 = (f32[528,128]{1,0:T(8,128)S(1)}, f32[528,128]{1,0:T(8,128)S(1)}, u32[]{:S(2)}, u32[]{:S(2)}) collective-permute-start(f32[528,128]{1,0:T(8,128)S(1)} %add.15.part_e), channel_id=1, source_target_pairs={{0,8},{8,0},{16,24},{24,16},{1,9},{9,1},{17,25},{25,17},{2,10},{10... | collective-permute-start | bytes 811016 | tf_op jit(solution)/shard_map/ppermute | solution.py:735
  35.8 1.2 %bed_own.1 = (f32[256,1024]{1,0:T(8,128)}, f32[256,1024]{1,0:T(8,128)}) custom-call(f32[256,1024]{1,0:T(8,128)S(1)} %get-tuple-element.37.bed, f32[72,128]{1,0:T(8,128)S(1)} %collective-permute-done.side, f32[272,128]{1,0:T(8,128)S(1)} %collective-permute-done.1.far_a, ...), custom_call_target="tpu_custom_call", output_to_operand_aliasing={{0}: (7, {}), {1}: (8, {})} | custom-call | flops 3000000000 | tf_op jit(solution)/shard_map/bed_own/pallas_call | solution.py:677
  37.0 1.2 %bed_other.1 = (f32[256,1024]{1,0:T(8,128)}, f32[256,1024]{1,0:T(8,128)}) custom-call(f32[256,1024]{1,0:T(8,128)S(1)} %get-tuple-element.37.bed, f32[72,128]{1,0:T(8,128)S(1)} %collective-permute-done.side, f32[272,128]{1,0:T(8,128)S(1)} %collective-permute-done.1.far_a, ...), custom_call_target="tpu_custom_call", output_to_operand_aliasing={{0}: (7, {}), {1}: (8, {})} | custom-call | flops 3000000000 | tf_op jit(solution)/shard_map/bed_other/pallas_call | solution.py:677
  (16 shorter events, 0.2 us)
Async XLA Ops:
  2.4 4.1 %copy-start = (f32[1,3,256,1024]{3,2,1,0:T(8,128)S(1)}, f32[1,3,256,1024]{3,2,1,0:T(8,128)}, u32[]{:S(2)}) copy-start(f32[1,3,256,1024]{3,2,1,0:T(8,128)} %hydro.11) | copy-start | bytes 9437188
  2.4 4.1 %copy-start.1 = (f32[1,2,256,1024]{3,2,1,0:T(8,128)S(1)}, f32[1,2,256,1024]{3,2,1,0:T(8,128)}, u32[]{:S(2)}) copy-start(f32[1,2,256,1024]{3,2,1,0:T(8,128)} %stress.11) | copy-start | bytes 6291460
  2.4 4.1 %copy-start.2 = (f32[1,4]{1,0:T(1,128)S(1)}, f32[1,4]{1,0:T(1,128)}, u32[]{:S(2)}) copy-start(f32[1,4]{1,0:T(1,128)} %params.7) | copy-start | bytes 52
  2.4 4.1 %copy-start.3 = (s32[4]{0:T(128)S(1)}, s32[4]{0:T(128)}, u32[]{:S(2)}) copy-start(s32[4]{0:T(128)} %weights.7) | copy-start | bytes 52
  2.5 3.9 %collective-permute-start = (f32[72,128]{1,0:T(8,128)S(1)}, f32[72,128]{1,0:T(8,128)S(1)}, u32[]{:S(2)}, u32[]{:S(2)}) collective-permute-start(f32[72,128]{1,0:T(8,128)S(1)} %pack_side.1), channel_id=1, source_target_pairs={{0,1},{1,0},{2,3},{3,2},{4,5},{5,4},{6,7},{7,6},{8,9},{9,8},{10,11... | collective-permute-start | bytes 110600 | tf_op jit(solution)/shard_map/ppermute | solution.py:714
  6.4 4.6 %collective-permute-start.1 = (f32[272,128]{1,0:T(8,128)S(1)}, f32[272,128]{1,0:T(8,128)S(1)}, u32[]{:S(2)}, u32[]{:S(2)}) collective-permute-start(f32[272,128]{1,0:T(8,128)S(1)} %get-tuple-element.44), channel_id=1, source_target_pairs={{0,2},{2,0},{4,6},{6,4},{1,3},{3,1},{5,7},{7,5},{8,10},{10,8},{12,... | collective-permute-start | bytes 417800 | tf_op jit(solution)/shard_map/ppermute | solution.py:718
  9.3 8.4 %collective-permute-start.3 = (f32[520,128]{1,0:T(8,128)S(1)}, f32[520,128]{1,0:T(8,128)S(1)}, u32[]{:S(2)}, u32[]{:S(2)}) collective-permute-start(f32[520,128]{1,0:T(8,128)S(1)} %get-tuple-element.51), channel_id=1, source_target_pairs={{0,8},{8,0},{16,24},{24,16},{1,9},{9,1},{17,25},{25,17},{2,10},{10... | collective-permute-start | bytes 798728 | tf_op jit(solution)/shard_map/ppermute | solution.py:722
  10.9 8.1 %collective-permute-start.2 = (f32[272,128]{1,0:T(8,128)S(1)}, f32[272,128]{1,0:T(8,128)S(1)}, u32[]{:S(2)}, u32[]{:S(2)}) collective-permute-start(f32[272,128]{1,0:T(8,128)S(1)} %get-tuple-element.47), channel_id=1, source_target_pairs={{0,0},{2,4},{4,2},{6,6},{1,1},{3,5},{5,3},{7,7},{8,8},{10,12},{12,... | collective-permute-start | bytes 417800 | tf_op jit(solution)/shard_map/ppermute | solution.py:721
  17.7 8.7 %collective-permute-start.4 = (f32[520,128]{1,0:T(8,128)S(1)}, f32[520,128]{1,0:T(8,128)S(1)}, u32[]{:S(2)}, u32[]{:S(2)}) collective-permute-start(f32[520,128]{1,0:T(8,128)S(1)} %add.12), channel_id=1, source_target_pairs={{0,16},{8,24},{16,0},{24,8},{1,17},{9,25},{17,1},{25,9},{2,18},{10... | collective-permute-start | bytes 798728 | tf_op jit(solution)/shard_map/ppermute | solution.py:708
  22.1 4.4 %collective-permute-start.5 = (f32[528,128]{1,0:T(8,128)S(1)}, f32[528,128]{1,0:T(8,128)S(1)}, u32[]{:S(2)}, u32[]{:S(2)}) collective-permute-start(f32[528,128]{1,0:T(8,128)S(1)} %get-tuple-element.58), channel_id=1, source_target_pairs={{0,8},{8,0},{16,24},{24,16},{1,9},{9,1},{17,25},{25,17},{2,10},{10... | collective-permute-start | bytes 811016 | tf_op jit(solution)/shard_map/ppermute | solution.py:727
  26.5 1.6 %collective-permute-start.6 = (f32[520,128]{1,0:T(8,128)S(1)}, f32[520,128]{1,0:T(8,128)S(1)}, u32[]{:S(2)}, u32[]{:S(2)}) collective-permute-start(f32[520,128]{1,0:T(8,128)S(1)} %add.13.own_m), channel_id=1, source_target_pairs={{0,8},{8,0},{16,24},{24,16},{1,9},{9,1},{17,25},{25,17},{2,10},{10... | collective-permute-start | bytes 798728 | tf_op jit(solution)/shard_map/ppermute | solution.py:732
  26.8 7.7 %collective-permute-start.7 = (f32[528,128]{1,0:T(8,128)S(1)}, f32[528,128]{1,0:T(8,128)S(1)}, u32[]{:S(2)}, u32[]{:S(2)}) collective-permute-start(f32[528,128]{1,0:T(8,128)S(1)} %add.14), channel_id=1, source_target_pairs={{0,16},{8,24},{16,0},{24,8},{1,17},{9,25},{17,1},{25,9},{2,18},{10... | collective-permute-start | bytes 811016 | tf_op jit(solution)/shard_map/ppermute | solution.py:708
  34.5 2.4 %collective-permute-start.8 = (f32[528,128]{1,0:T(8,128)S(1)}, f32[528,128]{1,0:T(8,128)S(1)}, u32[]{:S(2)}, u32[]{:S(2)}) collective-permute-start(f32[528,128]{1,0:T(8,128)S(1)} %add.15.part_e), channel_id=1, source_target_pairs={{0,8},{8,0},{16,24},{24,16},{1,9},{9,1},{17,25},{25,17},{2,10},{10... | collective-permute-start | bytes 811016 | tf_op jit(solution)/shard_map/ppermute | solution.py:735

commit v15 on v14

--- a/solution.py
+++ b/solution.py
@@ -265,8 +265,9 @@
         + ["v1", "e2", "u2", "v2", "qc1", "qr1", "qc2", "qr2"]
     )
 
-    def __init__(self, count, wide, get, emit, weights, params, refs, trim):
-        self.count, self.wide, self.get, self.emit, self.trim = count, wide, get, emit, trim
+    def __init__(self, count, wide, get, emit, weights, params, refs, trim_first, trim_last):
+        self.count, self.wide, self.get, self.emit = count, wide, get, emit
+        self.trim_first, self.trim_last = trim_first, trim_last
         self.__dict__.update(zip(self.NAMES + ["fr_last", "qr_last"], refs))
         cond = lax.axis_index("cond")
         self.slow = 1.0 - 0.2 * params[0, 1]
@@ -340,7 +341,7 @@
         at, after = tile_at(i), tile_at(i + 1)
 
         def rest(u, v):
-            if not (self.trim and i == self.count - 1):
+            if not (self.trim_last and i == self.count - 1):
                 self.u2[at, :] = u
                 self.v2[at, :] = v
                 self.qc2[at, :] = self.qc1[at, :] + u * jnp.abs(u)
@@ -354,9 +355,9 @@
 
     def step_three(self, i):
         at, after = tile_at(i), tile_at(i + 1)
-        if self.trim and i == self.count - 1:
+        if self.trim_last and i == self.count - 1:
             return
-        if self.trim and i == 0:
+        if self.trim_first and i == 0:
             wr = self.wr[at, :]
             v = self.speed_r(i, self.e2[at, :], self.e2[after, :], self.v2[at, :], wr)
             self.fr_last[2] = self.fr[at, :] * v
@@ -438,7 +439,7 @@
         first = (2 * quarter if lower_half else quarter) - 1
         emit = quarter_writer(first, quarter, cols, hydro_out, pay)
         get = lambda f, i: read(f, first + i)
-        Sweep(quarter + 2, cols + LANE, get, emit, weights, params, refs, True).run()
+        Sweep(quarter + 2, cols + LANE, get, emit, weights, params, refs, True, True).run()
 
     by_flag(lax.axis_index("cond") % 2 == (1 if own else 0), run)
 
@@ -510,7 +511,9 @@
                 rim = change[:, :cols]
                 pay[tile_at(lanes * quarter + 1), :] = fold_row(pltpu.roll(rim, 1, 0) if top else rim)
 
-        Sweep(quarter + 2, cols + LANE, get, finish, weights, params, refs, False).run()
+        Sweep(
+            quarter + 2, cols + LANE, get, finish, weights, params, refs, not top, top
+        ).run()
 
     by_flag(lax.axis_index("cond") % 2 == (0 if own else 1), run)
 

time: 38.5 us -> 38.5 us (level)
  no operation moved by 1% of the time
where the time goes in v15:
time: 38.5 us; the launch traced here: 38.3 us
  Pallas kernels  20.5 us (53%)
  starting transfers between devices  12 us (31%)
  waiting for transfers between devices  4.65 us (12%)
  between operations  1 us (3%)
    pallas_call x2, Pallas kernels, edge(): pl.pallas_call(functools.partial(edge_kernel, own), name='edge_own' if ow...  5.91 us
    pallas_call x2, Pallas kernels, middle(): pl.pallas_call(functools.partial(middle_kernel, own), name='middle_own' i...  5.61 us
    ppermute x2, waiting for transfers between devices, over_chips(): got = lax.ppermute(part, 'cond', [(i, i ^ reach) for i in range(nc)])  4.07 us
    ppermute x1, starting transfers between devices, shards(): far_b = lax.ppermute(far_b, 'ty', pairs(1))  3.91 us
    ppermute x2, starting transfers between devices, shards(): got = lax.ppermute(pay, 'cond', swap)  2.72 us
    pallas_call x1, Pallas kernels, prepare(): pl.pallas_call(prepare_kernel, name='prepare', out_shape=[tile] * 4 + [pl...  2.58 us
    ppermute x2, starting transfers between devices, over_chips(): got = lax.ppermute(part, 'cond', [(i, i ^ reach) for i in range(nc)])  2.5 us
    pallas_call x2, Pallas kernels, bed_edge(): pl.pallas_call(functools.partial(bed_edge_kernel, own), name='bed_own' if...  2.38 us
  transfers between devices with their start and end apart: 9, of which 3 were waited for; matrix products, arithmetic and copies ran while one was open for 0% of the time, Pallas kernels for 46%

profile of v15, /device:TPU:9, one launch (start us, length us, event | category | flops | bytes accessed | tf_op | source)
XLA Modules:
  0.0 38.3 jit_solution(10778546873317902782)
XLA Ops:
  0.6 1.8 %pack_side.1 = f32[72,128]{1,0:T(8,128)S(1)} custom-call(f32[1,4]{1,0:T(1,128)} %params.7, f32[256,1024]{1,0:T(8,128)} %bed.3, s32[256,1024]{1,0:T(8,128)} %mask.3, s32[256,1024]{1,0:T(8,128)} %kind.3, f32[1,2,256,1024]{3,2,1,0:T(8,128)} %stress.11, f32[1,3,256,1024]{3,2,1,0:T(8,128)} %hydro.11), custom_call_target="tpu_custom_call" | custom-call | flops 2000000000 | tf_op jit(solution)/shard_map/pack_side/pallas_call | solution.py:114
  2.4 0.0 copy-start
  2.4 0.0 copy-start.1
  2.4 0.0 copy-start.2
  2.5 1.3 %collective-permute-start = (f32[72,128]{1,0:T(8,128)S(1)}, f32[72,128]{1,0:T(8,128)S(1)}, u32[]{:S(2)}, u32[]{:S(2)}) collective-permute-start(f32[72,128]{1,0:T(8,128)S(1)} %pack_side.1), channel_id=1, source_target_pairs={{0,1},{1,0},{2,3},{3,2},{4,5},{5,4},{6,7},{7,6},{8,9},{9,8},{10,11... | collective-permute-start | bytes 110600 | tf_op jit(solution)/shard_map/ppermute | solution.py:717
  3.8 2.6 %prepare.1 = (f32[256,1024]{1,0:T(8,128)S(1)}, f32[256,1024]{1,0:T(8,128)S(1)}, f32[256,1024]{1,0:T(8,128)S(1)}, f32[256,1024]{1,0:T(8,128)S(1)}, f32[272,128]{1,0:T(8,128)S(1)}, /*index=5*/f32[272,128]{1,0:T(8,128)S(1)}) custom-call(f32[1,4]{1,0:T(1,128)} %params.7, f32[256,1024]{1,0:T(8,128)} %bed.3, s32[256,1024]{1,0:T(8,128)} %mask.3, s32[256,1024]{1,0:T(8,128)} %kind.3, ...), custom_call_target="tpu_custom_call" | custom-call | flops 2000000000 | tf_op jit(solution)/shard_map/prepare/pallas_call | solution.py:203
  6.4 0.1 collective-permute-start.1
  6.5 2.8 %middle_other.1 = (f32[1,3,256,1024]{3,2,1,0:T(8,128)S(1)}, f32[520,128]{1,0:T(8,128)S(1)}) custom-call(s32[4]{0:T(128)S(1)} %copy-done.3, f32[1,4]{1,0:T(1,128)S(1)} %copy-done.2, f32[256,1024]{1,0:T(8,128)S(1)} %get-tuple-element.38.root, f32[256,1024]{1,0:T(8,128)S(1)} %get-tuple-element.39.a, f32[256,1024]{1,0:T(8,128)S(1)} %get-tuple-element.40.b, ...), custom_call_target="tpu_custom_call" | custom-call | flops 4000000000 | tf_op jit(solution)/shard_map/middle_other/pallas_call | solution.py:450
  9.3 1.2 %collective-permute-start.3 = (f32[520,128]{1,0:T(8,128)S(1)}, f32[520,128]{1,0:T(8,128)S(1)}, u32[]{:S(2)}, u32[]{:S(2)}) collective-permute-start(f32[520,128]{1,0:T(8,128)S(1)} %get-tuple-element.51), channel_id=1, source_target_pairs={{0,8},{8,0},{16,24},{24,16},{1,9},{9,1},{17,25},{25,17},{2,10},{10... | collective-permute-start | bytes 798728 | tf_op jit(solution)/shard_map/ppermute | solution.py:725
  10.5 0.4 %collective-permute-done.1.far_a = f32[272,128]{1,0:T(8,128)S(1)} collective-permute-done((f32[272,128]{1,0:T(8,128)S(1)}, f32[272,128]{1,0:T(8,128)S(1)}, u32[]{:S(2)}, u32[]{:S(2)}) %collective-permute-start.1) | collective-permute-done | bytes 139296 | tf_op jit(solution)/shard_map/ppermute | solution.py:721
  10.9 3.9 %collective-permute-start.2 = (f32[272,128]{1,0:T(8,128)S(1)}, f32[272,128]{1,0:T(8,128)S(1)}, u32[]{:S(2)}, u32[]{:S(2)}) collective-permute-start(f32[272,128]{1,0:T(8,128)S(1)} %get-tuple-element.47), channel_id=1, source_target_pairs={{0,0},{2,4},{4,2},{6,6},{1,1},{3,5},{5,3},{7,7},{8,8},{10,12},{12,... | collective-permute-start | bytes 417800 | tf_op jit(solution)/shard_map/ppermute | solution.py:724
  14.9 2.8 %middle_own.1 = (f32[1,3,256,1024]{3,2,1,0:T(8,128)S(1)}, f32[520,128]{1,0:T(8,128)S(1)}) custom-call(s32[4]{0:T(128)S(1)} %copy-done.3, f32[1,4]{1,0:T(1,128)S(1)} %copy-done.2, f32[256,1024]{1,0:T(8,128)S(1)} %get-tuple-element.38.root, f32[256,1024]{1,0:T(8,128)S(1)} %get-tuple-element.39.a, ...), custom_call_target="tpu_custom_call", output_to_operand_aliasing={{0}: (8, {})} | custom-call | flops 4000000000 | tf_op jit(solution)/shard_map/middle_own/pallas_call | solution.py:450
  17.7 1.3 %collective-permute-start.4 = (f32[520,128]{1,0:T(8,128)S(1)}, f32[520,128]{1,0:T(8,128)S(1)}, u32[]{:S(2)}, u32[]{:S(2)}) collective-permute-start(f32[520,128]{1,0:T(8,128)S(1)} %add.12), channel_id=1, source_target_pairs={{0,16},{8,24},{16,0},{24,8},{1,17},{9,25},{17,1},{25,9},{2,18},{10... | collective-permute-start | bytes 798728 | tf_op jit(solution)/shard_map/ppermute | solution.py:711
  19.0 3.0 %edge_other.1 = (f32[1,3,256,1024]{3,2,1,0:T(8,128)S(1)}, f32[528,128]{1,0:T(8,128)S(1)}) custom-call(s32[4]{0:T(128)S(1)} %copy-done.3, f32[1,4]{1,0:T(1,128)S(1)} %copy-done.2, f32[256,1024]{1,0:T(8,128)S(1)} %get-tuple-element.38.root, f32[256,1024]{1,0:T(8,128)S(1)} %get-tuple-element.39.a, ...), custom_call_target="tpu_custom_call", output_to_operand_aliasing={{0}: (10, {})} | custom-call | flops 3000000000 | tf_op jit(solution)/shard_map/edge_other/pallas_call | solution.py:524
  22.0 1.5 %collective-permute-start.5 = (f32[528,128]{1,0:T(8,128)S(1)}, f32[528,128]{1,0:T(8,128)S(1)}, u32[]{:S(2)}, u32[]{:S(2)}) collective-permute-start(f32[528,128]{1,0:T(8,128)S(1)} %get-tuple-element.58), channel_id=1, source_target_pairs={{0,8},{8,0},{16,24},{24,16},{1,9},{9,1},{17,25},{25,17},{2,10},{10... | collective-permute-start | bytes 811016 | tf_op jit(solution)/shard_map/ppermute | solution.py:730
  23.5 2.9 %edge_own.1 = (f32[1,3,256,1024]{3,2,1,0:T(8,128)S(1)}, f32[528,128]{1,0:T(8,128)S(1)}) custom-call(s32[4]{0:T(128)S(1)} %copy-done.3, f32[1,4]{1,0:T(1,128)S(1)} %copy-done.2, f32[256,1024]{1,0:T(8,128)S(1)} %get-tuple-element.38.root, f32[256,1024]{1,0:T(8,128)S(1)} %get-tuple-element.39.a, ...), custom_call_target="tpu_custom_call", output_to_operand_aliasing={{0}: (10, {})} | custom-call | flops 3000000000 | tf_op jit(solution)/shard_map/edge_own/pallas_call | solution.py:524
  26.5 0.2 collective-permute-start.6
  26.8 1.2 %collective-permute-start.7 = (f32[528,128]{1,0:T(8,128)S(1)}, f32[528,128]{1,0:T(8,128)S(1)}, u32[]{:S(2)}, u32[]{:S(2)}) collective-permute-start(f32[528,128]{1,0:T(8,128)S(1)} %add.14), channel_id=1, source_target_pairs={{0,16},{8,24},{16,0},{24,8},{1,17},{9,25},{17,1},{25,9},{2,18},{10... | collective-permute-start | bytes 811016 | tf_op jit(solution)/shard_map/ppermute | solution.py:711
  28.0 0.2 collective-permute-done.6.got_m
  28.2 2.2 %bed_middle.1 = (f32[256,1024]{1,0:T(8,128)}, f32[256,1024]{1,0:T(8,128)}, f32[1,3,256,1024]{3,2,1,0:T(8,128)}) custom-call(f32[256,1024]{1,0:T(8,128)S(1)} %get-tuple-element.37.bed, f32[72,128]{1,0:T(8,128)S(1)} %collective-permute-done.side, f32[272,128]{1,0:T(8,128)S(1)} %collective-permute-done.1.far_a, f32[272,128]{1,0:T(8,128)S(1)} %collective-permute-done.2.far_b, ...), custom_call_target="tpu_custom_call" | custom-call | flops 4000000000 | tf_op jit(solution)/shard_map/bed_middle/pallas_call | solution.py:667
  30.4 4.1 %collective-permute-done.7 = f32[528,128]{1,0:T(8,128)S(1)} collective-permute-done((f32[528,128]{1,0:T(8,128)S(1)}, f32[528,128]{1,0:T(8,128)S(1)}, u32[]{:S(2)}, u32[]{:S(2)}) %collective-permute-start.7) | collective-permute-done | bytes 270368 | tf_op jit(solution)/shard_map/ppermute | solution.py:711
  34.5 1.2 %collective-permute-start.8 = (f32[528,128]{1,0:T(8,128)S(1)}, f32[528,128]{1,0:T(8,128)S(1)}, u32[]{:S(2)}, u32[]{:S(2)}) collective-permute-start(f32[528,128]{1,0:T(8,128)S(1)} %add.15.part_e), channel_id=1, source_target_pairs={{0,8},{8,0},{16,24},{24,16},{1,9},{9,1},{17,25},{25,17},{2,10},{10... | collective-permute-start | bytes 811016 | tf_op jit(solution)/shard_map/ppermute | solution.py:738
  35.8 1.2 %bed_own.1 = (f32[256,1024]{1,0:T(8,128)}, f32[256,1024]{1,0:T(8,128)}) custom-call(f32[256,1024]{1,0:T(8,128)S(1)} %get-tuple-element.37.bed, f32[72,128]{1,0:T(8,128)S(1)} %collective-permute-done.side, f32[272,128]{1,0:T(8,128)S(1)} %collective-permute-done.1.far_a, ...), custom_call_target="tpu_custom_call", output_to_operand_aliasing={{0}: (7, {}), {1}: (8, {})} | custom-call | flops 3000000000 | tf_op jit(solution)/shard_map/bed_own/pallas_call | solution.py:680
  37.0 1.2 %bed_other.1 = (f32[256,1024]{1,0:T(8,128)}, f32[256,1024]{1,0:T(8,128)}) custom-call(f32[256,1024]{1,0:T(8,128)S(1)} %get-tuple-element.37.bed, f32[72,128]{1,0:T(8,128)S(1)} %collective-permute-done.side, f32[272,128]{1,0:T(8,128)S(1)} %collective-permute-done.1.far_a, ...), custom_call_target="tpu_custom_call", output_to_operand_aliasing={{0}: (7, {}), {1}: (8, {})} | custom-call | flops 3000000000 | tf_op jit(solution)/shard_map/bed_other/pallas_call | solution.py:680
  (16 shorter events, 0.2 us)
Async XLA Ops:
  2.4 4.1 %copy-start = (f32[1,3,256,1024]{3,2,1,0:T(8,128)S(1)}, f32[1,3,256,1024]{3,2,1,0:T(8,128)}, u32[]{:S(2)}) copy-start(f32[1,3,256,1024]{3,2,1,0:T(8,128)} %hydro.11) | copy-start | bytes 9437188
  2.4 4.1 %copy-start.1 = (f32[1,2,256,1024]{3,2,1,0:T(8,128)S(1)}, f32[1,2,256,1024]{3,2,1,0:T(8,128)}, u32[]{:S(2)}) copy-start(f32[1,2,256,1024]{3,2,1,0:T(8,128)} %stress.11) | copy-start | bytes 6291460
  2.4 4.1 %copy-start.2 = (f32[1,4]{1,0:T(1,128)S(1)}, f32[1,4]{1,0:T(1,128)}, u32[]{:S(2)}) copy-start(f32[1,4]{1,0:T(1,128)} %params.7) | copy-start | bytes 52
  2.4 4.1 %copy-start.3 = (s32[4]{0:T(128)S(1)}, s32[4]{0:T(128)}, u32[]{:S(2)}) copy-start(s32[4]{0:T(128)} %weights.7) | copy-start | bytes 52
  2.5 3.9 %collective-permute-start = (f32[72,128]{1,0:T(8,128)S(1)}, f32[72,128]{1,0:T(8,128)S(1)}, u32[]{:S(2)}, u32[]{:S(2)}) collective-permute-start(f32[72,128]{1,0:T(8,128)S(1)} %pack_side.1), channel_id=1, source_target_pairs={{0,1},{1,0},{2,3},{3,2},{4,5},{5,4},{6,7},{7,6},{8,9},{9,8},{10,11... | collective-permute-start | bytes 110600 | tf_op jit(solution)/shard_map/ppermute | solution.py:717
  6.4 4.6 %collective-permute-start.1 = (f32[272,128]{1,0:T(8,128)S(1)}, f32[272,128]{1,0:T(8,128)S(1)}, u32[]{:S(2)}, u32[]{:S(2)}) collective-permute-start(f32[272,128]{1,0:T(8,128)S(1)} %get-tuple-element.44), channel_id=1, source_target_pairs={{0,2},{2,0},{4,6},{6,4},{1,3},{3,1},{5,7},{7,5},{8,10},{10,8},{12,... | collective-permute-start | bytes 417800 | tf_op jit(solution)/shard_map/ppermute | solution.py:721
  9.3 8.4 %collective-permute-start.3 = (f32[520,128]{1,0:T(8,128)S(1)}, f32[520,128]{1,0:T(8,128)S(1)}, u32[]{:S(2)}, u32[]{:S(2)}) collective-permute-start(f32[520,128]{1,0:T(8,128)S(1)} %get-tuple-element.51), channel_id=1, source_target_pairs={{0,8},{8,0},{16,24},{24,16},{1,9},{9,1},{17,25},{25,17},{2,10},{10... | collective-permute-start | bytes 798728 | tf_op jit(solution)/shard_map/ppermute | solution.py:725
  10.9 8.1 %collective-permute-start.2 = (f32[272,128]{1,0:T(8,128)S(1)}, f32[272,128]{1,0:T(8,128)S(1)}, u32[]{:S(2)}, u32[]{:S(2)}) collective-permute-start(f32[272,128]{1,0:T(8,128)S(1)} %get-tuple-element.47), channel_id=1, source_target_pairs={{0,0},{2,4},{4,2},{6,6},{1,1},{3,5},{5,3},{7,7},{8,8},{10,12},{12,... | collective-permute-start | bytes 417800 | tf_op jit(solution)/shard_map/ppermute | solution.py:724
  17.7 8.7 %collective-permute-start.4 = (f32[520,128]{1,0:T(8,128)S(1)}, f32[520,128]{1,0:T(8,128)S(1)}, u32[]{:S(2)}, u32[]{:S(2)}) collective-permute-start(f32[520,128]{1,0:T(8,128)S(1)} %add.12), channel_id=1, source_target_pairs={{0,16},{8,24},{16,0},{24,8},{1,17},{9,25},{17,1},{25,9},{2,18},{10... | collective-permute-start | bytes 798728 | tf_op jit(solution)/shard_map/ppermute | solution.py:711
  22.0 4.5 %collective-permute-start.5 = (f32[528,128]{1,0:T(8,128)S(1)}, f32[528,128]{1,0:T(8,128)S(1)}, u32[]{:S(2)}, u32[]{:S(2)}) collective-permute-start(f32[528,128]{1,0:T(8,128)S(1)} %get-tuple-element.58), channel_id=1, source_target_pairs={{0,8},{8,0},{16,24},{24,16},{1,9},{9,1},{17,25},{25,17},{2,10},{10... | collective-permute-start | bytes 811016 | tf_op jit(solution)/shard_map/ppermute | solution.py:730
  26.5 1.6 %collective-permute-start.6 = (f32[520,128]{1,0:T(8,128)S(1)}, f32[520,128]{1,0:T(8,128)S(1)}, u32[]{:S(2)}, u32[]{:S(2)}) collective-permute-start(f32[520,128]{1,0:T(8,128)S(1)} %add.13.own_m), channel_id=1, source_target_pairs={{0,8},{8,0},{16,24},{24,16},{1,9},{9,1},{17,25},{25,17},{2,10},{10... | collective-permute-start | bytes 798728 | tf_op jit(solution)/shard_map/ppermute | solution.py:735
  26.8 7.7 %collective-permute-start.7 = (f32[528,128]{1,0:T(8,128)S(1)}, f32[528,128]{1,0:T(8,128)S(1)}, u32[]{:S(2)}, u32[]{:S(2)}) collective-permute-start(f32[528,128]{1,0:T(8,128)S(1)} %add.14), channel_id=1, source_target_pairs={{0,16},{8,24},{16,0},{24,8},{1,17},{9,25},{17,1},{25,9},{2,18},{10... | collective-permute-start | bytes 811016 | tf_op jit(solution)/shard_map/ppermute | solution.py:711
  34.5 2.4 %collective-permute-start.8 = (f32[528,128]{1,0:T(8,128)S(1)}, f32[528,128]{1,0:T(8,128)S(1)}, u32[]{:S(2)}, u32[]{:S(2)}) collective-permute-start(f32[528,128]{1,0:T(8,128)S(1)} %add.15.part_e), channel_id=1, source_target_pairs={{0,8},{8,0},{16,24},{24,16},{1,9},{9,1},{17,25},{25,17},{2,10},{10... | collective-permute-start | bytes 811016 | tf_op jit(solution)/shard_map/ppermute | solution.py:738
